TPU v7x, 32 devices: a whole 2x2x4 slice. The times are simulated.
32 devices in a mesh: img: 4 (over y, x), ha: 4 (over z), wa: 2 (over core).
Axes of the slice: x: 2, y: 2, z: 4, core: 2. Of those that a mesh axis runs over, the one named last changes fastest.
Arguments:
- images: bfloat16 [16, 64, 32, 512], P('img', 'ha', 'wa'), may hold values from -32 to 32
- cot_shared: bfloat16 [16, 32, 16, 512], P('img', 'ha', 'wa'), may hold values from -32 to 32
- cot_tasks: bfloat16 [16, 32, 16, 1536], P('img', 'ha', 'wa'), may hold values from -32 to 32
- depth_mask: int32 [16, 32, 16], P('img', 'ha', 'wa'), may hold values 0 or 1
- nash_weights: float32 [3], replicated, may hold values from 0.5 to 2
- conv_weight: float32 [16, 45, 128, 128], P(('img', 'ha')), may hold values from -0.09375 to 0.09375
- conv_left: float32 [16, 45, 128, 128], P(('img', 'ha')), as said below
- conv_right: float32 [16, 45, 128, 128], P(('img', 'ha')), as said below
- conv_left_root: float32 [16, 45, 128, 128], P(('img', 'ha')), as said below
- conv_right_root: float32 [16, 45, 128, 128], P(('img', 'ha')), as said below
- proj_weight: float32 [3, 2, 4, 128, 128], replicated
- proj_left: float32 [3, 2, 4, 128, 128], replicated, as said below
- proj_right: float32 [3, 2, 4, 128, 128], replicated, as said below
- proj_left_root: float32 [3, 2, 4, 128, 128], replicated, as said below
- proj_right_root: float32 [3, 2, 4, 128, 128], replicated, as said below
- norm_params: float32 [2, 2944], replicated
- norm_moment: float32 [2, 2944], replicated, as said below
Outputs:
- shared_out: bfloat16 [16, 32, 16, 512], P('img', 'ha', 'wa')
- task_out: bfloat16 [16, 32, 16, 1536], P('img', 'ha', 'wa')
- image_grad: bfloat16 [16, 64, 32, 512], P('img', 'ha', 'wa')
- gram: float32 [3, 3], replicated
- conv_grad: float32 [16, 45, 128, 128], P(('img', 'ha'))
- conv_left_new: float32 [16, 45, 128, 128], P(('img', 'ha'))
- conv_right_new: float32 [16, 45, 128, 128], P(('img', 'ha'))
- conv_weight_new: float32 [16, 45, 128, 128], P(('img', 'ha'))
- proj_grad: float32 [3, 2, 4, 128, 128], replicated
- proj_left_new: float32 [3, 2, 4, 128, 128], replicated
- proj_right_new: float32 [3, 2, 4, 128, 128], replicated
- proj_weight_new: float32 [3, 2, 4, 128, 128], replicated
- norm_grad: float32 [2, 2944], replicated
- norm_moment_new: float32 [2, 2944], replicated
- norm_new: float32 [2, 2944], replicated
Inputs may be any that keep to these rules, and one draw needn't show every extreme that they name: `conv_left`: symmetric. `conv_right`: symmetric. `conv_left_root`: symmetric. `conv_right_root`: symmetric. `proj_left`: symmetric. `proj_right`: symmetric. `proj_left_root`: symmetric. `proj_right_root`: symmetric. `norm_moment`: positive.
All inputs are finite; a program needn't handle non-finite values. No bound on the sum of `depth_mask` on one device may be relied on, other than what follows from the above.
Results may differ from a plain program's by a relative error of at most 0.015.
Values may be sent and summed in bfloat16 or wider, within the bound.
No kernel may reach another device: no remote copies, remote signals or barrier semaphores. Data moves between devices by JAX's collectives and lax.ppermute only.
A program may use at most 384 MiB of HBM per device.

v0:
```python
import jax
import jax.numpy as jnp
from jax import lax
from jax.sharding import PartitionSpec as P

C = 512
CA = 128
TASKS = 3
BLK = 128


eps_norm = 1e-05
conv_rate = 0.08
proj_rate = 0.2
norm_rate = 0.1
stat_decay = 0.9
moment_decay = 0.95
highest = lax.Precision.HIGHEST


def padded_2(block, sides, width):
    for axis, dim in sides:
        count = lax.axis_size(axis)
        forward = [(i, i + 1) for i in range(count - 1)]
        backward = [(target, source) for source, target in forward]
        low = lax.ppermute(
            lax.slice_in_dim(block, block.shape[dim] - width, None, axis=dim), axis, forward
        )
        high = lax.ppermute(lax.slice_in_dim(block, 0, width, axis=dim), axis, backward)
        block = jnp.concatenate([low, block, high], axis=dim)
    return block


def padded_tile(field):
    return padded_2(field, (("ha", 1), ("wa", 2)), 1)


def tap_window(padded, row_shift, col_shift, flipped):
    height = padded.shape[1] - 2
    across = padded.shape[2] - 2
    row_start = 2 - row_shift if flipped else row_shift
    col_start = 2 - col_shift if flipped else col_shift
    window = padded[:, row_start : row_start + height, col_start : col_start + across, :]
    return window.reshape(-1, C // BLK, BLK)


def conv_forward(padded, weights):
    total = None
    for row_shift in range(3):
        for col_shift in range(3):
            window = tap_window(padded, row_shift, col_shift, False)
            piece = jnp.einsum(
                "pic,ijcd->pjd",
                window,
                weights[:, :, 3 * row_shift + col_shift],
                preferred_element_type=jnp.float32,
            )
            total = piece if total is None else total + piece
    return total.reshape(total.shape[0], -1)


def conv_back(padded, weights):
    total = None
    for row_shift in range(3):
        for col_shift in range(3):
            window = tap_window(padded, row_shift, col_shift, True)
            piece = jnp.einsum(
                "pjd,ijcd->pic",
                window,
                weights[:, :, 3 * row_shift + col_shift],
                preferred_element_type=jnp.float32,
            )
            total = piece if total is None else total + piece
    return total.reshape(total.shape[0], -1)


def weight_grad(padded, incoming):
    blocks = incoming.reshape(incoming.shape[0], C // BLK, BLK)
    taps = []
    for row_shift in range(3):
        for col_shift in range(3):
            window = tap_window(padded, row_shift, col_shift, False)
            taps.append(
                jnp.einsum("pic,pjd->ijcd", window, blocks, preferred_element_type=jnp.float32)
            )
    return jnp.stack(taps, axis=2)


def silu_slope(values):
    sigmoid_value = jax.nn.sigmoid(values)
    return sigmoid_value * (1.0 + values * (1.0 - sigmoid_value))


def normalize(field, total, square_total, count_all, gain, bias):
    average = total / count_all
    variance = square_total / count_all - average * average
    rescale = lax.rsqrt(variance + eps_norm)
    centered = (field - average) * rescale
    return (centered, rescale, gain * centered + bias)


def norm_back(incoming, centered, rescale, gain, total, cross, count_all):
    return gain * rescale * (incoming - total / count_all - centered * cross / count_all)


def pool_mean(field):
    count_lead, height, width, depth = field.shape
    return jnp.mean(field.reshape(count_lead, height // 2, 2, width // 2, 2, depth), axis=(2, 4))


def spread_up(field):
    count_lead, half_h, half_w, depth = field.shape
    widened = jnp.broadcast_to(
        field[:, :, None, :, None, :], (count_lead, half_h, 2, half_w, 2, depth)
    )
    return widened.reshape(count_lead, 2 * half_h, 2 * half_w, depth)


def shampoo(grad_block, left, right, left_root, right_root, weight, rate):
    left_new = stat_decay * left + (1.0 - stat_decay) * jnp.einsum(
        "...ab,...cb->...ac", grad_block, grad_block, precision=highest
    )
    right_new = stat_decay * right + (1.0 - stat_decay) * jnp.einsum(
        "...ba,...bc->...ac", grad_block, grad_block, precision=highest
    )
    partial_step = jnp.einsum("...ab,...bc->...ac", left_root, grad_block, precision=highest)
    step_value = jnp.einsum("...ab,...bc->...ac", partial_step, right_root, precision=highest)
    return (left_new, right_new, weight - rate * step_value)


def shards(
    images,
    cot_shared,
    cot_tasks,
    depth_mask,
    nash_weights,
    conv_weight,
    conv_left,
    conv_right,
    conv_left_root,
    conv_right_root,
    proj_weight,
    proj_left,
    proj_right,
    proj_left_root,
    proj_right_root,
    norm_params,
    norm_moment,
):
    block_count = C // BLK
    gathered = lax.all_gather(conv_weight.astype(jnp.bfloat16), ("img", "ha"), axis=0, tiled=True)
    weight_grid = gathered.reshape(block_count, block_count, -1, 9, BLK, BLK)
    mask_field = depth_mask.astype(jnp.float32)
    batch_local, tile_height, tile_width, channels = images.shape
    half_h = tile_height // 2
    half_w = tile_width // 2
    pixel_rows = batch_local * tile_height * tile_width
    count_all = pixel_rows * lax.axis_size("img") * lax.axis_size("ha") * lax.axis_size("wa")
    gains = norm_params[0]
    biases = norm_params[1]
    off_down = 2 * C
    off_up = 2 * C + TASKS * CA
    down_gain = gains[off_down:off_up].reshape(TASKS, 1, CA)
    down_bias = biases[off_down:off_up].reshape(TASKS, 1, CA)
    up_gain = gains[off_up:].reshape(TASKS, 1, C)
    up_bias = biases[off_up:].reshape(TASKS, 1, C)
    padded_in = padded_tile(images)
    conv_first = conv_forward(padded_in, weight_grid[:, :, 0])
    first_sums = lax.psum(
        (jnp.sum(conv_first, 0), jnp.sum(conv_first * conv_first, 0)), ("img", "ha", "wa")
    )
    first_hat, first_rescale, first_pre = normalize(
        conv_first, first_sums[0], first_sums[1], count_all, gains[0:C], biases[0:C]
    )
    shared_low = jax.nn.silu(first_pre).astype(jnp.bfloat16)
    padded_mid = padded_tile(shared_low.reshape(batch_local, tile_height, tile_width, C))
    conv_second = conv_forward(padded_mid, weight_grid[:, :, 1])
    down_low = proj_weight[:, 0].astype(jnp.bfloat16)
    up_low = proj_weight[:, 1].astype(jnp.bfloat16)
    shared_blocks = shared_low.reshape(pixel_rows, block_count, BLK)
    down_pre = jnp.einsum(
        "pic,tica->tpa", shared_blocks, down_low, preferred_element_type=jnp.float32
    )
    pair_sums = lax.psum(
        (
            jnp.sum(conv_second, 0),
            jnp.sum(conv_second * conv_second, 0),
            jnp.sum(down_pre, 1),
            jnp.sum(down_pre * down_pre, 1),
        ),
        ("img", "ha", "wa"),
    )
    second_hat, second_rescale, second_pre = normalize(
        conv_second, pair_sums[0], pair_sums[1], count_all, gains[C : 2 * C], biases[C : 2 * C]
    )
    shared_field = jax.nn.silu(second_pre)
    down_hat, down_rescale, down_norm = normalize(
        down_pre,
        pair_sums[2][:, None, :],
        pair_sums[3][:, None, :],
        count_all,
        down_gain,
        down_bias,
    )
    hidden_low = jax.nn.silu(down_norm).astype(jnp.bfloat16)
    mask_pre = jnp.einsum(
        "tpa,tjab->tpjb", hidden_low, up_low, preferred_element_type=jnp.float32
    ).reshape(TASKS, pixel_rows, C)
    up_sums = lax.psum((jnp.sum(mask_pre, 1), jnp.sum(mask_pre * mask_pre, 1)), ("img", "ha", "wa"))
    mask_hat, mask_rescale, mask_norm = normalize(
        mask_pre, up_sums[0][:, None, :], up_sums[1][:, None, :], count_all, up_gain, up_bias
    )
    attention = jax.nn.sigmoid(mask_norm)
    attended = (attention * shared_field[None]).astype(jnp.bfloat16)
    padded_att = padded_tile(attended.reshape(TASKS * batch_local, tile_height, tile_width, C))
    att_tiles = [
        padded_att[task_index * batch_local : (task_index + 1) * batch_local]
        for task_index in range(TASKS)
    ]
    task_maps = jnp.stack(
        [
            conv_forward(att_tiles[task_index], weight_grid[:, :, 2 + task_index])
            for task_index in range(TASKS)
        ]
    )
    shared_out = pool_mean(shared_field.reshape(batch_local, tile_height, tile_width, C)).astype(
        jnp.bfloat16
    )
    task_pooled = pool_mean(task_maps.reshape(TASKS * batch_local, tile_height, tile_width, C))
    task_out = jnp.transpose(
        task_pooled.reshape(TASKS, batch_local, half_h, half_w, C), (1, 2, 3, 0, 4)
    )
    task_out = task_out.reshape(batch_local, half_h, half_w, TASKS * C).astype(jnp.bfloat16)
    depth_pick = jnp.arange(TASKS) == 1
    task_scale = jnp.where(depth_pick, mask_field[..., None], 1.0) * nash_weights
    task_cot = cot_tasks.astype(jnp.float32).reshape(batch_local, half_h, half_w, TASKS, C)
    weighted = task_cot * task_scale[..., None] * 0.25
    weighted = jnp.transpose(weighted, (3, 0, 1, 2, 4)).reshape(
        TASKS * batch_local, half_h, half_w, C
    )
    task_grad_low = spread_up(weighted).astype(jnp.bfloat16)
    padded_back = padded_tile(task_grad_low)
    task_grad_rows = task_grad_low.reshape(TASKS, pixel_rows, C)
    att_grad = jnp.stack(
        [
            conv_back(
                padded_back[task_index * batch_local : (task_index + 1) * batch_local],
                weight_grid[:, :, 2 + task_index],
            )
            for task_index in range(TASKS)
        ]
    )
    task_weight_grads = [
        weight_grad(att_tiles[task_index], task_grad_rows[task_index])
        for task_index in range(TASKS)
    ]
    branch_grad = attention * att_grad
    gram_part = jnp.einsum("tpc,spc->ts", branch_grad, branch_grad, precision=highest)
    shared_grad = spread_up(cot_shared.astype(jnp.float32) * 0.25).reshape(pixel_rows, C) + jnp.sum(
        branch_grad, 0
    )
    mask_grad = att_grad * shared_field[None] * attention * (1.0 - attention)
    second_grad = shared_grad * silu_slope(second_pre)
    up_items = (
        jnp.sum(mask_grad, 1),
        jnp.sum(mask_grad * mask_hat, 1),
        jnp.sum(second_grad, 0),
        jnp.sum(second_grad * second_hat, 0),
    )
    up_items = up_items + (gram_part,)
    up_results = lax.psum(up_items, ("img", "ha", "wa"))
    up_total, up_cross, second_total, second_cross = (
        up_results[0],
        up_results[1],
        up_results[2],
        up_results[3],
    )
    mask_low = norm_back(
        mask_grad,
        mask_hat,
        mask_rescale,
        up_gain,
        up_total[:, None, :],
        up_cross[:, None, :],
        count_all,
    ).astype(jnp.bfloat16)
    mask_blocks = mask_low.reshape(TASKS, pixel_rows, block_count, BLK)
    up_partial = jnp.einsum(
        "tpa,tpjb->tjab", hidden_low, mask_blocks, preferred_element_type=jnp.float32
    )
    hidden_grad = jnp.einsum(
        "tpjb,tjab->tpa", mask_blocks, up_low, preferred_element_type=jnp.float32
    )
    down_grad = hidden_grad * silu_slope(down_norm)
    down_total, down_cross = lax.psum(
        (jnp.sum(down_grad, 1), jnp.sum(down_grad * down_hat, 1)), ("img", "ha", "wa")
    )
    down_low_grad = norm_back(
        down_grad,
        down_hat,
        down_rescale,
        down_gain,
        down_total[:, None, :],
        down_cross[:, None, :],
        count_all,
    ).astype(jnp.bfloat16)
    down_partial = jnp.einsum(
        "pic,tpa->tica", shared_blocks, down_low_grad, preferred_element_type=jnp.float32
    )
    branch_back = jnp.einsum(
        "tpa,tica->pic", down_low_grad, down_low, preferred_element_type=jnp.float32
    ).reshape(pixel_rows, C)
    second_low = norm_back(
        second_grad,
        second_hat,
        second_rescale,
        gains[C : 2 * C],
        second_total,
        second_cross,
        count_all,
    ).astype(jnp.bfloat16)
    padded_second = padded_tile(second_low.reshape(batch_local, tile_height, tile_width, C))
    shared_back = conv_back(padded_second, weight_grid[:, :, 1]) + branch_back
    first_grad = shared_back * silu_slope(first_pre)
    proj_partial = jnp.stack([down_partial, up_partial], axis=1)
    first_items = (jnp.sum(first_grad, 0), jnp.sum(first_grad * first_hat, 0), proj_partial)
    first_items = first_items + ()
    first_results = lax.psum(first_items, ("img", "ha", "wa"))
    first_total, first_cross, proj_total = (first_results[0], first_results[1], first_results[2])
    gram = up_results[4]
    first_low = norm_back(
        first_grad, first_hat, first_rescale, gains[0:C], first_total, first_cross, count_all
    ).astype(jnp.bfloat16)
    padded_first = padded_tile(first_low.reshape(batch_local, tile_height, tile_width, C))
    image_grad = (
        conv_back(padded_first, weight_grid[:, :, 0])
        .astype(jnp.bfloat16)
        .reshape(batch_local, tile_height, tile_width, C)
    )
    conv_partial = jnp.stack(
        [weight_grad(padded_in, first_low), weight_grad(padded_mid, second_low)]
        + task_weight_grads,
        axis=2,
    )
    conv_partial = conv_partial.reshape(block_count * block_count, -1, BLK, BLK)
    conv_owned = lax.psum_scatter(
        conv_partial.astype(jnp.bfloat16), ("img", "ha"), scatter_dimension=0, tiled=True
    )
    conv_total = lax.psum(conv_owned, "wa").astype(jnp.float32)
    conv_left_new, conv_right_new, conv_weight_new = shampoo(
        conv_total, conv_left, conv_right, conv_left_root, conv_right_root, conv_weight, conv_rate
    )
    proj_left_new, proj_right_new, proj_weight_new = shampoo(
        proj_total, proj_left, proj_right, proj_left_root, proj_right_root, proj_weight, proj_rate
    )
    gain_grads = jnp.concatenate(
        [first_cross, second_cross, down_cross.reshape(-1), up_cross.reshape(-1)]
    )
    bias_grads = jnp.concatenate(
        [first_total, second_total, down_total.reshape(-1), up_total.reshape(-1)]
    )
    norm_grad = jnp.stack([gain_grads, bias_grads])
    moment_new = moment_decay * norm_moment + (1.0 - moment_decay) * norm_grad * norm_grad
    norm_new = norm_params - norm_rate * norm_grad / (jnp.sqrt(moment_new) + 1e-08)
    return (
        shared_out,
        task_out,
        image_grad,
        gram,
        conv_total,
        conv_left_new,
        conv_right_new,
        conv_weight_new,
        proj_total,
        proj_left_new,
        proj_right_new,
        proj_weight_new,
        norm_grad,
        moment_new,
        norm_new,
    )


def solution(mesh):
    placed = (
        P("img", "ha", "wa", None),
        P("img", "ha", "wa", None),
        P("img", "ha", "wa", None),
        P("img", "ha", "wa"),
        P(),
        P(("img", "ha"), None, None, None),
        P(("img", "ha"), None, None, None),
        P(("img", "ha"), None, None, None),
        P(("img", "ha"), None, None, None),
        P(("img", "ha"), None, None, None),
        P(),
        P(),
        P(),
        P(),
        P(),
        P(),
        P(),
    )
    return jax.shard_map(
        shards,
        mesh=mesh,
        in_specs=placed,
        out_specs=(
            P("img", "ha", "wa", None),
            P("img", "ha", "wa", None),
            P("img", "ha", "wa", None),
            P(),
            P(("img", "ha"), None, None, None),
            P(("img", "ha"), None, None, None),
            P(("img", "ha"), None, None, None),
            P(("img", "ha"), None, None, None),
            P(),
            P(),
            P(),
            P(),
            P(),
            P(),
            P(),
        ),
        check_vma=False,
    )
```

profile of v0, /device:TPU:0, one launch (start us, length us, event | category | flops | bytes accessed | tf_op | source)
XLA Modules:
  0.0 1605.7 jit_solution(5087404041963898241)
XLA Ops:
  14.3 5.6 collective-permute-start
  21.2 3.8 reshape.973
  28.6 5.0 broadcast_in_dim.32
  33.6 5.7 convert_element_type.108
  41.2 5.2 collective-permute-start.12
  54.0 3.7 fusion.534
  78.4 4.3 broadcast_in_dim.36
  106.2 3.7 pad_maximum_fusion.6
  143.0 4.2 constant_dynamic-update-slice_fusion.4
  151.6 5.0 collective-permute-start.15
  175.0 9.9 fusion.136
  187.1 8.3 fusion.130
  232.3 42.3 %all-gather.2.cloned.1.call-done = bf16[16,45,128,128]{3,2,1,0:T(8,128)(2,1)} async-done(((bf16[1,45,128,128]{3,2,1,0:T(8,128)(2,1)}), bf16[16,45,128,128]{3,2,1,0:T(8,128)(2,1)}) %all-gather.2.cloned.1.call-update) | async-done | bytes 23592976 | tf_op jit(solution)/shard_map/all_gather | solution.py:151
  274.6 22.3 %fusion.516 = (bf16[4,4,1,9,128,128]{5,4,3,2,1,0:T(8,128)(2,1)}, bf16[4,4,1,9,128,128]{5,4,3,2,1,0:T(8,128)(2,1)}, bf16[4,4,1,9,128,128]{5,4,3,2,1,0:T(8,128)(2,...) fusion(bf16[4,4,5,9,128,128]{5,4,3,2,1,0:T(8,128)(2,1)} %bitcast.1944), kind=kLoop, calls=%fused_computation.853 | loop fusion | bytes 47185920 | tf_op jit(solution)/shard_map/slice | solution.py:222
  296.8 6.8 copy.1773
  320.8 38.4 %all-reduce.5 = (f32[512]{0:T(512)S(1)}, f32[512]{0:T(512)S(1)}) all-reduce(f32[512]{0:T(512)S(1)} %bitcast.2094, f32[512]{0:T(512)S(1)} %bitcast.2093), channel_id=1, replica_groups=mesh['img'=4,'ha'=4,'wa'=2] {'img','ha','wa'}, use_global_device_ids=true, to_apply=%region_3.0 | all-reduce | flops 1024 | bytes 8192 | tf_op jit(solution)/shard_map/psum | solution.py:169
  366.3 40.7 %all-reduce.4 = (f32[3,128]{1,0:T(4,128)S(1)}, f32[3,128]{1,0:T(4,128)S(1)}) all-reduce(f32[3,128]{1,0:T(4,128)S(1)} %get-tuple-element.120, f32[3,128]{1,0:T(4,128)S(1)} %get-tuple-element.119), channel_id=1, replica_groups=mesh['img'=4,'ha'=4,'wa'=2] {'img','ha','wa'}, use_global_device_ids=true, to_apply=%region_12.13 | all-reduce | flops 768 | bytes 6144 | tf_op jit(solution)/shard_map/psum | solution.py:184
  424.0 7.0 copy.1774
  430.9 6.7 copy.1776
  437.6 3.6 fusion.199
  457.0 6.7 copy.1777
  463.6 3.6 fusion.182
  483.0 7.0 copy.1775
  510.1 3.9 bitcast_add_fusion.26
  514.1 7.2 bitcast_add_fusion.18
  523.6 4.5 bitcast_add_fusion.34
  531.2 7.7 copy.1216
  538.9 5.2 copy.1358
  554.0 7.9 reshape.886
  616.1 8.9 fusion.511
  625.0 42.0 %all-reduce.3 = (f32[512]{0:T(512)S(1)}, f32[512]{0:T(512)S(1)}, f32[3,512]{1,0:T(4,128)S(1)}, f32[3,512]{1,0:T(4,128)S(1)}) all-reduce(f32[512]{0:T(512)S(1)} %bitcast.2092, f32[512]{0:T(512)S(1)} %bitcast.2091, f32[3,512]{1,0:T(4,128)S(1)} %bitcast.2075, ...), channel_id=1, replica_groups=mesh['img'=4,'ha'=4,'wa'=2] {'img','ha','wa'}, use_global_device_ids=true, to_apply=%region_7.8 | all-reduce | flops 4096 | bytes 32768 | tf_op jit(solution)/shard_map/psum | solution.py:184
  676.0 5.7 add_divide_fusion
  682.4 7.0 fusion.507
  690.8 40.0 %all-reduce.2 = (f32[3,512]{1,0:T(4,128)S(1)}, f32[3,512]{1,0:T(4,128)S(1)}) all-reduce(f32[3,512]{1,0:T(4,128)S(1)} %bitcast.2077, f32[3,512]{1,0:T(4,128)S(1)} %bitcast.2078), channel_id=1, replica_groups=mesh['img'=4,'ha'=4,'wa'=2] {'img','ha','wa'}, use_global_device_ids=true, to_apply=%region_26.27 | all-reduce | flops 3072 | bytes 24576 | tf_op jit(solution)/shard_map/psum | solution.py:271
  731.6 5.7 multiply_convert_fusion
  737.4 4.0 fusion.513
  746.3 4.4 fusion.510
  750.7 40.7 %all-reduce.1 = (f32[512]{0:T(512)S(1)}, f32[512]{0:T(512)S(1)}, f32[3,128]{1,0:T(4,128)}, f32[3,128]{1,0:T(4,128)S(1)}) all-reduce(f32[512]{0:T(512)S(1)} %bitcast.2096, f32[512]{0:T(512)S(1)} %bitcast.2095, f32[3,128]{1,0:T(4,128)S(1)} %get-tuple-element.118, ...), channel_id=1, replica_groups=mesh['img'=4,'ha'=4,'wa'=2] {'img','ha','wa'}, use_global_device_ids=true, to_apply=%region_22.23 | all-reduce | flops 1792 | bytes 14336 | tf_op jit(solution)/shard_map/psum | solution.py:271
  801.5 15.3 divide_multiply_fusion.9
  816.8 38.5 %fusion.124 = f32[3,3]{1,0:T(4,128)S(1)} fusion(f32[3,1024,512]{1,0,2:T(4,128)S(1)} %divide_multiply_fusion.9), kind=kOutput, calls=%fused_computation.345 | convolution fusion | flops 56623104 | bytes 6291492 | tf_op jit(solution)/shard_map/tpc,spc->ts/dot_general | solution.py:258
  885.0 4.7 collective-permute-start.8
  903.2 4.3 collective-permute-start.19
  957.8 8.9 bitcast_add_fusion.10
  969.6 5.5 fusion.509
  975.1 42.4 %all-reduce = (f32[512]{0:T(512)S(1)}, f32[512]{0:T(512)S(1)}, f32[3,3]{1,0:T(4,128)}) all-reduce(f32[512]{0:T(512)S(1)} %get-tuple-element.110, f32[512]{0:T(512)S(1)} %get-tuple-element.109, f32[3,3]{1,0:T(4,128)S(1)} %fusion.124), channel_id=1, replica_groups=mesh['img'=4,'ha'=4,'wa'=2] {'img','ha','wa'}, use_global_device_ids=true, to_apply=%region_34.35 | all-reduce | flops 1033 | bytes 8264 | tf_op jit(solution)/shard_map/psum | solution.py:328
  1017.5 3.8 multiply_convert_fusion.2
  1049.1 4.0 pad_maximum_fusion.19
  1072.6 8.7 pad_maximum_fusion.2
  1081.2 3.7 fusion.518
  1087.1 9.6 fusion.517
  1179.4 6.3 bitcast_dynamic-update-slice_fusion
  1185.7 30.7 %copy.1441 = bf16[4,4,5,9,128,128]{5,4,3,2,1,0:T(8,128)(2,1)} copy(bf16[4,4,5,9,128,128]{4,5,0,1,3,2:T(8,128)(2,1)} %bitcast_dynamic-update-slice_fusion) | data formatting | bytes 47185920 | tf_op jit(solution)/shard_map/stack | solution.py:340
  1217.2 3.8 reshape.885
  1263.8 3.9 collective-permute-start.23
  1286.6 3.8 fusion.524
  1329.0 3.6 bitcast_add_fusion.59
  1369.2 6.6 pad_maximum_fusion
  1375.7 8.4 reshape_reshape.6
  1384.2 9.4 reduce_sum.208
  1399.1 161.6 %reduce-scatter.2.cloned.1.call-done = bf16[1,45,128,128]{3,2,1,0:T(8,128)(2,1)} async-done(((bf16[16,45,128,128]{3,2,1,0:T(8,128)(2,1)}), bf16[1,45,128,128]{3,2,1,0:T(8,128)(2,1)}) %reduce-scatter.2.cloned.1.call-update) | async-done | bytes 1474576 | tf_op jit(solution)/shard_map/reduce_scatter | solution.py:346
  1564.5 4.0 multiply_add_fusion.1
  1568.4 4.8 multiply_add_fusion.2
  1576.2 6.2 all-reduce.9.cloned.1.call-done
  1585.6 5.1 bitcast_subtract_fusion
  (958 shorter events, 736.8 us)
Async XLA Ops:
  7.2 1575.2 %copy-start = (f32[1,45,128,128]{3,2,1,0:T(8,128)S(1)}, f32[1,45,128,128]{3,2,1,0:T(8,128)}, u32[]{:S(2)}) copy-start(f32[1,45,128,128]{3,2,1,0:T(8,128)} %param.25) | copy-start | bytes 8847364
  7.2 267.4 %all-gather.2.cloned.1.call-start = ((), (), s32[]{:S(2)}) async-start(), calls=%async_computation.1 | async-start | bytes 25067520 | tf_op jit(solution)/shard_map/all_gather | solution.py:151
  10.6 1385.5 %all-reduce.11.cloned.1.call-start = ((), (), s32[]{:S(2)}) async-start(), calls=%async_computation.4 | async-start | bytes 3145728 | tf_op jit(solution)/shard_map/psum | solution.py:328
  13.4 11.6 copy-start.244
  13.4 11.6 copy-start.264
  14.3 80.4 %collective-permute-start = (bf16[4,1,16,512]{3,1,2,0:T(2,128)(2,1)}, bf16[4,1,16,512]{3,1,2,0:T(2,128)(2,1)}, u32[]{:S(2)}, u32[]{:S(2)}) collective-permute-start(bf16[4,1,16,512]{3,1,2,0:T(2,128)(2,1)} %get-tuple-element.279), channel_id=1, source_target_pairs={{0,2},{2,4},{4,6},{1,3},{3,5},{5,7},{8,10},{10,12},{12,14},{9,11},... | collective-permute-start | bytes 196616 | tf_op jit(solution)/shard_map/ppermute | solution.py:26
  19.9 74.8 %collective-permute-start.1 = (bf16[4,1,16,512]{3,1,2,0:T(2,128)(2,1)}, bf16[4,1,16,512]{3,1,2,0:T(2,128)(2,1)}, u32[]{:S(2)}, u32[]{:S(2)}) collective-permute-start(bf16[4,1,16,512]{3,1,2,0:T(2,128)(2,1)} %get-tuple-element.280), channel_id=1, source_target_pairs={{2,0},{4,2},{6,4},{3,1},{5,3},{7,5},{10,8},{12,10},{14,12},{11,9},... | collective-permute-start | bytes 196616 | tf_op jit(solution)/shard_map/ppermute | solution.py:29
  41.2 100.8 %collective-permute-start.12 = (bf16[12,1,16,512]{3,2,1,0:T(8,128)(2,1)}, bf16[12,1,16,512]{3,2,1,0:T(8,128)(2,1)}, u32[]{:S(2)}, u32[]{:S(2)}) collective-permute-start(bf16[12,1,16,512]{3,2,1,0:T(8,128)(2,1)} %get-tuple-element.213), channel_id=1, source_target_pairs={{0,2},{2,4},{4,6},{1,3},{3,5},{5,7},{8,10},{10,12},{12,14},{9,11},... | collective-permute-start | bytes 589832 | tf_op jit(solution)/shard_map/ppermute | solution.py:26
  46.3 100.9 %collective-permute-start.13 = (bf16[12,1,16,512]{3,2,1,0:T(8,128)(2,1)}, bf16[12,1,16,512]{3,2,1,0:T(8,128)(2,1)}, u32[]{:S(2)}, u32[]{:S(2)}) collective-permute-start(bf16[12,1,16,512]{3,2,1,0:T(8,128)(2,1)} %get-tuple-element.212), channel_id=1, source_target_pairs={{2,0},{4,2},{6,4},{3,1},{5,3},{7,5},{10,8},{12,10},{14,12},{11,9},... | collective-permute-start | bytes 589832 | tf_op jit(solution)/shard_map/ppermute | solution.py:29
  54.0 31.6 %copy-start.201 = (f32[3,512]{1,0:T(4,128)}, f32[3,512]{1,0:T(4,128)S(1)}, u32[]{:S(2)}) copy-start(f32[3,512]{1,0:T(4,128)S(1)} %mul.565) | copy-start | bytes 18436
  94.7 322.0 %copy-start.224 = (f32[1,512]{1,0:T(1,128)}, f32[1,512]{1,0:T(1,128)S(1)}, u32[]{:S(2)}) copy-start(f32[1,512]{1,0:T(1,128)S(1)} %get-tuple-element.292) | copy-start | bytes 6148
  94.7 322.0 %copy-start.233 = (f32[1,512]{1,0:T(1,128)}, f32[1,512]{1,0:T(1,128)S(1)}, u32[]{:S(2)}) copy-start(f32[1,512]{1,0:T(1,128)S(1)} %get-tuple-element.291) | copy-start | bytes 6148
  94.7 312.9 %copy-start.256 = (f32[384]{0:T(512)}, f32[384]{0:T(512)S(1)}, u32[]{:S(2)}) copy-start(f32[384]{0:T(512)S(1)} %get-tuple-element.123) | copy-start | bytes 4612
  94.7 312.9 %copy-start.262 = (f32[384]{0:T(512)}, f32[384]{0:T(512)S(1)}, u32[]{:S(2)}) copy-start(f32[384]{0:T(512)S(1)} %get-tuple-element.124) | copy-start | bytes 4612
  95.8 10.5 collective-permute-start.2
  97.1 9.2 collective-permute-start.3
  147.2 11.2 copy-start.54
  148.4 10.0 copy-start.15
  150.4 24.6 %collective-permute-start.14 = (bf16[12,18,1,512]{3,2,1,0:T(2,128)(2,1)}, bf16[12,18,1,512]{3,2,1,0:T(2,128)(2,1)}, u32[]{:S(2)}, u32[]{:S(2)}) collective-permute-start(bf16[12,18,1,512]{3,2,1,0:T(2,128)(2,1)} %get-tuple-element.192), channel_id=1, source_target_pairs={{1,0},{3,2},{5,4},{7,6},{9,8},{11,10},{13,12},{15,14},{17,16},{19,... | collective-permute-start | bytes 663560 | tf_op jit(solution)/shard_map/ppermute | solution.py:29
  151.6 35.5 %collective-permute-start.15 = (bf16[12,18,1,512]{3,2,1,0:T(2,128)(2,1)S(1)}, bf16[12,18,1,512]{3,2,1,0:T(2,128)(2,1)}, u32[]{:S(2)}, u32[]{:S(2)}) collective-permute-start(bf16[12,18,1,512]{3,2,1,0:T(2,128)(2,1)S(1)} %get-tuple-element.191), channel_id=1, source_target_pairs={{0,1},{2,3},{4,5},{6,7},{8,9},{10,11},{12,13},{14,15},{16,17},{18,... | collective-permute-start | bytes 663560 | tf_op jit(solution)/shard_map/ppermute | solution.py:26
  359.7 57.0 %copy-start.235 = (f32[512]{0:T(512)}, f32[512]{0:T(512)S(1)}, u32[]{:S(2)}) copy-start(f32[512]{0:T(512)S(1)} %get-tuple-element.296) | copy-start | bytes 6148
  359.7 57.0 %copy-start.237 = (f32[512]{0:T(512)}, f32[512]{0:T(512)S(1)}, u32[]{:S(2)}) copy-start(f32[512]{0:T(512)S(1)} %get-tuple-element.303) | copy-start | bytes 6148
  363.2 44.4 %copy-start.197 = (bf16[3,4,128,128]{2,3,1,0:T(8,128)(2,1)S(1)}, bf16[3,4,128,128]{2,3,1,0:T(8,128)(2,1)}, u32[]{:S(2)}) copy-start(bf16[3,4,128,128]{2,3,1,0:T(8,128)(2,1)} %copy.1215) | copy-start | bytes 1179652
  420.0 141.9 %collective-permute-start.4 = (bf16[4,1,16,512]{3,2,1,0:T(8,128)(2,1)S(1)}, bf16[4,1,16,512]{3,2,1,0:T(8,128)(2,1)S(1)}, u32[]{:S(2)}, u32[]{:S(2)}) collective-permute-start(bf16[4,1,16,512]{3,2,1,0:T(8,128)(2,1)S(1)} %get-tuple-element.275), channel_id=1, source_target_pairs={{0,2},{2,4},{4,6},{1,3},{3,5},{5,7},{8,10},{10,12},{12,14},{9,11},... | collective-permute-start | bytes 196616 | tf_op jit(solution)/shard_map/ppermute | solution.py:26
  422.7 139.2 %collective-permute-start.5 = (bf16[4,1,16,512]{3,2,1,0:T(8,128)(2,1)S(1)}, bf16[4,1,16,512]{3,2,1,0:T(8,128)(2,1)S(1)}, u32[]{:S(2)}, u32[]{:S(2)}) collective-permute-start(bf16[4,1,16,512]{3,2,1,0:T(8,128)(2,1)S(1)} %get-tuple-element.276), channel_id=1, source_target_pairs={{2,0},{4,2},{6,4},{3,1},{5,3},{7,5},{10,8},{12,10},{14,12},{11,9},... | collective-permute-start | bytes 196616 | tf_op jit(solution)/shard_map/ppermute | solution.py:29
  499.1 8.6 copy-start.161
  499.1 10.8 copy-start.78
  501.3 8.6 copy-start.76
  501.3 8.6 copy-start.77
  514.1 8.3 copy-start.86
  514.1 8.9 copy-start.87
  514.1 9.5 copy-start.88
  564.1 15.6 collective-permute-start.6
  565.4 14.3 collective-permute-start.7
  616.1 50.9 %copy-start.202 = (f32[3,512]{1,0:T(4,128)S(1)}, f32[3,512]{1,0:T(4,128)}, u32[]{:S(2)}) copy-start(f32[3,512]{1,0:T(4,128)} %copy-done.201) | copy-start | bytes 18436
  746.2 45.7 %copy-start.242 = (f32[512]{0:T(512)S(1)}, f32[512]{0:T(512)}, u32[]{:S(2)}) copy-start(f32[512]{0:T(512)} %get-tuple-element.299) | copy-start | bytes 6148
  791.3 64.0 %copy-start.260 = (f32[3,128]{1,0:T(4,128)}, f32[3,128]{1,0:T(4,128)S(1)}, u32[]{:S(2)}) copy-start(f32[3,128]{1,0:T(4,128)S(1)} %get-tuple-element.131) | copy-start | bytes 4612
  863.3 7.9 copy-start.91
  863.4 7.9 copy-start.92
  863.4 7.9 copy-start.245
  863.4 7.9 copy-start.248
  863.4 7.9 copy-start.251
  863.4 7.9 copy-start.252
  867.4 32.7 %collective-permute-start.16 = (bf16[4,1,16,512]{3,2,1,0:T(8,128)(2,1)}, bf16[4,1,16,512]{3,2,1,0:T(8,128)(2,1)S(1)}, u32[]{:S(2)}, u32[]{:S(2)}) collective-permute-start(bf16[4,1,16,512]{3,2,1,0:T(8,128)(2,1)} %get-tuple-element.269), channel_id=1, source_target_pairs={{0,2},{2,4},{4,6},{1,3},{3,5},{5,7},{8,10},{10,12},{12,14},{9,11},... | collective-permute-start | bytes 196616 | tf_op jit(solution)/shard_map/ppermute | solution.py:26
  870.0 30.1 %collective-permute-start.17 = (bf16[4,1,16,512]{3,2,1,0:T(8,128)(2,1)}, bf16[4,1,16,512]{3,2,1,0:T(8,128)(2,1)S(1)}, u32[]{:S(2)}, u32[]{:S(2)}) collective-permute-start(bf16[4,1,16,512]{3,2,1,0:T(8,128)(2,1)} %get-tuple-element.268), channel_id=1, source_target_pairs={{2,0},{4,2},{6,4},{3,1},{5,3},{7,5},{10,8},{12,10},{14,12},{11,9},... | collective-permute-start | bytes 196616 | tf_op jit(solution)/shard_map/ppermute | solution.py:29
  874.5 686.3 %reduce-scatter.2.cloned.1.call-start = ((), (), s32[]{:S(2)}) async-start(), calls=%async_computation.2 | async-start | bytes 25067520 | tf_op jit(solution)/shard_map/reduce_scatter | solution.py:346
  879.9 11.0 slice-start.2
  881.6 9.3 slice-start.3
  881.6 9.3 copy-start.100
  881.6 9.3 copy-start.136
  884.1 7.7 copy-start.4
  885.0 159.1 %collective-permute-start.8 = (bf16[12,1,16,512]{3,2,1,0:T(8,128)(2,1)}, bf16[12,1,16,512]{3,2,1,0:T(8,128)(2,1)S(1)}, u32[]{:S(2)}, u32[]{:S(2)}) collective-permute-start(bf16[12,1,16,512]{3,2,1,0:T(8,128)(2,1)} %get-tuple-element.220), channel_id=1, source_target_pairs={{0,2},{2,4},{4,6},{1,3},{3,5},{5,7},{8,10},{10,12},{12,14},{9,11},... | collective-permute-start | bytes 589832 | tf_op jit(solution)/shard_map/ppermute | solution.py:26
  889.6 154.4 %collective-permute-start.9 = (bf16[12,1,16,512]{3,2,1,0:T(8,128)(2,1)}, bf16[12,1,16,512]{3,2,1,0:T(8,128)(2,1)S(1)}, u32[]{:S(2)}, u32[]{:S(2)}) collective-permute-start(bf16[12,1,16,512]{3,2,1,0:T(8,128)(2,1)} %get-tuple-element.221), channel_id=1, source_target_pairs={{2,0},{4,2},{6,4},{3,1},{5,3},{7,5},{10,8},{12,10},{14,12},{11,9},... | collective-permute-start | bytes 589832 | tf_op jit(solution)/shard_map/ppermute | solution.py:29
  900.1 8.9 copy-start.40
  901.9 18.7 %collective-permute-start.18 = (bf16[4,18,1,512]{3,2,1,0:T(2,128)(2,1)}, bf16[4,18,1,512]{3,2,1,0:T(2,128)(2,1)}, u32[]{:S(2)}, u32[]{:S(2)}) collective-permute-start(bf16[4,18,1,512]{3,2,1,0:T(2,128)(2,1)} %get-tuple-element.257), channel_id=1, source_target_pairs={{1,0},{3,2},{5,4},{7,6},{9,8},{11,10},{13,12},{15,14},{17,16},{19,... | collective-permute-start | bytes 221192 | tf_op jit(solution)/shard_map/ppermute | solution.py:29
  903.2 17.4 %collective-permute-start.19 = (bf16[4,18,1,512]{3,2,1,0:T(2,128)(2,1)}, bf16[4,18,1,512]{3,2,1,0:T(2,128)(2,1)}, u32[]{:S(2)}, u32[]{:S(2)}) collective-permute-start(bf16[4,18,1,512]{3,2,1,0:T(2,128)(2,1)} %get-tuple-element.256), channel_id=1, source_target_pairs={{0,1},{2,3},{4,5},{6,7},{8,9},{10,11},{12,13},{14,15},{16,17},{18,... | collective-permute-start | bytes 221192 | tf_op jit(solution)/shard_map/ppermute | solution.py:26
  969.6 47.9 %copy-start.255 = (f32[512]{0:T(512)S(1)}, f32[512]{0:T(512)}, u32[]{:S(2)}) copy-start(f32[512]{0:T(512)} %get-tuple-element.294) | copy-start | bytes 6148
  1045.7 26.8 %collective-permute-start.10 = (bf16[12,18,1,512]{3,2,1,0:T(2,128)(2,1)}, bf16[12,18,1,512]{3,2,1,0:T(2,128)(2,1)}, u32[]{:S(2)}, u32[]{:S(2)}) collective-permute-start(bf16[12,18,1,512]{3,2,1,0:T(2,128)(2,1)} %get-tuple-element.196), channel_id=1, source_target_pairs={{0,1},{2,3},{4,5},{6,7},{8,9},{10,11},{12,13},{14,15},{16,17},{18,... | collective-permute-start | bytes 663560 | tf_op jit(solution)/shard_map/ppermute | solution.py:26
  1047.8 24.7 %collective-permute-start.11 = (bf16[12,18,1,512]{3,2,1,0:T(2,128)(2,1)}, bf16[12,18,1,512]{3,2,1,0:T(2,128)(2,1)}, u32[]{:S(2)}, u32[]{:S(2)}) collective-permute-start(bf16[12,18,1,512]{3,2,1,0:T(2,128)(2,1)} %get-tuple-element.195), channel_id=1, source_target_pairs={{1,0},{3,2},{5,4},{7,6},{9,8},{11,10},{13,12},{15,14},{17,16},{19,... | collective-permute-start | bytes 663560 | tf_op jit(solution)/shard_map/ppermute | solution.py:29
  1216.5 365.9 %all-reduce.9.cloned.1.call-start = ((), (), s32[]{:S(2)}) async-start(), calls=%async_computation.3 | async-start | bytes 2949120 | tf_op jit(solution)/shard_map/psum | solution.py:349
  1224.4 37.2 %collective-permute-start.20 = (bf16[4,1,16,512]{3,2,1,0:T(8,128)(2,1)S(1)}, bf16[4,1,16,512]{3,2,1,0:T(8,128)(2,1)S(1)}, u32[]{:S(2)}, u32[]{:S(2)}) collective-permute-start(bf16[4,1,16,512]{3,2,1,0:T(8,128)(2,1)S(1)} %get-tuple-element.265), channel_id=1, source_target_pairs={{0,2},{2,4},{4,6},{1,3},{3,5},{5,7},{8,10},{10,12},{12,14},{9,11},... | collective-permute-start | bytes 196616 | tf_op jit(solution)/shard_map/ppermute | solution.py:26
  1227.6 34.0 %collective-permute-start.21 = (bf16[4,1,16,512]{3,2,1,0:T(8,128)(2,1)S(1)}, bf16[4,1,16,512]{3,2,1,0:T(8,128)(2,1)S(1)}, u32[]{:S(2)}, u32[]{:S(2)}) collective-permute-start(bf16[4,1,16,512]{3,2,1,0:T(8,128)(2,1)S(1)} %get-tuple-element.264), channel_id=1, source_target_pairs={{2,0},{4,2},{6,4},{3,1},{5,3},{7,5},{10,8},{12,10},{14,12},{11,9},... | collective-permute-start | bytes 196616 | tf_op jit(solution)/shard_map/ppermute | solution.py:29
  1262.5 17.6 %collective-permute-start.22 = (bf16[4,18,1,512]{3,2,1,0:T(2,128)(2,1)}, bf16[4,18,1,512]{3,2,1,0:T(2,128)(2,1)S(1)}, u32[]{:S(2)}, u32[]{:S(2)}) collective-permute-start(bf16[4,18,1,512]{3,2,1,0:T(2,128)(2,1)} %get-tuple-element.253), channel_id=1, source_target_pairs={{1,0},{3,2},{5,4},{7,6},{9,8},{11,10},{13,12},{15,14},{17,16},{19,... | collective-permute-start | bytes 221192 | tf_op jit(solution)/shard_map/ppermute | solution.py:29
  1263.8 16.3 %collective-permute-start.23 = (bf16[4,18,1,512]{3,2,1,0:T(2,128)(2,1)S(1)}, bf16[4,18,1,512]{3,2,1,0:T(2,128)(2,1)S(1)}, u32[]{:S(2)}, u32[]{:S(2)}) collective-permute-start(bf16[4,18,1,512]{3,2,1,0:T(2,128)(2,1)S(1)} %get-tuple-element.252), channel_id=1, source_target_pairs={{0,1},{2,3},{4,5},{6,7},{8,9},{10,11},{12,13},{14,15},{16,17},{18,... | collective-permute-start | bytes 221192 | tf_op jit(solution)/shard_map/ppermute | solution.py:26
  (235 other events, 722.0 us)
Sparse Core Ops, SparseCore 0:
  11.4 263.1 all-gather.1
  874.6 135.0 all-reduce.10
  1216.6 344.1 reduce-scatter.1
  1563.0 19.3 all-reduce.8
where the time goes:
time: 1620 us; the launch traced here: 1610 us
  local copies, waits for them, and re-layouts  543 us (34%)
  matrix products  384 us (24%)
  blocking collectives  244 us (15%)
  waiting for transfers between devices  210 us (13%)
  other arithmetic  149 us (9%)
  starting transfers between devices  58.1 us (4%)
  between operations  17.3 us (1%)
    reshape x90, local copies, waits for them, and re-layouts, tap_window(): return window.reshape(-1, C // BLK, BLK)  198 us
    reduce_scatter x1, waiting for transfers between devices, shards(): lax.psum_scatter(conv_partial.astype(jnp.bfloat16), ('img', 'ha'), scatte...  162 us
    dot_general x45, matrix products, conv_back(): jnp.einsum('pjd,ijcd->pic', window, weights[:, :, 3 * row_shift + col_shi...  133 us
    dot_general x45, matrix products, conv_forward(): jnp.einsum('pic,ijcd->pjd', window, weights[:, :, 3 * row_shift + col_shi...  117 us
    unnamed x561, local copies, waits for them, and re-layouts  89.9 us
    psum x2, blocking collectives, shards(): lax.psum((jnp.sum(conv_second, 0), jnp.sum(conv_second * conv_second, 0),...  82.7 us
    psum x2, blocking collectives, shards(): up_results = lax.psum(up_items, ('img', 'ha', 'wa'))  80.7 us
    slice x18, local copies, waits for them, and re-layouts, tap_window(): padded[:, row_start:row_start + height, col_start:col_start + across, :]  55.6 us
  transfers between devices with their start and end apart: 28, of which 3 were waited for; matrix products, arithmetic and copies ran while one was open for 50% of the time, Pallas kernels for 0%

commit v1 on v0

v1 whole, which is shorter than its diff:
```python
import functools

import jax
import jax.numpy as jnp
from jax import lax
from jax.experimental import pallas as pl
from jax.experimental.pallas import tpu as pltpu
from jax.sharding import PartitionSpec as P

C = 512
CA = 128
TASKS = 3
BLK = 128
HB = 64
NB = C // BLK
PROJ_ROWS = TASKS * 2 * NB * BLK // (2 * NB * NB)

eps_norm = 1e-05
conv_rate = 0.08
proj_rate = 0.2
norm_rate = 0.1
stat_decay = 0.9
moment_decay = 0.95

BF = jnp.bfloat16
F32 = jnp.float32
VM = pl.BlockSpec(memory_space=pltpu.VMEM)
SM = pl.BlockSpec(memory_space=pltpu.SMEM)
ANY = pl.BlockSpec(memory_space=pl.ANY)
VMEM_LIMIT = 56 * 1024 * 1024
NT = (((1,), (1,)), ((), ()))
TN = (((0,), (0,)), ((), ()))


def sds(shape, dtype):
    return jax.ShapeDtypeStruct(shape, dtype)


def params(**kw):
    return pltpu.CompilerParams(vmem_limit_bytes=VMEM_LIMIT, **kw)


def cost(flops, nbytes, trans=0):
    return pl.CostEstimate(
        flops=int(flops / 16), bytes_accessed=int(nbytes / 16), transcendentals=int(trans / 16)
    )


def pairs(axis, step):
    return [(i, i ^ step) for i in range(lax.axis_size(axis))]


def swap(value, axis, step):
    return lax.ppermute(value, axis, pairs(axis, step))


def sum_all(value, fillers=(), axes=("wa", "ha", "img")):
    fillers = list(fillers)
    for axis in axes:
        step = 1
        while step < lax.axis_size(axis):
            total = value + swap(value, axis, step)
            if fillers:
                total = after(total, *fillers.pop(0)(value))
            value = total
            step *= 2
    return value


def row_halo(first, last):
    count = lax.axis_size("ha")
    up = [(i, (i + 1) % count) for i in range(count)]
    down = [((i + 1) % count, i) for i in range(count)]
    return lax.ppermute(last, "ha", up), lax.ppermute(first, "ha", down)


def col_halo(left_edge, right_edge):
    count = lax.axis_size("wa")
    if count == 2:
        mine = jnp.where(lax.axis_index("wa") == 0, right_edge, left_edge)
        got = swap(mine, "wa", 1)
        none = jnp.zeros_like(got)
        first = lax.axis_index("wa") == 0
        return jnp.where(first, none, got), jnp.where(first, got, none)
    up = [(i, i + 1) for i in range(count - 1)]
    down = [(i + 1, i) for i in range(count - 1)]
    return lax.ppermute(right_edge, "wa", up), lax.ppermute(left_edge, "wa", down)


def halo(field, batch):
    top, bottom = row_halo(field[0].astype(BF), field[-1].astype(BF))
    rows = jnp.stack([top, bottom])
    return rows, halo_cols(field, rows, batch)


def after(value, *deps):
    return lax.optimization_barrier((value,) + deps)[0]


class Gather:
    def __init__(self, own):
        self.own = own

    def near(self, *deps):
        self.near_got = swap(after(self.own, *deps), "ha", 2)
        return self.near_got

    def join(self, *deps):
        self.line_low = after(jnp.concatenate([self.own, self.near_got], axis=0), *deps)
        return self.line_low

    def far(self, *deps):
        self.line_high = swap(after(self.line_low, *deps), "ha", 1)
        return self.line_high

    def low(self, *deps):
        low = after(self.line_low, *deps)
        self.low_x, self.low_y = swap(low, "img", 1), swap(low, "img", 2)
        return self.low_x, self.low_y

    def high(self, *deps):
        high = after(self.line_high, *deps)
        self.high_x, self.high_y = swap(high, "img", 1), swap(high, "img", 2)
        return self.high_x, self.high_y

    def corner_a(self, *deps):
        self.corner_low = swap(after(self.low_x, *deps), "img", 2)
        return self.corner_low

    def corner_b(self, *deps):
        self.corner_high = swap(after(self.high_y, *deps), "img", 1)
        return self.corner_high

    def pieces(self, *deps):
        mine = (
            self.line_low, self.line_high, self.low_x, self.high_x,
            self.low_y, self.high_y, self.corner_low, self.corner_high,
        )
        return mine + tuple(swap(after(part, *deps), "wa", 1) for part in mine)


def edge_row(field, h):
    return to_rows(field[:, h : h + 1])[0]


def halo_cols(field, rows, batch):
    height, tall, chans = field.shape
    across = tall // (2 * batch)
    split = field.reshape(height, 2, batch, across, chans)
    around = rows.reshape(2, 2, batch, across, chans)

    def edge(parity, place):
        inner = split[:, parity, :, place].astype(BF)
        outer = around[:, parity, :, place]
        return jnp.concatenate([outer[0:1], inner, outer[1:2]], axis=0)

    left, right = col_halo(edge(0, 0), edge(1, across - 1))
    return jnp.stack([left, right], axis=2).reshape(height + 2, 2 * batch, chans).astype(F32)


def gather_proj(own):
    got = swap(own, "wa", 1)
    even = lax.axis_index("wa") % 2 == 0
    value = jnp.stack([jnp.where(even, own, got), jnp.where(even, got, own)])
    for axis in ("ha", "img"):
        place = lax.axis_index(axis)
        for step in (1, 2):
            came = swap(value, axis, step)
            first = (place // step) % 2 == 0
            value = jnp.stack([jnp.where(first, value, came), jnp.where(first, came, value)])
    return value.reshape(TASKS, 2, NB, BLK, BLK).astype(F32)


def add_low(*parts):
    total = parts[0].astype(F32)
    for part in parts[1:]:
        total = total + part.astype(F32)
    return total.astype(BF)


class Scatter:
    def __init__(self, mine, other):
        self.mine, self.other = mine, other

    def wa(self, *deps):
        self.came = swap(after(self.other, *deps), "wa", 1)
        return self.came

    def corner_sum(self, *deps):
        self.corner = add_low(self.mine[3], after(self.came, *deps)[3])
        return self.corner

    def corner_send(self, *deps):
        corner = after(self.corner, *deps)
        self.to_x = swap(corner[0:2], "img", 1)
        self.to_y = swap(corner[2:4], "img", 2)
        return self.to_x, self.to_y

    def high_sum(self, *deps):
        came = after(self.came, *deps)
        self.high = (
            add_low(self.mine[1][2:4], came[1][2:4], self.to_y),
            add_low(self.mine[2][2:4], came[2][2:4]),
        )
        return self.high

    def high_send(self, *deps):
        self.high_x = swap(after(self.high[0], *deps), "img", 1)
        self.high_y = swap(after(self.high[1], *deps), "img", 2)
        return self.high_x, self.high_y

    def low_sum(self, *deps):
        came = after(self.came, *deps)
        self.low = (
            add_low(self.mine[1][0:2], came[1][0:2]),
            add_low(self.mine[2][0:2], came[2][0:2], self.to_x),
        )
        return self.low

    def low_send(self, *deps):
        self.low_x = swap(after(self.low[0], *deps), "img", 1)
        self.low_y = swap(after(self.low[1], *deps), "img", 2)
        return self.low_x, self.low_y

    def far_sum(self, *deps):
        came = after(self.came, *deps)
        self.far = add_low(self.mine[0][2:4], came[0][2:4], self.high_x, self.high_y)
        return self.far

    def far_send(self, *deps):
        self.from_far = swap(after(self.far, *deps), "ha", 1)
        return self.from_far

    def near_sum(self, *deps):
        came = after(self.came, *deps)
        self.near = add_low(
            self.mine[0][1], came[0][1], self.low_x[1], self.low_y[1], self.from_far[1]
        )
        return self.near

    def near_send(self, *deps):
        self.from_near = swap(after(self.near, *deps), "ha", 2)
        return self.from_near

    def finish(self, *deps):
        total = add_low(
            after(self.mine[0][0], *deps), self.came[0][0], self.low_x[0], self.low_y[0], self.from_far[0], self.from_near
        )
        step = 2
        while step < lax.axis_size("wa"):
            total = add_low(total, swap(total, "wa", step))
            step *= 2
        return total, swap(total, "wa", 1)


def coef(sums, gb, count_all):
    mean = sums[0:1] / count_all
    var = sums[1:2] / count_all - mean * mean
    rs = lax.rsqrt(var + eps_norm)
    sc = gb[0:1] * rs
    return mean, rs, sc, gb[1:2] - mean * sc


def sigm(v):
    return 1.0 / (1.0 + jnp.exp(-v))


def side_mask(idx, rows, lanes, count):
    side = lax.broadcasted_iota(jnp.int32, (rows, lanes), 0) % 2
    return jnp.where(side == 0, idx[5], idx[6]).astype(F32)


def col_block(cols, r, side, batch, across):
    lanes = cols.shape[-1]
    parts = [
        jnp.broadcast_to(cols[r, pl.ds(2 * b + side, 1), :], (across, lanes)) for b in range(batch)
    ]
    return jnp.concatenate(parts, axis=0)


def shifted(even, odd, hl, hr, batch, across):
    lanes = even.shape[-1]
    shape = (batch, across, lanes)
    j = lax.broadcasted_iota(jnp.int32, shape, 1)
    lo = jnp.where(j == 0, hl.reshape(shape), pltpu.roll(odd.reshape(shape), 1, 1))
    hi = jnp.where(j == across - 1, hr.reshape(shape), pltpu.roll(even.reshape(shape), across - 1, 1))
    return lo.reshape(even.shape), hi.reshape(even.shape)


def put_row(x3, r, row, cols, batch, across):
    q = batch * across
    even, odd = row[0:q], row[q : 2 * q]
    hl = col_block(cols, r, 0, batch, across)
    hr = col_block(cols, r, 1, batch, across)
    lo, hi = shifted(even, odd, hl, hr, batch, across)
    x3[0, r] = jnp.concatenate([lo, even], axis=0).astype(BF)
    x3[1, r] = row.astype(BF)
    x3[2, r] = jnp.concatenate([odd, hi], axis=0).astype(BF)


def flip(s):
    return s // 2 + 2 * (s % 2)


def weight_copies_rel(idx, pieces, first, wv, sems):
    copies = []
    count = len(pieces) // 2
    for half in range(2):
        parts = pieces[half * count : (half + 1) * count]
        h = lax.bitwise_xor(idx[2], half)
        for e in range(4):
            i = lax.bitwise_xor(idx[0], e)
            row0 = pl.multiple_of(i * BLK + h * HB, HB)
            for s in range(4):
                j = lax.bitwise_xor(idx[1], flip(s))
                col0 = pl.multiple_of(j * BLK, BLK)
                copies.append(
                    pltpu.make_async_copy(
                        parts[2 * e + s // 2].at[s % 2, pl.ds(first, 9)],
                        wv.at[:, pl.ds(row0, HB), pl.ds(col0, BLK)],
                        sems.at[len(copies)],
                    )
                )
    return copies


def weight_copies_task(idx, pieces, first, wv, sems):
    copies = []
    for half in range(2):
        h = lax.bitwise_xor(idx[2], half)
        for i in range(NB):
            row0 = pl.multiple_of(i * BLK + h * HB, HB)
            for j in range(NB):
                copies.append(
                    pltpu.make_async_copy(
                        pieces[half].at[i * NB + j, pl.ds(first, 9)],
                        wv.at[:, pl.ds(row0, HB), j * BLK : (j + 1) * BLK],
                        sems.at[len(copies)],
                    )
                )
    return copies


def shift_kernel(batch, idx, x_ref, rows_ref, cols_ref, x3_ref, work):
    height, tall = x_ref.shape[0], x_ref.shape[1]
    across = tall // (2 * batch)
    top, bottom = idx[3].astype(F32), idx[4].astype(F32)
    work[...] = cols_ref[...]
    work[0] = work[0] * top
    work[height + 1] = work[height + 1] * bottom
    cols_ref = work
    put_row(x3_ref, 0, rows_ref[0].astype(F32) * top, cols_ref, batch, across)
    put_row(x3_ref, height + 1, rows_ref[1].astype(F32) * bottom, cols_ref, batch, across)

    @pl.loop(0, height)
    def _(h):
        put_row(x3_ref, h + 1, x_ref[h].astype(F32), cols_ref, batch, across)


def shift_copies(idx, field, rows, cols, batch):
    height, tall, chans = field.shape
    lanes = BLK
    return pl.pallas_call(
        functools.partial(shift_kernel, batch),
        grid=(chans // lanes,),
        in_specs=[
            SM,
            pl.BlockSpec((height, tall, lanes), lambda c: (0, 0, c)),
            pl.BlockSpec((2, tall, lanes), lambda c: (0, 0, c)),
            pl.BlockSpec((height + 2, 2 * batch, lanes), lambda c: (0, 0, c)),
        ],
        out_specs=pl.BlockSpec((3, height + 2, tall, lanes), lambda c: (0, 0, 0, c)),
        out_shape=sds((3, height + 2, tall, chans), BF),
        scratch_shapes=[pltpu.VMEM((height + 2, 2 * batch, lanes), F32)],
        compiler_params=params(),
        cost_estimate=cost(0, 8e6),
        name="shift_copies",
    )(idx, field, rows, cols)


def conv_kernel(n_pieces, transposed, want_sums, idx_ref, x_ref, *refs):
    pieces = refs[:n_pieces]
    o_ref = refs[n_pieces]
    s_ref = refs[n_pieces + 1] if want_sums else None
    wv, sems = refs[-2:]
    copies = weight_copies_rel(idx_ref, pieces, 0, wv, sems)
    for copy in copies:
        copy.start()
    for copy in copies:
        copy.wait()
    height, tall = x_ref.shape[1] - 2, x_ref.shape[2]
    step = height // 2
    rows = step * tall
    if want_sums:
        s_ref[...] = jnp.zeros(s_ref.shape, F32)

    @pl.loop(0, 2)
    def _(part):
        acc = None
        for dy in range(3):
            for dx in range(3):
                if transposed:
                    view = x_ref[2 - dx, pl.ds(part * step + 2 - dy, step)]
                    dims = NT
                else:
                    view = x_ref[dx, pl.ds(part * step + dy, step)]
                    dims = (((1,), (0,)), ((), ()))
                piece = lax.dot_general(
                    view.reshape(rows, C), wv[3 * dy + dx], dims, preferred_element_type=F32
                )
                acc = piece if acc is None else acc + piece
        o_ref[pl.ds(part * step, step)] = acc.reshape(step, tall, C).astype(o_ref.dtype)
        if want_sums:
            s_ref[0:1] += jnp.sum(acc, axis=0, keepdims=True)
            s_ref[1:2] += jnp.sum(acc * acc, axis=0, keepdims=True)


def conv(idx, x3, pieces, transposed, want_sums, dtype, name):
    height, tall = x3.shape[1] - 2, x3.shape[2]
    out_shape = [sds((height, tall, C), dtype)]
    if want_sums:
        out_shape.append(sds((2, C), F32))
    out = pl.pallas_call(
        functools.partial(conv_kernel, len(pieces), transposed, want_sums),
        in_specs=[SM, VM] + [ANY] * len(pieces),
        out_specs=[VM] * len(out_shape),
        out_shape=out_shape,
        scratch_shapes=[pltpu.VMEM((9, C, C), BF), pltpu.SemaphoreType.DMA((32,))],
        compiler_params=params(),
        cost_estimate=cost(2 * 9 * C * C * height * tall, 10e6),
        name=name,
    )(idx, x3, *pieces)
    return out if want_sums else out[0]


def mid_kernel(batch, count_all, idx, st, gb, z_ref, rows_ref, cols_ref, d_ref, u3, hp, hc, hs, uc):
    height, tall, lanes = z_ref.shape
    across = tall // (2 * batch)
    step = pl.program_id(0)
    mean, rs, sc, sh = coef(st[...], gb[...], count_all)

    def act(v):
        y = v * sc + sh
        return y * sigm(y)

    mask = side_mask(idx, 2 * batch, lanes, 0)
    flat = act(cols_ref[...].reshape(-1, lanes)).reshape(height + 2, 2 * batch, lanes)
    uc[...] = flat * mask[None]
    uc[0] = uc[0] * idx[3].astype(F32)
    uc[height + 1] = uc[height + 1] * idx[4].astype(F32)
    put_row(u3, 0, act(rows_ref[0].astype(F32)) * idx[3].astype(F32), uc, batch, across)
    put_row(u3, height + 1, act(rows_ref[1].astype(F32)) * idx[4].astype(F32), uc, batch, across)

    @pl.loop(0, height)
    def _(h):
        put_row(u3, h + 1, act(z_ref[h]), uc, batch, across)

    @pl.when(step == 0)
    def _():
        hp[...] = jnp.zeros(hp.shape, F32)
        hc[...] = jnp.zeros(hc.shape, F32)

    hc[...] += jnp.dot(
        uc[...].reshape(-1, lanes).astype(BF), d_ref[...], preferred_element_type=F32
    )
    part = (height + 2) // 2
    size = part * tall

    @pl.loop(0, 2)
    def _(k):
        hp[pl.ds(pl.multiple_of(k * size, size), size)] += jnp.dot(
            u3[1, pl.ds(k * part, part)].reshape(size, lanes),
            d_ref[...],
            preferred_element_type=F32,
        )

    @pl.when(step == pl.num_programs(0) - 1)
    def _():
        inner = hp[tall : (height + 1) * tall]
        hs[0:1] = jnp.sum(inner, axis=0, keepdims=True)
        hs[1:2] = jnp.sum(inner * inner, axis=0, keepdims=True)


def mid(idx, st, gb, z, rows, cols, down, batch, count_all):
    height, tall, chans = z.shape
    lanes = BLK
    r = height + 2
    wide = TASKS * CA
    return pl.pallas_call(
        functools.partial(mid_kernel, batch, count_all),
        grid=(chans // lanes,),
        in_specs=[
            SM,
            pl.BlockSpec((2, lanes), lambda c: (0, c)),
            pl.BlockSpec((2, lanes), lambda c: (0, c)),
            pl.BlockSpec((height, tall, lanes), lambda c: (0, 0, c)),
            pl.BlockSpec((2, tall, lanes), lambda c: (0, 0, c)),
            pl.BlockSpec((r, 2 * batch, lanes), lambda c: (0, 0, c)),
            pl.BlockSpec((lanes, wide), lambda c: (c, 0)),
        ],
        out_specs=[
            pl.BlockSpec((3, r, tall, lanes), lambda c: (0, 0, 0, c)),
            pl.BlockSpec((r * tall, wide), lambda c: (0, 0)),
            pl.BlockSpec((r * 2 * batch, wide), lambda c: (0, 0)),
            pl.BlockSpec((2, wide), lambda c: (0, 0)),
        ],
        out_shape=[
            sds((3, r, tall, chans), BF),
            sds((r * tall, wide), F32),
            sds((r * 2 * batch, wide), F32),
            sds((2, wide), F32),
        ],
        scratch_shapes=[pltpu.VMEM((r, 2 * batch, lanes), F32)],
        compiler_params=params(),
        cost_estimate=cost(2 * r * tall * chans * wide, 10e6, 2e6),
        name="mid",
    )(idx, st, gb, z, rows, cols, down)


def hidden_kernel(tall, count_all, st, gb, hp, hc, up, h_ref, hcb, ms):
    mean, rs, sc, sh = coef(st[...], gb[...], count_all)
    yc = hc[...] * sc + sh
    hcb[...] = (yc * sigm(yc)).astype(BF)
    n_rows = hp.shape[0] // tall
    ms[...] = jnp.zeros(ms.shape, F32)

    def row(r):
        at = pl.ds(pl.multiple_of(r * tall, tall), tall)
        y = hp[at] * sc + sh
        h_ref[at] = (y * sigm(y)).astype(BF)

    @pl.loop(0, n_rows)
    def _(r):
        row(r)

    chunk = 4 * tall
    for t in range(TASKS):

        @pl.loop(0, (n_rows - 2) // 4)
        def _(k):
            at = pl.ds(pl.multiple_of(tall + k * chunk, tall), chunk)
            pre = jnp.dot(h_ref[at, t * CA : (t + 1) * CA], up[t], preferred_element_type=F32)
            ms[2 * t : 2 * t + 1] += jnp.sum(pre, axis=0, keepdims=True)
            ms[2 * t + 1 : 2 * t + 2] += jnp.sum(pre * pre, axis=0, keepdims=True)


def hidden(st, gb, hp, hc, up, tall, count_all):
    return pl.pallas_call(
        functools.partial(hidden_kernel, tall, count_all),
        in_specs=[VM] * 5,
        out_specs=[VM] * 3,
        out_shape=[sds(hp.shape, BF), sds(hc.shape, BF), sds((2 * TASKS, C), F32)],
        compiler_params=params(),
        cost_estimate=cost(2 * hp.shape[0] * CA * C * TASKS, 5e6, 2e6),
        name="hidden",
    )(st, gb, hp, hc, up)


def da_kernel(task, n_pieces, n_prev, idx, go, *refs):
    pieces = refs[:n_pieces]
    da, wv, ws, sems = refs[n_pieces + n_prev :]
    q = go.shape[3]
    half_h = go.shape[2] - 2
    copies = weight_copies_task(idx, pieces, task * 9, wv, sems)
    for copy in copies:
        copy.start()
    for copy in copies:
        copy.wait()

    def add(a, b):
        return (a.astype(F32) + b.astype(F32)).astype(BF)

    for a in range(2):
        for k in range(2):
            taps = []
            for dx in range(3):
                if k == 0:
                    taps.append(add(wv[3 * a + dx], wv[3 * (a + 1) + dx]))
                else:
                    taps.append(wv[3 * (2 if a == 0 else 0) + dx])
            ws[a, k, 0, 0] = add(taps[0], taps[1])
            ws[a, k, 0, 1] = taps[2]
            ws[a, k, 1, 0] = add(taps[1], taps[2])
            ws[a, k, 1, 1] = taps[0]
    for a in range(2):
        for bb in range(2):
            acc = None
            for k in range(2):
                for m in range(2):
                    ro = 0 if k == 0 else (-1 if a == 0 else 1)
                    co = 0 if m == 0 else (-1 if bb == 0 else 1)
                    view = go[0, co + 1, 1 + ro : 1 + ro + half_h].reshape(half_h * q, C)
                    piece = lax.dot_general(
                        view, ws[a, k, bb, m], NT, preferred_element_type=F32
                    )
                    acc = piece if acc is None else acc + piece
            da[0, :, a, bb] = acc.reshape(half_h, q, C).astype(BF)


def task_back(idx, go, pieces, task, prev):
    half_h, q = go.shape[2] - 2, go.shape[3]
    return pl.pallas_call(
        functools.partial(da_kernel, task, len(pieces), len(prev)),
        grid=(1,),
        in_specs=[SM, pl.BlockSpec((1,) + go.shape[1:], lambda k: (task, 0, 0, 0, 0))]
        + [ANY] * (len(pieces) + len(prev)),
        out_specs=pl.BlockSpec((1, half_h, 2, 2, q, C), lambda k: (task, 0, 0, 0, 0, 0)),
        out_shape=sds((TASKS, half_h, 2, 2, q, C), BF),
        scratch_shapes=[
            pltpu.VMEM((9, C, C), BF),
            pltpu.VMEM((2, 2, 2, 2, C, C), BF),
            pltpu.SemaphoreType.DMA((32,)),
        ],
        input_output_aliases={2 + len(pieces) + k: k for k in range(len(prev))},
        compiler_params=params(),
        cost_estimate=cost(2 * 16 * C * C * half_h * q, 8e6),
        name="task_back",
    )(idx, go, *pieces, *prev)


def attend_kernel(
    batch, count_all, idx, st, gb, mst, mgb, z_ref, rows_ref, cols_ref, h_ref, hc_ref, up, da, cot,
    se, so, dym, dy2, pooled, sums,
    ac, pre, prev,
):
    height, tall, lanes = z_ref.shape
    across = tall // (2 * batch)
    q = tall // 2
    mean, rs, sc, sh = coef(st[...], gb[...], count_all)
    mcoef = [
        coef(mst[2 * t : 2 * t + 2], mgb[2 * t : 2 * t + 2], count_all) for t in range(TASKS)
    ]
    mask = side_mask(idx, 2 * batch, lanes, 0)
    top, bottom = idx[3].astype(F32), idx[4].astype(F32)

    y = cols_ref[...].reshape(-1, lanes) * sc + sh
    pc = (y * sigm(y)).reshape(height + 2, 2 * batch, lanes) * mask[None]
    for t in range(TASKS):
        mc = jnp.dot(hc_ref[:, t * CA : (t + 1) * CA], up[t], preferred_element_type=F32)
        _, _, msc, msh = mcoef[t]
        mc = sigm(mc * msc + msh).reshape(height + 2, 2 * batch, lanes)
        ac[t] = (mc * pc).astype(BF).astype(F32)
        ac[t, 0] = ac[t, 0] * top
        ac[t, height + 1] = ac[t, height + 1] * bottom
        pre[t] = jnp.dot(
            h_ref[:, t * CA : (t + 1) * CA], up[t], preferred_element_type=F32
        ).reshape(height + 2, tall, lanes)
    sums[...] = jnp.zeros(sums.shape, F32)

    def col_sums(t, r, a):
        even, odd = a[0:q], a[q : 2 * q]
        lo, hi = shifted(
            even,
            odd,
            col_block(ac.at[t], r, 0, batch, across),
            col_block(ac.at[t], r, 1, batch, across),
            batch,
            across,
        )
        return lo + even, even + odd, odd + hi

    def halo_row(r, place, scale):
        yy = rows_ref[place].astype(F32) * sc + sh
        p = yy * sigm(yy) * scale
        out = []
        for t in range(TASKS):
            _, _, msc, msh = mcoef[t]
            a = (sigm(pre[t, r] * msc + msh) * p).astype(BF).astype(F32)
            out.append(col_sums(t, r, a))
        return out

    first = halo_row(0, 0, top)
    for t in range(TASKS):
        for dx in range(3):
            prev[t, dx] = first[t][dx]

    def inner(i, par):
        h = 2 * i + par
        r = h + 1
        z = z_ref[h]
        yy = z * sc + sh
        s = sigm(yy)
        p = yy * s
        slope = s * (1.0 + yy * (1.0 - s))
        shared = cot[i]
        shared = jnp.concatenate([shared, shared], axis=0)
        cs = []
        branches = []
        for t in range(TASKS):
            mmean, mrs, msc, msh = mcoef[t]
            mp = pre[t, r]
            m = sigm(mp * msc + msh)
            a = (m * p).astype(BF).astype(F32)
            cs.append(col_sums(t, r, a))
            d = da[t, h].astype(F32)
            br = m * d
            branches.append(br)
            shared = shared + br
            dm = br * p * (1.0 - m)
            dym[t, h] = dm.astype(BF)
            sums[2 * t : 2 * t + 1] += jnp.sum(dm, axis=0, keepdims=True)
            sums[2 * t + 1 : 2 * t + 2] += jnp.sum(dm * (mp - mmean), axis=0, keepdims=True)
        g2 = shared * slope
        dy2[h] = g2
        sums[6:7] += jnp.sum(g2, axis=0, keepdims=True)
        sums[7:8] += jnp.sum(g2 * (z - mean), axis=0, keepdims=True)
        k = 8
        for t in range(TASKS):
            for s2 in range(t, TASKS):
                sums[k : k + 1] += jnp.sum(branches[t] * branches[s2], axis=0, keepdims=True)
                k += 1
        return cs, p[0:q] + p[q : 2 * q]

    @pl.loop(0, height // 2)
    def _(i):
        cs, pool_a = inner(i, 0)
        for t in range(TASKS):
            for dx in range(3):
                se[t, dx, i] = (prev[t, dx] + cs[t][dx]).astype(BF)
                prev[t, dx] = cs[t][dx]
        cs, pool_b = inner(i, 1)
        for t in range(TASKS):
            for dx in range(3):
                so[t, dx, i] = (prev[t, dx] + cs[t][dx]).astype(BF)
                prev[t, dx] = cs[t][dx]
        pooled[i] = (pool_a + pool_b) * 0.25

    last = halo_row(height + 1, 1, bottom)
    for t in range(TASKS):
        for dx in range(3):
            se[t, dx, height // 2] = (prev[t, dx] + last[t][dx]).astype(BF)
        sums[2 * t + 1 : 2 * t + 2] = sums[2 * t + 1 : 2 * t + 2] * mcoef[t][1]
    sums[7:8] = sums[7:8] * rs


def attend(idx, st, gb, mst, mgb, z, rows, cols, h, hc, up, da, cot, batch, count_all):
    height, tall, chans = z.shape
    lanes = BLK
    r, q, half = height + 2, tall // 2, height // 2

    def two(n):
        return pl.BlockSpec((n, lanes), lambda c: (0, c))

    def three(a, b):
        return pl.BlockSpec((a, b, lanes), lambda c: (0, 0, c))

    def four(a, b, d):
        return pl.BlockSpec((a, b, d, lanes), lambda c: (0, 0, 0, c))

    def five(a, b, d, e):
        return pl.BlockSpec((a, b, d, e, lanes), lambda c: (0, 0, 0, 0, c))

    def whole(a):
        return pl.BlockSpec(a.shape, lambda c: (0,) * a.ndim)

    return pl.pallas_call(
        functools.partial(attend_kernel, batch, count_all),
        grid=(chans // lanes,),
        in_specs=[
            SM,
            two(2),
            two(2),
            two(2 * TASKS),
            two(2 * TASKS),
            three(height, tall),
            three(2, tall),
            three(r, 2 * batch),
            whole(h),
            whole(hc),
            three(TASKS, CA),
            four(TASKS, height, tall),
            three(half, q),
        ],
        out_specs=[
            five(TASKS, 3, half + 1, q),
            five(TASKS, 3, half, q),
            four(TASKS, height, tall),
            three(height, tall),
            three(half, q),
            two(14),
        ],
        out_shape=[
            sds((TASKS, 3, half + 1, q, chans), BF),
            sds((TASKS, 3, half, q, chans), BF),
            sds((TASKS, height, tall, chans), BF),
            sds((height, tall, chans), F32),
            sds((half, q, chans), F32),
            sds((14, chans), F32),
        ],
        scratch_shapes=[
            pltpu.VMEM((TASKS, r, 2 * batch, lanes), F32),
            pltpu.VMEM((TASKS, r, tall, lanes), F32),
            pltpu.VMEM((TASKS, 3, q, lanes), F32),
        ],
        compiler_params=params(),
        cost_estimate=cost(2 * r * tall * CA * chans * TASKS, 25e6, 6e6),
        name="attend",
    )(idx, st, gb, mst, mgb, z, rows, cols, h, hc, up, da, cot)


def mask_back_kernel(
    tall, count_all, mst, mgb, msum, hst, hgb, dym, h_ref, hp, up, du, dh, hs, acc
):
    step = pl.program_id(0)
    n_rows = h_ref.shape[0]

    @pl.when(step == 0)
    def _():
        acc[...] = jnp.zeros(acc.shape, F32)

    inner = pl.ds(tall, n_rows - 2 * tall)
    for t in range(TASKS):
        mean, rs, sc, _ = coef(mst[2 * t : 2 * t + 2], mgb[2 * t : 2 * t + 2], count_all)
        tot = msum[2 * t : 2 * t + 1] / count_all
        cross = msum[2 * t + 1 : 2 * t + 2] * rs / count_all
        ht = h_ref[inner, t * CA : (t + 1) * CA]
        pre = jnp.dot(ht, up[t], preferred_element_type=F32)
        dm = dym[t].reshape(pre.shape).astype(F32)
        dz = (sc * (dm - tot - (pre - mean) * cross)).astype(BF)
        du[t] = lax.dot_general(ht, dz, TN, preferred_element_type=F32)
        acc[:, t * CA : (t + 1) * CA] += lax.dot_general(dz, up[t], NT, preferred_element_type=F32)

    @pl.when(step == pl.num_programs(0) - 1)
    def _():
        mean, rs, sc, sh = coef(hst[...], hgb[...], count_all)
        hs[...] = jnp.zeros(hs.shape, F32)
        chunk = 2 * tall

        @pl.loop(0, (n_rows - 2 * tall) // chunk)
        def _(k):
            at = pl.ds(pl.multiple_of(k * chunk, chunk), chunk)
            v = hp[pl.ds(pl.multiple_of(tall + k * chunk, tall), chunk)]
            y = v * sc + sh
            s = sigm(y)
            g = acc[at] * (s * (1.0 + y * (1.0 - s)))
            dh[at] = g
            hs[0:1] += jnp.sum(g, axis=0, keepdims=True)
            hs[1:2] += jnp.sum(g * (v - mean) * rs, axis=0, keepdims=True)


def mask_back(mst, mgb, msum, hst, hgb, dym, h, hp, up, tall, count_all):
    lanes = BLK
    wide = TASKS * CA
    pixels = h.shape[0] - 2 * tall

    def two(n):
        return pl.BlockSpec((n, lanes), lambda c: (0, c))

    def whole(a):
        return pl.BlockSpec(a.shape, lambda c: (0,) * a.ndim)

    return pl.pallas_call(
        functools.partial(mask_back_kernel, tall, count_all),
        grid=(C // lanes,),
        in_specs=[
            two(2 * TASKS),
            two(2 * TASKS),
            two(2 * TASKS),
            whole(hst),
            whole(hgb),
            pl.BlockSpec(dym.shape[:3] + (lanes,), lambda c: (0, 0, 0, c)),
            whole(h),
            whole(hp),
            pl.BlockSpec((TASKS, CA, lanes), lambda c: (0, 0, c)),
        ],
        out_specs=[
            pl.BlockSpec((TASKS, CA, lanes), lambda c: (0, 0, c)),
            pl.BlockSpec((pixels, wide), lambda c: (0, 0)),
            pl.BlockSpec((2, wide), lambda c: (0, 0)),
        ],
        out_shape=[sds((TASKS, CA, C), F32), sds((pixels, wide), F32), sds((2, wide), F32)],
        scratch_shapes=[pltpu.VMEM((pixels, wide), F32)],
        compiler_params=params(),
        cost_estimate=cost(6 * pixels * C * wide, 8e6, 1e6),
        name="mask_back",
    )(mst, mgb, msum, hst, hgb, dym, h, hp, up)


def norm_back_kernel(
    batch, count_all, idx, st, gb, gs, dy, drows, dcols, z, zrows, zcols, x3, work
):
    height, tall, lanes = z.shape
    across = tall // (2 * batch)
    mean, rs, sc, _ = coef(st[...], gb[...], count_all)
    tot = gs[0:1] / count_all
    cross = gs[1:2] * rs / count_all

    def back(d, v):
        return sc * (d - tot - (v - mean) * cross)

    mask = side_mask(idx, 2 * batch, lanes, 0)
    flat = back(dcols[...].reshape(-1, lanes), zcols[...].reshape(-1, lanes))
    work[...] = flat.reshape(height + 2, 2 * batch, lanes) * mask[None]
    top, bottom = idx[3].astype(F32), idx[4].astype(F32)
    work[0] = work[0] * top
    work[height + 1] = work[height + 1] * bottom
    put_row(x3, 0, back(drows[0].astype(F32), zrows[0].astype(F32)) * top, work, batch, across)
    put_row(
        x3, height + 1, back(drows[1].astype(F32), zrows[1].astype(F32)) * bottom, work, batch, across
    )

    @pl.loop(0, height)
    def _(h):
        put_row(x3, h + 1, back(dy[h], z[h]), work, batch, across)


def norm_back(idx, st, gb, gs, dy, dhalo, z, zhalo, batch, count_all, name):
    height, tall, chans = z.shape
    lanes = BLK
    r = height + 2

    def two(n):
        return pl.BlockSpec((n, lanes), lambda c: (0, c))

    def three(a, b):
        return pl.BlockSpec((a, b, lanes), lambda c: (0, 0, c))

    field = [three(height, tall), three(2, tall), three(r, 2 * batch)]
    return pl.pallas_call(
        functools.partial(norm_back_kernel, batch, count_all),
        grid=(chans // lanes,),
        in_specs=[SM, two(2), two(2), two(2)] + field + field,
        out_specs=pl.BlockSpec((3, r, tall, lanes), lambda c: (0, 0, 0, c)),
        out_shape=sds((3, r, tall, chans), BF),
        scratch_shapes=[pltpu.VMEM((r, 2 * batch, lanes), F32)],
        compiler_params=params(),
        cost_estimate=cost(0, 10e6),
        name=name,
    )(idx, st, gb, gs, dy, *dhalo, z, *zhalo)


def first_back_kernel(
    count_all, hst, hgb, hsum, st, gb, dh, hp, u3, part, z, down, dd, dy, gs, low
):
    height, tall, lanes = z.shape

    @pl.when(pl.program_id(0) == 0)
    def _():
        mean, rs, sc, _ = coef(hst[...], hgb[...], count_all)
        tot = hsum[0:1] / count_all
        cross = hsum[1:2] * rs / count_all
        chunk = 2 * tall

        @pl.loop(0, height // 2)
        def _(k):
            at = pl.ds(pl.multiple_of(k * chunk, chunk), chunk)
            v = hp[pl.ds(pl.multiple_of(tall + k * chunk, tall), chunk)]
            low[at] = (sc * (dh[at] - tot - (v - mean) * cross)).astype(BF)

    u = u3[0, 1 : height + 1].reshape(height * tall, lanes)
    dd[...] = lax.dot_general(u, low[...], TN, preferred_element_type=F32)
    mean, rs, sc, sh = coef(st[...], gb[...], count_all)
    gs[...] = jnp.zeros(gs.shape, F32)
    rows = 4

    @pl.loop(0, height // rows)
    def _(k):
        at = pl.ds(pl.multiple_of(k * rows * tall, rows * tall), rows * tall)
        back = lax.dot_general(low[at], down[...], NT, preferred_element_type=F32)
        v = z[pl.ds(k * rows, rows)].reshape(rows * tall, lanes)
        y = v * sc + sh
        s = sigm(y)
        total = part[pl.ds(k * rows, rows)].reshape(rows * tall, lanes) + back
        g = total * (s * (1.0 + y * (1.0 - s)))
        dy[pl.ds(k * rows, rows)] = g.reshape(rows, tall, lanes)
        gs[0:1] += jnp.sum(g, axis=0, keepdims=True)
        gs[1:2] += jnp.sum(g * (v - mean) * rs, axis=0, keepdims=True)


def first_back(hst, hgb, hsum, st, gb, dh, hp, u3, part, z, down, count_all):
    height, tall, chans = z.shape
    lanes = BLK
    wide = TASKS * CA

    def two(n):
        return pl.BlockSpec((n, lanes), lambda c: (0, c))

    def whole(a):
        return pl.BlockSpec(a.shape, lambda c: (0,) * a.ndim)

    field = pl.BlockSpec((height, tall, lanes), lambda c: (0, 0, c))
    return pl.pallas_call(
        functools.partial(first_back_kernel, count_all),
        grid=(chans // lanes,),
        in_specs=[
            whole(hst),
            whole(hgb),
            whole(hsum),
            two(2),
            two(2),
            whole(dh),
            whole(hp),
            pl.BlockSpec((1, height + 2, tall, lanes), lambda c: (1, 0, 0, c)),
            field,
            field,
            pl.BlockSpec((lanes, wide), lambda c: (c, 0)),
        ],
        out_specs=[pl.BlockSpec((lanes, wide), lambda c: (c, 0)), field, two(2)],
        out_shape=[sds((chans, wide), F32), sds((height, tall, chans), F32), sds((2, chans), F32)],
        scratch_shapes=[pltpu.VMEM((height * tall, wide), BF)],
        compiler_params=params(),
        cost_estimate=cost(4 * height * tall * chans * wide, 12e6, 1e6),
        name="first_back",
    )(hst, hgb, hsum, st, gb, dh, hp, u3, part, z, down)


def flip_place(place, j):
    s = lax.bitwise_xor(place, j)
    return lax.shift_right_logical(s, 1) + 2 * lax.bitwise_and(s, 1)


def put_blocks(idx, grad, mine, other, m):
    low = grad.astype(BF)
    even = idx[2] == 0
    for i in range(NB):
        e = lax.bitwise_xor(idx[0], i)
        for j in range(NB):
            s = flip_place(idx[1], j)
            block = low[i * BLK : (i + 1) * BLK, j * BLK : (j + 1) * BLK]
            a, b = block[0:HB], block[HB:BLK]
            at = pl.ds(pl.multiple_of(m * HB, HB), HB)
            mine[e, s, at] = jnp.where(even, a, b)
            other[e, s, at] = jnp.where(even, b, a)


def put_in_order(idx, grad, mine, other, m):
    low = grad.astype(BF)
    even = idx[2] == 0
    at = slice(m * HB, (m + 1) * HB)
    for i in range(NB):
        for j in range(NB):
            block = low[i * BLK : (i + 1) * BLK, j * BLK : (j + 1) * BLK]
            a, b = block[0:HB], block[HB:BLK]
            mine[i * NB + j, at] = jnp.where(even, a, b)
            other[i * NB + j, at] = jnp.where(even, b, a)


def wgrad_kernel(n_extra, idx, x3, g3, *refs):
    mine, other = refs[n_extra:]
    height, tall = x3.shape[1] - 2, x3.shape[2]
    g = g3[0, 1 : height + 1].reshape(height * tall, C)

    @pl.loop(0, 3)
    def _(dy):
        for dx in range(3):
            view = x3[dx, pl.ds(dy, height)].reshape(height * tall, C)
            grad = lax.dot_general(view, g, TN, preferred_element_type=F32)
            put_blocks(idx, grad, mine, other, 3 * dy + dx)

    if n_extra:
        ddown, dup = refs[:2]
        even = idx[2] == 0
        unit = BLK // 4

        def chunk(c):
            block, r = divmod(c, 4)
            t, block = divmod(block, 2 * NB)
            kind, n = divmod(block, NB)
            if kind == 0:
                return ddown[n * BLK + r * unit : n * BLK + (r + 1) * unit, t * CA : (t + 1) * CA]
            return dup[t, r * unit : (r + 1) * unit, n * BLK : (n + 1) * BLK]

        at = pl.ds(9 * HB, PROJ_ROWS)
        for n in range(NB * NB):
            e = lax.bitwise_xor(idx[0], n // NB)
            s = flip_place(idx[1], n % NB)
            a, b = [
                jnp.concatenate([chunk(6 * n + 3 * k + c) for c in range(3)], axis=0).astype(BF)
                for k in range(2)
            ]
            mine[e, s, at] = jnp.where(even, a, b)
            other[e, s, at] = jnp.where(even, b, a)


def wgrad(idx, x3, g3, name, extra=()):
    r, tall = x3.shape[1], x3.shape[2]
    rows = 9 * HB + (PROJ_ROWS if extra else 0)
    return pl.pallas_call(
        functools.partial(wgrad_kernel, len(extra)),
        grid=(1,),
        in_specs=[
            SM,
            pl.BlockSpec(x3.shape, lambda c: (0, 0, 0, 0)),
            pl.BlockSpec((1,) + g3.shape[1:], lambda c: (1, 0, 0, 0)),
        ]
        + [VM] * len(extra),
        out_specs=[pl.BlockSpec((4, 4, rows, BLK), lambda c: (0, 0, 0, 0))] * 2,
        out_shape=[sds((4, 4, rows, BLK), BF)] * 2,
        compiler_params=params(),
        cost_estimate=cost(2 * 9 * C * C * (r - 2) * tall, 10e6),
        name=name,
    )(idx, x3, g3, *extra)


def task_wgrad_kernel(n_prev, idx, se, so, go, *refs):
    mine, other = refs[n_prev:]
    half, q = so.shape[2], so.shape[3]
    g = go[0, 0, 1 : half + 1].reshape(half * q, C)
    for dy in range(3):
        for dx in range(3):
            if dy == 1:
                view = so[0, dx]
            else:
                view = se[0, dx, dy // 2 : dy // 2 + half]
            grad = lax.dot_general(view.reshape(half * q, C), g, TN, preferred_element_type=F32)
            put_in_order(idx, grad, mine, other, 3 * dy + dx)


def task_wgrad(idx, se, so, go, task, prev):
    half, q = so.shape[2], so.shape[3]
    return pl.pallas_call(
        functools.partial(task_wgrad_kernel, len(prev)),
        grid=(1,),
        in_specs=[
            SM,
            pl.BlockSpec((1,) + se.shape[1:], lambda k: (task, 0, 0, 0, 0)),
            pl.BlockSpec((1,) + so.shape[1:], lambda k: (task, 0, 0, 0, 0)),
            pl.BlockSpec((1, 1) + go.shape[2:], lambda k: (task, 1, 0, 0, 0)),
        ]
        + [ANY] * len(prev),
        out_specs=[pl.BlockSpec((NB * NB, 9 * HB, BLK), lambda k: (0, task, 0))] * 2,
        out_shape=[sds((NB * NB, 9 * TASKS * HB, BLK), BF)] * 2,
        input_output_aliases={4 + k: k for k in range(len(prev))},
        compiler_params=params(),
        cost_estimate=cost(2 * 9 * C * C * half * q, 8e6),
        name="task_wgrad",
    )(idx, se, so, go, *prev)


def task_fwd_kernel(task, n_pieces, n_prev, idx, se, so, *refs):
    pieces = refs[:n_pieces]
    out, wv, sems = refs[n_pieces + n_prev :]
    half, q = so.shape[2], so.shape[3]
    copies = weight_copies_task(idx, pieces, task * 9, wv, sems)
    for copy in copies:
        copy.start()
    for copy in copies:
        copy.wait()
    acc = None
    for dy in range(3):
        for dx in range(3):
            if dy == 1:
                view = so[0, dx]
            else:
                view = se[0, dx, dy // 2 : dy // 2 + half]
            piece = jnp.dot(
                view.reshape(half * q, C), wv[3 * dy + dx], preferred_element_type=F32
            )
            acc = piece if acc is None else acc + piece
    out[0] = (acc * 0.25).reshape(half, q, C).astype(BF)


def task_fwd(idx, se, so, pieces, task, prev):
    half, q = so.shape[2], so.shape[3]
    return pl.pallas_call(
        functools.partial(task_fwd_kernel, task, len(pieces), len(prev)),
        grid=(1,),
        in_specs=[
            SM,
            pl.BlockSpec((1,) + se.shape[1:], lambda k: (task, 0, 0, 0, 0)),
            pl.BlockSpec((1,) + so.shape[1:], lambda k: (task, 0, 0, 0, 0)),
        ]
        + [ANY] * (len(pieces) + len(prev)),
        out_specs=pl.BlockSpec((1, half, q, C), lambda k: (task, 0, 0, 0)),
        out_shape=sds((TASKS, half, q, C), BF),
        scratch_shapes=[pltpu.VMEM((9, C, C), BF), pltpu.SemaphoreType.DMA((32,))],
        input_output_aliases={3 + len(pieces) + k: k for k in range(len(prev))},
        compiler_params=params(),
        cost_estimate=cost(2 * 9 * C * C * half * q, 8e6),
        name="task_fwd",
    )(idx, se, so, *pieces, *prev)


def shampoo_step(g, left, right, lroot, rroot, weight, rate):
    low = g.astype(BF)
    ln = stat_decay * left + (1.0 - stat_decay) * lax.dot_general(
        low, low, NT, preferred_element_type=F32
    )
    rn = stat_decay * right + (1.0 - stat_decay) * lax.dot_general(
        low, low, TN, preferred_element_type=F32
    )
    step = jnp.dot(lroot.astype(BF), low, preferred_element_type=F32)
    step = jnp.dot(step.astype(BF), rroot.astype(BF), preferred_element_type=F32)
    return ln, rn, weight - rate * step


def shampoo_kernel(n_prev, idx, mine, other, left, right, lroot, rroot, weight, *refs):
    gr, ln, rn, wn = refs[n_prev:]
    even = idx[2] == 0
    for k in range(mine.shape[0] // HB):
        a, b = mine[k * HB : (k + 1) * HB], other[k * HB : (k + 1) * HB]
        g = jnp.concatenate([jnp.where(even, a, b), jnp.where(even, b, a)], axis=0).astype(F32)
        gr[0, k] = g
        ln[0, k], rn[0, k], wn[0, k] = shampoo_step(
            g, left[0, k], right[0, k], lroot[0, k], rroot[0, k], weight[0, k], conv_rate
        )


def shampoo_conv(idx, mine, other, state, first, prev):
    n = mine.shape[0] // HB
    each = 3
    block = pl.BlockSpec((1, each, BLK, BLK), lambda k: (0, first // each + k, 0, 0))
    half = pl.BlockSpec((each * HB, BLK), lambda k: (k, 0))
    full = state[0].shape
    return pl.pallas_call(
        functools.partial(shampoo_kernel, len(prev)),
        grid=(n // each,),
        in_specs=[SM, half, half] + [block] * 5 + [ANY] * len(prev),
        out_specs=[block] * 4,
        out_shape=[sds(full, F32)] * 4,
        input_output_aliases={8 + k: k for k in range(len(prev))},
        compiler_params=params(),
        cost_estimate=cost(n * 8 * BLK**3, n * 9 * BLK * BLK * 4),
        name="shampoo_conv",
    )(idx, mine, other, *state, *prev)


def shampoo_proj_kernel(g, left, right, lroot, rroot, weight, ln, rn, wn):
    for k in range(g.shape[2]):
        ln[0, 0, k], rn[0, 0, k], wn[0, 0, k] = shampoo_step(
            g[0, 0, k], left[0, 0, k], right[0, 0, k], lroot[0, 0, k], rroot[0, 0, k],
            weight[0, 0, k], proj_rate,
        )


def shampoo_proj(g, left, right, lroot, rroot, weight):
    block = pl.BlockSpec((1, 1) + g.shape[2:], lambda t, k: (t, k, 0, 0, 0))
    return pl.pallas_call(
        shampoo_proj_kernel,
        grid=g.shape[:2],
        in_specs=[block] * 6,
        out_specs=[block] * 3,
        out_shape=[sds(g.shape, F32)] * 3,
        compiler_params=params(),
        cost_estimate=cost(24 * 8 * BLK**3, 24 * 9 * BLK * BLK * 4),
        name="shampoo_proj",
    )(g, left, right, lroot, rroot, weight)


def to_rows(field):
    b, h, w, c = field.shape
    split = field.reshape(b, h, w // 2, 2, c)
    return jnp.transpose(split, (1, 3, 0, 2, 4)).reshape(h, w * b, c)


def from_rows(field, b):
    h, tall, c = field.shape
    split = field.reshape(h, 2, b, tall // (2 * b), c)
    return jnp.transpose(split, (2, 0, 3, 1, 4)).reshape(b, h, tall // b, c)


def pooled_rows(field):
    b, h, w, c = field.shape
    return jnp.transpose(field, (1, 0, 2, 3)).reshape(h, b * w, c)


def shards(
    images,
    cot_shared,
    cot_tasks,
    depth_mask,
    nash_weights,
    conv_weight,
    conv_left,
    conv_right,
    conv_left_root,
    conv_right_root,
    proj_weight,
    proj_left,
    proj_right,
    proj_left_root,
    proj_right_root,
    norm_params,
    norm_moment,
):
    batch, tile_h, tile_w, _ = images.shape
    half_h, half_w = tile_h // 2, tile_w // 2
    tall = batch * tile_w
    q = batch * half_w
    ha, wa = lax.axis_index("ha"), lax.axis_index("wa")
    count_all = float(
        batch * tile_h * tile_w * lax.axis_size("img") * lax.axis_size("ha") * lax.axis_size("wa")
    )
    idx = jnp.stack(
        [
            lax.axis_index("img"),
            ha,
            wa % 2,
            ha > 0,
            ha < lax.axis_size("ha") - 1,
            wa > 0,
            wa < lax.axis_size("wa") - 1,
        ]
    ).astype(jnp.int32)

    halves = conv_weight[0].reshape(conv_weight.shape[1], 2, HB, BLK)
    own = lax.dynamic_index_in_dim(halves, wa % 2, axis=1, keepdims=False).astype(BF)
    g0, g1 = Gather(own[None, 0:9]), Gather(own[None, 9:18])
    g0.near()
    edges = after(images, own)
    rows0 = jnp.stack(row_halo(edge_row(edges, 0), edge_row(edges, tile_h - 1)))
    g0.join(rows0)
    g0.far()
    g0.low()
    images = after(images, g0.line_low)
    off_down = 2 * C
    off_up = off_down + TASKS * CA
    gb1 = norm_params[:, 0:C]
    gb2 = norm_params[:, C : 2 * C]
    gbd = norm_params[:, off_down:off_up]
    gbu = jnp.transpose(norm_params[:, off_up:].reshape(2, TASKS, C), (1, 0, 2)).reshape(-1, C)
    proj_low = proj_weight.astype(BF)
    down = jnp.transpose(proj_low[:, 0].reshape(TASKS, C, CA), (1, 0, 2)).reshape(C, TASKS * CA)
    up = jnp.transpose(proj_low[:, 1], (0, 2, 1, 3)).reshape(TASKS, CA, C)

    image_rows = to_rows(images)
    x3 = shift_copies(idx, image_rows, rows0, halo_cols(image_rows, rows0, batch), batch)
    g0.high(g0.low_x, g0.low_y)
    g0.corner_a(x3)
    g0.corner_b()
    g1.near(g0.line_high)
    cot_tasks = after(cot_tasks, g0.line_high)

    depth_pick = jnp.arange(TASKS) == 1
    scale = jnp.where(depth_pick, depth_mask.astype(F32)[..., None], 1.0) * nash_weights
    weighted = cot_tasks.astype(F32).reshape(batch, half_h, half_w, TASKS, C)
    weighted = (weighted * (scale * 0.25)[..., None]).astype(BF)
    grid = jnp.transpose(weighted, (3, 1, 0, 2, 4))
    top, bottom = row_halo(grid[:, 0:1], grid[:, half_h - 1 :])
    top = jnp.where(ha > 0, top, jnp.zeros_like(top))
    bottom = jnp.where(ha < lax.axis_size("ha") - 1, bottom, jnp.zeros_like(bottom))
    grid = jnp.concatenate([top, grid, bottom], axis=1)
    left, right = col_halo(grid[:, :, :, 0:1], grid[:, :, :, half_w - 1 :])
    grid = jnp.concatenate([left, grid, right], axis=3)
    go3 = jnp.stack([grid[:, :, :, k : k + half_w] for k in range(3)], axis=1)
    go3 = go3.reshape(TASKS, 3, half_h + 2, q, C)
    cot = pooled_rows(cot_shared.astype(F32) * 0.25)

    g1.join(g0.corner_high)
    g1.far()
    g1.low()
    w0 = g0.pieces()
    z1, s1 = conv(after(idx, g1.line_low, go3), x3, w0, False, True, F32, "conv_first")

    def none(dep):
        return ()

    halo1 = halo(z1, batch)
    s1 = after(s1, g1.line_high)
    wt_mine = lax.all_gather(after(own[18:], s1), ("img", "ha"), axis=0, tiled=False)
    g1.high(s1)

    def s1_img1(dep):
        return g1.high_x, g1.high_y

    def s1_img2(dep):
        g1.corner_a(dep)
        g1.corner_b(dep)
        return ()

    s1 = sum_all(s1, [none, none, none, s1_img1, s1_img2])
    u3, hp, hc, hs = mid(idx, s1, gb1, z1, *halo1, down, batch, count_all)
    w1 = g1.pieces(hs)
    kept = {}

    def s2_ha1(dep):
        kept["z2"], kept["s2"] = conv(idx, after(u3, dep), w1, False, True, F32, "conv_second")
        return (kept["s2"],)

    hs = sum_all(hs, [none, none, none, s2_ha1, none], ("wa", "img", "ha"))
    z2, s2 = kept["z2"], kept["s2"]
    halo2 = halo(z2, batch)
    h, hcb, ms = hidden(hs, gbd, hp, hc, up, tall, count_all)
    s2m = sum_all(jnp.concatenate([s2, ms], axis=0), (), ("wa", "img", "ha"))
    wt_mine = after(wt_mine, s2m)
    wt = (wt_mine, swap(wt_mine, "wa", 1))
    kept["da"] = ()
    for task in range(TASKS):
        kept["da"] = (task_back(idx, go3, wt, task, kept["da"]),)
    s2, ms = s2m[0:2], s2m[2:]
    da = kept["da"][0].reshape(TASKS, tile_h, tall, C)
    se, so, dym, dy2, pooled, gsum = attend(
        idx, s2, gb2, ms, gbu, z2, *halo2, h, hcb, up, da, cot, batch, count_all
    )

    dhalo2 = halo(dy2, batch)
    kept["wt"] = ()

    def run_wgrad(task):
        def run(dep):
            kept["wt"] = task_wgrad(after(idx, dep), se, so, go3, task, kept["wt"])
            return tuple(kept["wt"])

        return run

    gsum = sum_all(gsum, [none, run_wgrad(0), run_wgrad(1), run_wgrad(2)])
    mine_t, other_t = kept["wt"]
    other_t = swap(other_t, "wa", 1)
    dup, dh, dhs = mask_back(ms, gbu, gsum[0:6], hs, gbd, dym, h, hp, up, tall, count_all)

    def run_second_back(dep):
        gs = after(gsum[6:8], dep)
        kept["z3"] = norm_back(
            idx, s2, gb2, gs, dy2, dhalo2, z2, halo2, batch, count_all, "second_back"
        )
        part_t = add_low(mine_t, after(other_t, dep))
        kept["gt"] = lax.psum_scatter(part_t, ("img", "ha"), scatter_dimension=0, tiled=True)
        return kept["z3"], part_t

    def run_conv_back(dep):
        kept["part"] = conv(idx, after(kept["z3"], dep), w1, True, False, F32, "conv_second_back")
        return (kept["part"],)

    dhs = sum_all(dhs, [run_second_back, none, run_conv_back, none, none])
    z3, part = kept["z3"], kept["part"]
    ddown, dy1, gs1 = first_back(hs, gbd, dhs, s1, gb1, dh, hp, u3, part, z1, down, count_all)
    dhalo1 = halo(dy1, batch)

    def run_wgrad_second(dep):
        kept["r1"] = Scatter(*wgrad(after(idx, dep), u3, z3, "wgrad_second", (ddown, dup)))
        return (kept["r1"].other,)

    def run_wa(dep):
        kept["r1"].wa(dep)
        return ()

    gs1 = sum_all(gs1, [none, run_wgrad_second, none, none, run_wa])
    r1 = kept["r1"]
    y3 = norm_back(idx, s1, gb1, gs1, dy1, dhalo1, z1, halo1, batch, count_all, "first_norm_back")
    y3 = after(y3, r1.corner_sum(y3))
    r1.corner_send()
    r0 = Scatter(*wgrad(idx, x3, y3, "wgrad_first"))
    state = (conv_left, conv_right, conv_left_root, conv_right_root, conv_weight)
    r0.wa()
    r1.high_sum(r0.mine)
    r1.high_send()
    r1.low_sum(*r1.high)
    r0.corner_sum(*r1.low)
    r0.corner_send()
    r1.low_send(r0.corner)
    outs = (task_fwd(after(idx, r0.corner, *r1.low), se, so, wt, 0, ()),)
    r0.high_sum(*outs)
    r0.high_send()
    r0.low_sum(*r0.high)
    r0.low_send()
    r1.far_sum(*r0.low)
    r1.far_send()
    outs = (task_fwd(after(idx, r1.far), se, so, wt, 1, outs),)
    r0.far_sum(*outs)
    r0.far_send()
    r1.near_sum(r0.far)
    r1.near_send()
    outs = (task_fwd(after(idx, r1.near), se, so, wt, 2, outs),)
    r0.near_sum(*outs)
    r0.near_send()
    grad1, grad1_other = r1.finish(r0.near)
    proj_total = gather_proj(grad1[9 * HB :])
    image_grad = conv(idx, after(y3, grad1), w0, True, False, BF, "conv_first_back")
    new = shampoo_conv(
        after(idx, image_grad), grad1[: 9 * HB], grad1_other[: 9 * HB], state, 9, ()
    )
    grad0, grad0_other = r0.finish(image_grad)
    new = shampoo_conv(idx, grad0, grad0_other, state, 0, new)
    gradt = after(kept["gt"][0], new[0])
    new = shampoo_conv(idx, gradt, swap(gradt, "wa", 1), state, 18, new)
    conv_total, conv_left_new, conv_right_new, conv_weight_new = new
    task_out = outs[0]

    image_grad = from_rows(image_grad, batch)
    task_out = jnp.transpose(
        task_out.reshape(TASKS, half_h, batch, half_w, C), (2, 1, 3, 0, 4)
    ).reshape(batch, half_h, half_w, TASKS * C)
    shared_out = jnp.transpose(
        pooled.astype(BF).reshape(half_h, batch, half_w, C), (1, 0, 2, 3)
    )

    proj_left_new, proj_right_new, proj_weight_new = shampoo_proj(
        proj_total, proj_left, proj_right, proj_left_root, proj_right_root, proj_weight
    )

    corner = jnp.sum(gsum[8:14], axis=1)
    gram = jnp.stack(
        [corner[0], corner[1], corner[2], corner[1], corner[3], corner[4], corner[2], corner[4], corner[5]]
    ).reshape(TASKS, TASKS)
    gain_grads = jnp.concatenate([gs1[1], gsum[7], dhs[1], gsum[1], gsum[3], gsum[5]])
    bias_grads = jnp.concatenate([gs1[0], gsum[6], dhs[0], gsum[0], gsum[2], gsum[4]])
    norm_grad = jnp.stack([gain_grads, bias_grads])
    moment_new = moment_decay * norm_moment + (1.0 - moment_decay) * norm_grad * norm_grad
    norm_new = norm_params - norm_rate * norm_grad / (jnp.sqrt(moment_new) + 1e-08)
    return (
        shared_out,
        task_out,
        image_grad,
        gram,
        conv_total,
        conv_left_new,
        conv_right_new,
        conv_weight_new,
        proj_total,
        proj_left_new,
        proj_right_new,
        proj_weight_new,
        norm_grad,
        moment_new,
        norm_new,
    )


def solution(mesh):
    tile = P("img", "ha", "wa", None)
    owned = P(("img", "ha"), None, None, None)
    return jax.shard_map(
        shards,
        mesh=mesh,
        in_specs=(tile, tile, tile, P("img", "ha", "wa"), P()) + (owned,) * 5 + (P(),) * 7,
        out_specs=(tile, tile, tile, P()) + (owned,) * 4 + (P(),) * 7,
        check_vma=False,
    )
```

time: 1620 us -> 569 us (0.35)
  local copies, waits for them, and re-layouts: 543 us -> 39.3 us
  matrix products: 384 us -> 0 us
  blocking collectives: 244 us -> 0 us
  Pallas kernels: 0 us -> 217 us
  other arithmetic: 149 us -> 56.4 us
  waiting for transfers between devices: 210 us -> 127 us
  starting transfers between devices: 58.1 us -> 102 us
    dot_general x149 -> x0, matrix products: 381 us -> none  [the longest x45 133 us: conv_back(): jnp.einsum('pjd,ijcd->pic', window, weights[:, :, 3 * row_shift + col_shi...]
    psum x6 -> x0, blocking collectives: 244 us -> none  [the longest x2 82.7 us: shards(): lax.psum((jnp.sum(conv_second, 0), jnp.sum(conv_second * conv_second, 0),...]
    reshape x100 -> x10, local copies, waits for them, and re-layouts: 228 us -> 4.34 us  [the longest x1 1.22 us: from_rows(): return jnp.transpose(split, (2, 0, 3, 1, 4)).reshape(b, h, tall // b, c)]
    pallas_call x0 -> x27, Pallas kernels: none -> 217 us  [the longest x4 44.9 us: conv(): pl.pallas_call(functools.partial(conv_kernel, len(pieces), transposed, wa...]
    reduce_scatter x1, waiting for transfers between devices: 162 us -> 0.01 us  [run_second_back(): lax.psum_scatter(part_t, ('img', 'ha'), scatter_dimension=0, tiled=True)]
    ppermute x24 -> x108, waiting for transfers between devices: 0.06 us -> 127 us  [the longest x96 101 us: swap(): return lax.ppermute(value, axis, pairs(axis, step))]
    unnamed x561 -> x155, local copies, waits for them, and re-layouts: 89.9 us -> 8.97 us
    slice x30 -> x56, local copies, waits for them, and re-layouts: 87.5 us -> 10.5 us  [the longest x2 1.2 us: shards(): s2, ms = (s2m[0:2], s2m[2:])]
  transfers between devices with their start and end apart: 28 -> 110, of which waited for: 3 -> 51; matrix products, arithmetic and copies ran while one was open for 50% -> 14% of each run, Pallas kernels for 0% -> 29%
where the time goes in v1:
time: 569 us; the launch traced here: 559 us
  Pallas kernels  217 us (38%)
  waiting for transfers between devices  127 us (22%)
  starting transfers between devices  102 us (18%)
  other arithmetic  56.4 us (10%)
  local copies, waits for them, and re-layouts  39.3 us (7%)
  between operations  16.7 us (3%)
    ppermute x96, waiting for transfers between devices, swap(): return lax.ppermute(value, axis, pairs(axis, step))  101 us
    ppermute x96, starting transfers between devices, swap(): return lax.ppermute(value, axis, pairs(axis, step))  82.9 us
    pallas_call x4, Pallas kernels, conv(): pl.pallas_call(functools.partial(conv_kernel, len(pieces), transposed, wa...  44.9 us
    convert_element_type x17, other arithmetic, add_low(): return total.astype(BF)  30.2 us
    ppermute x12, waiting for transfers between devices, row_halo(): return (lax.ppermute(last, 'ha', up), lax.ppermute(first, 'ha', down))  26.6 us
    pallas_call x3, Pallas kernels, task_back(): pl.pallas_call(functools.partial(da_kernel, task, len(pieces), len(prev))...  23.3 us
    pallas_call x2, Pallas kernels, wgrad(): pl.pallas_call(functools.partial(wgrad_kernel, len(extra)), grid=(1,), in...  21.5 us
    pallas_call x3, Pallas kernels, shampoo_conv(): pl.pallas_call(functools.partial(shampoo_kernel, len(prev)), grid=(n // e...  21.4 us
  transfers between devices with their start and end apart: 110, of which 51 were waited for; matrix products, arithmetic and copies ran while one was open for 14% of the time, Pallas kernels for 29%

profile of v1, /device:TPU:0, one launch (start us, length us, event | category | flops | bytes accessed | tf_op | source)
XLA Modules:
  0.0 559.5 jit_solution(17761199206033951382)
XLA Ops:
  9.5 4.0 collective-permute-start
  16.7 2.5 collective-permute-done.2
  19.2 3.0 collective-permute-done.1
  34.3 3.4 collective-permute-start.10
  38.9 4.4 shift_copies.1.x_ref.x3
  49.3 4.2 collective-permute-done.9
  61.9 4.2 collective-permute-done.8.refs_7_
  73.9 11.3 %conv_first.1 = (f32[16,64,512]{2,1,0:T(8,128)}, f32[2,512]{1,0:T(2,128)}) custom-call(s32[7]{0:T(128)} %stack.227.idx.idx_ref, bf16[3,18,64,512]{3,2,1,0:T(8,128)(2,1)} %shift_copies.1.x_ref.x3, bf16[2,9,64,128]{3,2,1,0:T(8,128)(2,1)} %copy-done.7, bf16[2,9,64,128]{3,2,1,0:T(8,128)(2,1)} %copy-done.11, bf16[2,9,64,128]{3,2,1,0:T(8,128)(2,1)} %copy-done.12, ...), custom_call_target="tpu_custom_call" | custom-call | flops 301989888 | bytes 625000 | tf_op jit(solution)/shard_map/conv_first/pallas_call | solution.py:423
  94.5 3.8 collective-permute-start.26
  100.8 9.5 %collective-permute-done.27 = f32[2,512]{1,0:T(2,128)S(1)} collective-permute-done((f32[2,512]{1,0:T(2,128)S(1)}, f32[2,512]{1,0:T(2,128)S(1)}, u32[]{:S(2)}, u32[]{:S(2)}) %collective-permute-start.27) | collective-permute-done | bytes 4128 | tf_op jit(solution)/shard_map/ppermute | solution.py:54
  112.9 4.3 collective-permute-done.31
  124.5 8.2 %mid.1 = (bf16[3,18,64,512]{3,2,1,0:T(8,128)(2,1)}, f32[1152,384]{1,0:T(8,128)}, f32[144,384]{1,0:T(8,128)}, f32[2,384]{1,0:T(2,128)}) custom-call(s32[7]{0:T(128)} %stack.227.idx.idx_ref, f32[2,512]{1,0:T(2,128)} %add.280.st, f32[2,512]{1,0:T(2,128)} %get-tuple-element.322.gb, f32[16,64,512]{2,1,0:T(8,128)} %get-tuple-element.135.z_ref.z, ...), custom_call_target="tpu_custom_call" | custom-call | flops 28311552 | bytes 625000 | tf_op jit(solution)/shard_map/mid/pallas_call | solution.py:489
  135.6 2.8 collective-permute-done.35
  139.7 4.4 collective-permute-done.36
  145.5 2.5 collective-permute-done.40.refs_7_
  152.3 11.3 %conv_second.1 = (f32[16,64,512]{2,1,0:T(8,128)}, f32[2,512]{1,0:T(2,128)}) custom-call(s32[7]{0:T(128)} %stack.227.idx.idx_ref, bf16[3,18,64,512]{3,2,1,0:T(8,128)(2,1)} %get-tuple-element.138.x_ref.u3.x3, bf16[2,9,64,128]{3,2,1,0:T(8,128)(2,1)} %copy-done.8, bf16[2,9,64,128]{3,2,1,0:T(8,128)(2,1)} %copy-done.24, bf16[2,9,64,128]{3,2,1,0:T(8,128)(2,1)} %copy-done.26, ...), custom_call_target="tpu_custom_call" | custom-call | flops 301989888 | bytes 625000 | tf_op jit(solution)/shard_map/conv_second/pallas_call | solution.py:423
  163.6 8.1 %collective-permute-start.50 = (f32[2,384]{1,0:T(2,128)S(1)}, f32[2,384]{1,0:T(2,128)S(1)}, u32[]{:S(2)}, u32[]{:S(2)}) collective-permute-start(f32[2,384]{1,0:T(2,128)S(1)} %add.284), channel_id=1, source_target_pairs={{0,4},{2,6},{4,0},{6,2},{1,5},{3,7},{5,1},{7,3},{8,12},{10,14},{12... | collective-permute-start | bytes 9224 | tf_op jit(solution)/shard_map/ppermute | solution.py:54
  173.9 5.9 %hidden.1 = (bf16[1152,384]{1,0:T(8,128)(2,1)}, bf16[144,384]{1,0:T(8,128)(2,1)}, f32[6,512]{1,0:T(8,128)}) custom-call(f32[2,384]{1,0:T(2,128)} %add.285.st.hst, f32[2,384]{1,0:T(2,128)} %slice.642.gb.hgb, f32[1152,384]{1,0:T(8,128)} %get-tuple-element.151.hp, f32[144,384]{1,0:T(8,128)} %get-tuple-element.152.hc, bf16[3,128,512]{2,1,0:T(8,128)(2,1)} %bitcast.380), custom_call_target="tpu_custom_call" | custom-call | flops 28311552 | bytes 312500 | tf_op jit(solution)/shard_map/hidden/pallas_call | solution.py:548
  183.4 2.9 collective-permute-done.52
  186.2 2.4 collective-permute-start.53
  190.3 3.7 collective-permute-done.54
  194.1 3.2 collective-permute-start.55
  200.7 2.4 collective-permute-start.57
  205.6 4.0 collective-permute-done.56
  212.9 7.7 %task_back.3.refs_2_ = bf16[3,8,2,2,32,512]{5,4,3,2,1,0:T(8,128)(2,1)} custom-call(s32[7]{0:T(128)} %stack.227.idx.idx_ref, bf16[3,3,10,32,512]{4,3,2,1,0:T(8,128)(2,1)} %pad_maximum_fusion.go, bf16[16,27,64,128]{3,2,1,0:T(8,128)(2,1)} %bitcast.371, bf16[16,27,64,128]{3,2,1,0:T(8,128)(2,1)} %collective-permute-done.59.refs_1_), custom_call_target="tpu_custom_call" | custom-call | flops 134217728 | bytes 500000 | tf_op jit(solution)/shard_map/task_back/pallas_call | solution.py:602
  220.7 7.8 %task_back.4.refs_2_ = bf16[3,8,2,2,32,512]{5,4,3,2,1,0:T(8,128)(2,1)} custom-call(s32[7]{0:T(128)} %stack.227.idx.idx_ref, bf16[3,3,10,32,512]{4,3,2,1,0:T(8,128)(2,1)} %pad_maximum_fusion.go, bf16[16,27,64,128]{3,2,1,0:T(8,128)(2,1)} %bitcast.372, bf16[16,27,64,128]{3,2,1,0:T(8,128)(2,1)} %collective-permute-done.59.refs_1_, ...), custom_call_target="tpu_custom_call", output_to_operand_aliasing={{}: (4, {})} | custom-call | flops 134217728 | bytes 500000 | tf_op jit(solution)/shard_map/task_back/pallas_call | solution.py:602
  228.4 7.8 %task_back.5 = bf16[3,8,2,2,32,512]{5,4,3,2,1,0:T(8,128)(2,1)} custom-call(s32[7]{0:T(128)} %stack.227.idx.idx_ref, bf16[3,3,10,32,512]{4,3,2,1,0:T(8,128)(2,1)} %pad_maximum_fusion.go, bf16[16,27,64,128]{3,2,1,0:T(8,128)(2,1)} %bitcast.373, bf16[16,27,64,128]{3,2,1,0:T(8,128)(2,1)} %collective-permute-done.59.refs_1_, ...), custom_call_target="tpu_custom_call", output_to_operand_aliasing={{}: (4, {})} | custom-call | flops 134217728 | bytes 500000 | tf_op jit(solution)/shard_map/task_back/pallas_call | solution.py:602
  236.3 14.9 %attend.1 = (bf16[3,3,9,32,512]{4,3,2,1,0:T(8,128)(2,1)}, bf16[3,3,8,32,512]{4,3,2,1,0:T(8,128)(2,1)}, bf16[3,16,64,512]{3,2,1,0:T(8,128)(2,1)}, f32[16,64,512]{...) custom-call(s32[7]{0:T(128)} %stack.227.idx.idx_ref, f32[2,512]{1,0:T(2,128)} %slice.781.st, ...), custom_call_target="tpu_custom_call" | custom-call | flops 28311552 | bytes 1562500 | tf_op jit(solution)/shard_map/attend/pallas_call | solution.py:756
  253.6 5.2 task_wgrad.3
  260.6 5.1 task_wgrad.4
  265.8 5.1 task_wgrad.5
  270.9 3.9 collective-permute-done.63
  279.4 9.6 %mask_back.1 = (f32[3,128,512]{2,1,0:T(8,128)}, f32[1024,384]{1,0:T(8,128)}, f32[2,384]{1,0:T(2,128)}) custom-call(f32[6,512]{1,0:T(8,128)} %slice.782.mst, f32[6,512]{1,0:T(8,128)} %reshape.315.mgb, f32[6,512]{1,0:T(8,128)} %get-tuple-element.320.msum, f32[2,384]{1,0:T(2,128)} %add.285.st.hst, f32[2,384]{1,0:T(2,128)} %slice.642.gb.hgb, ...), custom_call_target="tpu_custom_call" | custom-call | flops 75497472 | bytes 500000 | tf_op jit(solution)/shard_map/mask_back/pallas_call | solution.py:852
  289.0 9.8 %add_convert_fusion = bf16[16,1728,128]{2,1,0:T(8,128)(2,1)} fusion(bf16[16,1728,128]{2,1,0:T(8,128)(2,1)} %collective-permute-done.69, bf16[16,1728,128]{2,1,0:T(8,128)(2,1)} %get-tuple-element.172), kind=kLoop, calls=%fused_computation | loop fusion | flops 14155776 | bytes 21233664 | tf_op jit(solution)/shard_map/convert_element_type | solution.py:178
  300.6 2.6 collective-permute-start.67
  305.1 4.2 collective-permute-done.66
  312.9 5.5 second_back.1.x_ref.g3
  318.5 3.6 collective-permute-done.70
  322.1 11.4 %conv_second_back.1.part = f32[16,64,512]{2,1,0:T(8,128)} custom-call(s32[7]{0:T(128)} %stack.227.idx.idx_ref, bf16[3,18,64,512]{3,2,1,0:T(8,128)(2,1)} %second_back.1.x_ref.g3, bf16[2,9,64,128]{3,2,1,0:T(8,128)(2,1)} %copy-done.8, bf16[2,9,64,128]{3,2,1,0:T(8,128)(2,1)} %copy-done.24, bf16[2,9,64,128]{3,2,1,0:T(8,128)(2,1)} %copy-done.26, ...), custom_call_target="tpu_custom_call" | custom-call | flops 301989888 | bytes 625000 | tf_op jit(solution)/shard_map/conv_second_back/pallas_call | solution.py:423
  333.8 3.5 collective-permute-done.72
  341.5 9.5 %first_back.1 = (f32[512,384]{1,0:T(8,128)}, f32[16,64,512]{2,1,0:T(8,128)}, f32[2,512]{1,0:T(2,128)}) custom-call(f32[2,384]{1,0:T(2,128)} %add.285.st.hst, f32[2,384]{1,0:T(2,128)} %slice.642.gb.hgb, f32[2,384]{1,0:T(2,128)} %add.301.hsum, f32[2,512]{1,0:T(2,128)} %add.280.st, f32[2,512]{1,0:T(2,128)} %get-tuple-element.322.gb, ...), custom_call_target="tpu_custom_call" | custom-call | flops 50331648 | bytes 750000 | tf_op jit(solution)/shard_map/first_back/pallas_call | solution.py:982
  353.8 11.3 %wgrad_second.1 = (bf16[4,4,672,128]{3,2,1,0:T(8,128)(2,1)}, bf16[4,4,672,128]{3,2,1,0:T(8,128)(2,1)}) custom-call(s32[7]{0:T(128)} %stack.227.idx.idx_ref, bf16[3,18,64,512]{3,2,1,0:T(8,128)(2,1)} %get-tuple-element.138.x_ref.u3.x3, bf16[3,18,64,512]{3,2,1,0:T(8,128)(2,1)} %second_back.1.x_ref.g3, f32[512,384]{1,0:T(8,128)} %get-tuple-element.186.refs_0_, ...), custom_call_target="tpu_custom_call" | custom-call | flops 301989888 | bytes 625000 | tf_op jit(solution)/shard_map/wgrad_second/pallas_call | solution.py:1078
  365.0 2.4 collective-permute-start.76
  367.4 2.2 collective-permute-done.76
  370.0 3.2 collective-permute-done.77
  377.6 3.9 collective-permute-start.81
  382.1 2.0 collective-permute-start.79
  390.3 5.7 %first_norm_back.1.g3.x_ref = bf16[3,18,64,512]{3,2,1,0:T(8,128)(2,1)} custom-call(s32[7]{0:T(128)} %stack.227.idx.idx_ref, f32[2,512]{1,0:T(2,128)} %add.280.st, f32[2,512]{1,0:T(2,128)} %get-tuple-element.322.gb, f32[2,512]{1,0:T(2,128)} %add.306.gs, f32[16,64,512]{2,1,0:T(8,128)} %get-tuple-element.192.dy, bf16[2,64,512]{2,1,0:T(8,128)(2,1)} %pad_maximum_fusion.17.drows, ...), custom_call_target="tpu_custom_call" | custom-call | bytes 625000 | tf_op jit(solution)/shard_map/first_norm_back/pallas_call | solution.py:919
  397.3 10.2 %wgrad_first.1 = (bf16[4,4,576,128]{3,2,1,0:T(8,128)(2,1)}, bf16[4,4,576,128]{3,2,1,0:T(8,128)(2,1)}) custom-call(s32[7]{0:T(128)} %stack.227.idx.idx_ref, bf16[3,18,64,512]{3,2,1,0:T(8,128)(2,1)} %shift_copies.1.x_ref.x3, bf16[3,18,64,512]{3,2,1,0:T(8,128)(2,1)} %first_norm_back.1.g3.x_ref), custom_call_target="tpu_custom_call" | custom-call | flops 301989888 | bytes 625000 | tf_op jit(solution)/shard_map/wgrad_first/pallas_call | solution.py:1078
  408.4 2.1 collective-permute-start.84
  412.4 12.5 %collective-permute-done.84 = bf16[2,672,128]{2,1,0:T(8,128)(2,1)S(1)} collective-permute-done((bf16[2,672,128]{2,1,0:T(8,128)(2,1)S(1)}, bf16[2,672,128]{2,1,0:T(8,128)(2,1)S(1)}, u32[]{:S(2)}, u32[]{:S(2)}) %collective-permute-start.84) | collective-permute-done | bytes 344096 | tf_op jit(solution)/shard_map/ppermute | solution.py:54
  434.1 6.2 %task_fwd.3.refs_2_ = bf16[3,8,32,512]{3,2,1,0:T(8,128)(2,1)} custom-call(s32[7]{0:T(128)} %stack.227.idx.idx_ref, bf16[3,3,9,32,512]{4,3,2,1,0:T(8,128)(2,1)} %get-tuple-element.162.se, bf16[3,3,8,32,512]{4,3,2,1,0:T(8,128)(2,1)} %get-tuple-element.163.so, bf16[16,27,64,128]{3,2,1,0:T(8,128)(2,1)} %bitcast.374, ...), custom_call_target="tpu_custom_call" | custom-call | flops 75497472 | bytes 500000 | tf_op jit(solution)/shard_map/task_fwd/pallas_call | solution.py:1155
  445.6 6.2 %collective-permute-done.87 = bf16[2,576,128]{2,1,0:T(8,128)(2,1)S(1)} collective-permute-done((bf16[2,576,128]{2,1,0:T(8,128)(2,1)S(1)}, bf16[2,576,128]{2,1,0:T(8,128)(2,1)S(1)}, u32[]{:S(2)}, u32[]{:S(2)}) %collective-permute-start.87) | collective-permute-done | bytes 294944 | tf_op jit(solution)/shard_map/ppermute | solution.py:54
  454.8 2.1 fusion.6
  458.3 6.2 %task_fwd.4.refs_2_ = bf16[3,8,32,512]{3,2,1,0:T(8,128)(2,1)} custom-call(s32[7]{0:T(128)} %stack.227.idx.idx_ref, bf16[3,3,9,32,512]{4,3,2,1,0:T(8,128)(2,1)} %get-tuple-element.162.se, bf16[3,3,8,32,512]{4,3,2,1,0:T(8,128)(2,1)} %get-tuple-element.163.so, bf16[16,27,64,128]{3,2,1,0:T(8,128)(2,1)} %bitcast.375, ...), custom_call_target="tpu_custom_call", output_to_operand_aliasing={{}: (5, {})} | custom-call | flops 75497472 | bytes 500000 | tf_op jit(solution)/shard_map/task_fwd/pallas_call | solution.py:1155
  471.1 2.8 collective-permute-start.98
  473.9 6.2 %task_fwd.5 = bf16[3,8,32,512]{3,2,1,0:T(8,128)(2,1)} custom-call(s32[7]{0:T(128)} %stack.227.idx.idx_ref, bf16[3,3,9,32,512]{4,3,2,1,0:T(8,128)(2,1)} %get-tuple-element.162.se, bf16[3,3,8,32,512]{4,3,2,1,0:T(8,128)(2,1)} %get-tuple-element.163.so, bf16[16,27,64,128]{3,2,1,0:T(8,128)(2,1)} %bitcast.376, ...), custom_call_target="tpu_custom_call", output_to_operand_aliasing={{}: (5, {})} | custom-call | flops 75497472 | bytes 500000 | tf_op jit(solution)/shard_map/task_fwd/pallas_call | solution.py:1155
  486.7 11.0 %conv_first_back.1 = bf16[16,64,512]{2,1,0:T(8,128)(2,1)} custom-call(s32[7]{0:T(128)} %stack.227.idx.idx_ref, bf16[3,18,64,512]{3,2,1,0:T(8,128)(2,1)} %first_norm_back.1.g3.x_ref, bf16[2,9,64,128]{3,2,1,0:T(8,128)(2,1)} %copy-done.7, bf16[2,9,64,128]{3,2,1,0:T(8,128)(2,1)} %copy-done.11, bf16[2,9,64,128]{3,2,1,0:T(8,128)(2,1)} %copy-done.12, ...), custom_call_target="tpu_custom_call" | custom-call | flops 301989888 | bytes 625000 | tf_op jit(solution)/shard_map/conv_first_back/pallas_call | solution.py:423
  500.6 4.5 collective-permute-done.105
  507.3 4.8 shampoo_conv.3
  512.8 5.2 shampoo_conv.4
  523.7 5.4 collective-permute-done.107
  531.5 8.5 %shampoo_proj.1 = (f32[3,2,4,128,128]{4,3,2,1,0:T(8,128)}, f32[3,2,4,128,128]{4,3,2,1,0:T(8,128)}, f32[3,2,4,128,128]{4,3,2,1,0:T(8,128)}) custom-call(f32[3,2,4,128,128]{4,3,2,1,0:T(8,128)} %convert.69.g, f32[3,2,4,128,128]{4,3,2,1,0:T(8,128)} %left.7, f32[3,2,4,128,128]{4,3,2,1,0:T(8,128)} %right.7, f32[3,2,4,128,128]{4,3,2,1,0:T(8,128)} %lroot.7, ...), custom_call_target="tpu_custom_call" | custom-call | flops 25165824 | bytes 884736 | tf_op jit(solution)/shard_map/shampoo_proj/pallas_call | solution.py:1228
  540.8 11.4 %shampoo_conv.5 = (f32[1,45,128,128]{3,2,1,0:T(8,128)}, f32[1,45,128,128]{3,2,1,0:T(8,128)}, f32[1,45,128,128]{3,2,1,0:T(8,128)}, f32[1,45,128,128]{3,2,1,0:T(8,128)}) custom-call(s32[7]{0:T(128)} %stack.227.idx.idx_ref, bf16[1728,128]{1,0:T(8,128)(2,1)} %bitcast.397, ...), custom_call_target="tpu_custom_call", output_to_operand_aliasing={{0}: (8, {}), {1}: (9, {}), {2}: (10, {}), {3}: (11, {})} | custom-call | flops 28311552 | bytes 995328 | tf_op jit(solution)/shard_map/shampoo_conv/pallas_call | solution.py:1205
  (541 shorter events, 173.2 us)
Async XLA Ops:
  7.2 191.8 %all-gather.3.cloned.1.call-start = ((), (), s32[]{:S(2)}) async-start(), calls=%async_computation.2 | async-start | bytes 7520256 | tf_op jit(solution)/shard_map/all_gather | solution.py:1350
  9.5 13.4 %collective-permute-start = (bf16[1,9,64,128]{3,2,1,0:T(8,128)(2,1)S(1)}, bf16[1,9,64,128]{3,2,1,0:T(8,128)(2,1)S(1)}, u32[]{:S(2)}, u32[]{:S(2)}) collective-permute-start(bf16[1,9,64,128]{3,2,1,0:T(8,128)(2,1)S(1)} %get-tuple-element.265), channel_id=1, source_target_pairs={{0,4},{2,6},{4,0},{6,2},{1,5},{3,7},{5,1},{7,3},{8,12},{10,14},{12... | collective-permute-start | bytes 442376 | tf_op jit(solution)/shard_map/ppermute | solution.py:54
  16.0 6.2 %collective-permute-start.1 = (bf16[64,512]{1,0:T(8,128)(2,1)S(1)}, bf16[64,512]{1,0:T(8,128)(2,1)S(1)}, u32[]{:S(2)}, u32[]{:S(2)}) collective-permute-start(bf16[64,512]{1,0:T(8,128)(2,1)S(1)} %bitcast.428), channel_id=1, source_target_pairs={{0,2},{2,4},{4,6},{6,0},{1,3},{3,5},{5,7},{7,1},{8,10},{10,12},{12... | collective-permute-start | bytes 196616 | tf_op jit(solution)/shard_map/ppermute | solution.py:74
  23.0 9.2 %collective-permute-start.3 = (bf16[2,9,64,128]{3,2,1,0:T(8,128)(2,1)S(1)}, bf16[2,9,64,128]{3,2,1,0:T(8,128)(2,1)S(1)}, u32[]{:S(2)}, u32[]{:S(2)}) collective-permute-start(bf16[2,9,64,128]{3,2,1,0:T(8,128)(2,1)S(1)} %pad_maximum_fusion.10.refs_0_), channel_id=1, source_target_pairs={{0,2},{2,0},{4,6},{6,4},{1,3},{3,1},{5,7},{7,5},{8,10},{10,8},{12,... | collective-permute-start | bytes 884744 | tf_op jit(solution)/shard_map/ppermute | solution.py:54
  26.6 16.8 %collective-permute-start.5 = (bf16[2,9,64,128]{3,2,1,0:T(8,128)(2,1)S(1)}, bf16[2,9,64,128]{3,2,1,0:T(8,128)(2,1)S(1)}, u32[]{:S(2)}, u32[]{:S(2)}) collective-permute-start(bf16[2,9,64,128]{3,2,1,0:T(8,128)(2,1)S(1)} %pad_maximum_fusion.10.refs_0_), channel_id=1, source_target_pairs={{0,8},{8,0},{16,24},{24,16},{1,9},{9,1},{17,25},{25,17},{2,10},{10... | collective-permute-start | bytes 884744 | tf_op jit(solution)/shard_map/ppermute | solution.py:54
  28.1 15.3 %collective-permute-start.6 = (bf16[2,9,64,128]{3,2,1,0:T(8,128)(2,1)S(1)}, bf16[2,9,64,128]{3,2,1,0:T(8,128)(2,1)S(1)}, u32[]{:S(2)}, u32[]{:S(2)}) collective-permute-start(bf16[2,9,64,128]{3,2,1,0:T(8,128)(2,1)S(1)} %pad_maximum_fusion.10.refs_0_), channel_id=1, source_target_pairs={{0,16},{8,24},{16,0},{24,8},{1,17},{9,25},{17,1},{25,9},{2,18},{10... | collective-permute-start | bytes 884744 | tf_op jit(solution)/shard_map/ppermute | solution.py:54
  34.3 14.4 %collective-permute-start.10 = (bf16[3,1,4,8,512]{4,3,2,1,0:T(8,128)(2,1)S(1)}, bf16[3,1,4,8,512]{4,3,2,1,0:T(8,128)(2,1)S(1)}, u32[]{:S(2)}, u32[]{:S(2)}) collective-permute-start(bf16[3,1,4,8,512]{4,3,2,1,0:T(8,128)(2,1)S(1)} %get-tuple-element.264), channel_id=1, source_target_pairs={{2,0},{4,2},{6,4},{0,6},{3,1},{5,3},{7,5},{1,7},{10,8},{12,10},{14... | collective-permute-start | bytes 294920 | tf_op jit(solution)/shard_map/ppermute | solution.py:74
  43.4 12.1 %collective-permute-start.7 = (bf16[2,9,64,128]{3,2,1,0:T(8,128)(2,1)S(1)}, bf16[2,9,64,128]{3,2,1,0:T(8,128)(2,1)S(1)}, u32[]{:S(2)}, u32[]{:S(2)}) collective-permute-start(bf16[2,9,64,128]{3,2,1,0:T(8,128)(2,1)S(1)} %collective-permute-done.3.refs_1_), channel_id=1, source_target_pairs={{0,16},{8,24},{16,0},{24,8},{1,17},{9,25},{17,1},{25,9},{2,18},{10... | collective-permute-start | bytes 884744 | tf_op jit(solution)/shard_map/ppermute | solution.py:54
  44.9 11.8 %collective-permute-start.13 = (bf16[2,9,64,128]{3,2,1,0:T(8,128)(2,1)S(1)}, bf16[2,9,64,128]{3,2,1,0:T(8,128)(2,1)}, u32[]{:S(2)}, u32[]{:S(2)}) collective-permute-start(bf16[2,9,64,128]{3,2,1,0:T(8,128)(2,1)S(1)} %collective-permute-done.3.refs_1_), channel_id=1, source_target_pairs={{0,8},{8,0},{16,24},{24,16},{1,9},{9,1},{17,25},{25,17},{2,10},{10... | collective-permute-start | bytes 884744 | tf_op jit(solution)/shard_map/ppermute | solution.py:54
  46.4 9.6 %collective-permute-start.4 = (bf16[1,9,64,128]{3,2,1,0:T(8,128)(2,1)S(1)}, bf16[1,9,64,128]{3,2,1,0:T(8,128)(2,1)}, u32[]{:S(2)}, u32[]{:S(2)}) collective-permute-start(bf16[1,9,64,128]{3,2,1,0:T(8,128)(2,1)S(1)} %copy-done.40), channel_id=1, source_target_pairs={{0,4},{2,6},{4,0},{6,2},{1,5},{3,7},{5,1},{7,3},{8,12},{10,14},{12... | collective-permute-start | bytes 442376 | tf_op jit(solution)/shard_map/ppermute | solution.py:54
  46.7 6.8 %collective-permute-start.9 = (bf16[3,1,4,8,512]{4,3,2,1,0:T(8,128)(2,1)}, bf16[3,1,4,8,512]{4,3,2,1,0:T(8,128)(2,1)S(1)}, u32[]{:S(2)}, u32[]{:S(2)}) collective-permute-start(bf16[3,1,4,8,512]{4,3,2,1,0:T(8,128)(2,1)} %get-tuple-element.263), channel_id=1, source_target_pairs={{0,2},{2,4},{4,6},{6,0},{1,3},{3,5},{5,7},{7,1},{8,10},{10,12},{12... | collective-permute-start | bytes 294920 | tf_op jit(solution)/shard_map/ppermute | solution.py:74
  48.7 9.2 %collective-permute-start.14 = (bf16[2,9,64,128]{3,2,1,0:T(8,128)(2,1)S(1)}, bf16[2,9,64,128]{3,2,1,0:T(8,128)(2,1)}, u32[]{:S(2)}, u32[]{:S(2)}) collective-permute-start(bf16[2,9,64,128]{3,2,1,0:T(8,128)(2,1)S(1)} %collective-permute-done.5.refs_2_), channel_id=1, source_target_pairs={{0,16},{8,24},{16,0},{24,8},{1,17},{9,25},{17,1},{25,9},{2,18},{10... | collective-permute-start | bytes 884744 | tf_op jit(solution)/shard_map/ppermute | solution.py:54
  55.5 10.6 %collective-permute-start.15 = (bf16[2,9,64,128]{3,2,1,0:T(8,128)(2,1)S(1)}, bf16[2,9,64,128]{3,2,1,0:T(8,128)(2,1)S(1)}, u32[]{:S(2)}, u32[]{:S(2)}) collective-permute-start(bf16[2,9,64,128]{3,2,1,0:T(8,128)(2,1)S(1)} %pad_maximum_fusion.10.refs_0_), channel_id=1, source_target_pairs={{0,1},{1,0},{2,3},{3,2},{4,5},{5,4},{6,7},{7,6},{8,9},{9,8},{10,11... | collective-permute-start | bytes 884744 | tf_op jit(solution)/shard_map/ppermute | solution.py:54
  56.1 10.6 %collective-permute-start.16 = (bf16[2,9,64,128]{3,2,1,0:T(8,128)(2,1)S(1)}, bf16[2,9,64,128]{3,2,1,0:T(8,128)(2,1)S(1)}, u32[]{:S(2)}, u32[]{:S(2)}) collective-permute-start(bf16[2,9,64,128]{3,2,1,0:T(8,128)(2,1)S(1)} %collective-permute-done.3.refs_1_), channel_id=1, source_target_pairs={{0,1},{1,0},{2,3},{3,2},{4,5},{5,4},{6,7},{7,6},{8,9},{9,8},{10,11... | collective-permute-start | bytes 884744 | tf_op jit(solution)/shard_map/ppermute | solution.py:54
  56.6 10.2 %collective-permute-start.17 = (bf16[2,9,64,128]{3,2,1,0:T(8,128)(2,1)S(1)}, bf16[2,9,64,128]{3,2,1,0:T(8,128)(2,1)S(1)}, u32[]{:S(2)}, u32[]{:S(2)}) collective-permute-start(bf16[2,9,64,128]{3,2,1,0:T(8,128)(2,1)S(1)} %collective-permute-done.5.refs_2_), channel_id=1, source_target_pairs={{0,1},{1,0},{2,3},{3,2},{4,5},{5,4},{6,7},{7,6},{8,9},{9,8},{10,11... | collective-permute-start | bytes 884744 | tf_op jit(solution)/shard_map/ppermute | solution.py:54
  56.7 10.5 %collective-permute-start.19 = (bf16[2,9,64,128]{3,2,1,0:T(8,128)(2,1)S(1)}, bf16[2,9,64,128]{3,2,1,0:T(8,128)(2,1)S(1)}, u32[]{:S(2)}, u32[]{:S(2)}) collective-permute-start(bf16[2,9,64,128]{3,2,1,0:T(8,128)(2,1)S(1)} %collective-permute-done.6.refs_4_), channel_id=1, source_target_pairs={{0,1},{1,0},{2,3},{3,2},{4,5},{5,4},{6,7},{7,6},{8,9},{9,8},{10,11... | collective-permute-start | bytes 884744 | tf_op jit(solution)/shard_map/ppermute | solution.py:54
  58.0 8.2 %collective-permute-start.8 = (bf16[2,9,64,128]{3,2,1,0:T(8,128)(2,1)S(1)}, bf16[2,9,64,128]{3,2,1,0:T(8,128)(2,1)S(1)}, u32[]{:S(2)}, u32[]{:S(2)}) collective-permute-start(bf16[2,9,64,128]{3,2,1,0:T(8,128)(2,1)S(1)} %collective-permute-done.7.refs_5_), channel_id=1, source_target_pairs={{0,8},{8,0},{16,24},{24,16},{1,9},{9,1},{17,25},{25,17},{2,10},{10... | collective-permute-start | bytes 884744 | tf_op jit(solution)/shard_map/ppermute | solution.py:54
  67.2 18.0 %collective-permute-start.23 = (bf16[2,9,64,128]{3,2,1,0:T(8,128)(2,1)S(1)}, bf16[2,9,64,128]{3,2,1,0:T(8,128)(2,1)S(1)}, u32[]{:S(2)}, u32[]{:S(2)}) collective-permute-start(bf16[2,9,64,128]{3,2,1,0:T(8,128)(2,1)S(1)} %pad_maximum_fusion.11.refs_0_), channel_id=1, source_target_pairs={{0,2},{2,0},{4,6},{6,4},{1,3},{3,1},{5,7},{7,5},{8,10},{10,8},{12,... | collective-permute-start | bytes 884744 | tf_op jit(solution)/shard_map/ppermute | solution.py:54
  86.0 433.8 %reduce-scatter.2.cloned.1.call-start = ((), (), s32[]{:S(2)}) async-start(), calls=%async_computation.1 | async-start | bytes 7520256 | tf_op jit(solution)/shard_map/reduce_scatter | solution.py:1407
  91.7 43.1 %collective-permute-start.37 = (bf16[2,9,64,128]{3,2,1,0:T(8,128)(2,1)S(1)}, bf16[2,9,64,128]{3,2,1,0:T(8,128)(2,1)S(1)}, u32[]{:S(2)}, u32[]{:S(2)}) collective-permute-start(bf16[2,9,64,128]{3,2,1,0:T(8,128)(2,1)S(1)} %pad_maximum_fusion.11.refs_0_), channel_id=1, source_target_pairs={{0,8},{8,0},{16,24},{24,16},{1,9},{9,1},{17,25},{25,17},{2,10},{10... | collective-permute-start | bytes 884744 | tf_op jit(solution)/shard_map/ppermute | solution.py:54
  92.2 47.0 %collective-permute-start.38 = (bf16[2,9,64,128]{3,2,1,0:T(8,128)(2,1)S(1)}, bf16[2,9,64,128]{3,2,1,0:T(8,128)(2,1)}, u32[]{:S(2)}, u32[]{:S(2)}) collective-permute-start(bf16[2,9,64,128]{3,2,1,0:T(8,128)(2,1)S(1)} %pad_maximum_fusion.11.refs_0_), channel_id=1, source_target_pairs={{0,16},{8,24},{16,0},{24,8},{1,17},{9,25},{17,1},{25,9},{2,18},{10... | collective-permute-start | bytes 884744 | tf_op jit(solution)/shard_map/ppermute | solution.py:54
  93.7 25.1 %collective-permute-start.28 = (bf16[2,9,64,128]{3,2,1,0:T(8,128)(2,1)S(1)}, bf16[2,9,64,128]{3,2,1,0:T(8,128)(2,1)S(1)}, u32[]{:S(2)}, u32[]{:S(2)}) collective-permute-start(bf16[2,9,64,128]{3,2,1,0:T(8,128)(2,1)S(1)} %copy-done.25), channel_id=1, source_target_pairs={{0,8},{8,0},{16,24},{24,16},{1,9},{9,1},{17,25},{25,17},{2,10},{10... | collective-permute-start | bytes 884744 | tf_op jit(solution)/shard_map/ppermute | solution.py:54
  98.3 12.6 %collective-permute-start.32 = (bf16[64,512]{1,0:T(8,128)(2,1)S(1)}, bf16[64,512]{1,0:T(8,128)(2,1)S(1)}, u32[]{:S(2)}, u32[]{:S(2)}) collective-permute-start(bf16[64,512]{1,0:T(8,128)(2,1)S(1)} %get-tuple-element.251), channel_id=1, source_target_pairs={{2,0},{4,2},{6,4},{0,6},{3,1},{5,3},{7,5},{1,7},{10,8},{12,10},{14... | collective-permute-start | bytes 196616 | tf_op jit(solution)/shard_map/ppermute | solution.py:74
  100.0 10.4 %collective-permute-start.27 = (f32[2,512]{1,0:T(2,128)S(1)}, f32[2,512]{1,0:T(2,128)S(1)}, u32[]{:S(2)}, u32[]{:S(2)}) collective-permute-start(f32[2,512]{1,0:T(2,128)S(1)} %add.278), channel_id=1, source_target_pairs={{0,8},{8,0},{16,24},{24,16},{1,9},{9,1},{17,25},{25,17},{2,10},{10... | collective-permute-start | bytes 12296 | tf_op jit(solution)/shard_map/ppermute | solution.py:54
  110.4 9.8 %collective-permute-start.29 = (bf16[2,9,64,128]{3,2,1,0:T(8,128)(2,1)S(1)}, bf16[2,9,64,128]{3,2,1,0:T(8,128)(2,1)S(1)}, u32[]{:S(2)}, u32[]{:S(2)}) collective-permute-start(bf16[2,9,64,128]{3,2,1,0:T(8,128)(2,1)S(1)} %copy-done.25), channel_id=1, source_target_pairs={{0,16},{8,24},{16,0},{24,8},{1,17},{9,25},{17,1},{25,9},{2,18},{10... | collective-permute-start | bytes 884744 | tf_op jit(solution)/shard_map/ppermute | solution.py:54
  110.9 6.3 %collective-permute-start.31 = (bf16[64,512]{1,0:T(8,128)(2,1)S(1)}, bf16[64,512]{1,0:T(8,128)(2,1)S(1)}, u32[]{:S(2)}, u32[]{:S(2)}) collective-permute-start(bf16[64,512]{1,0:T(8,128)(2,1)S(1)} %get-tuple-element.250), channel_id=1, source_target_pairs={{0,2},{2,4},{4,6},{6,0},{1,3},{3,5},{5,7},{7,1},{8,10},{10,12},{12... | collective-permute-start | bytes 196616 | tf_op jit(solution)/shard_map/ppermute | solution.py:74
  134.9 9.2 %collective-permute-start.39 = (bf16[2,9,64,128]{3,2,1,0:T(8,128)(2,1)S(1)}, bf16[2,9,64,128]{3,2,1,0:T(8,128)(2,1)S(1)}, u32[]{:S(2)}, u32[]{:S(2)}) collective-permute-start(bf16[2,9,64,128]{3,2,1,0:T(8,128)(2,1)S(1)} %collective-permute-done.37.refs_2_), channel_id=1, source_target_pairs={{0,16},{8,24},{16,0},{24,8},{1,17},{9,25},{17,1},{25,9},{2,18},{10... | collective-permute-start | bytes 884744 | tf_op jit(solution)/shard_map/ppermute | solution.py:54
  139.1 8.9 %collective-permute-start.40 = (bf16[2,9,64,128]{3,2,1,0:T(8,128)(2,1)S(1)}, bf16[2,9,64,128]{3,2,1,0:T(8,128)(2,1)S(1)}, u32[]{:S(2)}, u32[]{:S(2)}) collective-permute-start(bf16[2,9,64,128]{3,2,1,0:T(8,128)(2,1)S(1)} %collective-permute-done.29.refs_5_), channel_id=1, source_target_pairs={{0,8},{8,0},{16,24},{24,16},{1,9},{9,1},{17,25},{25,17},{2,10},{10... | collective-permute-start | bytes 884744 | tf_op jit(solution)/shard_map/ppermute | solution.py:54
  139.2 9.3 %collective-permute-start.41 = (bf16[2,9,64,128]{3,2,1,0:T(8,128)(2,1)S(1)}, bf16[2,9,64,128]{3,2,1,0:T(8,128)(2,1)S(1)}, u32[]{:S(2)}, u32[]{:S(2)}) collective-permute-start(bf16[2,9,64,128]{3,2,1,0:T(8,128)(2,1)S(1)} %pad_maximum_fusion.11.refs_0_), channel_id=1, source_target_pairs={{0,1},{1,0},{2,3},{3,2},{4,5},{5,4},{6,7},{7,6},{8,9},{9,8},{10,11... | collective-permute-start | bytes 884744 | tf_op jit(solution)/shard_map/ppermute | solution.py:54
  139.2 9.4 %collective-permute-start.42 = (bf16[2,9,64,128]{3,2,1,0:T(8,128)(2,1)S(1)}, bf16[2,9,64,128]{3,2,1,0:T(8,128)(2,1)S(1)}, u32[]{:S(2)}, u32[]{:S(2)}) collective-permute-start(bf16[2,9,64,128]{3,2,1,0:T(8,128)(2,1)S(1)} %copy-done.25), channel_id=1, source_target_pairs={{0,1},{1,0},{2,3},{3,2},{4,5},{5,4},{6,7},{7,6},{8,9},{9,8},{10,11... | collective-permute-start | bytes 884744 | tf_op jit(solution)/shard_map/ppermute | solution.py:54
  163.6 9.7 %collective-permute-start.50 = (f32[2,384]{1,0:T(2,128)S(1)}, f32[2,384]{1,0:T(2,128)S(1)}, u32[]{:S(2)}, u32[]{:S(2)}) collective-permute-start(f32[2,384]{1,0:T(2,128)S(1)} %add.284), channel_id=1, source_target_pairs={{0,4},{2,6},{4,0},{6,2},{1,5},{3,7},{5,1},{7,3},{8,12},{10,14},{12... | collective-permute-start | bytes 9224 | tf_op jit(solution)/shard_map/ppermute | solution.py:54
  199.0 14.0 %collective-permute-start.59 = (bf16[16,27,64,128]{3,2,1,0:T(8,128)(2,1)}, bf16[16,27,64,128]{3,2,1,0:T(8,128)(2,1)}, u32[]{:S(2)}, u32[]{:S(2)}) collective-permute-start(bf16[16,27,64,128]{3,2,1,0:T(8,128)(2,1)} %bitcast.370), channel_id=1, source_target_pairs={{0,1},{1,0},{2,3},{3,2},{4,5},{5,4},{6,7},{7,6},{8,9},{9,8},{10,11... | collective-permute-start | bytes 21233672 | tf_op jit(solution)/shard_map/ppermute | solution.py:54
  203.1 6.4 %collective-permute-start.56 = (bf16[64,512]{1,0:T(8,128)(2,1)S(1)}, bf16[64,512]{1,0:T(8,128)(2,1)S(1)}, u32[]{:S(2)}, u32[]{:S(2)}) collective-permute-start(bf16[64,512]{1,0:T(8,128)(2,1)S(1)} %get-tuple-element.246), channel_id=1, source_target_pairs={{0,2},{2,4},{4,6},{6,0},{1,3},{3,5},{5,7},{7,1},{8,10},{10,12},{12... | collective-permute-start | bytes 196616 | tf_op jit(solution)/shard_map/ppermute | solution.py:74
  258.7 7.0 %collective-permute-start.62 = (f32[14,512]{1,0:T(8,128)S(1)}, f32[14,512]{1,0:T(8,128)S(1)}, u32[]{:S(2)}, u32[]{:S(2)}) collective-permute-start(f32[14,512]{1,0:T(8,128)S(1)} %add.292), channel_id=1, source_target_pairs={{0,4},{2,6},{4,0},{6,2},{1,5},{3,7},{5,1},{7,3},{8,12},{10,14},{12... | collective-permute-start | bytes 86024 | tf_op jit(solution)/shard_map/ppermute | solution.py:54
  270.8 18.2 %collective-permute-start.69 = (bf16[16,1728,128]{2,1,0:T(8,128)(2,1)}, bf16[16,1728,128]{2,1,0:T(8,128)(2,1)}, u32[]{:S(2)}, u32[]{:S(2)}) collective-permute-start(bf16[16,1728,128]{2,1,0:T(8,128)(2,1)} %get-tuple-element.173), channel_id=1, source_target_pairs={{0,1},{1,0},{2,3},{3,2},{4,5},{5,4},{6,7},{7,6},{8,9},{9,8},{10,11... | collective-permute-start | bytes 21233672 | tf_op jit(solution)/shard_map/ppermute | solution.py:54
  310.9 7.5 %collective-permute-start.65 = (f32[2,384]{1,0:T(2,128)S(1)}, f32[2,384]{1,0:T(2,128)S(1)}, u32[]{:S(2)}, u32[]{:S(2)}) collective-permute-start(f32[2,384]{1,0:T(2,128)S(1)} %copy-done.58), channel_id=1, source_target_pairs={{0,1},{1,0},{2,3},{3,2},{4,5},{5,4},{6,7},{7,6},{8,9},{9,8},{10,11... | collective-permute-start | bytes 9224 | tf_op jit(solution)/shard_map/ppermute | solution.py:54
  322.1 11.4 %collective-permute-start.71 = (f32[2,384]{1,0:T(2,128)S(1)}, f32[2,384]{1,0:T(2,128)S(1)}, u32[]{:S(2)}, u32[]{:S(2)}) collective-permute-start(f32[2,384]{1,0:T(2,128)S(1)} %add.298), channel_id=1, source_target_pairs={{0,4},{2,6},{4,0},{6,2},{1,5},{3,7},{5,1},{7,3},{8,12},{10,14},{12... | collective-permute-start | bytes 9224 | tf_op jit(solution)/shard_map/ppermute | solution.py:54
  353.1 11.9 %collective-permute-start.75 = (f32[2,512]{1,0:T(2,128)S(1)}, f32[2,512]{1,0:T(2,128)S(1)}, u32[]{:S(2)}, u32[]{:S(2)}) collective-permute-start(f32[2,512]{1,0:T(2,128)S(1)} %add.302), channel_id=1, source_target_pairs={{0,2},{2,0},{4,6},{6,4},{1,3},{3,1},{5,7},{7,5},{8,10},{10,8},{12,... | collective-permute-start | bytes 12296 | tf_op jit(solution)/shard_map/ppermute | solution.py:54
  373.2 22.8 %collective-permute-start.78 = (bf16[4,4,672,128]{3,2,1,0:T(8,128)(2,1)}, bf16[4,4,672,128]{3,2,1,0:T(8,128)(2,1)}, u32[]{:S(2)}, u32[]{:S(2)}) collective-permute-start(bf16[4,4,672,128]{3,2,1,0:T(8,128)(2,1)} %get-tuple-element.191), channel_id=1, source_target_pairs={{0,1},{1,0},{2,3},{3,2},{4,5},{5,4},{6,7},{7,6},{8,9},{9,8},{10,11... | collective-permute-start | bytes 8257544 | tf_op jit(solution)/shard_map/ppermute | solution.py:54
  377.6 8.7 %collective-permute-start.81 = (bf16[64,512]{1,0:T(8,128)(2,1)S(1)}, bf16[64,512]{1,0:T(8,128)(2,1)S(1)}, u32[]{:S(2)}, u32[]{:S(2)}) collective-permute-start(bf16[64,512]{1,0:T(8,128)(2,1)S(1)} %get-tuple-element.239), channel_id=1, source_target_pairs={{2,0},{4,2},{6,4},{0,6},{3,1},{5,3},{7,5},{1,7},{10,8},{12,10},{14... | collective-permute-start | bytes 196616 | tf_op jit(solution)/shard_map/ppermute | solution.py:74
  407.5 22.2 %collective-permute-start.83 = (bf16[4,4,576,128]{3,2,1,0:T(8,128)(2,1)}, bf16[4,4,576,128]{3,2,1,0:T(8,128)(2,1)S(1)}, u32[]{:S(2)}, u32[]{:S(2)}) collective-permute-start(bf16[4,4,576,128]{3,2,1,0:T(8,128)(2,1)} %get-tuple-element.196), channel_id=1, source_target_pairs={{0,1},{1,0},{2,3},{3,2},{4,5},{5,4},{6,7},{7,6},{8,9},{9,8},{10,11... | collective-permute-start | bytes 7077896 | tf_op jit(solution)/shard_map/ppermute | solution.py:54
  408.4 16.5 %collective-permute-start.84 = (bf16[2,672,128]{2,1,0:T(8,128)(2,1)S(1)}, bf16[2,672,128]{2,1,0:T(8,128)(2,1)S(1)}, u32[]{:S(2)}, u32[]{:S(2)}) collective-permute-start(bf16[2,672,128]{2,1,0:T(8,128)(2,1)S(1)} %get-tuple-element.268), channel_id=1, source_target_pairs={{0,16},{8,24},{16,0},{24,8},{1,17},{9,25},{17,1},{25,9},{2,18},{10... | collective-permute-start | bytes 1032200 | tf_op jit(solution)/shard_map/ppermute | solution.py:54
  410.5 17.3 %collective-permute-start.85 = (bf16[2,672,128]{2,1,0:T(8,128)(2,1)S(1)}, bf16[2,672,128]{2,1,0:T(8,128)(2,1)S(1)}, u32[]{:S(2)}, u32[]{:S(2)}) collective-permute-start(bf16[2,672,128]{2,1,0:T(8,128)(2,1)S(1)} %get-tuple-element.267), channel_id=1, source_target_pairs={{0,8},{8,0},{16,24},{24,16},{1,9},{9,1},{17,25},{25,17},{2,10},{10... | collective-permute-start | bytes 1032200 | tf_op jit(solution)/shard_map/ppermute | solution.py:54
  430.6 11.5 %collective-permute-start.86 = (bf16[2,576,128]{2,1,0:T(8,128)(2,1)}, bf16[2,576,128]{2,1,0:T(8,128)(2,1)}, u32[]{:S(2)}, u32[]{:S(2)}) collective-permute-start(bf16[2,576,128]{2,1,0:T(8,128)(2,1)} %get-tuple-element.270), channel_id=1, source_target_pairs={{0,16},{8,24},{16,0},{24,8},{1,17},{9,25},{17,1},{25,9},{2,18},{10... | collective-permute-start | bytes 884744 | tf_op jit(solution)/shard_map/ppermute | solution.py:54
  430.9 23.3 %collective-permute-start.89 = (bf16[2,672,128]{2,1,0:T(8,128)(2,1)}, bf16[2,672,128]{2,1,0:T(8,128)(2,1)}, u32[]{:S(2)}, u32[]{:S(2)}) collective-permute-start(bf16[2,672,128]{2,1,0:T(8,128)(2,1)} %fusion.14), channel_id=1, source_target_pairs={{0,16},{8,24},{16,0},{24,8},{1,17},{9,25},{17,1},{25,9},{2,18},{10... | collective-permute-start | bytes 1032200 | tf_op jit(solution)/shard_map/ppermute | solution.py:54
  432.7 22.1 %collective-permute-start.88 = (bf16[2,672,128]{2,1,0:T(8,128)(2,1)}, bf16[2,672,128]{2,1,0:T(8,128)(2,1)}, u32[]{:S(2)}, u32[]{:S(2)}) collective-permute-start(bf16[2,672,128]{2,1,0:T(8,128)(2,1)} %fusion.8), channel_id=1, source_target_pairs={{0,8},{8,0},{16,24},{24,16},{1,9},{9,1},{17,25},{25,17},{2,10},{10... | collective-permute-start | bytes 1032200 | tf_op jit(solution)/shard_map/ppermute | solution.py:54
  440.4 11.4 %collective-permute-start.87 = (bf16[2,576,128]{2,1,0:T(8,128)(2,1)S(1)}, bf16[2,576,128]{2,1,0:T(8,128)(2,1)S(1)}, u32[]{:S(2)}, u32[]{:S(2)}) collective-permute-start(bf16[2,576,128]{2,1,0:T(8,128)(2,1)S(1)} %get-tuple-element.269), channel_id=1, source_target_pairs={{0,8},{8,0},{16,24},{24,16},{1,9},{9,1},{17,25},{25,17},{2,10},{10... | collective-permute-start | bytes 884744 | tf_op jit(solution)/shard_map/ppermute | solution.py:54
  441.8 26.4 %collective-permute-start.93 = (bf16[2,672,128]{2,1,0:T(8,128)(2,1)}, bf16[2,672,128]{2,1,0:T(8,128)(2,1)}, u32[]{:S(2)}, u32[]{:S(2)}) collective-permute-start(bf16[2,672,128]{2,1,0:T(8,128)(2,1)} %fusion.7), channel_id=1, source_target_pairs={{0,16},{8,24},{16,0},{24,8},{1,17},{9,25},{17,1},{25,9},{2,18},{10... | collective-permute-start | bytes 1032200 | tf_op jit(solution)/shard_map/ppermute | solution.py:54
  442.1 22.4 %collective-permute-start.91 = (bf16[2,576,128]{2,1,0:T(8,128)(2,1)}, bf16[2,576,128]{2,1,0:T(8,128)(2,1)}, u32[]{:S(2)}, u32[]{:S(2)}) collective-permute-start(bf16[2,576,128]{2,1,0:T(8,128)(2,1)} %fusion.19), channel_id=1, source_target_pairs={{0,16},{8,24},{16,0},{24,8},{1,17},{9,25},{17,1},{25,9},{2,18},{10... | collective-permute-start | bytes 884744 | tf_op jit(solution)/shard_map/ppermute | solution.py:54
  451.8 13.4 %collective-permute-start.90 = (bf16[2,576,128]{2,1,0:T(8,128)(2,1)}, bf16[2,576,128]{2,1,0:T(8,128)(2,1)}, u32[]{:S(2)}, u32[]{:S(2)}) collective-permute-start(bf16[2,576,128]{2,1,0:T(8,128)(2,1)} %fusion.13), channel_id=1, source_target_pairs={{0,8},{8,0},{16,24},{24,16},{1,9},{9,1},{17,25},{25,17},{2,10},{10... | collective-permute-start | bytes 884744 | tf_op jit(solution)/shard_map/ppermute | solution.py:54
  454.2 15.6 %collective-permute-start.92 = (bf16[2,672,128]{2,1,0:T(8,128)(2,1)S(1)}, bf16[2,672,128]{2,1,0:T(8,128)(2,1)}, u32[]{:S(2)}, u32[]{:S(2)}) collective-permute-start(bf16[2,672,128]{2,1,0:T(8,128)(2,1)S(1)} %fusion.15), channel_id=1, source_target_pairs={{0,8},{8,0},{16,24},{24,16},{1,9},{9,1},{17,25},{25,17},{2,10},{10... | collective-permute-start | bytes 1032200 | tf_op jit(solution)/shard_map/ppermute | solution.py:54
  456.9 12.9 %collective-permute-start.94 = (bf16[2,672,128]{2,1,0:T(8,128)(2,1)}, bf16[2,672,128]{2,1,0:T(8,128)(2,1)}, u32[]{:S(2)}, u32[]{:S(2)}) collective-permute-start(bf16[2,672,128]{2,1,0:T(8,128)(2,1)} %fusion.6), channel_id=1, source_target_pairs={{0,2},{2,0},{4,6},{6,4},{1,3},{3,1},{5,7},{7,5},{8,10},{10,8},{12,... | collective-permute-start | bytes 1032200 | tf_op jit(solution)/shard_map/ppermute | solution.py:54
  464.5 15.6 %collective-permute-start.96 = (bf16[2,576,128]{2,1,0:T(8,128)(2,1)}, bf16[2,576,128]{2,1,0:T(8,128)(2,1)}, u32[]{:S(2)}, u32[]{:S(2)}) collective-permute-start(bf16[2,576,128]{2,1,0:T(8,128)(2,1)} %fusion.12), channel_id=1, source_target_pairs={{0,16},{8,24},{16,0},{24,8},{1,17},{9,25},{17,1},{25,9},{2,18},{10... | collective-permute-start | bytes 884744 | tf_op jit(solution)/shard_map/ppermute | solution.py:54
  465.2 15.0 %collective-permute-start.95 = (bf16[2,576,128]{2,1,0:T(8,128)(2,1)S(1)}, bf16[2,576,128]{2,1,0:T(8,128)(2,1)}, u32[]{:S(2)}, u32[]{:S(2)}) collective-permute-start(bf16[2,576,128]{2,1,0:T(8,128)(2,1)S(1)} %fusion.20), channel_id=1, source_target_pairs={{0,8},{8,0},{16,24},{24,16},{1,9},{9,1},{17,25},{25,17},{2,10},{10... | collective-permute-start | bytes 884744 | tf_op jit(solution)/shard_map/ppermute | solution.py:54
  468.2 11.9 %collective-permute-start.97 = (bf16[2,576,128]{2,1,0:T(8,128)(2,1)}, bf16[2,576,128]{2,1,0:T(8,128)(2,1)}, u32[]{:S(2)}, u32[]{:S(2)}) collective-permute-start(bf16[2,576,128]{2,1,0:T(8,128)(2,1)} %fusion.11), channel_id=1, source_target_pairs={{0,2},{2,0},{4,6},{6,4},{1,3},{3,1},{5,7},{7,5},{8,10},{10,8},{12,... | collective-permute-start | bytes 884744 | tf_op jit(solution)/shard_map/ppermute | solution.py:54
  471.1 10.2 %collective-permute-start.98 = (bf16[672,128]{1,0:T(8,128)(2,1)S(1)}, bf16[672,128]{1,0:T(8,128)(2,1)S(1)}, u32[]{:S(2)}, u32[]{:S(2)}) collective-permute-start(bf16[672,128]{1,0:T(8,128)(2,1)S(1)} %fusion.18), channel_id=1, source_target_pairs={{0,4},{2,6},{4,0},{6,2},{1,5},{3,7},{5,1},{7,3},{8,12},{10,14},{12... | collective-permute-start | bytes 516104 | tf_op jit(solution)/shard_map/ppermute | solution.py:54
  484.0 13.8 %collective-permute-start.104 = (bf16[2,96,128]{2,1,0:T(8,128)(2,1)S(1)}, bf16[2,96,128]{2,1,0:T(8,128)(2,1)S(1)}, u32[]{:S(2)}, u32[]{:S(2)}) collective-permute-start(bf16[2,96,128]{2,1,0:T(8,128)(2,1)S(1)} %pad_maximum_fusion.19), channel_id=1, source_target_pairs={{0,2},{2,0},{4,6},{6,4},{1,3},{3,1},{5,7},{7,5},{8,10},{10,8},{12,... | collective-permute-start | bytes 147464 | tf_op jit(solution)/shard_map/ppermute | solution.py:54
  485.2 21.4 %collective-permute-start.101 = (bf16[672,128]{1,0:T(8,128)(2,1)S(1)}, bf16[672,128]{1,0:T(8,128)(2,1)S(1)}, u32[]{:S(2)}, u32[]{:S(2)}) collective-permute-start(bf16[672,128]{1,0:T(8,128)(2,1)S(1)} %fusion.17), channel_id=1, source_target_pairs={{0,1},{1,0},{2,3},{3,2},{4,5},{5,4},{6,7},{7,6},{8,9},{9,8},{10,11... | collective-permute-start | bytes 516104 | tf_op jit(solution)/shard_map/ppermute | solution.py:54
  485.3 14.1 %collective-permute-start.99 = (bf16[576,128]{1,0:T(8,128)(2,1)S(1)}, bf16[576,128]{1,0:T(8,128)(2,1)S(1)}, u32[]{:S(2)}, u32[]{:S(2)}) collective-permute-start(bf16[576,128]{1,0:T(8,128)(2,1)S(1)} %fusion.23), channel_id=1, source_target_pairs={{0,4},{2,6},{4,0},{6,2},{1,5},{3,7},{5,1},{7,3},{8,12},{10,14},{12... | collective-permute-start | bytes 442376 | tf_op jit(solution)/shard_map/ppermute | solution.py:54
  497.8 7.4 %collective-permute-start.105 = (bf16[2,2,96,128]{3,2,1,0:T(8,128)(2,1)S(1)}, bf16[2,2,96,128]{3,2,1,0:T(8,128)(2,1)S(1)}, u32[]{:S(2)}, u32[]{:S(2)}) collective-permute-start(bf16[2,2,96,128]{3,2,1,0:T(8,128)(2,1)S(1)} %pad_maximum_fusion.18), channel_id=1, source_target_pairs={{0,4},{2,6},{4,0},{6,2},{1,5},{3,7},{5,1},{7,3},{8,12},{10,14},{12... | collective-permute-start | bytes 294920 | tf_op jit(solution)/shard_map/ppermute | solution.py:54
  500.5 11.6 %collective-permute-start.100 = (bf16[576,128]{1,0:T(8,128)(2,1)S(1)}, bf16[576,128]{1,0:T(8,128)(2,1)S(1)}, u32[]{:S(2)}, u32[]{:S(2)}) collective-permute-start(bf16[576,128]{1,0:T(8,128)(2,1)S(1)} %fusion.22.mine), channel_id=1, source_target_pairs={{0,1},{1,0},{2,3},{3,2},{4,5},{5,4},{6,7},{7,6},{8,9},{9,8},{10,11... | collective-permute-start | bytes 442376 | tf_op jit(solution)/shard_map/ppermute | solution.py:54
  505.2 12.8 %collective-permute-start.106 = (bf16[2,2,2,96,128]{4,3,2,1,0:T(8,128)(2,1)S(1)}, bf16[2,2,2,96,128]{4,3,2,1,0:T(8,128)(2,1)S(1)}, u32[]{:S(2)}, u32[]{:S(2)}) collective-permute-start(bf16[2,2,2,96,128]{4,3,2,1,0:T(8,128)(2,1)S(1)} %pad_maximum_fusion.12), channel_id=1, source_target_pairs={{0,8},{8,0},{16,24},{24,16},{1,9},{9,1},{17,25},{25,17},{2,10},{10... | collective-permute-start | bytes 589832 | tf_op jit(solution)/shard_map/ppermute | solution.py:54
  518.1 11.0 %collective-permute-start.107 = (bf16[2,2,2,2,96,128]{5,4,3,2,1,0:T(8,128)(2,1)S(1)}, bf16[2,2,2,2,96,128]{5,4,3,2,1,0:T(8,128)(2,1)}, u32[]{:S(2)}, u32[]{:S(2)}) collective-permute-start(bf16[2,2,2,2,96,128]{5,4,3,2,1,0:T(8,128)(2,1)S(1)} %pad_maximum_fusion.9), channel_id=1, source_target_pairs={{0,16},{8,24},{16,0},{24,8},{1,17},{9,25},{17,1},{25,9},{2,18},{10... | collective-permute-start | bytes 1179656 | tf_op jit(solution)/shard_map/ppermute | solution.py:54
  519.7 20.2 %collective-permute-start.102 = (bf16[1728,128]{1,0:T(8,128)(2,1)}, bf16[1728,128]{1,0:T(8,128)(2,1)S(1)}, u32[]{:S(2)}, u32[]{:S(2)}) collective-permute-start(bf16[1728,128]{1,0:T(8,128)(2,1)} %bitcast.396), channel_id=1, source_target_pairs={{0,1},{1,0},{2,3},{3,2},{4,5},{5,4},{6,7},{7,6},{8,9},{9,8},{10,11... | collective-permute-start | bytes 1327112 | tf_op jit(solution)/shard_map/ppermute | solution.py:54
  (107 other events, 901.9 us)
Sparse Core Ops, SparseCore 0:
  86.1 104.1 all-gather.2
  298.9 161.6 reduce-scatter.1

commit v2 on v1

--- a/solution.py
+++ b/solution.py
@@ -54,24 +54,34 @@
     return lax.ppermute(value, axis, pairs(axis, step))
 
 
-def sum_all(value, fillers=(), axes=("wa", "ha", "img")):
-    fillers = list(fillers)
+def sum_all(value, axes=("wa", "ha", "img"), **fillers):
     for axis in axes:
-        step = 1
-        while step < lax.axis_size(axis):
-            total = value + swap(value, axis, step)
-            if fillers:
-                total = after(total, *fillers.pop(0)(value))
-            value = total
-            step *= 2
+        count = lax.axis_size(axis)
+        total = value
+        if count <= 4:
+            for step in range(1, count):
+                total = total + swap(value, axis, step)
+        else:
+            step = 1
+            while step < count:
+                total = total + swap(total, axis, step)
+                step *= 2
+        if axis in fillers:
+            total = after(total, *fillers[axis](value))
+        value = total
     return value
 
 
 def row_halo(first, last):
     count = lax.axis_size("ha")
-    up = [(i, (i + 1) % count) for i in range(count)]
-    down = [((i + 1) % count, i) for i in range(count)]
-    return lax.ppermute(last, "ha", up), lax.ppermute(first, "ha", down)
+    odd = lax.axis_index("ha") % 2 == 1
+    got = []
+    for shift in (0, 1):
+        upper = [i for i in range(count) if i % 2 == shift and i + 1 < count]
+        pairing = {i: i + 1 for i in upper} | {i + 1: i for i in upper}
+        send = jnp.where(odd == (shift == 1), last, first)
+        got.append(lax.ppermute(send, "ha", [(i, pairing.get(i, i)) for i in range(count)]))
+    return jnp.where(odd, got[0], got[1]), jnp.where(odd, got[1], got[0])
 
 
 def col_halo(left_edge, right_edge):
@@ -87,10 +97,11 @@
     return lax.ppermute(right_edge, "wa", up), lax.ppermute(left_edge, "wa", down)
 
 
-def halo(field, batch):
-    top, bottom = row_halo(field[0].astype(BF), field[-1].astype(BF))
+def halo(edges, batch):
+    edge_rows, edge_cols = edges
+    top, bottom = row_halo(edge_rows[0], edge_rows[1])
     rows = jnp.stack([top, bottom])
-    return rows, halo_cols(field, rows, batch)
+    return rows, halo_cols(edge_cols.astype(BF), rows, batch)
 
 
 def after(value, *deps):
@@ -143,32 +154,39 @@
     return to_rows(field[:, h : h + 1])[0]
 
 
-def halo_cols(field, rows, batch):
-    height, tall, chans = field.shape
+def halo_cols(edge_cols, rows, batch):
+    tall, chans = rows.shape[1:]
     across = tall // (2 * batch)
-    split = field.reshape(height, 2, batch, across, chans)
     around = rows.reshape(2, 2, batch, across, chans)
 
-    def edge(parity, place):
-        inner = split[:, parity, :, place].astype(BF)
-        outer = around[:, parity, :, place]
+    def edge(side):
+        inner = edge_cols[:, side * batch : (side + 1) * batch]
+        outer = around[:, side, :, (across - 1) * side]
         return jnp.concatenate([outer[0:1], inner, outer[1:2]], axis=0)
 
-    left, right = col_halo(edge(0, 0), edge(1, across - 1))
-    return jnp.stack([left, right], axis=2).reshape(height + 2, 2 * batch, chans).astype(F32)
-
-
-def gather_proj(own):
+    return jnp.concatenate(col_halo(edge(0), edge(1)), axis=1).astype(F32)
+
+
+def ring_gather(value, axis):
+    count = lax.axis_size(axis)
+    parts = [value] + [
+        lax.ppermute(value, axis, [(i, (i + step) % count) for i in range(count)])
+        for step in range(1, count)
+    ]
+    ring = jnp.stack(parts[::-1] + parts[:0:-1])
+    start = count - 1 - lax.axis_index(axis)
+    return lax.dynamic_slice_in_dim(ring, start, count, axis=0)
+
+
+def gather_proj_line(own):
     got = swap(own, "wa", 1)
     even = lax.axis_index("wa") % 2 == 0
     value = jnp.stack([jnp.where(even, own, got), jnp.where(even, got, own)])
-    for axis in ("ha", "img"):
-        place = lax.axis_index(axis)
-        for step in (1, 2):
-            came = swap(value, axis, step)
-            first = (place // step) % 2 == 0
-            value = jnp.stack([jnp.where(first, value, came), jnp.where(first, came, value)])
-    return value.reshape(TASKS, 2, NB, BLK, BLK).astype(F32)
+    return ring_gather(value, "ha")
+
+
+def gather_proj(line):
+    return ring_gather(line, "img").reshape(TASKS, 2, NB, BLK, BLK).astype(F32)
 
 
 def add_low(*parts):
@@ -262,18 +280,19 @@
 
 
 def sigm(v):
-    return 1.0 / (1.0 + jnp.exp(-v))
+    return pl.reciprocal(1.0 + jnp.exp(-v), approx=True)
 
 
 def side_mask(idx, rows, lanes, count):
-    side = lax.broadcasted_iota(jnp.int32, (rows, lanes), 0) % 2
-    return jnp.where(side == 0, idx[5], idx[6]).astype(F32)
+    row = lax.broadcasted_iota(jnp.int32, (rows, lanes), 0)
+    return jnp.where(row < rows // 2, idx[5], idx[6]).astype(F32)
 
 
 def col_block(cols, r, side, batch, across):
     lanes = cols.shape[-1]
     parts = [
-        jnp.broadcast_to(cols[r, pl.ds(2 * b + side, 1), :], (across, lanes)) for b in range(batch)
+        jnp.broadcast_to(cols[r, pl.ds(side * batch + b, 1), :], (across, lanes))
+        for b in range(batch)
     ]
     return jnp.concatenate(parts, axis=0)
 
@@ -341,6 +360,20 @@
     return copies
 
 
+def put_edges(field, edge_rows, edge_cols, batch):
+    height, tall = field.shape[0], field.shape[1]
+    across = tall // (2 * batch)
+    edge_rows[0] = field[0].astype(BF)
+    edge_rows[1] = field[height - 1].astype(BF)
+
+    @pl.loop(0, height)
+    def _(h):
+        for side in range(2):
+            for b in range(batch):
+                place = side * (tall // 2 + across - 1) + b * across
+                edge_cols[h, side * batch + b : side * batch + b + 1] = field[h, place : place + 1]
+
+
 def shift_kernel(batch, idx, x_ref, rows_ref, cols_ref, x3_ref, work):
     height, tall = x_ref.shape[0], x_ref.shape[1]
     across = tall // (2 * batch)
@@ -378,10 +411,10 @@
     )(idx, field, rows, cols)
 
 
-def conv_kernel(n_pieces, transposed, want_sums, idx_ref, x_ref, *refs):
+def conv_kernel(n_pieces, batch, transposed, want_sums, idx_ref, x_ref, *refs):
     pieces = refs[:n_pieces]
     o_ref = refs[n_pieces]
-    s_ref = refs[n_pieces + 1] if want_sums else None
+    s_ref, er_ref, ec_ref = refs[n_pieces + 1 : n_pieces + 4] if want_sums else (None,) * 3
     wv, sems = refs[-2:]
     copies = weight_copies_rel(idx_ref, pieces, 0, wv, sems)
     for copy in copies:
@@ -414,14 +447,18 @@
             s_ref[0:1] += jnp.sum(acc, axis=0, keepdims=True)
             s_ref[1:2] += jnp.sum(acc * acc, axis=0, keepdims=True)
 
-
-def conv(idx, x3, pieces, transposed, want_sums, dtype, name):
+    if want_sums:
+        put_edges(o_ref, er_ref, ec_ref, batch)
+
+
+def conv(idx, x3, pieces, transposed, dtype, name, batch=0):
+    want_sums = batch > 0
     height, tall = x3.shape[1] - 2, x3.shape[2]
     out_shape = [sds((height, tall, C), dtype)]
     if want_sums:
-        out_shape.append(sds((2, C), F32))
+        out_shape += [sds((2, C), F32), sds((2, tall, C), BF), sds((height, 2 * batch, C), F32)]
     out = pl.pallas_call(
-        functools.partial(conv_kernel, len(pieces), transposed, want_sums),
+        functools.partial(conv_kernel, len(pieces), batch, transposed, want_sums),
         in_specs=[SM, VM] + [ANY] * len(pieces),
         out_specs=[VM] * len(out_shape),
         out_shape=out_shape,
@@ -430,7 +467,7 @@
         cost_estimate=cost(2 * 9 * C * C * height * tall, 10e6),
         name=name,
     )(idx, x3, *pieces)
-    return out if want_sums else out[0]
+    return (out[0], out[1], out[2:]) if want_sums else out[0]
 
 
 def mid_kernel(batch, count_all, idx, st, gb, z_ref, rows_ref, cols_ref, d_ref, u3, hp, hc, hs, uc):
@@ -556,16 +593,33 @@
     )(st, gb, hp, hc, up)
 
 
-def da_kernel(task, n_pieces, n_prev, idx, go, *refs):
-    pieces = refs[:n_pieces]
-    da, wv, ws, sems = refs[n_pieces + n_prev :]
+def task_weights(idx, pieces, wv, sems):
+    t = pl.program_id(0)
+    slot = lax.rem(t, 2)
+
+    def copies(task, place):
+        return weight_copies_task(idx, pieces, task * 9, wv.at[place], sems.at[place])
+
+    @pl.when(t == 0)
+    def _():
+        for copy in copies(0, 0):
+            copy.start()
+
+    for copy in copies(t, slot):
+        copy.wait()
+
+    @pl.when(t + 1 < pl.num_programs(0))
+    def _():
+        for copy in copies(t + 1, 1 - slot):
+            copy.start()
+
+    return slot
+
+
+def da_kernel(idx, go, mine, other, da, wv, ws, sems):
     q = go.shape[3]
     half_h = go.shape[2] - 2
-    copies = weight_copies_task(idx, pieces, task * 9, wv, sems)
-    for copy in copies:
-        copy.start()
-    for copy in copies:
-        copy.wait()
+    slot = task_weights(idx, (mine, other), wv, sems)
 
     def add(a, b):
         return (a.astype(F32) + b.astype(F32)).astype(BF)
@@ -575,9 +629,9 @@
             taps = []
             for dx in range(3):
                 if k == 0:
-                    taps.append(add(wv[3 * a + dx], wv[3 * (a + 1) + dx]))
+                    taps.append(add(wv[slot, 3 * a + dx], wv[slot, 3 * (a + 1) + dx]))
                 else:
-                    taps.append(wv[3 * (2 if a == 0 else 0) + dx])
+                    taps.append(wv[slot, 3 * (2 if a == 0 else 0) + dx])
             ws[a, k, 0, 0] = add(taps[0], taps[1])
             ws[a, k, 0, 1] = taps[2]
             ws[a, k, 1, 0] = add(taps[1], taps[2])
@@ -597,36 +651,35 @@
             da[0, :, a, bb] = acc.reshape(half_h, q, C).astype(BF)
 
 
-def task_back(idx, go, pieces, task, prev):
+def task_back(idx, go, pieces):
     half_h, q = go.shape[2] - 2, go.shape[3]
-    return pl.pallas_call(
-        functools.partial(da_kernel, task, len(pieces), len(prev)),
-        grid=(1,),
-        in_specs=[SM, pl.BlockSpec((1,) + go.shape[1:], lambda k: (task, 0, 0, 0, 0))]
-        + [ANY] * (len(pieces) + len(prev)),
-        out_specs=pl.BlockSpec((1, half_h, 2, 2, q, C), lambda k: (task, 0, 0, 0, 0, 0)),
+    out = pl.pallas_call(
+        da_kernel,
+        grid=(TASKS,),
+        in_specs=[SM, pl.BlockSpec((1,) + go.shape[1:], lambda t: (t, 0, 0, 0, 0)), ANY, ANY],
+        out_specs=pl.BlockSpec((1, half_h, 2, 2, q, C), lambda t: (t, 0, 0, 0, 0, 0)),
         out_shape=sds((TASKS, half_h, 2, 2, q, C), BF),
         scratch_shapes=[
-            pltpu.VMEM((9, C, C), BF),
+            pltpu.VMEM((2, 9, C, C), BF),
             pltpu.VMEM((2, 2, 2, 2, C, C), BF),
-            pltpu.SemaphoreType.DMA((32,)),
+            pltpu.SemaphoreType.DMA((2, 32)),
         ],
-        input_output_aliases={2 + len(pieces) + k: k for k in range(len(prev))},
         compiler_params=params(),
-        cost_estimate=cost(2 * 16 * C * C * half_h * q, 8e6),
+        cost_estimate=cost(TASKS * 2 * 16 * C * C * half_h * q, 24e6),
         name="task_back",
-    )(idx, go, *pieces, *prev)
+    )(idx, go, *pieces)
+    return out.reshape(TASKS, 2 * half_h, 2 * q, C)
 
 
 def attend_kernel(
-    batch, count_all, idx, st, gb, mst, mgb, z_ref, rows_ref, cols_ref, h_ref, hc_ref, up, da, cot,
-    se, so, dym, dy2, pooled, sums,
+    batch, count_all, idx, st, gb, mst, mgb, z_ref, rows_ref, cols_ref, h_ref, hc_ref, up,
+    se, so, pooled,
     ac, pre, prev,
 ):
     height, tall, lanes = z_ref.shape
     across = tall // (2 * batch)
     q = tall // 2
-    mean, rs, sc, sh = coef(st[...], gb[...], count_all)
+    _, _, sc, sh = coef(st[...], gb[...], count_all)
     mcoef = [
         coef(mst[2 * t : 2 * t + 2], mgb[2 * t : 2 * t + 2], count_all) for t in range(TASKS)
     ]
@@ -645,62 +698,135 @@
         pre[t] = jnp.dot(
             h_ref[:, t * CA : (t + 1) * CA], up[t], preferred_element_type=F32
         ).reshape(height + 2, tall, lanes)
-    sums[...] = jnp.zeros(sums.shape, F32)
-
-    def col_sums(t, r, a):
-        even, odd = a[0:q], a[q : 2 * q]
-        lo, hi = shifted(
-            even,
-            odd,
-            col_block(ac.at[t], r, 0, batch, across),
-            col_block(ac.at[t], r, 1, batch, across),
-            batch,
-            across,
-        )
-        return lo + even, even + odd, odd + hi
-
-    def halo_row(r, place, scale):
-        yy = rows_ref[place].astype(F32) * sc + sh
-        p = yy * sigm(yy) * scale
+
+    def sums_of(r, p):
         out = []
         for t in range(TASKS):
             _, _, msc, msh = mcoef[t]
             a = (sigm(pre[t, r] * msc + msh) * p).astype(BF).astype(F32)
-            out.append(col_sums(t, r, a))
+            even, odd = a[0:q], a[q : 2 * q]
+            lo, hi = shifted(
+                even,
+                odd,
+                col_block(ac.at[t], r, 0, batch, across),
+                col_block(ac.at[t], r, 1, batch, across),
+                batch,
+                across,
+            )
+            out.append((lo + even, even + odd, odd + hi))
         return out
+
+    def halo_row(r, place, scale):
+        yy = rows_ref[place].astype(F32) * sc + sh
+        return sums_of(r, yy * sigm(yy) * scale)
+
+    def inner(h):
+        yy = z_ref[h] * sc + sh
+        p = yy * sigm(yy)
+        return sums_of(h + 1, p), p[0:q] + p[q : 2 * q]
 
     first = halo_row(0, 0, top)
     for t in range(TASKS):
         for dx in range(3):
             prev[t, dx] = first[t][dx]
 
-    def inner(i, par):
-        h = 2 * i + par
-        r = h + 1
+    @pl.loop(0, height // 2)
+    def _(i):
+        cs, pool_a = inner(2 * i)
+        for t in range(TASKS):
+            for dx in range(3):
+                se[t, dx, i] = (prev[t, dx] + cs[t][dx]).astype(BF)
+                prev[t, dx] = cs[t][dx]
+        cs, pool_b = inner(2 * i + 1)
+        for t in range(TASKS):
+            for dx in range(3):
+                so[t, dx, i] = (prev[t, dx] + cs[t][dx]).astype(BF)
+                prev[t, dx] = cs[t][dx]
+        pooled[i] = ((pool_a + pool_b) * 0.25).astype(BF)
+
+    last = halo_row(height + 1, 1, bottom)
+    for t in range(TASKS):
+        for dx in range(3):
+            se[t, dx, height // 2] = (prev[t, dx] + last[t][dx]).astype(BF)
+
+
+def lane_blocks(lanes):
+    def block(*lead):
+        return pl.BlockSpec(lead + (lanes,), lambda c: (0,) * len(lead) + (c,))
+
+    return block
+
+
+def whole(a):
+    return pl.BlockSpec(a.shape, lambda c: (0,) * a.ndim)
+
+
+def attend(idx, st, gb, mst, mgb, z, rows, cols, h, hc, up, batch, count_all):
+    height, tall, chans = z.shape
+    lanes = BLK
+    r, q, half = height + 2, tall // 2, height // 2
+    block = lane_blocks(lanes)
+    return pl.pallas_call(
+        functools.partial(attend_kernel, batch, count_all),
+        grid=(chans // lanes,),
+        in_specs=[
+            SM, block(2), block(2), block(2 * TASKS), block(2 * TASKS), block(height, tall), block(2, tall),
+            block(r, 2 * batch), whole(h), whole(hc), block(TASKS, CA),
+        ],
+        out_specs=[block(TASKS, 3, half + 1, q), block(TASKS, 3, half, q), block(half, q)],
+        out_shape=[
+            sds((TASKS, 3, half + 1, q, chans), BF),
+            sds((TASKS, 3, half, q, chans), BF),
+            sds((half, q, chans), BF),
+        ],
+        scratch_shapes=[
+            pltpu.VMEM((TASKS, r, 2 * batch, lanes), F32),
+            pltpu.VMEM((TASKS, r, tall, lanes), F32),
+            pltpu.VMEM((TASKS, 3, q, lanes), F32),
+        ],
+        compiler_params=params(),
+        cost_estimate=cost(2 * r * tall * CA * chans * TASKS, 15e6, 6e6),
+        name="attend",
+    )(idx, st, gb, mst, mgb, z, rows, cols, h, hc, up)
+
+
+def attend_back_kernel(
+    batch, count_all, st, gb, mst, mgb, z_ref, h_ref, up, da, cot, dym, dy2, sums, er, ec, pre
+):
+    height, tall, lanes = z_ref.shape
+    mean, rs, sc, sh = coef(st[...], gb[...], count_all)
+    mcoef = [
+        coef(mst[2 * t : 2 * t + 2], mgb[2 * t : 2 * t + 2], count_all) for t in range(TASKS)
+    ]
+    for t in range(TASKS):
+        pre[t] = jnp.dot(
+            h_ref[tall : (height + 1) * tall, t * CA : (t + 1) * CA],
+            up[t],
+            preferred_element_type=F32,
+        ).reshape(height, tall, lanes)
+    sums[...] = jnp.zeros(sums.shape, F32)
+
+    @pl.loop(0, height)
+    def _(h):
         z = z_ref[h]
         yy = z * sc + sh
         s = sigm(yy)
         p = yy * s
-        slope = s * (1.0 + yy * (1.0 - s))
-        shared = cot[i]
+        shared = cot[h // 2]
         shared = jnp.concatenate([shared, shared], axis=0)
-        cs = []
         branches = []
         for t in range(TASKS):
-            mmean, mrs, msc, msh = mcoef[t]
-            mp = pre[t, r]
+            mmean, _, msc, msh = mcoef[t]
+            mp = pre[t, h]
             m = sigm(mp * msc + msh)
-            a = (m * p).astype(BF).astype(F32)
-            cs.append(col_sums(t, r, a))
-            d = da[t, h].astype(F32)
-            br = m * d
+            br = m * da[t, h].astype(F32)
             branches.append(br)
             shared = shared + br
             dm = br * p * (1.0 - m)
             dym[t, h] = dm.astype(BF)
             sums[2 * t : 2 * t + 1] += jnp.sum(dm, axis=0, keepdims=True)
             sums[2 * t + 1 : 2 * t + 2] += jnp.sum(dm * (mp - mmean), axis=0, keepdims=True)
-        g2 = shared * slope
+        g2 = shared * (s * (1.0 + yy * (1.0 - s)))
         dy2[h] = g2
         sums[6:7] += jnp.sum(g2, axis=0, keepdims=True)
         sums[7:8] += jnp.sum(g2 * (z - mean), axis=0, keepdims=True)
@@ -709,93 +835,40 @@
             for s2 in range(t, TASKS):
                 sums[k : k + 1] += jnp.sum(branches[t] * branches[s2], axis=0, keepdims=True)
                 k += 1
-        return cs, p[0:q] + p[q : 2 * q]
-
-    @pl.loop(0, height // 2)
-    def _(i):
-        cs, pool_a = inner(i, 0)
-        for t in range(TASKS):
-            for dx in range(3):
-                se[t, dx, i] = (prev[t, dx] + cs[t][dx]).astype(BF)
-                prev[t, dx] = cs[t][dx]
-        cs, pool_b = inner(i, 1)
-        for t in range(TASKS):
-            for dx in range(3):
-                so[t, dx, i] = (prev[t, dx] + cs[t][dx]).astype(BF)
-                prev[t, dx] = cs[t][dx]
-        pooled[i] = (pool_a + pool_b) * 0.25
-
-    last = halo_row(height + 1, 1, bottom)
+
     for t in range(TASKS):
-        for dx in range(3):
-            se[t, dx, height // 2] = (prev[t, dx] + last[t][dx]).astype(BF)
         sums[2 * t + 1 : 2 * t + 2] = sums[2 * t + 1 : 2 * t + 2] * mcoef[t][1]
     sums[7:8] = sums[7:8] * rs
-
-
-def attend(idx, st, gb, mst, mgb, z, rows, cols, h, hc, up, da, cot, batch, count_all):
+    put_edges(dy2, er, ec, batch)
+
+
+def attend_back(st, gb, mst, mgb, z, h, up, da, cot, batch, count_all):
     height, tall, chans = z.shape
     lanes = BLK
-    r, q, half = height + 2, tall // 2, height // 2
-
-    def two(n):
-        return pl.BlockSpec((n, lanes), lambda c: (0, c))
-
-    def three(a, b):
-        return pl.BlockSpec((a, b, lanes), lambda c: (0, 0, c))
-
-    def four(a, b, d):
-        return pl.BlockSpec((a, b, d, lanes), lambda c: (0, 0, 0, c))
-
-    def five(a, b, d, e):
-        return pl.BlockSpec((a, b, d, e, lanes), lambda c: (0, 0, 0, 0, c))
-
-    def whole(a):
-        return pl.BlockSpec(a.shape, lambda c: (0,) * a.ndim)
-
+    block = lane_blocks(lanes)
     return pl.pallas_call(
-        functools.partial(attend_kernel, batch, count_all),
+        functools.partial(attend_back_kernel, batch, count_all),
         grid=(chans // lanes,),
         in_specs=[
-            SM,
-            two(2),
-            two(2),
-            two(2 * TASKS),
-            two(2 * TASKS),
-            three(height, tall),
-            three(2, tall),
-            three(r, 2 * batch),
-            whole(h),
-            whole(hc),
-            three(TASKS, CA),
-            four(TASKS, height, tall),
-            three(half, q),
+            block(2), block(2), block(2 * TASKS), block(2 * TASKS), block(height, tall), whole(h),
+            block(TASKS, CA), block(TASKS, height, tall), block(height // 2, tall // 2),
         ],
         out_specs=[
-            five(TASKS, 3, half + 1, q),
-            five(TASKS, 3, half, q),
-            four(TASKS, height, tall),
-            three(height, tall),
-            three(half, q),
-            two(14),
+            block(TASKS, height, tall), block(height, tall), block(14), block(2, tall),
+            block(height, 2 * batch),
         ],
         out_shape=[
-            sds((TASKS, 3, half + 1, q, chans), BF),
-            sds((TASKS, 3, half, q, chans), BF),
             sds((TASKS, height, tall, chans), BF),
             sds((height, tall, chans), F32),
-            sds((half, q, chans), F32),
             sds((14, chans), F32),
+            sds((2, tall, chans), BF),
+            sds((height, 2 * batch, chans), F32),
         ],
-        scratch_shapes=[
-            pltpu.VMEM((TASKS, r, 2 * batch, lanes), F32),
-            pltpu.VMEM((TASKS, r, tall, lanes), F32),
-            pltpu.VMEM((TASKS, 3, q, lanes), F32),
-        ],
+        scratch_shapes=[pltpu.VMEM((TASKS, height, tall, lanes), F32)],
         compiler_params=params(),
-        cost_estimate=cost(2 * r * tall * CA * chans * TASKS, 25e6, 6e6),
-        name="attend",
-    )(idx, st, gb, mst, mgb, z, rows, cols, h, hc, up, da, cot)
+        cost_estimate=cost(2 * height * tall * CA * chans * TASKS, 15e6, 4e6),
+        name="attend_back",
+    )(st, gb, mst, mgb, z, h, up, da, cot)
 
 
 def mask_back_kernel(
@@ -930,7 +1003,7 @@
 
 
 def first_back_kernel(
-    count_all, hst, hgb, hsum, st, gb, dh, hp, u3, part, z, down, dd, dy, gs, low
+    batch, count_all, hst, hgb, hsum, st, gb, dh, hp, u3, part, z, down, dd, dy, gs, er, ec, low
 ):
     height, tall, lanes = z.shape
 
@@ -966,8 +1039,10 @@
         gs[0:1] += jnp.sum(g, axis=0, keepdims=True)
         gs[1:2] += jnp.sum(g * (v - mean) * rs, axis=0, keepdims=True)
 
-
-def first_back(hst, hgb, hsum, st, gb, dh, hp, u3, part, z, down, count_all):
+    put_edges(dy, er, ec, batch)
+
+
+def first_back(hst, hgb, hsum, st, gb, dh, hp, u3, part, z, down, batch, count_all):
     height, tall, chans = z.shape
     lanes = BLK
     wide = TASKS * CA
@@ -980,7 +1055,7 @@
 
     field = pl.BlockSpec((height, tall, lanes), lambda c: (0, 0, c))
     return pl.pallas_call(
-        functools.partial(first_back_kernel, count_all),
+        functools.partial(first_back_kernel, batch, count_all),
         grid=(chans // lanes,),
         in_specs=[
             whole(hst),
@@ -995,8 +1070,20 @@
             field,
             pl.BlockSpec((lanes, wide), lambda c: (c, 0)),
         ],
-        out_specs=[pl.BlockSpec((lanes, wide), lambda c: (c, 0)), field, two(2)],
-        out_shape=[sds((chans, wide), F32), sds((height, tall, chans), F32), sds((2, chans), F32)],
+        out_specs=[
+            pl.BlockSpec((lanes, wide), lambda c: (c, 0)),
+            field,
+            two(2),
+            pl.BlockSpec((2, tall, lanes), lambda c: (0, 0, c)),
+            pl.BlockSpec((height, 2 * batch, lanes), lambda c: (0, 0, c)),
+        ],
+        out_shape=[
+            sds((chans, wide), F32),
+            sds((height, tall, chans), F32),
+            sds((2, chans), F32),
+            sds((2, tall, chans), BF),
+            sds((height, 2 * batch, chans), F32),
+        ],
         scratch_shapes=[pltpu.VMEM((height * tall, wide), BF)],
         compiler_params=params(),
         cost_estimate=cost(4 * height * tall * chans * wide, 12e6, 1e6),
@@ -1023,16 +1110,14 @@
             other[e, s, at] = jnp.where(even, b, a)
 
 
-def put_in_order(idx, grad, mine, other, m):
+def put_in_order(grad, halves, m):
     low = grad.astype(BF)
-    even = idx[2] == 0
     at = slice(m * HB, (m + 1) * HB)
     for i in range(NB):
         for j in range(NB):
-            block = low[i * BLK : (i + 1) * BLK, j * BLK : (j + 1) * BLK]
-            a, b = block[0:HB], block[HB:BLK]
-            mine[i * NB + j, at] = jnp.where(even, a, b)
-            other[i * NB + j, at] = jnp.where(even, b, a)
+            for h in range(2):
+                row = i * BLK + h * HB
+                halves[h, i * NB + j, at] = low[row : row + HB, j * BLK : (j + 1) * BLK]
 
 
 def wgrad_kernel(n_extra, idx, x3, g3, *refs):
@@ -1092,8 +1177,7 @@
     )(idx, x3, g3, *extra)
 
 
-def task_wgrad_kernel(n_prev, idx, se, so, go, *refs):
-    mine, other = refs[n_prev:]
+def task_wgrad_kernel(idx, se, so, go, halves):
     half, q = so.shape[2], so.shape[3]
     g = go[0, 0, 1 : half + 1].reshape(half * q, C)
     for dy in range(3):
@@ -1103,39 +1187,31 @@
             else:
                 view = se[0, dx, dy // 2 : dy // 2 + half]
             grad = lax.dot_general(view.reshape(half * q, C), g, TN, preferred_element_type=F32)
-            put_in_order(idx, grad, mine, other, 3 * dy + dx)
-
-
-def task_wgrad(idx, se, so, go, task, prev):
+            put_in_order(grad, halves, 3 * dy + dx)
+
+
+def task_wgrad(idx, se, so, go):
     half, q = so.shape[2], so.shape[3]
     return pl.pallas_call(
-        functools.partial(task_wgrad_kernel, len(prev)),
-        grid=(1,),
+        task_wgrad_kernel,
+        grid=(TASKS,),
         in_specs=[
             SM,
-            pl.BlockSpec((1,) + se.shape[1:], lambda k: (task, 0, 0, 0, 0)),
-            pl.BlockSpec((1,) + so.shape[1:], lambda k: (task, 0, 0, 0, 0)),
-            pl.BlockSpec((1, 1) + go.shape[2:], lambda k: (task, 1, 0, 0, 0)),
-        ]
-        + [ANY] * len(prev),
-        out_specs=[pl.BlockSpec((NB * NB, 9 * HB, BLK), lambda k: (0, task, 0))] * 2,
-        out_shape=[sds((NB * NB, 9 * TASKS * HB, BLK), BF)] * 2,
-        input_output_aliases={4 + k: k for k in range(len(prev))},
+            pl.BlockSpec((1,) + se.shape[1:], lambda t: (t, 0, 0, 0, 0)),
+            pl.BlockSpec((1,) + so.shape[1:], lambda t: (t, 0, 0, 0, 0)),
+            pl.BlockSpec((1, 1) + go.shape[2:], lambda t: (t, 1, 0, 0, 0)),
+        ],
+        out_specs=pl.BlockSpec((2, NB * NB, 9 * HB, BLK), lambda t: (0, 0, t, 0)),
+        out_shape=sds((2, NB * NB, 9 * TASKS * HB, BLK), BF),
         compiler_params=params(),
-        cost_estimate=cost(2 * 9 * C * C * half * q, 8e6),
+        cost_estimate=cost(TASKS * 2 * 9 * C * C * half * q, 24e6),
         name="task_wgrad",
-    )(idx, se, so, go, *prev)
-
-
-def task_fwd_kernel(task, n_pieces, n_prev, idx, se, so, *refs):
-    pieces = refs[:n_pieces]
-    out, wv, sems = refs[n_pieces + n_prev :]
+    )(idx, se, so, go)
+
+
+def task_fwd_kernel(idx, se, so, mine, other, out, wv, sems):
     half, q = so.shape[2], so.shape[3]
-    copies = weight_copies_task(idx, pieces, task * 9, wv, sems)
-    for copy in copies:
-        copy.start()
-    for copy in copies:
-        copy.wait()
+    slot = task_weights(idx, (mine, other), wv, sems)
     acc = None
     for dy in range(3):
         for dx in range(3):
@@ -1144,61 +1220,73 @@
             else:
                 view = se[0, dx, dy // 2 : dy // 2 + half]
             piece = jnp.dot(
-                view.reshape(half * q, C), wv[3 * dy + dx], preferred_element_type=F32
+                view.reshape(half * q, C), wv[slot, 3 * dy + dx], preferred_element_type=F32
             )
             acc = piece if acc is None else acc + piece
     out[0] = (acc * 0.25).reshape(half, q, C).astype(BF)
 
 
-def task_fwd(idx, se, so, pieces, task, prev):
+def task_fwd(idx, se, so, pieces):
     half, q = so.shape[2], so.shape[3]
     return pl.pallas_call(
-        functools.partial(task_fwd_kernel, task, len(pieces), len(prev)),
-        grid=(1,),
+        task_fwd_kernel,
+        grid=(TASKS,),
         in_specs=[
             SM,
-            pl.BlockSpec((1,) + se.shape[1:], lambda k: (task, 0, 0, 0, 0)),
-            pl.BlockSpec((1,) + so.shape[1:], lambda k: (task, 0, 0, 0, 0)),
-        ]
-        + [ANY] * (len(pieces) + len(prev)),
-        out_specs=pl.BlockSpec((1, half, q, C), lambda k: (task, 0, 0, 0)),
+            pl.BlockSpec((1,) + se.shape[1:], lambda t: (t, 0, 0, 0, 0)),
+            pl.BlockSpec((1,) + so.shape[1:], lambda t: (t, 0, 0, 0, 0)),
+            ANY,
+            ANY,
+        ],
+        out_specs=pl.BlockSpec((1, half, q, C), lambda t: (t, 0, 0, 0)),
         out_shape=sds((TASKS, half, q, C), BF),
-        scratch_shapes=[pltpu.VMEM((9, C, C), BF), pltpu.SemaphoreType.DMA((32,))],
-        input_output_aliases={3 + len(pieces) + k: k for k in range(len(prev))},
+        scratch_shapes=[pltpu.VMEM((2, 9, C, C), BF), pltpu.SemaphoreType.DMA((2, 32))],
         compiler_params=params(),
-        cost_estimate=cost(2 * 9 * C * C * half * q, 8e6),
+        cost_estimate=cost(TASKS * 2 * 9 * C * C * half * q, 20e6),
         name="task_fwd",
-    )(idx, se, so, *pieces, *prev)
-
-
-def shampoo_step(g, left, right, lroot, rroot, weight, rate):
-    low = g.astype(BF)
-    ln = stat_decay * left + (1.0 - stat_decay) * lax.dot_general(
-        low, low, NT, preferred_element_type=F32
-    )
-    rn = stat_decay * right + (1.0 - stat_decay) * lax.dot_general(
-        low, low, TN, preferred_element_type=F32
-    )
-    step = jnp.dot(lroot.astype(BF), low, preferred_element_type=F32)
-    step = jnp.dot(step.astype(BF), rroot.astype(BF), preferred_element_type=F32)
-    return ln, rn, weight - rate * step
+    )(idx, se, so, *pieces)
+
+
+def shampoo_steps(grads, left, right, lroot, rroot, weight, rate):
+    count = len(grads)
+    low = [g.astype(BF) for g in grads]
+    step = [jnp.dot(lroot(k).astype(BF), low[k], preferred_element_type=F32) for k in range(count)]
+    ll = [lax.dot_general(g, g, NT, preferred_element_type=F32) for g in low]
+    rr = [lax.dot_general(g, g, TN, preferred_element_type=F32) for g in low]
+    step = [
+        jnp.dot(step[k].astype(BF), rroot(k).astype(BF), preferred_element_type=F32)
+        for k in range(count)
+    ]
+    keep, add = stat_decay, 1.0 - stat_decay
+    return [
+        (keep * left(k) + add * ll[k], keep * right(k) + add * rr[k], weight(k) - rate * step[k])
+        for k in range(count)
+    ]
 
 
 def shampoo_kernel(n_prev, idx, mine, other, left, right, lroot, rroot, weight, *refs):
     gr, ln, rn, wn = refs[n_prev:]
     even = idx[2] == 0
-    for k in range(mine.shape[0] // HB):
-        a, b = mine[k * HB : (k + 1) * HB], other[k * HB : (k + 1) * HB]
-        g = jnp.concatenate([jnp.where(even, a, b), jnp.where(even, b, a)], axis=0).astype(F32)
-        gr[0, k] = g
-        ln[0, k], rn[0, k], wn[0, k] = shampoo_step(
-            g, left[0, k], right[0, k], lroot[0, k], rroot[0, k], weight[0, k], conv_rate
-        )
+    together = 3
+    for first in range(0, mine.shape[0] // HB, together):
+        places = range(first, first + together)
+        grads = []
+        for k in places:
+            a, b = mine[k * HB : (k + 1) * HB], other[k * HB : (k + 1) * HB]
+            grads.append(jnp.concatenate([jnp.where(even, a, b), jnp.where(even, b, a)], axis=0))
+        state = [
+            functools.partial(lambda ref, k: ref[0, first + k], ref)
+            for ref in (left, right, lroot, rroot, weight)
+        ]
+        done = shampoo_steps(grads, *state, conv_rate)
+        for k, g, (new_l, new_r, new_w) in zip(places, grads, done):
+            gr[0, k] = g.astype(F32)
+            ln[0, k], rn[0, k], wn[0, k] = new_l, new_r, new_w
 
 
 def shampoo_conv(idx, mine, other, state, first, prev):
     n = mine.shape[0] // HB
-    each = 3
+    each = 9
     block = pl.BlockSpec((1, each, BLK, BLK), lambda k: (0, first // each + k, 0, 0))
     half = pl.BlockSpec((each * HB, BLK), lambda k: (k, 0))
     full = state[0].shape
@@ -1216,18 +1304,23 @@
 
 
 def shampoo_proj_kernel(g, left, right, lroot, rroot, weight, ln, rn, wn):
-    for k in range(g.shape[2]):
-        ln[0, 0, k], rn[0, 0, k], wn[0, 0, k] = shampoo_step(
-            g[0, 0, k], left[0, 0, k], right[0, 0, k], lroot[0, 0, k], rroot[0, 0, k],
-            weight[0, 0, k], proj_rate,
-        )
+    kinds, count = g.shape[1], g.shape[2]
+    for kind in range(kinds):
+        grads = [g[0, kind, k] for k in range(count)]
+        state = [
+            functools.partial(lambda ref, k: ref[0, kind, k], ref)
+            for ref in (left, right, lroot, rroot, weight)
+        ]
+        done = shampoo_steps(grads, *state, proj_rate)
+        for k, (new_l, new_r, new_w) in enumerate(done):
+            ln[0, kind, k], rn[0, kind, k], wn[0, kind, k] = new_l, new_r, new_w
 
 
 def shampoo_proj(g, left, right, lroot, rroot, weight):
-    block = pl.BlockSpec((1, 1) + g.shape[2:], lambda t, k: (t, k, 0, 0, 0))
+    block = pl.BlockSpec((1,) + g.shape[1:], lambda t: (t, 0, 0, 0, 0))
     return pl.pallas_call(
         shampoo_proj_kernel,
-        grid=g.shape[:2],
+        grid=g.shape[:1],
         in_specs=[block] * 6,
         out_specs=[block] * 3,
         out_shape=[sds(g.shape, F32)] * 3,
@@ -1235,6 +1328,47 @@
         cost_estimate=cost(24 * 8 * BLK**3, 24 * 9 * BLK * BLK * 4),
         name="shampoo_proj",
     )(g, left, right, lroot, rroot, weight)
+
+
+def norm_step_kernel(gs1, gsum, dhs, norm, moment, gram, grad, moment_new, norm_new):
+    off_down = 2 * C
+    off_up = off_down + TASKS * CA
+    for row in range(2):
+        k = 1 - row
+        at = slice(row, row + 1)
+        grad[at, 0:C] = gs1[k : k + 1]
+        grad[at, C : 2 * C] = gsum[6 + k : 7 + k]
+        grad[at, off_down:off_up] = dhs[k : k + 1]
+        for t in range(TASKS):
+            grad[at, off_up + t * C : off_up + (t + 1) * C] = gsum[2 * t + k : 2 * t + k + 1]
+    g = grad[...]
+    new = moment_decay * moment[...] + (1.0 - moment_decay) * g * g
+    moment_new[...] = new
+    norm_new[...] = norm[...] - norm_rate * g / (jnp.sqrt(new) + 1e-08)
+    row = lax.broadcasted_iota(jnp.int32, (TASKS, TASKS), 0)
+    col = lax.broadcasted_iota(jnp.int32, (TASKS, TASKS), 1)
+    value = jnp.zeros((TASKS, TASKS), F32)
+    k = 8
+    for t in range(TASKS):
+        for s in range(t, TASKS):
+            total = jnp.sum(gsum[k : k + 1], axis=1, keepdims=True)
+            hit = ((row == t) & (col == s)) | ((row == s) & (col == t))
+            value = jnp.where(hit, total, value)
+            k += 1
+    gram[...] = value
+
+
+def norm_step(gs1, gsum, dhs, norm, moment):
+    like = sds(norm.shape, F32)
+    return pl.pallas_call(
+        norm_step_kernel,
+        in_specs=[VM] * 5,
+        out_specs=[VM] * 4,
+        out_shape=[sds((TASKS, TASKS), F32), like, like, like],
+        compiler_params=params(),
+        cost_estimate=cost(0, 1e5),
+        name="norm_step",
+    )(gs1, gsum, dhs, norm, moment)
 
 
 def to_rows(field):
@@ -1297,6 +1431,111 @@
     own = lax.dynamic_index_in_dim(halves, wa % 2, axis=1, keepdims=False).astype(BF)
     g0, g1 = Gather(own[None, 0:9]), Gather(own[None, 9:18])
     g0.near()
+    g0.join()
+    g0.far()
+    g0.low()
+    images = after(images, g0.line_low)
+    rows0 = jnp.stack(row_halo(edge_row(images, 0), edge_row(images, tile_h - 1)))
+    off_down = 2 * C
+    off_up = off_down + TASKS * CA
+    for row in range(2):
+        k = 1 - row
+        at = slice(row, row + 1)
+        grad[at, 0:C] = gs1[k : k + 1]
+        grad[at, C : 2 * C] = gsum[6 + k : 7 + k]
+        grad[at, off_down:off_up] = dhs[k : k + 1]
+        for t in range(TASKS):
+            grad[at, off_up + t * C : off_up + (t + 1) * C] = gsum[2 * t + k : 2 * t + k + 1]
+    g = grad[...]
+    new = moment_decay * moment[...] + (1.0 - moment_decay) * g * g
+    moment_new[...] = new
+    norm_new[...] = norm[...] - norm_rate * g / (jnp.sqrt(new) + 1e-08)
+    row = lax.broadcasted_iota(jnp.int32, (TASKS, TASKS), 0)
+    col = lax.broadcasted_iota(jnp.int32, (TASKS, TASKS), 1)
+    value = jnp.zeros((TASKS, TASKS), F32)
+    k = 8
+    for t in range(TASKS):
+        for s in range(t, TASKS):
+            total = jnp.sum(gsum[k : k + 1], axis=1, keepdims=True)
+            hit = ((row == t) & (col == s)) | ((row == s) & (col == t))
+            value = jnp.where(hit, total, value)
+            k += 1
+    gram[...] = value
+
+
+def norm_step(gs1, gsum, dhs, norm, moment):
+    like = sds(norm.shape, F32)
+    return pl.pallas_call(
+        norm_step_kernel,
+        in_specs=[VM] * 5,
+        out_specs=[VM] * 4,
+        out_shape=[sds((TASKS, TASKS), F32), like, like, like],
+        compiler_params=params(),
+        cost_estimate=cost(0, 1e5),
+        name="norm_step",
+    )(gs1, gsum, dhs, norm, moment)
+
+
+def to_rows(field):
+    b, h, w, c = field.shape
+    split = field.reshape(b, h, w // 2, 2, c)
+    return jnp.transpose(split, (1, 3, 0, 2, 4)).reshape(h, w * b, c)
+
+
+def from_rows(field, b):
+    h, tall, c = field.shape
+    split = field.reshape(h, 2, b, tall // (2 * b), c)
+    return jnp.transpose(split, (2, 0, 3, 1, 4)).reshape(b, h, tall // b, c)
+
+
+def pooled_rows(field):
+    b, h, w, c = field.shape
+    return jnp.transpose(field, (1, 0, 2, 3)).reshape(h, b * w, c)
+
+
+def shards(
+    images,
+    cot_shared,
+    cot_tasks,
+    depth_mask,
+    nash_weights,
+    conv_weight,
+    conv_left,
+    conv_right,
+    conv_left_root,
+    conv_right_root,
+    proj_weight,
+    proj_left,
+    proj_right,
+    proj_left_root,
+    proj_right_root,
+    norm_params,
+    norm_moment,
+):
+    batch, tile_h, tile_w, _ = images.shape
+    half_h, half_w = tile_h // 2, tile_w // 2
+    tall = batch * tile_w
+    q = batch * half_w
+    ha, wa = lax.axis_index("ha"), lax.axis_index("wa")
+    count_all = float(
+        batch * tile_h * tile_w * lax.axis_size("img") * lax.axis_size("ha") * lax.axis_size("wa")
+    )
+    idx = jnp.stack(
+        [
+            lax.axis_index("img"),
+            ha,
+            wa % 2,
+            ha > 0,
+            ha < lax.axis_size("ha") - 1,
+            wa > 0,
+            wa < lax.axis_size("wa") - 1,
+        ]
+    ).astype(jnp.int32)
+
+    halves = conv_weight[0].reshape(conv_weight.shape[1], 2, HB, BLK)
+    own = lax.dynamic_index_in_dim(halves, wa % 2, axis=1, keepdims=False).astype(BF)
+    g0, g1 = Gather(own[None, 0:9]), Gather(own[None, 9:18])
+    g0.near()
     edges = after(images, own)
     rows0 = jnp.stack(row_halo(edge_row(edges, 0), edge_row(edges, tile_h - 1)))
     g0.join(rows0)
@@ -1314,13 +1553,27 @@
     up = jnp.transpose(proj_low[:, 1], (0, 2, 1, 3)).reshape(TASKS, CA, C)
 
     image_rows = to_rows(images)
-    x3 = shift_copies(idx, image_rows, rows0, halo_cols(image_rows, rows0, batch), batch)
+    edges = jnp.concatenate([images[:, :, 0], images[:, :, tile_w - 1]], axis=0)
+    edges = jnp.transpose(edges, (1, 0, 2))
+    x3 = shift_copies(idx, image_rows, rows0, halo_cols(edges, rows0, batch), batch)
     g0.high(g0.low_x, g0.low_y)
     g0.corner_a(x3)
-    g0.corner_b()
     g1.near(g0.line_high)
-    cot_tasks = after(cot_tasks, g0.line_high)
-
+    g0.corner_b(g0.high_x, g1.near_got)
+
+    cot = pooled_rows(cot_shared.astype(F32) * 0.25)
+
+    g1.join(g0.corner_high)
+    g1.far()
+    g1.low()
+    w0 = g0.pieces()
+    z1, s1, edges1 = conv(after(idx, g1.line_low), x3, w0, False, F32, "conv_first", batch)
+
+    halo1 = halo(edges1, batch)
+    s1 = after(s1, g1.line_high, g1.low_x, g1.low_y)
+    wt_mine = lax.all_gather(after(own[18:], s1), ("img", "ha"), axis=0, tiled=False)
+
+    cot_tasks = after(cot_tasks, z1)
     depth_pick = jnp.arange(TASKS) == 1
     scale = jnp.where(depth_pick, depth_mask.astype(F32)[..., None], 1.0) * nash_weights
     weighted = cot_tasks.astype(F32).reshape(batch, half_h, half_w, TASKS, C)
@@ -1334,68 +1587,62 @@
     grid = jnp.concatenate([left, grid, right], axis=3)
     go3 = jnp.stack([grid[:, :, :, k : k + half_w] for k in range(3)], axis=1)
     go3 = go3.reshape(TASKS, 3, half_h + 2, q, C)
-    cot = pooled_rows(cot_shared.astype(F32) * 0.25)
-
-    g1.join(g0.corner_high)
-    g1.far()
-    g1.low()
-    w0 = g0.pieces()
-    z1, s1 = conv(after(idx, g1.line_low, go3), x3, w0, False, True, F32, "conv_first")
-
-    def none(dep):
-        return ()
-
-    halo1 = halo(z1, batch)
-    s1 = after(s1, g1.line_high)
-    wt_mine = lax.all_gather(after(own[18:], s1), ("img", "ha"), axis=0, tiled=False)
-    g1.high(s1)
-
-    def s1_img1(dep):
-        return g1.high_x, g1.high_y
-
-    def s1_img2(dep):
-        g1.corner_a(dep)
-        g1.corner_b(dep)
-        return ()
-
-    s1 = sum_all(s1, [none, none, none, s1_img1, s1_img2])
+    def s1_img(dep):
+        g1.high(dep)
+        return halo1
+
+    s1 = after(sum_all(s1, img=s1_img), g1.high_x, g1.high_y)
+    g1.corner_a(s1)
+    g1.corner_b(s1)
     u3, hp, hc, hs = mid(idx, s1, gb1, z1, *halo1, down, batch, count_all)
+    hs = after(hs, g1.corner_low, g1.corner_high)
     w1 = g1.pieces(hs)
     kept = {}
 
     def s2_ha1(dep):
-        kept["z2"], kept["s2"] = conv(idx, after(u3, dep), w1, False, True, F32, "conv_second")
+        kept["z2"], kept["s2"], kept["edges2"] = conv(
+            idx, after(u3, dep), w1, False, F32, "conv_second", batch
+        )
         return (kept["s2"],)
 
-    hs = sum_all(hs, [none, none, none, s2_ha1, none], ("wa", "img", "ha"))
+    hs = sum_all(hs, ("wa", "img", "ha"), ha=s2_ha1)
     z2, s2 = kept["z2"], kept["s2"]
-    halo2 = halo(z2, batch)
+    halo2 = halo(kept["edges2"], batch)
     h, hcb, ms = hidden(hs, gbd, hp, hc, up, tall, count_all)
-    s2m = sum_all(jnp.concatenate([s2, ms], axis=0), (), ("wa", "img", "ha"))
+
+    def s3_img(dep):
+        return halo2 + (go3,)
+
+    s2m = sum_all(jnp.concatenate([s2, ms], axis=0), ("wa", "img", "ha"), img=s3_img)
+    s2, ms = s2m[0:2], s2m[2:]
+    se, so, pooled = attend(
+        idx, s2, gb2, ms, gbu, z2, *halo2, h, hcb, up, batch, count_all
+    )
+    halves_t = task_wgrad(idx, se, so, go3)
+    if lax.axis_size("wa") == 2:
+        part_t = lax.psum_scatter(halves_t, "wa", scatter_dimension=0, tiled=True)[0]
+    else:
+        mine_t = lax.dynamic_index_in_dim(halves_t, wa % 2, keepdims=False)
+        other_t = lax.dynamic_index_in_dim(halves_t, 1 - wa % 2, keepdims=False)
+        part_t = add_low(mine_t, swap(other_t, "wa", 1))
     wt_mine = after(wt_mine, s2m)
     wt = (wt_mine, swap(wt_mine, "wa", 1))
-    kept["da"] = ()
-    for task in range(TASKS):
-        kept["da"] = (task_back(idx, go3, wt, task, kept["da"]),)
-    s2, ms = s2m[0:2], s2m[2:]
-    da = kept["da"][0].reshape(TASKS, tile_h, tall, C)
-    se, so, dym, dy2, pooled, gsum = attend(
-        idx, s2, gb2, ms, gbu, z2, *halo2, h, hcb, up, da, cot, batch, count_all
+    da = task_back(after(idx, halves_t), go3, wt)
+    dym, dy2, gsum, *edges2 = attend_back(
+        s2, gb2, ms, gbu, z2, h, up, da, cot, batch, count_all
     )
 
-    dhalo2 = halo(dy2, batch)
-    kept["wt"] = ()
-
-    def run_wgrad(task):
-        def run(dep):
-            kept["wt"] = task_wgrad(after(idx, dep), se, so, go3, task, kept["wt"])
-            return tuple(kept["wt"])
-
-        return run
-
-    gsum = sum_all(gsum, [none, run_wgrad(0), run_wgrad(1), run_wgrad(2)])
-    mine_t, other_t = kept["wt"]
-    other_t = swap(other_t, "wa", 1)
+    grad_t = lax.psum_scatter(
+        after(part_t, gsum), ("img", "ha"), scatter_dimension=0, tiled=True
+    )
+
+    dhalo2 = halo(edges2, batch)
+
+    def run_task_fwd(dep):
+        kept["task_out"] = task_fwd(after(idx, dep), se, so, wt)
+        return (kept["task_out"],) + tuple(dhalo2)
+
+    gsum = sum_all(gsum, ha=run_task_fwd)
     dup, dh, dhs = mask_back(ms, gbu, gsum[0:6], hs, gbd, dym, h, hp, up, tall, count_all)
 
     def run_second_back(dep):
@@ -1403,90 +1650,86 @@
         kept["z3"] = norm_back(
             idx, s2, gb2, gs, dy2, dhalo2, z2, halo2, batch, count_all, "second_back"
         )
-        part_t = add_low(mine_t, after(other_t, dep))
-        kept["gt"] = lax.psum_scatter(part_t, ("img", "ha"), scatter_dimension=0, tiled=True)
-        return kept["z3"], part_t
+        return (kept["z3"],)
 
     def run_conv_back(dep):
-        kept["part"] = conv(idx, after(kept["z3"], dep), w1, True, False, F32, "conv_second_back")
+        kept["part"] = conv(idx, after(kept["z3"], dep), w1, True, F32, "conv_second_back")
         return (kept["part"],)
 
-    dhs = sum_all(dhs, [run_second_back, none, run_conv_back, none, none])
+    dhs = sum_all(dhs, ha=run_second_back, img=run_conv_back)
     z3, part = kept["z3"], kept["part"]
-    ddown, dy1, gs1 = first_back(hs, gbd, dhs, s1, gb1, dh, hp, u3, part, z1, down, count_all)
-    dhalo1 = halo(dy1, batch)
+    ddown, dy1, gs1, *edges1 = first_back(
+        hs, gbd, dhs, s1, gb1, dh, hp, u3, part, z1, down, batch, count_all
+    )
+    dhalo1 = halo(edges1, batch)
 
     def run_wgrad_second(dep):
         kept["r1"] = Scatter(*wgrad(after(idx, dep), u3, z3, "wgrad_second", (ddown, dup)))
-        return (kept["r1"].other,)
+        return (kept["r1"].other,) + tuple(dhalo1)
 
     def run_wa(dep):
         kept["r1"].wa(dep)
         return ()
 
-    gs1 = sum_all(gs1, [none, run_wgrad_second, none, none, run_wa])
+    gs1 = sum_all(gs1, ha=run_wgrad_second, img=run_wa)
     r1 = kept["r1"]
-    y3 = norm_back(idx, s1, gb1, gs1, dy1, dhalo1, z1, halo1, batch, count_all, "first_norm_back")
-    y3 = after(y3, r1.corner_sum(y3))
+    r1.corner_sum(gs1)
     r1.corner_send()
-    r0 = Scatter(*wgrad(idx, x3, y3, "wgrad_first"))
+    y3 = norm_back(
+        after(idx, r1.corner), s1, gb1, gs1, dy1, dhalo1, z1, halo1, batch, count_all, "first_norm_back"
+    )
+    r1.high_sum(y3)
+    r1.low_sum(y3)
+    r1.high_send()
+    r1.low_send(*r1.high)
+    r0 = Scatter(*wgrad(after(idx, *r1.high, *r1.low), x3, y3, "wgrad_first"))
     state = (conv_left, conv_right, conv_left_root, conv_right_root, conv_weight)
-    r0.wa()
-    r1.high_sum(r0.mine)
-    r1.high_send()
-    r1.low_sum(*r1.high)
-    r0.corner_sum(*r1.low)
+    r0.wa(r1.high_x, r1.high_y, r1.low_x, r1.low_y)
+    r0.corner_sum()
     r0.corner_send()
-    r1.low_send(r0.corner)
-    outs = (task_fwd(after(idx, r0.corner, *r1.low), se, so, wt, 0, ()),)
-    r0.high_sum(*outs)
+    r1.far_sum(r0.corner)
+    r1.far_send()
+    image_grad = conv(after(idx, r0.corner, r1.far), y3, w0, True, BF, "conv_first_back")
+    image_grad = after(image_grad, r0.to_x, r0.to_y, r1.from_far)
+    gradt = after(grad_t[0], image_grad)
+    step = 2
+    while step < lax.axis_size("wa"):
+        gradt = add_low(gradt, swap(gradt, "wa", step))
+        step *= 2
+    gradt_other = swap(gradt, "wa", 1)
+    r0.high_sum(image_grad)
     r0.high_send()
     r0.low_sum(*r0.high)
     r0.low_send()
-    r1.far_sum(*r0.low)
-    r1.far_send()
-    outs = (task_fwd(after(idx, r1.far), se, so, wt, 1, outs),)
-    r0.far_sum(*outs)
+    r1.near_sum(*r0.low)
+    r1.near_send()
+    new = shampoo_conv(after(idx, *r0.low, r1.near), gradt, gradt_other, state, 18, ())
+    r0.far_sum(new[0], r0.low_x, r0.low_y, r1.from_near)
     r0.far_send()
-    r1.near_sum(r0.far)
-    r1.near_send()
-    outs = (task_fwd(after(idx, r1.near), se, so, wt, 2, outs),)
-    r0.near_sum(*outs)
+    grad1, grad1_other = r1.finish(r0.far)
+    new = shampoo_conv(
+        after(idx, grad1), grad1[: 9 * HB], grad1_other[: 9 * HB], state, 9, new
+    )
+    r0.near_sum(new[0])
     r0.near_send()
-    grad1, grad1_other = r1.finish(r0.near)
-    proj_total = gather_proj(grad1[9 * HB :])
-    image_grad = conv(idx, after(y3, grad1), w0, True, False, BF, "conv_first_back")
-    new = shampoo_conv(
-        after(idx, image_grad), grad1[: 9 * HB], grad1_other[: 9 * HB], state, 9, ()
+    proj = gather_proj_line(after(grad1[9 * HB :], r0.near))
+    grad0, grad0_other = r0.finish(proj)
+    proj_total = gather_proj(after(proj, grad0))
+    new = shampoo_conv(idx, grad0, grad0_other, state, 0, new)
+    proj_left_new, proj_right_new, proj_weight_new = shampoo_proj(
+        after(proj_total, new[0]), proj_left, proj_right, proj_left_root, proj_right_root, proj_weight
     )
-    grad0, grad0_other = r0.finish(image_grad)
-    new = shampoo_conv(idx, grad0, grad0_other, state, 0, new)
-    gradt = after(kept["gt"][0], new[0])
-    new = shampoo_conv(idx, gradt, swap(gradt, "wa", 1), state, 18, new)
     conv_total, conv_left_new, conv_right_new, conv_weight_new = new
-    task_out = outs[0]
 
     image_grad = from_rows(image_grad, batch)
     task_out = jnp.transpose(
-        task_out.reshape(TASKS, half_h, batch, half_w, C), (2, 1, 3, 0, 4)
+        kept["task_out"].reshape(TASKS, half_h, batch, half_w, C), (2, 1, 3, 0, 4)
     ).reshape(batch, half_h, half_w, TASKS * C)
     shared_out = jnp.transpose(
-        pooled.astype(BF).reshape(half_h, batch, half_w, C), (1, 0, 2, 3)
+        pooled.reshape(half_h, batch, half_w, C), (1, 0, 2, 3)
     )
 
-    proj_left_new, proj_right_new, proj_weight_new = shampoo_proj(
-        proj_total, proj_left, proj_right, proj_left_root, proj_right_root, proj_weight
-    )
-
-    corner = jnp.sum(gsum[8:14], axis=1)
-    gram = jnp.stack(
-        [corner[0], corner[1], corner[2], corner[1], corner[3], corner[4], corner[2], corner[4], corner[5]]
-    ).reshape(TASKS, TASKS)
-    gain_grads = jnp.concatenate([gs1[1], gsum[7], dhs[1], gsum[1], gsum[3], gsum[5]])
-    bias_grads = jnp.concatenate([gs1[0], gsum[6], dhs[0], gsum[0], gsum[2], gsum[4]])
-    norm_grad = jnp.stack([gain_grads, bias_grads])
-    moment_new = moment_decay * norm_moment + (1.0 - moment_decay) * norm_grad * norm_grad
-    norm_new = norm_params - norm_rate * norm_grad / (jnp.sqrt(moment_new) + 1e-08)
+    gram, norm_grad, moment_new, norm_new = norm_step(gs1, gsum, dhs, norm_params, norm_moment)
     return (
         shared_out,
         task_out,

time: 569 us -> 498 us (0.88)
  waiting for transfers between devices: 127 us -> 85.3 us
  Pallas kernels: 217 us -> 198 us
  starting transfers between devices: 102 us -> 116 us
  other arithmetic: 56.4 us -> 44 us
  local copies, waits for them, and re-layouts: 39.3 us -> 28.5 us
    ppermute x96 -> x103, waiting for transfers between devices: 101 us -> 71.2 us  [swap(): return lax.ppermute(value, axis, pairs(axis, step))]
    convert_element_type x17 -> x14, other arithmetic: 30.2 us -> 17.6 us  [add_low(): return total.astype(BF)]
    ppermute x12 -> x18, waiting for transfers between devices: 26.6 us -> 14 us  [the longest x6 14 us: ring_gather(): lax.ppermute(value, axis, [(i, (i + step) % count) for i in range(count)])]
    ppermute x96 -> x103, starting transfers between devices: 82.9 us -> 92.2 us  [swap(): return lax.ppermute(value, axis, pairs(axis, step))]
    pallas_call x15 -> x11, Pallas kernels: 120 us -> 113 us  [the longest x4 45.7 us: conv(): pl.pallas_call(functools.partial(conv_kernel, len(pieces), batch, transpo...]
    pallas_call x1, Pallas kernels: 14.9 us -> 8.64 us  [attend(): pl.pallas_call(functools.partial(attend_kernel, batch, count_all), grid=(...]
    pallas_call x3, Pallas kernels: 21.4 us -> 15.5 us  [shampoo_conv(): pl.pallas_call(functools.partial(shampoo_kernel, len(prev)), grid=(n // e...]
    convert_element_type x14 -> x0, local copies, waits for them, and re-layouts: 5.79 us -> none  [the longest x10 5.75 us: halo_cols(): jnp.stack([left, right], axis=2).reshape(height + 2, 2 * batch, chans)]
  transfers between devices with their start and end apart: 110 -> 124, of which waited for: 51 -> 43; matrix products, arithmetic and copies ran while one was open for 14% -> 12% of each run, Pallas kernels for 29% -> 39%
where the time goes in v2:
time: 498 us; the launch traced here: 489 us
  Pallas kernels  198 us (40%)
  starting transfers between devices  116 us (23%)
  waiting for transfers between devices  85.3 us (17%)
  other arithmetic  44 us (9%)
  local copies, waits for them, and re-layouts  28.5 us (6%)
  between operations  17.6 us (4%)
    ppermute x103, starting transfers between devices, swap(): return lax.ppermute(value, axis, pairs(axis, step))  92.2 us
    ppermute x103, waiting for transfers between devices, swap(): return lax.ppermute(value, axis, pairs(axis, step))  71.2 us
    pallas_call x4, Pallas kernels, conv(): pl.pallas_call(functools.partial(conv_kernel, len(pieces), batch, transpo...  45.7 us
    pallas_call x2, Pallas kernels, wgrad(): pl.pallas_call(functools.partial(wgrad_kernel, len(extra)), grid=(1,), in...  21.3 us
    convert_element_type x14, other arithmetic, add_low(): return total.astype(BF)  17.6 us
    pallas_call x1, Pallas kernels, task_back(): pl.pallas_call(da_kernel, grid=(TASKS,), in_specs=[SM, pl.BlockSpec((1,)...  16 us
    pallas_call x3, Pallas kernels, shampoo_conv(): pl.pallas_call(functools.partial(shampoo_kernel, len(prev)), grid=(n // e...  15.5 us
    ppermute x12, starting transfers between devices, row_halo(): lax.ppermute(send, 'ha', [(i, pairing.get(i, i)) for i in range(count)])  14.8 us
  transfers between devices with their start and end apart: 124, of which 43 were waited for; matrix products, arithmetic and copies ran while one was open for 12% of the time, Pallas kernels for 39%

profile of v2, /device:TPU:0, one launch (start us, length us, event | category | flops | bytes accessed | tf_op | source)
XLA Modules:
  0.0 489.3 jit_solution(7700296446859579091)
XLA Ops:
  9.1 3.1 collective-permute-start.1
  15.1 3.8 collective-permute-start
  19.8 6.0 %collective-permute-done = bf16[1,9,64,128]{3,2,1,0:T(8,128)(2,1)S(1)} collective-permute-done((bf16[1,9,64,128]{3,2,1,0:T(8,128)(2,1)S(1)}, bf16[1,9,64,128]{3,2,1,0:T(8,128)(2,1)S(1)}, u32[]{:S(2)}, u32[]{:S(2)}) %collective-permute-start) | collective-permute-done | bytes 147488 | tf_op jit(solution)/shard_map/ppermute | solution.py:54
  36.7 3.4 collective-permute-start.4
  41.8 4.5 shift_copies.1.x_ref.x3
  48.9 4.2 collective-permute-done.11.refs_6_
  59.4 11.6 %conv_first.1 = (f32[16,64,512]{2,1,0:T(8,128)}, f32[2,512]{1,0:T(2,128)}, bf16[2,64,512]{2,1,0:T(8,128)(2,1)}, f32[16,8,512]{2,1,0:T(8,128)}) custom-call(s32[7]{0:T(128)} %stack.169.idx.idx_ref, bf16[3,18,64,512]{3,2,1,0:T(8,128)(2,1)} %shift_copies.1.x_ref.x3, bf16[2,9,64,128]{3,2,1,0:T(8,128)(2,1)} %copy-done.7, bf16[2,9,64,128]{3,2,1,0:T(8,128)(2,1)} %copy-done.10, ...), custom_call_target="tpu_custom_call" | custom-call | flops 301989888 | bytes 625000 | tf_op jit(solution)/shard_map/conv_first/pallas_call | solution.py:460
  72.1 1.7 collective-permute-start.30
  75.3 2.7 collective-permute-start.25
  80.2 2.2 collective-permute-done.24
  83.7 2.2 collective-permute-start.27
  87.6 2.3 collective-permute-start.60
  94.9 2.0 collective-permute-done.33.refs_3_
  98.1 2.0 collective-permute-start.35
  104.5 8.2 %mid.1 = (bf16[3,18,64,512]{3,2,1,0:T(8,128)(2,1)}, f32[1152,384]{1,0:T(8,128)}, f32[144,384]{1,0:T(8,128)}, f32[2,384]{1,0:T(2,128)}) custom-call(s32[7]{0:T(128)} %stack.169.idx.idx_ref, f32[2,512]{1,0:T(2,128)} %add_add_fusion.6.st, f32[2,512]{1,0:T(2,128)} %get-tuple-element.335.gb, f32[16,64,512]{2,1,0:T(8,128)} %get-tuple-element.147.z_ref.z, ...), custom_call_target="tpu_custom_call" | custom-call | flops 28311552 | bytes 625000 | tf_op jit(solution)/shard_map/mid/pallas_call | solution.py:526
  115.2 1.7 collective-permute-start.40
  121.7 2.1 collective-permute-start.51
  124.2 1.7 collective-permute-start.50
  128.9 1.8 collective-permute-done.49
  131.9 1.9 pad_maximum_fusion.go
  136.2 11.6 %conv_second.1 = (f32[16,64,512]{2,1,0:T(8,128)}, f32[2,512]{1,0:T(2,128)}, bf16[2,64,512]{2,1,0:T(8,128)(2,1)}, f32[16,8,512]{2,1,0:T(8,128)}) custom-call(s32[7]{0:T(128)} %stack.169.idx.idx_ref, bf16[3,18,64,512]{3,2,1,0:T(8,128)(2,1)} %get-tuple-element.153.x_ref.u3.x3, bf16[2,9,64,128]{3,2,1,0:T(8,128)(2,1)} %copy-done.8, ...), custom_call_target="tpu_custom_call" | custom-call | flops 301989888 | bytes 625000 | tf_op jit(solution)/shard_map/conv_second/pallas_call | solution.py:460
  147.9 6.0 %hidden.1 = (bf16[1152,384]{1,0:T(8,128)(2,1)}, bf16[144,384]{1,0:T(8,128)(2,1)}, f32[6,512]{1,0:T(8,128)}) custom-call(f32[2,384]{1,0:T(2,128)} %add_add_fusion.10.st.hst, f32[2,384]{1,0:T(2,128)} %slice.567.gb.hgb, f32[1152,384]{1,0:T(8,128)} %get-tuple-element.164.hp, f32[144,384]{1,0:T(8,128)} %get-tuple-element.165.hc, bf16[3,128,512]{2,1,0:T(8,128)(2,1)} %bitcast.324), custom_call_target="tpu_custom_call" | custom-call | flops 28311552 | bytes 312500 | tf_op jit(solution)/shard_map/hidden/pallas_call | solution.py:585
  158.8 1.8 collective-permute-start.53
  165.0 1.8 collective-permute-start.64
  166.7 3.5 collective-permute-start.63
  171.0 3.1 collective-permute-done.63
  175.5 8.6 %attend.1 = (bf16[3,3,9,32,512]{4,3,2,1,0:T(8,128)(2,1)}, bf16[3,3,8,32,512]{4,3,2,1,0:T(8,128)(2,1)}, bf16[8,32,512]{2,1,0:T(8,128)(2,1)}) custom-call(s32[7]{0:T(128)} %stack.169.idx.idx_ref, f32[2,512]{1,0:T(2,128)} %slice.700.st, f32[2,512]{1,0:T(2,128)} %get-tuple-element.334.gb, f32[6,512]{1,0:T(8,128)} %slice.701.mst, f32[6,512]{1,0:T(8,128)} %reshape.286.mgb, ...), custom_call_target="tpu_custom_call" | custom-call | flops 28311552 | bytes 937500 | tf_op jit(solution)/shard_map/attend/pallas_call | solution.py:769
  184.1 9.5 %task_wgrad.1 = bf16[2,16,1728,128]{3,2,1,0:T(8,128)(2,1)} custom-call(s32[7]{0:T(128)} %stack.169.idx.idx_ref, bf16[3,3,9,32,512]{4,3,2,1,0:T(8,128)(2,1)} %get-tuple-element.175.se, bf16[3,3,8,32,512]{4,3,2,1,0:T(8,128)(2,1)} %get-tuple-element.176.so, bf16[3,3,10,32,512]{4,3,2,1,0:T(8,128)(2,1)} %pad_maximum_fusion.go), custom_call_target="tpu_custom_call" | custom-call | flops 226492416 | bytes 1500000 | tf_op jit(solution)/shard_map/task_wgrad/pallas_call | solution.py:1195
  195.4 10.1 %collective-permute-done.65.other = bf16[16,27,64,128]{3,2,1,0:T(8,128)(2,1)S(1)} collective-permute-done((bf16[16,27,64,128]{3,2,1,0:T(8,128)(2,1)}, bf16[16,27,64,128]{3,2,1,0:T(8,128)(2,1)S(1)}, u32[]{:S(2)}, u32[]{:S(2)}) %collective-permute-start.65) | collective-permute-done | bytes 7077920 | tf_op jit(solution)/shard_map/ppermute | solution.py:54
  205.5 3.3 copy-done
  208.8 16.0 %task_back.1 = bf16[3,8,2,2,32,512]{5,4,3,2,1,0:T(8,128)(2,1)} custom-call(s32[7]{0:T(128)} %stack.169.idx.idx_ref, bf16[3,3,10,32,512]{4,3,2,1,0:T(8,128)(2,1)} %pad_maximum_fusion.go, bf16[16,27,64,128]{3,2,1,0:T(8,128)(2,1)} %bitcast.321, bf16[16,27,64,128]{3,2,1,0:T(8,128)(2,1)} %copy-done), custom_call_target="tpu_custom_call" | custom-call | flops 402653184 | bytes 1500000 | tf_op jit(solution)/shard_map/task_back/pallas_call | solution.py:656
  224.8 12.3 %attend_back.1 = (bf16[3,16,64,512]{3,2,1,0:T(8,128)(2,1)}, f32[16,64,512]{2,1,0:T(8,128)}, f32[14,512]{1,0:T(8,128)}, bf16[2,64,512]{2,1,0:T(8,128)(2,1)}, f32[16,8,512]{2,1,0:T(8,128)}) custom-call(f32[2,512]{1,0:T(2,128)} %slice.700.st, f32[2,512]{1,0:T(2,128)} %get-tuple-element.334.gb, f32[6,512]{1,0:T(8,128)} %slice.701.mst, f32[6,512]{1,0:T(8,128)} %reshape.286.mgb, ...), custom_call_target="tpu_custom_call" | custom-call | flops 25165824 | bytes 937500 | tf_op jit(solution)/shard_map/attend_back/pallas_call | solution.py:849
  240.0 2.0 collective-permute-start.69
  242.0 3.5 collective-permute-start.68
  245.6 11.4 %task_fwd.1 = bf16[3,8,32,512]{3,2,1,0:T(8,128)(2,1)} custom-call(s32[7]{0:T(128)} %stack.169.idx.idx_ref, bf16[3,3,9,32,512]{4,3,2,1,0:T(8,128)(2,1)} %get-tuple-element.175.se, bf16[3,3,8,32,512]{4,3,2,1,0:T(8,128)(2,1)} %get-tuple-element.176.so, bf16[16,27,64,128]{3,2,1,0:T(8,128)(2,1)} %bitcast.322, bf16[16,27,64,128]{3,2,1,0:T(8,128)(2,1)} %copy-done), custom_call_target="tpu_custom_call" | custom-call | flops 226492416 | bytes 1250000 | tf_op jit(solution)/shard_map/task_fwd/pallas_call | solution.py:1231
  263.0 1.8 collective-permute-done.75
  266.4 9.7 %mask_back.1 = (f32[3,128,512]{2,1,0:T(8,128)}, f32[1024,384]{1,0:T(8,128)}, f32[2,384]{1,0:T(2,128)}) custom-call(f32[6,512]{1,0:T(8,128)} %slice.701.mst, f32[6,512]{1,0:T(8,128)} %reshape.286.mgb, f32[6,512]{1,0:T(8,128)} %slice.709.msum, f32[2,384]{1,0:T(2,128)} %add_add_fusion.10.st.hst, f32[2,384]{1,0:T(2,128)} %slice.567.gb.hgb, ...), custom_call_target="tpu_custom_call" | custom-call | flops 75497472 | bytes 500000 | tf_op jit(solution)/shard_map/mask_back/pallas_call | solution.py:925
  278.2 2.0 collective-permute-start.79
  283.2 5.4 %second_back.1.x_ref.g3 = bf16[3,18,64,512]{3,2,1,0:T(8,128)(2,1)} custom-call(s32[7]{0:T(128)} %stack.169.idx.idx_ref, f32[2,512]{1,0:T(2,128)} %slice.700.st, f32[2,512]{1,0:T(2,128)} %get-tuple-element.334.gb, f32[2,512]{1,0:T(2,128)} %slice.710.gs, f32[16,64,512]{2,1,0:T(8,128)} %get-tuple-element.188.dy, bf16[2,64,512]{2,1,0:T(8,128)(2,1)} %pad_maximum_fusion.13.drows, ...), custom_call_target="tpu_custom_call" | custom-call | bytes 625000 | tf_op jit(solution)/shard_map/second_back/pallas_call | solution.py:992
  288.6 1.9 collective-permute-start.82
  292.2 11.5 %conv_second_back.1.part = f32[16,64,512]{2,1,0:T(8,128)} custom-call(s32[7]{0:T(128)} %stack.169.idx.idx_ref, bf16[3,18,64,512]{3,2,1,0:T(8,128)(2,1)} %second_back.1.x_ref.g3, bf16[2,9,64,128]{3,2,1,0:T(8,128)(2,1)} %copy-done.8, bf16[2,9,64,128]{3,2,1,0:T(8,128)(2,1)} %collective-permute-done.20.refs_1_, ...), custom_call_target="tpu_custom_call" | custom-call | flops 301989888 | bytes 625000 | tf_op jit(solution)/shard_map/conv_second_back/pallas_call | solution.py:460
  304.3 10.0 %first_back.1 = (f32[512,384]{1,0:T(8,128)}, f32[16,64,512]{2,1,0:T(8,128)}, f32[2,512]{1,0:T(2,128)}, bf16[2,64,512]{2,1,0:T(8,128)(2,1)}, f32[16,8,512]{2,1,0:T(8,128)}) custom-call(f32[2,384]{1,0:T(2,128)} %add_add_fusion.10.st.hst, f32[2,384]{1,0:T(2,128)} %slice.567.gb.hgb, f32[2,384]{1,0:T(2,128)} %add_add_fusion.8.hsum.dhs, ...), custom_call_target="tpu_custom_call" | custom-call | flops 50331648 | bytes 750000 | tf_op jit(solution)/shard_map/first_back/pallas_call | solution.py:1057
  319.3 1.9 collective-permute-start.86
  321.2 2.8 collective-permute-start.85
  324.0 11.1 %wgrad_second.1 = (bf16[4,4,672,128]{3,2,1,0:T(8,128)(2,1)}, bf16[4,4,672,128]{3,2,1,0:T(8,128)(2,1)}) custom-call(s32[7]{0:T(128)} %stack.169.idx.idx_ref, bf16[3,18,64,512]{3,2,1,0:T(8,128)(2,1)} %get-tuple-element.153.x_ref.u3.x3, bf16[3,18,64,512]{3,2,1,0:T(8,128)(2,1)} %second_back.1.x_ref.g3, f32[512,384]{1,0:T(8,128)} %get-tuple-element.195.refs_0_, ...), custom_call_target="tpu_custom_call" | custom-call | flops 301989888 | bytes 625000 | tf_op jit(solution)/shard_map/wgrad_second/pallas_call | solution.py:1163
  344.3 1.8 fusion.4
  347.9 5.4 %first_norm_back.1.g3.x_ref = bf16[3,18,64,512]{3,2,1,0:T(8,128)(2,1)} custom-call(s32[7]{0:T(128)} %stack.169.idx.idx_ref, f32[2,512]{1,0:T(2,128)} %add_add_fusion.6.st, f32[2,512]{1,0:T(2,128)} %get-tuple-element.335.gb, f32[2,512]{1,0:T(2,128)} %add_add_fusion.4.gs.gs1, f32[16,64,512]{2,1,0:T(8,128)} %get-tuple-element.205.dy, ...), custom_call_target="tpu_custom_call" | custom-call | bytes 625000 | tf_op jit(solution)/shard_map/first_norm_back/pallas_call | solution.py:992
  357.0 7.1 %collective-permute-done.94 = bf16[2,672,128]{2,1,0:T(8,128)(2,1)S(1)} collective-permute-done((bf16[2,672,128]{2,1,0:T(8,128)(2,1)S(1)}, bf16[2,672,128]{2,1,0:T(8,128)(2,1)S(1)}, u32[]{:S(2)}, u32[]{:S(2)}) %collective-permute-start.94) | collective-permute-done | bytes 344096 | tf_op jit(solution)/shard_map/ppermute | solution.py:54
  366.7 10.2 %wgrad_first.1 = (bf16[4,4,576,128]{3,2,1,0:T(8,128)(2,1)}, bf16[4,4,576,128]{3,2,1,0:T(8,128)(2,1)}) custom-call(s32[7]{0:T(128)} %stack.169.idx.idx_ref, bf16[3,18,64,512]{3,2,1,0:T(8,128)(2,1)} %shift_copies.1.x_ref.x3, bf16[3,18,64,512]{3,2,1,0:T(8,128)(2,1)} %first_norm_back.1.g3.x_ref), custom_call_target="tpu_custom_call" | custom-call | flops 301989888 | bytes 625000 | tf_op jit(solution)/shard_map/wgrad_first/pallas_call | solution.py:1163
  376.9 3.2 collective-permute-done.98
  380.1 4.7 collective-permute-done.100
  386.7 1.8 collective-permute-start.103
  390.7 11.0 %conv_first_back.1 = bf16[16,64,512]{2,1,0:T(8,128)(2,1)} custom-call(s32[7]{0:T(128)} %stack.169.idx.idx_ref, bf16[3,18,64,512]{3,2,1,0:T(8,128)(2,1)} %first_norm_back.1.g3.x_ref, bf16[2,9,64,128]{3,2,1,0:T(8,128)(2,1)} %copy-done.7, bf16[2,9,64,128]{3,2,1,0:T(8,128)(2,1)} %copy-done.10, bf16[2,9,64,128]{3,2,1,0:T(8,128)(2,1)} %collective-permute-done.5.refs_2_, ...), custom_call_target="tpu_custom_call" | custom-call | flops 301989888 | bytes 625000 | tf_op jit(solution)/shard_map/conv_first_back/pallas_call | solution.py:460
  402.4 1.8 fusion.19
  405.7 1.9 fusion.13
  408.1 1.8 fusion.20
  415.8 8.1 %shampoo_conv.3 = (f32[1,45,128,128]{3,2,1,0:T(8,128)}, f32[1,45,128,128]{3,2,1,0:T(8,128)}, f32[1,45,128,128]{3,2,1,0:T(8,128)}, f32[1,45,128,128]{3,2,1,0:T(8,128)}) custom-call(s32[7]{0:T(128)} %stack.169.idx.idx_ref, bf16[1728,128]{1,0:T(8,128)(2,1)} %bitcast.338, bf16[1728,128]{1,0:T(8,128)(2,1)} %copy-done.36, f32[1,45,128,128]{3,2,1,0:T(8,128)} %left.6, ...), custom_call_target="tpu_custom_call" | custom-call | flops 28311552 | bytes 995328 | tf_op jit(solution)/shard_map/shampoo_conv/pallas_call | solution.py:1293
  430.6 3.7 shampoo_conv.4
  438.3 2.3 collective-permute-start.113
  441.5 2.9 collective-permute-start.114
  444.6 9.0 %collective-permute-done.114 = bf16[2,96,128]{2,1,0:T(8,128)(2,1)S(1)} collective-permute-done((bf16[2,96,128]{2,1,0:T(8,128)(2,1)S(1)}, bf16[2,96,128]{2,1,0:T(8,128)(2,1)S(1)}, u32[]{:S(2)}, u32[]{:S(2)}) %collective-permute-start.114) | collective-permute-done | bytes 49184 | tf_op jit(solution)/shard_map/ppermute | solution.py:173
  464.3 3.7 shampoo_conv.5
  468.0 5.0 %collective-permute-done.119 = bf16[4,2,96,128]{3,2,1,0:T(8,128)(2,1)S(1)} collective-permute-done((bf16[4,2,96,128]{3,2,1,0:T(8,128)(2,1)S(1)}, bf16[4,2,96,128]{3,2,1,0:T(8,128)(2,1)S(1)}, u32[]{:S(2)}, u32[]{:S(2)}) %collective-permute-start.119) | collective-permute-done | bytes 196640 | tf_op jit(solution)/shard_map/ppermute | solution.py:173
  474.6 7.0 %shampoo_proj.1 = (f32[3,2,4,128,128]{4,3,2,1,0:T(8,128)}, f32[3,2,4,128,128]{4,3,2,1,0:T(8,128)}, f32[3,2,4,128,128]{4,3,2,1,0:T(8,128)}) custom-call(f32[3,2,4,128,128]{4,3,2,1,0:T(8,128)} %convert.20.g, f32[3,2,4,128,128]{4,3,2,1,0:T(8,128)} %left.7, f32[3,2,4,128,128]{4,3,2,1,0:T(8,128)} %right.7, f32[3,2,4,128,128]{4,3,2,1,0:T(8,128)} %lroot.7, ...), custom_call_target="tpu_custom_call" | custom-call | flops 25165824 | bytes 884736 | tf_op jit(solution)/shard_map/shampoo_proj/pallas_call | solution.py:1321
  (496 shorter events, 147.5 us)
Async XLA Ops:
  8.0 185.9 %all-gather.3.cloned.1.call-start = ((), (), s32[]{:S(2)}) async-start(), calls=%async_computation.4 | async-start | bytes 7520256 | tf_op jit(solution)/shard_map/all_gather | solution.py:1574
  9.1 9.9 %collective-permute-start.1 = (bf16[64,512]{1,0:T(8,128)(2,1)S(1)}, bf16[64,512]{1,0:T(8,128)(2,1)S(1)}, u32[]{:S(2)}, u32[]{:S(2)}) collective-permute-start(bf16[64,512]{1,0:T(8,128)(2,1)S(1)} %bitcast.360), channel_id=1, source_target_pairs={{0,2},{2,0},{4,6},{6,4},{1,3},{3,1},{5,7},{7,5},{8,10},{10,8},{12,... | collective-permute-start | bytes 196616 | tf_op jit(solution)/shard_map/ppermute | solution.py:83
  15.1 10.6 %collective-permute-start = (bf16[1,9,64,128]{3,2,1,0:T(8,128)(2,1)S(1)}, bf16[1,9,64,128]{3,2,1,0:T(8,128)(2,1)S(1)}, u32[]{:S(2)}, u32[]{:S(2)}) collective-permute-start(bf16[1,9,64,128]{3,2,1,0:T(8,128)(2,1)S(1)} %get-tuple-element.264), channel_id=1, source_target_pairs={{0,4},{2,6},{4,0},{6,2},{1,5},{3,7},{5,1},{7,3},{8,12},{10,14},{12... | collective-permute-start | bytes 442376 | tf_op jit(solution)/shard_map/ppermute | solution.py:54
  25.8 7.6 %collective-permute-start.5 = (bf16[2,9,64,128]{3,2,1,0:T(8,128)(2,1)S(1)}, bf16[2,9,64,128]{3,2,1,0:T(8,128)(2,1)}, u32[]{:S(2)}, u32[]{:S(2)}) collective-permute-start(bf16[2,9,64,128]{3,2,1,0:T(8,128)(2,1)S(1)} %pad_maximum_fusion.8.refs_0_), channel_id=1, source_target_pairs={{0,8},{8,0},{16,24},{24,16},{1,9},{9,1},{17,25},{25,17},{2,10},{10... | collective-permute-start | bytes 884744 | tf_op jit(solution)/shard_map/ppermute | solution.py:54
  27.4 7.2 %collective-permute-start.6 = (bf16[2,9,64,128]{3,2,1,0:T(8,128)(2,1)S(1)}, bf16[2,9,64,128]{3,2,1,0:T(8,128)(2,1)}, u32[]{:S(2)}, u32[]{:S(2)}) collective-permute-start(bf16[2,9,64,128]{3,2,1,0:T(8,128)(2,1)S(1)} %pad_maximum_fusion.8.refs_0_), channel_id=1, source_target_pairs={{0,16},{8,24},{16,0},{24,8},{1,17},{9,25},{17,1},{25,9},{2,18},{10... | collective-permute-start | bytes 884744 | tf_op jit(solution)/shard_map/ppermute | solution.py:54
  30.0 10.0 %collective-permute-start.10 = (bf16[18,4,512]{2,1,0:T(4,128)(2,1)S(1)}, bf16[18,4,512]{2,1,0:T(4,128)(2,1)}, u32[]{:S(2)}, u32[]{:S(2)}) collective-permute-start(bf16[18,4,512]{2,1,0:T(4,128)(2,1)S(1)} %maximum_select_fusion), channel_id=1, source_target_pairs={{0,1},{1,0},{2,3},{3,2},{4,5},{5,4},{6,7},{7,6},{8,9},{9,8},{10,11... | collective-permute-start | bytes 221192 | tf_op jit(solution)/shard_map/ppermute | solution.py:54
  31.2 17.6 %collective-permute-start.12 = (bf16[2,9,64,128]{3,2,1,0:T(8,128)(2,1)S(1)}, bf16[2,9,64,128]{3,2,1,0:T(8,128)(2,1)S(1)}, u32[]{:S(2)}, u32[]{:S(2)}) collective-permute-start(bf16[2,9,64,128]{3,2,1,0:T(8,128)(2,1)S(1)} %pad_maximum_fusion.8.refs_0_), channel_id=1, source_target_pairs={{0,1},{1,0},{2,3},{3,2},{4,5},{5,4},{6,7},{7,6},{8,9},{9,8},{10,11... | collective-permute-start | bytes 884744 | tf_op jit(solution)/shard_map/ppermute | solution.py:54
  34.6 12.1 %collective-permute-start.7 = (bf16[2,9,64,128]{3,2,1,0:T(8,128)(2,1)S(1)}, bf16[2,9,64,128]{3,2,1,0:T(8,128)(2,1)S(1)}, u32[]{:S(2)}, u32[]{:S(2)}) collective-permute-start(bf16[2,9,64,128]{3,2,1,0:T(8,128)(2,1)S(1)} %collective-permute-done.3.refs_1_), channel_id=1, source_target_pairs={{0,16},{8,24},{16,0},{24,8},{1,17},{9,25},{17,1},{25,9},{2,18},{10... | collective-permute-start | bytes 884744 | tf_op jit(solution)/shard_map/ppermute | solution.py:54
  36.2 10.6 %collective-permute-start.8 = (bf16[2,9,64,128]{3,2,1,0:T(8,128)(2,1)S(1)}, bf16[2,9,64,128]{3,2,1,0:T(8,128)(2,1)S(1)}, u32[]{:S(2)}, u32[]{:S(2)}) collective-permute-start(bf16[2,9,64,128]{3,2,1,0:T(8,128)(2,1)S(1)} %collective-permute-done.3.refs_1_), channel_id=1, source_target_pairs={{0,8},{8,0},{16,24},{24,16},{1,9},{9,1},{17,25},{25,17},{2,10},{10... | collective-permute-start | bytes 884744 | tf_op jit(solution)/shard_map/ppermute | solution.py:54
  36.7 10.1 %collective-permute-start.4 = (bf16[1,9,64,128]{3,2,1,0:T(8,128)(2,1)}, bf16[1,9,64,128]{3,2,1,0:T(8,128)(2,1)S(1)}, u32[]{:S(2)}, u32[]{:S(2)}) collective-permute-start(bf16[1,9,64,128]{3,2,1,0:T(8,128)(2,1)} %get-tuple-element.133), channel_id=1, source_target_pairs={{0,4},{2,6},{4,0},{6,2},{1,5},{3,7},{5,1},{7,3},{8,12},{10,14},{12... | collective-permute-start | bytes 442376 | tf_op jit(solution)/shard_map/ppermute | solution.py:54
  54.4 16.7 %collective-permute-start.20 = (bf16[2,9,64,128]{3,2,1,0:T(8,128)(2,1)S(1)}, bf16[2,9,64,128]{3,2,1,0:T(8,128)(2,1)}, u32[]{:S(2)}, u32[]{:S(2)}) collective-permute-start(bf16[2,9,64,128]{3,2,1,0:T(8,128)(2,1)S(1)} %pad_maximum_fusion.9.refs_0_), channel_id=1, source_target_pairs={{0,2},{2,0},{4,6},{6,4},{1,3},{3,1},{5,7},{7,5},{8,10},{10,8},{12,... | collective-permute-start | bytes 884744 | tf_op jit(solution)/shard_map/ppermute | solution.py:54
  54.8 16.3 %collective-permute-start.21 = (bf16[2,9,64,128]{3,2,1,0:T(8,128)(2,1)S(1)}, bf16[2,9,64,128]{3,2,1,0:T(8,128)(2,1)}, u32[]{:S(2)}, u32[]{:S(2)}) collective-permute-start(bf16[2,9,64,128]{3,2,1,0:T(8,128)(2,1)S(1)} %pad_maximum_fusion.9.refs_0_), channel_id=1, source_target_pairs={{0,8},{8,0},{16,24},{24,16},{1,9},{9,1},{17,25},{25,17},{2,10},{10... | collective-permute-start | bytes 884744 | tf_op jit(solution)/shard_map/ppermute | solution.py:54
  56.3 14.8 %collective-permute-start.22 = (bf16[2,9,64,128]{3,2,1,0:T(8,128)(2,1)S(1)}, bf16[2,9,64,128]{3,2,1,0:T(8,128)(2,1)}, u32[]{:S(2)}, u32[]{:S(2)}) collective-permute-start(bf16[2,9,64,128]{3,2,1,0:T(8,128)(2,1)S(1)} %pad_maximum_fusion.9.refs_0_), channel_id=1, source_target_pairs={{0,16},{8,24},{16,0},{24,8},{1,17},{9,25},{17,1},{25,9},{2,18},{10... | collective-permute-start | bytes 884744 | tf_op jit(solution)/shard_map/ppermute | solution.py:54
  71.1 166.1 %reduce-scatter.3.cloned.1.call-start = ((), (), s32[]{:S(2)}) async-start(), calls=%async_computation.2 | async-start | bytes 21233664 | tf_op jit(solution)/shard_map/reduce_scatter | solution.py:1623
  72.1 19.1 %collective-permute-start.30 = (bf16[64,512]{1,0:T(8,128)(2,1)S(1)}, bf16[64,512]{1,0:T(8,128)(2,1)S(1)}, u32[]{:S(2)}, u32[]{:S(2)}) collective-permute-start(bf16[64,512]{1,0:T(8,128)(2,1)S(1)} %get-tuple-element.296), channel_id=1, source_target_pairs={{0,2},{2,0},{4,6},{6,4},{1,3},{3,1},{5,7},{7,5},{8,10},{10,8},{12,... | collective-permute-start | bytes 196616 | tf_op jit(solution)/shard_map/ppermute | solution.py:83
  73.8 18.7 %collective-permute-start.31 = (bf16[64,512]{1,0:T(8,128)(2,1)S(1)}, bf16[64,512]{1,0:T(8,128)(2,1)S(1)}, u32[]{:S(2)}, u32[]{:S(2)}) collective-permute-start(bf16[64,512]{1,0:T(8,128)(2,1)S(1)} %get-tuple-element.297), channel_id=1, source_target_pairs={{0,0},{2,4},{4,2},{6,6},{1,1},{3,5},{5,3},{7,7},{8,8},{10,12},{12,... | collective-permute-start | bytes 196616 | tf_op jit(solution)/shard_map/ppermute | solution.py:83
  86.9 16.6 %collective-permute-start.59 = (bf16[3,1,4,8,512]{4,3,2,1,0:T(8,128)(2,1)}, bf16[3,1,4,8,512]{4,3,2,1,0:T(8,128)(2,1)}, u32[]{:S(2)}, u32[]{:S(2)}) collective-permute-start(bf16[3,1,4,8,512]{4,3,2,1,0:T(8,128)(2,1)} %get-tuple-element.260), channel_id=1, source_target_pairs={{0,2},{2,0},{4,6},{6,4},{1,3},{3,1},{5,7},{7,5},{8,10},{10,8},{12,... | collective-permute-start | bytes 294920 | tf_op jit(solution)/shard_map/ppermute | solution.py:83
  87.6 15.9 %collective-permute-start.60 = (bf16[3,1,4,8,512]{4,3,2,1,0:T(8,128)(2,1)}, bf16[3,1,4,8,512]{4,3,2,1,0:T(8,128)(2,1)}, u32[]{:S(2)}, u32[]{:S(2)}) collective-permute-start(bf16[3,1,4,8,512]{4,3,2,1,0:T(8,128)(2,1)} %get-tuple-element.261), channel_id=1, source_target_pairs={{0,0},{2,4},{4,2},{6,6},{1,1},{3,5},{5,3},{7,7},{8,8},{10,12},{12,... | collective-permute-start | bytes 294920 | tf_op jit(solution)/shard_map/ppermute | solution.py:83
  98.1 14.5 %collective-permute-start.35 = (bf16[2,9,64,128]{3,2,1,0:T(8,128)(2,1)}, bf16[2,9,64,128]{3,2,1,0:T(8,128)(2,1)S(1)}, u32[]{:S(2)}, u32[]{:S(2)}) collective-permute-start(bf16[2,9,64,128]{3,2,1,0:T(8,128)(2,1)} %collective-permute-done.21.refs_2_), channel_id=1, source_target_pairs={{0,16},{8,24},{16,0},{24,8},{1,17},{9,25},{17,1},{25,9},{2,18},{10... | collective-permute-start | bytes 884744 | tf_op jit(solution)/shard_map/ppermute | solution.py:54
  100.1 13.0 %collective-permute-start.36 = (bf16[2,9,64,128]{3,2,1,0:T(8,128)(2,1)S(1)}, bf16[2,9,64,128]{3,2,1,0:T(8,128)(2,1)S(1)}, u32[]{:S(2)}, u32[]{:S(2)}) collective-permute-start(bf16[2,9,64,128]{3,2,1,0:T(8,128)(2,1)S(1)} %collective-permute-done.34.refs_5_), channel_id=1, source_target_pairs={{0,8},{8,0},{16,24},{24,16},{1,9},{9,1},{17,25},{25,17},{2,10},{10... | collective-permute-start | bytes 884744 | tf_op jit(solution)/shard_map/ppermute | solution.py:54
  119.2 11.5 %collective-permute-start.41 = (bf16[2,9,64,128]{3,2,1,0:T(8,128)(2,1)S(1)}, bf16[2,9,64,128]{3,2,1,0:T(8,128)(2,1)S(1)}, u32[]{:S(2)}, u32[]{:S(2)}) collective-permute-start(bf16[2,9,64,128]{3,2,1,0:T(8,128)(2,1)S(1)} %pad_maximum_fusion.9.refs_0_), channel_id=1, source_target_pairs={{0,1},{1,0},{2,3},{3,2},{4,5},{5,4},{6,7},{7,6},{8,9},{9,8},{10,11... | collective-permute-start | bytes 884744 | tf_op jit(solution)/shard_map/ppermute | solution.py:54
  119.7 11.6 %collective-permute-start.42 = (bf16[2,9,64,128]{3,2,1,0:T(8,128)(2,1)}, bf16[2,9,64,128]{3,2,1,0:T(8,128)(2,1)S(1)}, u32[]{:S(2)}, u32[]{:S(2)}) collective-permute-start(bf16[2,9,64,128]{3,2,1,0:T(8,128)(2,1)} %collective-permute-done.20.refs_1_), channel_id=1, source_target_pairs={{0,1},{1,0},{2,3},{3,2},{4,5},{5,4},{6,7},{7,6},{8,9},{9,8},{10,11... | collective-permute-start | bytes 884744 | tf_op jit(solution)/shard_map/ppermute | solution.py:54
  120.5 10.9 %collective-permute-start.43 = (bf16[2,9,64,128]{3,2,1,0:T(8,128)(2,1)}, bf16[2,9,64,128]{3,2,1,0:T(8,128)(2,1)S(1)}, u32[]{:S(2)}, u32[]{:S(2)}) collective-permute-start(bf16[2,9,64,128]{3,2,1,0:T(8,128)(2,1)} %collective-permute-done.21.refs_2_), channel_id=1, source_target_pairs={{0,1},{1,0},{2,3},{3,2},{4,5},{5,4},{6,7},{7,6},{8,9},{9,8},{10,11... | collective-permute-start | bytes 884744 | tf_op jit(solution)/shard_map/ppermute | solution.py:54
  154.6 7.9 %collective-permute-start.56 = (bf16[64,512]{1,0:T(8,128)(2,1)S(1)}, bf16[64,512]{1,0:T(8,128)(2,1)S(1)}, u32[]{:S(2)}, u32[]{:S(2)}) collective-permute-start(bf16[64,512]{1,0:T(8,128)(2,1)S(1)} %get-tuple-element.290), channel_id=1, source_target_pairs={{0,2},{2,0},{4,6},{6,4},{1,3},{3,1},{5,7},{7,5},{8,10},{10,8},{12,... | collective-permute-start | bytes 196616 | tf_op jit(solution)/shard_map/ppermute | solution.py:83
  166.7 7.3 %collective-permute-start.63 = (f32[8,512]{1,0:T(8,128)S(1)}, f32[8,512]{1,0:T(8,128)S(1)}, u32[]{:S(2)}, u32[]{:S(2)}) collective-permute-start(f32[8,512]{1,0:T(8,128)S(1)} %add_add_fusion.3), channel_id=1, source_target_pairs={{0,4},{2,6},{4,0},{6,2},{1,5},{3,7},{5,1},{7,3},{8,12},{10,14},{12... | collective-permute-start | bytes 49160 | tf_op jit(solution)/shard_map/ppermute | solution.py:54
  193.6 216.3 %reduce-scatter.5.cloned.1.call-start = ((), (), s32[]{:S(2)}) async-start(), calls=%async_computation.3 | async-start | bytes 7520256 | tf_op jit(solution)/shard_map/reduce_scatter | solution.py:1635
  193.9 11.6 %collective-permute-start.65 = (bf16[16,27,64,128]{3,2,1,0:T(8,128)(2,1)}, bf16[16,27,64,128]{3,2,1,0:T(8,128)(2,1)S(1)}, u32[]{:S(2)}, u32[]{:S(2)}) collective-permute-start(bf16[16,27,64,128]{3,2,1,0:T(8,128)(2,1)} %bitcast.320), channel_id=1, source_target_pairs={{0,1},{1,0},{2,3},{3,2},{4,5},{5,4},{6,7},{7,6},{8,9},{9,8},{10,11... | collective-permute-start | bytes 21233672 | tf_op jit(solution)/shard_map/ppermute | solution.py:54
  238.2 18.9 %collective-permute-start.70 = (bf16[64,512]{1,0:T(8,128)(2,1)S(1)}, bf16[64,512]{1,0:T(8,128)(2,1)S(1)}, u32[]{:S(2)}, u32[]{:S(2)}) collective-permute-start(bf16[64,512]{1,0:T(8,128)(2,1)S(1)} %get-tuple-element.284), channel_id=1, source_target_pairs={{0,2},{2,0},{4,6},{6,4},{1,3},{3,1},{5,7},{7,5},{8,10},{10,8},{12,... | collective-permute-start | bytes 196616 | tf_op jit(solution)/shard_map/ppermute | solution.py:83
  239.3 17.8 %collective-permute-start.71 = (bf16[64,512]{1,0:T(8,128)(2,1)S(1)}, bf16[64,512]{1,0:T(8,128)(2,1)S(1)}, u32[]{:S(2)}, u32[]{:S(2)}) collective-permute-start(bf16[64,512]{1,0:T(8,128)(2,1)S(1)} %get-tuple-element.285), channel_id=1, source_target_pairs={{0,0},{2,4},{4,2},{6,6},{1,1},{3,5},{5,3},{7,7},{8,8},{10,12},{12,... | collective-permute-start | bytes 196616 | tf_op jit(solution)/shard_map/ppermute | solution.py:83
  240.0 17.0 %collective-permute-start.69 = (f32[14,512]{1,0:T(8,128)S(1)}, f32[14,512]{1,0:T(8,128)S(1)}, u32[]{:S(2)}, u32[]{:S(2)}) collective-permute-start(f32[14,512]{1,0:T(8,128)S(1)} %add.324), channel_id=1, source_target_pairs={{0,6},{2,4},{4,2},{6,0},{1,7},{3,5},{5,3},{7,1},{8,14},{10,12},{12... | collective-permute-start | bytes 86024 | tf_op jit(solution)/shard_map/ppermute | solution.py:54
  242.0 15.0 %collective-permute-start.68 = (f32[14,512]{1,0:T(8,128)S(1)}, f32[14,512]{1,0:T(8,128)S(1)}, u32[]{:S(2)}, u32[]{:S(2)}) collective-permute-start(f32[14,512]{1,0:T(8,128)S(1)} %add.324), channel_id=1, source_target_pairs={{0,4},{2,6},{4,0},{6,2},{1,5},{3,7},{5,1},{7,3},{8,12},{10,14},{12... | collective-permute-start | bytes 86024 | tf_op jit(solution)/shard_map/ppermute | solution.py:54
  245.5 11.5 %collective-permute-start.67 = (f32[14,512]{1,0:T(8,128)S(1)}, f32[14,512]{1,0:T(8,128)S(1)}, u32[]{:S(2)}, u32[]{:S(2)}) collective-permute-start(f32[14,512]{1,0:T(8,128)S(1)} %add.324), channel_id=1, source_target_pairs={{0,2},{2,0},{4,6},{6,4},{1,3},{3,1},{5,7},{7,5},{8,10},{10,8},{12,... | collective-permute-start | bytes 86024 | tf_op jit(solution)/shard_map/ppermute | solution.py:54
  278.2 10.4 %collective-permute-start.79 = (f32[2,384]{1,0:T(2,128)S(1)}, f32[2,384]{1,0:T(2,128)S(1)}, u32[]{:S(2)}, u32[]{:S(2)}) collective-permute-start(f32[2,384]{1,0:T(2,128)S(1)} %add.331), channel_id=1, source_target_pairs={{0,6},{2,4},{4,2},{6,0},{1,7},{3,5},{5,3},{7,1},{8,14},{10,12},{12... | collective-permute-start | bytes 9224 | tf_op jit(solution)/shard_map/ppermute | solution.py:54
  280.3 8.3 %collective-permute-start.78 = (f32[2,384]{1,0:T(2,128)S(1)}, f32[2,384]{1,0:T(2,128)S(1)}, u32[]{:S(2)}, u32[]{:S(2)}) collective-permute-start(f32[2,384]{1,0:T(2,128)S(1)} %add.331), channel_id=1, source_target_pairs={{0,4},{2,6},{4,0},{6,2},{1,5},{3,7},{5,1},{7,3},{8,12},{10,14},{12... | collective-permute-start | bytes 9224 | tf_op jit(solution)/shard_map/ppermute | solution.py:54
  288.6 15.0 %collective-permute-start.82 = (f32[2,384]{1,0:T(2,128)S(1)}, f32[2,384]{1,0:T(2,128)S(1)}, u32[]{:S(2)}, u32[]{:S(2)}) collective-permute-start(f32[2,384]{1,0:T(2,128)S(1)} %add_add_fusion.9), channel_id=1, source_target_pairs={{0,24},{8,16},{16,8},{24,0},{1,25},{9,17},{17,9},{25,1},{2,26},{10... | collective-permute-start | bytes 9224 | tf_op jit(solution)/shard_map/ppermute | solution.py:54
  290.5 13.2 %collective-permute-start.81 = (f32[2,384]{1,0:T(2,128)S(1)}, f32[2,384]{1,0:T(2,128)S(1)}, u32[]{:S(2)}, u32[]{:S(2)}) collective-permute-start(f32[2,384]{1,0:T(2,128)S(1)} %add_add_fusion.9), channel_id=1, source_target_pairs={{0,16},{8,24},{16,0},{24,8},{1,17},{9,25},{17,1},{25,9},{2,18},{10... | collective-permute-start | bytes 9224 | tf_op jit(solution)/shard_map/ppermute | solution.py:54
  291.2 12.4 %collective-permute-start.80 = (f32[2,384]{1,0:T(2,128)S(1)}, f32[2,384]{1,0:T(2,128)S(1)}, u32[]{:S(2)}, u32[]{:S(2)}) collective-permute-start(f32[2,384]{1,0:T(2,128)S(1)} %add_add_fusion.9), channel_id=1, source_target_pairs={{0,8},{8,0},{16,24},{24,16},{1,9},{9,1},{17,25},{25,17},{2,10},{10... | collective-permute-start | bytes 9224 | tf_op jit(solution)/shard_map/ppermute | solution.py:54
  315.3 19.9 %collective-permute-start.87 = (bf16[64,512]{1,0:T(8,128)(2,1)S(1)}, bf16[64,512]{1,0:T(8,128)(2,1)S(1)}, u32[]{:S(2)}, u32[]{:S(2)}) collective-permute-start(bf16[64,512]{1,0:T(8,128)(2,1)S(1)} %get-tuple-element.278), channel_id=1, source_target_pairs={{0,2},{2,0},{4,6},{6,4},{1,3},{3,1},{5,7},{7,5},{8,10},{10,8},{12,... | collective-permute-start | bytes 196616 | tf_op jit(solution)/shard_map/ppermute | solution.py:83
  316.4 18.7 %collective-permute-start.88 = (bf16[64,512]{1,0:T(8,128)(2,1)S(1)}, bf16[64,512]{1,0:T(8,128)(2,1)S(1)}, u32[]{:S(2)}, u32[]{:S(2)}) collective-permute-start(bf16[64,512]{1,0:T(8,128)(2,1)S(1)} %get-tuple-element.279), channel_id=1, source_target_pairs={{0,0},{2,4},{4,2},{6,6},{1,1},{3,5},{5,3},{7,7},{8,8},{10,12},{12,... | collective-permute-start | bytes 196616 | tf_op jit(solution)/shard_map/ppermute | solution.py:83
  319.3 15.9 %collective-permute-start.86 = (f32[2,512]{1,0:T(2,128)S(1)}, f32[2,512]{1,0:T(2,128)S(1)}, u32[]{:S(2)}, u32[]{:S(2)}) collective-permute-start(f32[2,512]{1,0:T(2,128)S(1)} %add.338), channel_id=1, source_target_pairs={{0,6},{2,4},{4,2},{6,0},{1,7},{3,5},{5,3},{7,1},{8,14},{10,12},{12... | collective-permute-start | bytes 12296 | tf_op jit(solution)/shard_map/ppermute | solution.py:54
  321.2 14.0 %collective-permute-start.85 = (f32[2,512]{1,0:T(2,128)S(1)}, f32[2,512]{1,0:T(2,128)S(1)}, u32[]{:S(2)}, u32[]{:S(2)}) collective-permute-start(f32[2,512]{1,0:T(2,128)S(1)} %add.338), channel_id=1, source_target_pairs={{0,4},{2,6},{4,0},{6,2},{1,5},{3,7},{5,1},{7,3},{8,12},{10,14},{12... | collective-permute-start | bytes 12296 | tf_op jit(solution)/shard_map/ppermute | solution.py:54
  324.0 11.1 %collective-permute-start.84 = (f32[2,512]{1,0:T(2,128)S(1)}, f32[2,512]{1,0:T(2,128)S(1)}, u32[]{:S(2)}, u32[]{:S(2)}) collective-permute-start(f32[2,512]{1,0:T(2,128)S(1)} %add.338), channel_id=1, source_target_pairs={{0,2},{2,0},{4,6},{6,4},{1,3},{3,1},{5,7},{7,5},{8,10},{10,8},{12,... | collective-permute-start | bytes 12296 | tf_op jit(solution)/shard_map/ppermute | solution.py:54
  346.1 10.9 %collective-permute-start.95 = (bf16[2,672,128]{2,1,0:T(8,128)(2,1)S(1)}, bf16[2,672,128]{2,1,0:T(8,128)(2,1)S(1)}, u32[]{:S(2)}, u32[]{:S(2)}) collective-permute-start(bf16[2,672,128]{2,1,0:T(8,128)(2,1)S(1)} %get-tuple-element.266), channel_id=1, source_target_pairs={{0,8},{8,0},{16,24},{24,16},{1,9},{9,1},{17,25},{25,17},{2,10},{10... | collective-permute-start | bytes 1032200 | tf_op jit(solution)/shard_map/ppermute | solution.py:54
  347.3 16.8 %collective-permute-start.94 = (bf16[2,672,128]{2,1,0:T(8,128)(2,1)S(1)}, bf16[2,672,128]{2,1,0:T(8,128)(2,1)S(1)}, u32[]{:S(2)}, u32[]{:S(2)}) collective-permute-start(bf16[2,672,128]{2,1,0:T(8,128)(2,1)S(1)} %get-tuple-element.267), channel_id=1, source_target_pairs={{0,16},{8,24},{16,0},{24,8},{1,17},{9,25},{17,1},{25,9},{2,18},{10... | collective-permute-start | bytes 1032200 | tf_op jit(solution)/shard_map/ppermute | solution.py:54
  354.2 22.7 %collective-permute-start.97 = (bf16[2,672,128]{2,1,0:T(8,128)(2,1)}, bf16[2,672,128]{2,1,0:T(8,128)(2,1)S(1)}, u32[]{:S(2)}, u32[]{:S(2)}) collective-permute-start(bf16[2,672,128]{2,1,0:T(8,128)(2,1)} %get-tuple-element.252), channel_id=1, source_target_pairs={{0,16},{8,24},{16,0},{24,8},{1,17},{9,25},{17,1},{25,9},{2,18},{10... | collective-permute-start | bytes 1032200 | tf_op jit(solution)/shard_map/ppermute | solution.py:54
  364.4 12.5 %collective-permute-start.96 = (bf16[2,672,128]{2,1,0:T(8,128)(2,1)S(1)}, bf16[2,672,128]{2,1,0:T(8,128)(2,1)S(1)}, u32[]{:S(2)}, u32[]{:S(2)}) collective-permute-start(bf16[2,672,128]{2,1,0:T(8,128)(2,1)S(1)} %get-tuple-element.250), channel_id=1, source_target_pairs={{0,8},{8,0},{16,24},{24,16},{1,9},{9,1},{17,25},{25,17},{2,10},{10... | collective-permute-start | bytes 1032200 | tf_op jit(solution)/shard_map/ppermute | solution.py:54
  365.9 14.2 %collective-permute-start.98 = (bf16[2,672,128]{2,1,0:T(8,128)(2,1)S(1)}, bf16[2,672,128]{2,1,0:T(8,128)(2,1)S(1)}, u32[]{:S(2)}, u32[]{:S(2)}) collective-permute-start(bf16[2,672,128]{2,1,0:T(8,128)(2,1)S(1)} %get-tuple-element.210), channel_id=1, source_target_pairs={{0,8},{8,0},{16,24},{24,16},{1,9},{9,1},{17,25},{25,17},{2,10},{10... | collective-permute-start | bytes 1032200 | tf_op jit(solution)/shard_map/ppermute | solution.py:54
  366.5 13.6 %collective-permute-start.99 = (bf16[2,672,128]{2,1,0:T(8,128)(2,1)S(1)}, bf16[2,672,128]{2,1,0:T(8,128)(2,1)S(1)}, u32[]{:S(2)}, u32[]{:S(2)}) collective-permute-start(bf16[2,672,128]{2,1,0:T(8,128)(2,1)S(1)} %get-tuple-element.211), channel_id=1, source_target_pairs={{0,16},{8,24},{16,0},{24,8},{1,17},{9,25},{17,1},{25,9},{2,18},{10... | collective-permute-start | bytes 1032200 | tf_op jit(solution)/shard_map/ppermute | solution.py:54
  386.7 15.1 %collective-permute-start.103 = (bf16[2,672,128]{2,1,0:T(8,128)(2,1)S(1)}, bf16[2,672,128]{2,1,0:T(8,128)(2,1)}, u32[]{:S(2)}, u32[]{:S(2)}) collective-permute-start(bf16[2,672,128]{2,1,0:T(8,128)(2,1)S(1)} %fusion.6), channel_id=1, source_target_pairs={{0,2},{2,0},{4,6},{6,4},{1,3},{3,1},{5,7},{7,5},{8,10},{10,8},{12,... | collective-permute-start | bytes 1032200 | tf_op jit(solution)/shard_map/ppermute | solution.py:54
  388.5 13.3 %collective-permute-start.101 = (bf16[2,576,128]{2,1,0:T(8,128)(2,1)S(1)}, bf16[2,576,128]{2,1,0:T(8,128)(2,1)S(1)}, u32[]{:S(2)}, u32[]{:S(2)}) collective-permute-start(bf16[2,576,128]{2,1,0:T(8,128)(2,1)S(1)} %get-tuple-element.269), channel_id=1, source_target_pairs={{0,8},{8,0},{16,24},{24,16},{1,9},{9,1},{17,25},{25,17},{2,10},{10... | collective-permute-start | bytes 884744 | tf_op jit(solution)/shard_map/ppermute | solution.py:54
  390.1 11.7 %collective-permute-start.102 = (bf16[2,576,128]{2,1,0:T(8,128)(2,1)S(1)}, bf16[2,576,128]{2,1,0:T(8,128)(2,1)S(1)}, u32[]{:S(2)}, u32[]{:S(2)}) collective-permute-start(bf16[2,576,128]{2,1,0:T(8,128)(2,1)S(1)} %get-tuple-element.268), channel_id=1, source_target_pairs={{0,16},{8,24},{16,0},{24,8},{1,17},{9,25},{17,1},{25,9},{2,18},{10... | collective-permute-start | bytes 884744 | tf_op jit(solution)/shard_map/ppermute | solution.py:54
  404.3 21.0 %collective-permute-start.109 = (bf16[2,576,128]{2,1,0:T(8,128)(2,1)}, bf16[2,576,128]{2,1,0:T(8,128)(2,1)}, u32[]{:S(2)}, u32[]{:S(2)}) collective-permute-start(bf16[2,576,128]{2,1,0:T(8,128)(2,1)} %fusion.19), channel_id=1, source_target_pairs={{0,16},{8,24},{16,0},{24,8},{1,17},{9,25},{17,1},{25,9},{2,18},{10... | collective-permute-start | bytes 884744 | tf_op jit(solution)/shard_map/ppermute | solution.py:54
  407.6 17.8 %collective-permute-start.108 = (bf16[2,576,128]{2,1,0:T(8,128)(2,1)}, bf16[2,576,128]{2,1,0:T(8,128)(2,1)}, u32[]{:S(2)}, u32[]{:S(2)}) collective-permute-start(bf16[2,576,128]{2,1,0:T(8,128)(2,1)} %fusion.13), channel_id=1, source_target_pairs={{0,8},{8,0},{16,24},{24,16},{1,9},{9,1},{17,25},{25,17},{2,10},{10... | collective-permute-start | bytes 884744 | tf_op jit(solution)/shard_map/ppermute | solution.py:54
  411.2 14.1 %collective-permute-start.105 = (bf16[2,576,128]{2,1,0:T(8,128)(2,1)}, bf16[2,576,128]{2,1,0:T(8,128)(2,1)S(1)}, u32[]{:S(2)}, u32[]{:S(2)}) collective-permute-start(bf16[2,576,128]{2,1,0:T(8,128)(2,1)} %fusion.20), channel_id=1, source_target_pairs={{0,8},{8,0},{16,24},{24,16},{1,9},{9,1},{17,25},{25,17},{2,10},{10... | collective-permute-start | bytes 884744 | tf_op jit(solution)/shard_map/ppermute | solution.py:54
  412.8 12.5 %collective-permute-start.106 = (bf16[2,576,128]{2,1,0:T(8,128)(2,1)S(1)}, bf16[2,576,128]{2,1,0:T(8,128)(2,1)S(1)}, u32[]{:S(2)}, u32[]{:S(2)}) collective-permute-start(bf16[2,576,128]{2,1,0:T(8,128)(2,1)S(1)} %fusion.12), channel_id=1, source_target_pairs={{0,16},{8,24},{16,0},{24,8},{1,17},{9,25},{17,1},{25,9},{2,18},{10... | collective-permute-start | bytes 884744 | tf_op jit(solution)/shard_map/ppermute | solution.py:54
  414.5 10.7 %collective-permute-start.107 = (bf16[672,128]{1,0:T(8,128)(2,1)S(1)}, bf16[672,128]{1,0:T(8,128)(2,1)S(1)}, u32[]{:S(2)}, u32[]{:S(2)}) collective-permute-start(bf16[672,128]{1,0:T(8,128)(2,1)S(1)} %fusion.18), channel_id=1, source_target_pairs={{0,4},{2,6},{4,0},{6,2},{1,5},{3,7},{5,1},{7,3},{8,12},{10,14},{12... | collective-permute-start | bytes 516104 | tf_op jit(solution)/shard_map/ppermute | solution.py:54
  426.9 9.0 %collective-permute-start.111 = (bf16[2,576,128]{2,1,0:T(8,128)(2,1)S(1)}, bf16[2,576,128]{2,1,0:T(8,128)(2,1)S(1)}, u32[]{:S(2)}, u32[]{:S(2)}) collective-permute-start(bf16[2,576,128]{2,1,0:T(8,128)(2,1)S(1)} %fusion.11), channel_id=1, source_target_pairs={{0,2},{2,0},{4,6},{6,4},{1,3},{3,1},{5,7},{7,5},{8,10},{10,8},{12,... | collective-permute-start | bytes 884744 | tf_op jit(solution)/shard_map/ppermute | solution.py:54
  441.5 12.3 %collective-permute-start.116 = (bf16[576,128]{1,0:T(8,128)(2,1)S(1)}, bf16[576,128]{1,0:T(8,128)(2,1)S(1)}, u32[]{:S(2)}, u32[]{:S(2)}) collective-permute-start(bf16[576,128]{1,0:T(8,128)(2,1)S(1)} %fusion.23), channel_id=1, source_target_pairs={{0,4},{2,6},{4,0},{6,2},{1,5},{3,7},{5,1},{7,3},{8,12},{10,14},{12... | collective-permute-start | bytes 442376 | tf_op jit(solution)/shard_map/ppermute | solution.py:54
  441.5 12.1 %collective-permute-start.114 = (bf16[2,96,128]{2,1,0:T(8,128)(2,1)S(1)}, bf16[2,96,128]{2,1,0:T(8,128)(2,1)S(1)}, u32[]{:S(2)}, u32[]{:S(2)}) collective-permute-start(bf16[2,96,128]{2,1,0:T(8,128)(2,1)S(1)} %pad_maximum_fusion.15), channel_id=1, source_target_pairs={{0,4},{2,6},{4,0},{6,2},{1,5},{3,7},{5,1},{7,3},{8,12},{10,14},{12... | collective-permute-start | bytes 147464 | tf_op jit(solution)/shard_map/ppermute | solution.py:173
  444.5 9.2 %collective-permute-start.115 = (bf16[2,96,128]{2,1,0:T(8,128)(2,1)S(1)}, bf16[2,96,128]{2,1,0:T(8,128)(2,1)S(1)}, u32[]{:S(2)}, u32[]{:S(2)}) collective-permute-start(bf16[2,96,128]{2,1,0:T(8,128)(2,1)S(1)} %pad_maximum_fusion.15), channel_id=1, source_target_pairs={{0,2},{2,4},{4,6},{6,0},{1,3},{3,5},{5,7},{7,1},{8,10},{10,12},{12... | collective-permute-start | bytes 147464 | tf_op jit(solution)/shard_map/ppermute | solution.py:173
  455.0 8.7 %collective-permute-start.117 = (bf16[576,128]{1,0:T(8,128)(2,1)S(1)}, bf16[576,128]{1,0:T(8,128)(2,1)S(1)}, u32[]{:S(2)}, u32[]{:S(2)}) collective-permute-start(bf16[576,128]{1,0:T(8,128)(2,1)S(1)} %fusion.22.mine), channel_id=1, source_target_pairs={{0,1},{1,0},{2,3},{3,2},{4,5},{5,4},{6,7},{7,6},{8,9},{9,8},{10,11... | collective-permute-start | bytes 442376 | tf_op jit(solution)/shard_map/ppermute | solution.py:54
  455.1 12.9 %collective-permute-start.118 = (bf16[4,2,96,128]{3,2,1,0:T(8,128)(2,1)S(1)}, bf16[4,2,96,128]{3,2,1,0:T(8,128)(2,1)S(1)}, u32[]{:S(2)}, u32[]{:S(2)}) collective-permute-start(bf16[4,2,96,128]{3,2,1,0:T(8,128)(2,1)S(1)} %constant_dynamic-slice_fusion.1), channel_id=1, source_target_pairs={{0,24},{8,0},{16,8},{24,16},{1,25},{9,1},{17,9},{25,17},{2,26},{10... | collective-permute-start | bytes 589832 | tf_op jit(solution)/shard_map/ppermute | solution.py:173
  461.8 11.2 %collective-permute-start.119 = (bf16[4,2,96,128]{3,2,1,0:T(8,128)(2,1)S(1)}, bf16[4,2,96,128]{3,2,1,0:T(8,128)(2,1)S(1)}, u32[]{:S(2)}, u32[]{:S(2)}) collective-permute-start(bf16[4,2,96,128]{3,2,1,0:T(8,128)(2,1)S(1)} %constant_dynamic-slice_fusion.1), channel_id=1, source_target_pairs={{0,16},{8,24},{16,0},{24,8},{1,17},{9,25},{17,1},{25,9},{2,18},{10... | collective-permute-start | bytes 589832 | tf_op jit(solution)/shard_map/ppermute | solution.py:173
  462.4 10.7 %collective-permute-start.120 = (bf16[4,2,96,128]{3,2,1,0:T(8,128)(2,1)S(1)}, bf16[4,2,96,128]{3,2,1,0:T(8,128)(2,1)S(1)}, u32[]{:S(2)}, u32[]{:S(2)}) collective-permute-start(bf16[4,2,96,128]{3,2,1,0:T(8,128)(2,1)S(1)} %constant_dynamic-slice_fusion.1), channel_id=1, source_target_pairs={{0,8},{8,16},{16,24},{24,0},{1,9},{9,17},{17,25},{25,1},{2,10},{10... | collective-permute-start | bytes 589832 | tf_op jit(solution)/shard_map/ppermute | solution.py:173
  (117 other events, 817.8 us)
Sparse Core Ops, SparseCore 0:
  71.2 105.9 all-gather.2
  237.4 160.0 reduce-scatter.4
Sparse Core Ops, SparseCore 1:
  193.7 28.3 reduce-scatter.2

commit v3 on v2

--- a/solution.py
+++ b/solution.py
@@ -169,24 +169,31 @@
 
 def ring_gather(value, axis):
     count = lax.axis_size(axis)
-    parts = [value] + [
-        lax.ppermute(value, axis, [(i, (i + step) % count) for i in range(count)])
-        for step in range(1, count)
-    ]
-    ring = jnp.stack(parts[::-1] + parts[:0:-1])
-    start = count - 1 - lax.axis_index(axis)
-    return lax.dynamic_slice_in_dim(ring, start, count, axis=0)
-
-
-def gather_proj_line(own):
+    place = lax.axis_index(axis)
+    value = value[None]
+    if count == 4:
+        value = jnp.concatenate([value] + [swap(value, axis, step) for step in (1, 2, 3)], axis=0)
+        for step in (1, 2):
+            parts = value.reshape((2, 2) + value.shape[1:])
+            along = 1 if step == 1 else 0
+            turned = jnp.flip(parts, along)
+            value = jnp.where((place // step) % 2 == 0, parts, turned).reshape(value.shape)
+        return value
+    step = 1
+    while step < count:
+        came = swap(value, axis, step)
+        first = (place // step) % 2 == 0
+        value = jnp.concatenate(
+            [jnp.where(first, value, came), jnp.where(first, came, value)], axis=0
+        )
+        step *= 2
+    return value
+
+
+def gather_proj_core(own):
     got = swap(own, "wa", 1)
     even = lax.axis_index("wa") % 2 == 0
-    value = jnp.stack([jnp.where(even, own, got), jnp.where(even, got, own)])
-    return ring_gather(value, "ha")
-
-
-def gather_proj(line):
-    return ring_gather(line, "img").reshape(TASKS, 2, NB, BLK, BLK).astype(F32)
+    return jnp.stack([jnp.where(even, own, got), jnp.where(even, got, own)])
 
 
 def add_low(*parts):
@@ -321,43 +328,49 @@
     return s // 2 + 2 * (s % 2)
 
 
-def weight_copies_rel(idx, pieces, first, wv, sems):
-    copies = []
+WEIGHTS = (NB * NB, 9, 2, HB, BLK)
+
+
+def weight_copies_rel(idx, pieces, wv, sems):
+    rows = ([], [], [])
     count = len(pieces) // 2
     for half in range(2):
         parts = pieces[half * count : (half + 1) * count]
         h = lax.bitwise_xor(idx[2], half)
         for e in range(4):
-            i = lax.bitwise_xor(idx[0], e)
-            row0 = pl.multiple_of(i * BLK + h * HB, HB)
-            for s in range(4):
-                j = lax.bitwise_xor(idx[1], flip(s))
-                col0 = pl.multiple_of(j * BLK, BLK)
-                copies.append(
-                    pltpu.make_async_copy(
-                        parts[2 * e + s // 2].at[s % 2, pl.ds(first, 9)],
-                        wv.at[:, pl.ds(row0, HB), pl.ds(col0, BLK)],
-                        sems.at[len(copies)],
+            for k in range(2):
+                src = parts[2 * e + k]
+                for dy, copies in enumerate(rows):
+                    taps = pl.ds(3 * dy, 3)
+                    copies.append(
+                        pltpu.make_async_copy(
+                            src.at[:, taps],
+                            wv.at[pl.ds(NB * e + 2 * k, 2), taps, h],
+                            sems.at[dy, len(copies)],
+                        )
                     )
-                )
-    return copies
+    return rows
 
 
 def weight_copies_task(idx, pieces, first, wv, sems):
-    copies = []
-    for half in range(2):
-        h = lax.bitwise_xor(idx[2], half)
-        for i in range(NB):
-            row0 = pl.multiple_of(i * BLK + h * HB, HB)
-            for j in range(NB):
-                copies.append(
-                    pltpu.make_async_copy(
-                        pieces[half].at[i * NB + j, pl.ds(first, 9)],
-                        wv.at[:, pl.ds(row0, HB), j * BLK : (j + 1) * BLK],
-                        sems.at[len(copies)],
-                    )
-                )
-    return copies
+    return [
+        pltpu.make_async_copy(
+            pieces[half].at[:, pl.ds(first, 9)],
+            wv.at[:, :, lax.bitwise_xor(idx[2], half)],
+            sems.at[half],
+        )
+        for half in range(2)
+    ]
+
+
+def tap(wv, m, idx=None):
+    def block(i, j):
+        if idx is not None:
+            i, j = lax.bitwise_xor(idx[0], i), flip_place(idx[1], j)
+        return wv[NB * i + j, m].reshape(BLK, BLK)
+
+    rows = [jnp.concatenate([block(i, j) for j in range(NB)], axis=1) for i in range(NB)]
+    return jnp.concatenate(rows, axis=0)
 
 
 def put_edges(field, edge_rows, edge_cols, batch):
@@ -411,44 +424,75 @@
     )(idx, field, rows, cols)
 
 
-def conv_kernel(n_pieces, batch, transposed, want_sums, idx_ref, x_ref, *refs):
+def conv_kernel(n_pieces, batch, transposed, want_sums, idx_ref, x_hbm, *refs):
     pieces = refs[:n_pieces]
-    o_ref = refs[n_pieces]
+    o_hbm = refs[n_pieces]
     s_ref, er_ref, ec_ref = refs[n_pieces + 1 : n_pieces + 4] if want_sums else (None,) * 3
-    wv, sems = refs[-2:]
-    copies = weight_copies_rel(idx_ref, pieces, 0, wv, sems)
-    for copy in copies:
-        copy.start()
-    for copy in copies:
-        copy.wait()
+    wv, x_ref, acc_ref, o_ref, w_sems, x_sems, o_sems = refs[-7:]
     height, tall = x_ref.shape[1] - 2, x_ref.shape[2]
     step = height // 2
     rows = step * tall
-    if want_sums:
-        s_ref[...] = jnp.zeros(s_ref.shape, F32)
-
-    @pl.loop(0, 2)
-    def _(part):
-        acc = None
-        for dy in range(3):
+    cut = ((0, step + 2), (step + 2, step))
+    x_copies = [
+        pltpu.make_async_copy(
+            x_hbm.at[:, pl.ds(first, count)], x_ref.at[:, pl.ds(first, count)], x_sems.at[k]
+        )
+        for k, (first, count) in enumerate(cut)
+    ]
+    w_copies = weight_copies_rel(idx_ref, pieces, wv, w_sems)
+    order = (2, 1, 0) if transposed else (0, 1, 2)
+    x_copies[0].start()
+    for dy in order:
+        for copy in w_copies[dy]:
+            copy.start()
+    x_copies[1].start()
+
+    def part_of(part, waits):
+        for n, dy in enumerate(order):
+            if waits:
+                for copy in w_copies[dy]:
+                    copy.wait()
+                if n == 0:
+                    x_copies[0].wait()
+            acc = None
             for dx in range(3):
                 if transposed:
-                    view = x_ref[2 - dx, pl.ds(part * step + 2 - dy, step)]
+                    view = x_ref[2 - dx, part * step + 2 - dy : (part + 1) * step + 2 - dy]
                     dims = NT
                 else:
-                    view = x_ref[dx, pl.ds(part * step + dy, step)]
+                    view = x_ref[dx, part * step + dy : (part + 1) * step + dy]
                     dims = (((1,), (0,)), ((), ()))
                 piece = lax.dot_general(
-                    view.reshape(rows, C), wv[3 * dy + dx], dims, preferred_element_type=F32
+                    view.reshape(rows, C), tap(wv, 3 * dy + dx, idx_ref), dims, preferred_element_type=F32
                 )
                 acc = piece if acc is None else acc + piece
-        o_ref[pl.ds(part * step, step)] = acc.reshape(step, tall, C).astype(o_ref.dtype)
+            if n == 0:
+                acc_ref[...] = acc
+            elif n == 1:
+                acc_ref[...] += acc
+        total = acc_ref[...] + acc
+        o_ref[part * step : (part + 1) * step] = total.reshape(step, tall, C).astype(o_ref.dtype)
+        out = pltpu.make_async_copy(
+            o_ref.at[pl.ds(part * step, step)], o_hbm.at[pl.ds(part * step, step)], o_sems.at[part]
+        )
+        out.start()
         if want_sums:
-            s_ref[0:1] += jnp.sum(acc, axis=0, keepdims=True)
-            s_ref[1:2] += jnp.sum(acc * acc, axis=0, keepdims=True)
-
+            first = jnp.sum(total, axis=0, keepdims=True)
+            second = jnp.sum(total * total, axis=0, keepdims=True)
+            if part == 0:
+                s_ref[0:1], s_ref[1:2] = first, second
+            else:
+                s_ref[0:1] += first
+                s_ref[1:2] += second
+        return out
+
+    first = part_of(0, True)
+    x_copies[1].wait()
+    second = part_of(1, False)
     if want_sums:
         put_edges(o_ref, er_ref, ec_ref, batch)
+    first.wait()
+    second.wait()
 
 
 def conv(idx, x3, pieces, transposed, dtype, name, batch=0):
@@ -459,10 +503,18 @@
         out_shape += [sds((2, C), F32), sds((2, tall, C), BF), sds((height, 2 * batch, C), F32)]
     out = pl.pallas_call(
         functools.partial(conv_kernel, len(pieces), batch, transposed, want_sums),
-        in_specs=[SM, VM] + [ANY] * len(pieces),
-        out_specs=[VM] * len(out_shape),
+        in_specs=[SM, ANY] + [ANY] * len(pieces),
+        out_specs=[ANY] + [VM] * (len(out_shape) - 1),
         out_shape=out_shape,
-        scratch_shapes=[pltpu.VMEM((9, C, C), BF), pltpu.SemaphoreType.DMA((32,))],
+        scratch_shapes=[
+            pltpu.VMEM(WEIGHTS, BF),
+            pltpu.VMEM(x3.shape, BF),
+            pltpu.VMEM((height // 2 * tall, C), F32),
+            pltpu.VMEM((height, tall, C), dtype),
+            pltpu.SemaphoreType.DMA((3, 16)),
+            pltpu.SemaphoreType.DMA((2,)),
+            pltpu.SemaphoreType.DMA((2,)),
+        ],
         compiler_params=params(),
         cost_estimate=cost(2 * 9 * C * C * height * tall, 10e6),
         name=name,
@@ -520,7 +572,7 @@
 
 def mid(idx, st, gb, z, rows, cols, down, batch, count_all):
     height, tall, chans = z.shape
-    lanes = BLK
+    lanes = 2 * BLK
     r = height + 2
     wide = TASKS * CA
     return pl.pallas_call(
@@ -629,9 +681,9 @@
             taps = []
             for dx in range(3):
                 if k == 0:
-                    taps.append(add(wv[slot, 3 * a + dx], wv[slot, 3 * (a + 1) + dx]))
+                    taps.append(add(tap(wv.at[slot], 3 * a + dx), tap(wv.at[slot], 3 * (a + 1) + dx)))
                 else:
-                    taps.append(wv[slot, 3 * (2 if a == 0 else 0) + dx])
+                    taps.append(tap(wv.at[slot], 3 * (2 if a == 0 else 0) + dx))
             ws[a, k, 0, 0] = add(taps[0], taps[1])
             ws[a, k, 0, 1] = taps[2]
             ws[a, k, 1, 0] = add(taps[1], taps[2])
@@ -660,9 +712,9 @@
         out_specs=pl.BlockSpec((1, half_h, 2, 2, q, C), lambda t: (t, 0, 0, 0, 0, 0)),
         out_shape=sds((TASKS, half_h, 2, 2, q, C), BF),
         scratch_shapes=[
-            pltpu.VMEM((2, 9, C, C), BF),
+            pltpu.VMEM((2,) + WEIGHTS, BF),
             pltpu.VMEM((2, 2, 2, 2, C, C), BF),
-            pltpu.SemaphoreType.DMA((2, 32)),
+            pltpu.SemaphoreType.DMA((2, 2)),
         ],
         compiler_params=params(),
         cost_estimate=cost(TASKS * 2 * 16 * C * C * half_h * q, 24e6),
@@ -791,7 +843,7 @@
 
 
 def attend_back_kernel(
-    batch, count_all, st, gb, mst, mgb, z_ref, h_ref, up, da, cot, dym, dy2, sums, er, ec, pre
+    batch, count_all, st, gb, mst, mgb, z_ref, h_ref, up, da, cot, dym, dy2, sums, er, ec, pre, acc
 ):
     height, tall, lanes = z_ref.shape
     mean, rs, sc, sh = coef(st[...], gb[...], count_all)
@@ -804,7 +856,10 @@
             up[t],
             preferred_element_type=F32,
         ).reshape(height, tall, lanes)
-    sums[...] = jnp.zeros(sums.shape, F32)
+    acc[...] = jnp.zeros(acc.shape, F32)
+
+    def add(k, value):
+        acc[k] += jnp.sum(value.reshape(-1, 8, lanes), axis=0)
 
     @pl.loop(0, height)
     def _(h):
@@ -824,18 +879,19 @@
             shared = shared + br
             dm = br * p * (1.0 - m)
             dym[t, h] = dm.astype(BF)
-            sums[2 * t : 2 * t + 1] += jnp.sum(dm, axis=0, keepdims=True)
-            sums[2 * t + 1 : 2 * t + 2] += jnp.sum(dm * (mp - mmean), axis=0, keepdims=True)
+            add(2 * t, dm)
+            add(2 * t + 1, dm * (mp - mmean))
         g2 = shared * (s * (1.0 + yy * (1.0 - s)))
         dy2[h] = g2
-        sums[6:7] += jnp.sum(g2, axis=0, keepdims=True)
-        sums[7:8] += jnp.sum(g2 * (z - mean), axis=0, keepdims=True)
+        add(6, g2)
+        add(7, g2 * (z - mean))
         k = 8
         for t in range(TASKS):
             for s2 in range(t, TASKS):
-                sums[k : k + 1] += jnp.sum(branches[t] * branches[s2], axis=0, keepdims=True)
+                add(k, branches[t] * branches[s2])
                 k += 1
 
+    sums[...] = jnp.sum(acc[...], axis=1)
     for t in range(TASKS):
         sums[2 * t + 1 : 2 * t + 2] = sums[2 * t + 1 : 2 * t + 2] * mcoef[t][1]
     sums[7:8] = sums[7:8] * rs
@@ -864,7 +920,10 @@
             sds((2, tall, chans), BF),
             sds((height, 2 * batch, chans), F32),
         ],
-        scratch_shapes=[pltpu.VMEM((TASKS, height, tall, lanes), F32)],
+        scratch_shapes=[
+            pltpu.VMEM((TASKS, height, tall, lanes), F32),
+            pltpu.VMEM((14, 8, lanes), F32),
+        ],
         compiler_params=params(),
         cost_estimate=cost(2 * height * tall * CA * chans * TASKS, 15e6, 4e6),
         name="attend_back",
@@ -912,7 +971,7 @@
 
 
 def mask_back(mst, mgb, msum, hst, hgb, dym, h, hp, up, tall, count_all):
-    lanes = BLK
+    lanes = 2 * BLK
     wide = TASKS * CA
     pixels = h.shape[0] - 2 * tall
 
@@ -979,7 +1038,7 @@
 
 def norm_back(idx, st, gb, gs, dy, dhalo, z, zhalo, batch, count_all, name):
     height, tall, chans = z.shape
-    lanes = BLK
+    lanes = 2 * BLK
     r = height + 2
 
     def two(n):
@@ -1044,7 +1103,7 @@
 
 def first_back(hst, hgb, hsum, st, gb, dh, hp, u3, part, z, down, batch, count_all):
     height, tall, chans = z.shape
-    lanes = BLK
+    lanes = 2 * BLK
     wide = TASKS * CA
 
     def two(n):
@@ -1120,17 +1179,34 @@
                 halves[h, i * NB + j, at] = low[row : row + HB, j * BLK : (j + 1) * BLK]
 
 
-def wgrad_kernel(n_extra, idx, x3, g3, *refs):
-    mine, other = refs[n_extra:]
+def wgrad_kernel(n_extra, idx, x_hbm, g_hbm, *refs):
+    mine_hbm, other_hbm, x3, g3, mine, other, sems, o_sems = refs[n_extra:]
     height, tall = x3.shape[1] - 2, x3.shape[2]
-    g = g3[0, 1 : height + 1].reshape(height * tall, C)
-
-    @pl.loop(0, 3)
-    def _(dy):
-        for dx in range(3):
-            view = x3[dx, pl.ds(dy, height)].reshape(height * tall, C)
+    g_copy = pltpu.make_async_copy(g_hbm.at[1, pl.ds(1, height)], g3, sems.at[3])
+    x_copies = [pltpu.make_async_copy(x_hbm.at[k], x3.at[k], sems.at[k]) for k in range(3)]
+    g_copy.start()
+    for copy in x_copies:
+        copy.start()
+    g_copy.wait()
+    outs = []
+
+    def send(first, count):
+        at = pl.ds(first, count)
+        for k, (source, target) in enumerate(((mine, mine_hbm), (other, other_hbm))):
+            copy = pltpu.make_async_copy(
+                source.at[:, :, at], target.at[:, :, at], o_sems.at[len(outs)]
+            )
+            copy.start()
+            outs.append(copy)
+
+    g = g3[...].reshape(height * tall, C)
+    for dx in range(3):
+        x_copies[dx].wait()
+        for dy in range(3):
+            view = x3[dx, dy : dy + height].reshape(height * tall, C)
             grad = lax.dot_general(view, g, TN, preferred_element_type=F32)
             put_blocks(idx, grad, mine, other, 3 * dy + dx)
+            send((3 * dy + dx) * HB, HB)
 
     if n_extra:
         ddown, dup = refs[:2]
@@ -1155,22 +1231,29 @@
             ]
             mine[e, s, at] = jnp.where(even, a, b)
             other[e, s, at] = jnp.where(even, b, a)
+        send(9 * HB, PROJ_ROWS)
+
+    for copy in outs:
+        copy.wait()
 
 
 def wgrad(idx, x3, g3, name, extra=()):
     r, tall = x3.shape[1], x3.shape[2]
     rows = 9 * HB + (PROJ_ROWS if extra else 0)
+    blocks = (4, 4, rows, BLK)
     return pl.pallas_call(
         functools.partial(wgrad_kernel, len(extra)),
-        grid=(1,),
-        in_specs=[
-            SM,
-            pl.BlockSpec(x3.shape, lambda c: (0, 0, 0, 0)),
-            pl.BlockSpec((1,) + g3.shape[1:], lambda c: (1, 0, 0, 0)),
-        ]
-        + [VM] * len(extra),
-        out_specs=[pl.BlockSpec((4, 4, rows, BLK), lambda c: (0, 0, 0, 0))] * 2,
-        out_shape=[sds((4, 4, rows, BLK), BF)] * 2,
+        in_specs=[SM, ANY, ANY] + [VM] * len(extra),
+        out_specs=[ANY, ANY],
+        out_shape=[sds(blocks, BF)] * 2,
+        scratch_shapes=[
+            pltpu.VMEM(x3.shape, BF),
+            pltpu.VMEM((r - 2, tall, C), BF),
+            pltpu.VMEM(blocks, BF),
+            pltpu.VMEM(blocks, BF),
+            pltpu.SemaphoreType.DMA((4,)),
+            pltpu.SemaphoreType.DMA((20,)),
+        ],
         compiler_params=params(),
         cost_estimate=cost(2 * 9 * C * C * (r - 2) * tall, 10e6),
         name=name,
@@ -1220,7 +1303,7 @@
             else:
                 view = se[0, dx, dy // 2 : dy // 2 + half]
             piece = jnp.dot(
-                view.reshape(half * q, C), wv[slot, 3 * dy + dx], preferred_element_type=F32
+                view.reshape(half * q, C), tap(wv.at[slot], 3 * dy + dx), preferred_element_type=F32
             )
             acc = piece if acc is None else acc + piece
     out[0] = (acc * 0.25).reshape(half, q, C).astype(BF)
@@ -1240,7 +1323,7 @@
         ],
         out_specs=pl.BlockSpec((1, half, q, C), lambda t: (t, 0, 0, 0)),
         out_shape=sds((TASKS, half, q, C), BF),
-        scratch_shapes=[pltpu.VMEM((2, 9, C, C), BF), pltpu.SemaphoreType.DMA((2, 32))],
+        scratch_shapes=[pltpu.VMEM((2,) + WEIGHTS, BF), pltpu.SemaphoreType.DMA((2, 2))],
         compiler_params=params(),
         cost_estimate=cost(TASKS * 2 * 9 * C * C * half * q, 20e6),
         name="task_fwd",
@@ -1284,11 +1367,10 @@
             ln[0, k], rn[0, k], wn[0, k] = new_l, new_r, new_w
 
 
-def shampoo_conv(idx, mine, other, state, first, prev):
-    n = mine.shape[0] // HB
+def shampoo_conv(idx, mine, other, state, first, prev, begin=0, n=9):
     each = 9
-    block = pl.BlockSpec((1, each, BLK, BLK), lambda k: (0, first // each + k, 0, 0))
-    half = pl.BlockSpec((each * HB, BLK), lambda k: (k, 0))
+    block = pl.BlockSpec((1, each, BLK, BLK), lambda k: (0, (first + begin) // each + k, 0, 0))
+    half = pl.BlockSpec((each * HB, BLK), lambda k: (begin // each + k, 0))
     full = state[0].shape
     return pl.pallas_call(
         functools.partial(shampoo_kernel, len(prev)),
@@ -1303,7 +1385,8 @@
     )(idx, mine, other, *state, *prev)
 
 
-def shampoo_proj_kernel(g, left, right, lroot, rroot, weight, ln, rn, wn):
+def shampoo_proj_kernel(g, left, right, lroot, rroot, weight, gr, ln, rn, wn):
+    gr[...] = g[...].astype(F32)
     kinds, count = g.shape[1], g.shape[2]
     for kind in range(kinds):
         grads = [g[0, kind, k] for k in range(count)]
@@ -1322,8 +1405,8 @@
         shampoo_proj_kernel,
         grid=g.shape[:1],
         in_specs=[block] * 6,
-        out_specs=[block] * 3,
-        out_shape=[sds(g.shape, F32)] * 3,
+        out_specs=[block] * 4,
+        out_shape=[sds(g.shape, F32)] * 4,
         compiler_params=params(),
         cost_estimate=cost(24 * 8 * BLK**3, 24 * 9 * BLK * BLK * 4),
         name="shampoo_proj",
@@ -1431,113 +1514,7 @@
     own = lax.dynamic_index_in_dim(halves, wa % 2, axis=1, keepdims=False).astype(BF)
     g0, g1 = Gather(own[None, 0:9]), Gather(own[None, 9:18])
     g0.near()
-    g0.join()
-    g0.far()
-    g0.low()
-    images = after(images, g0.line_low)
     rows0 = jnp.stack(row_halo(edge_row(images, 0), edge_row(images, tile_h - 1)))
-    off_down = 2 * C
-    off_up = off_down + TASKS * CA
-    for row in range(2):
-        k = 1 - row
-        at = slice(row, row + 1)
-        grad[at, 0:C] = gs1[k : k + 1]
-        grad[at, C : 2 * C] = gsum[6 + k : 7 + k]
-        grad[at, off_down:off_up] = dhs[k : k + 1]
-        for t in range(TASKS):
-            grad[at, off_up + t * C : off_up + (t + 1) * C] = gsum[2 * t + k : 2 * t + k + 1]
-    g = grad[...]
-    new = moment_decay * moment[...] + (1.0 - moment_decay) * g * g
-    moment_new[...] = new
-    norm_new[...] = norm[...] - norm_rate * g / (jnp.sqrt(new) + 1e-08)
-    row = lax.broadcasted_iota(jnp.int32, (TASKS, TASKS), 0)
-    col = lax.broadcasted_iota(jnp.int32, (TASKS, TASKS), 1)
-    value = jnp.zeros((TASKS, TASKS), F32)
-    k = 8
-    for t in range(TASKS):
-        for s in range(t, TASKS):
-            total = jnp.sum(gsum[k : k + 1], axis=1, keepdims=True)
-            hit = ((row == t) & (col == s)) | ((row == s) & (col == t))
-            value = jnp.where(hit, total, value)
-            k += 1
-    gram[...] = value
-
-
-def norm_step(gs1, gsum, dhs, norm, moment):
-    like = sds(norm.shape, F32)
-    return pl.pallas_call(
-        norm_step_kernel,
-        in_specs=[VM] * 5,
-        out_specs=[VM] * 4,
-        out_shape=[sds((TASKS, TASKS), F32), like, like, like],
-        compiler_params=params(),
-        cost_estimate=cost(0, 1e5),
-        name="norm_step",
-    )(gs1, gsum, dhs, norm, moment)
-
-
-def to_rows(field):
-    b, h, w, c = field.shape
-    split = field.reshape(b, h, w // 2, 2, c)
-    return jnp.transpose(split, (1, 3, 0, 2, 4)).reshape(h, w * b, c)
-
-
-def from_rows(field, b):
-    h, tall, c = field.shape
-    split = field.reshape(h, 2, b, tall // (2 * b), c)
-    return jnp.transpose(split, (2, 0, 3, 1, 4)).reshape(b, h, tall // b, c)
-
-
-def pooled_rows(field):
-    b, h, w, c = field.shape
-    return jnp.transpose(field, (1, 0, 2, 3)).reshape(h, b * w, c)
-
-
-def shards(
-    images,
-    cot_shared,
-    cot_tasks,
-    depth_mask,
-    nash_weights,
-    conv_weight,
-    conv_left,
-    conv_right,
-    conv_left_root,
-    conv_right_root,
-    proj_weight,
-    proj_left,
-    proj_right,
-    proj_left_root,
-    proj_right_root,
-    norm_params,
-    norm_moment,
-):
-    batch, tile_h, tile_w, _ = images.shape
-    half_h, half_w = tile_h // 2, tile_w // 2
-    tall = batch * tile_w
-    q = batch * half_w
-    ha, wa = lax.axis_index("ha"), lax.axis_index("wa")
-    count_all = float(
-        batch * tile_h * tile_w * lax.axis_size("img") * lax.axis_size("ha") * lax.axis_size("wa")
-    )
-    idx = jnp.stack(
-        [
-            lax.axis_index("img"),
-            ha,
-            wa % 2,
-            ha > 0,
-            ha < lax.axis_size("ha") - 1,
-            wa > 0,
-            wa < lax.axis_size("wa") - 1,
-        ]
-    ).astype(jnp.int32)
-
-    halves = conv_weight[0].reshape(conv_weight.shape[1], 2, HB, BLK)
-    own = lax.dynamic_index_in_dim(halves, wa % 2, axis=1, keepdims=False).astype(BF)
-    g0, g1 = Gather(own[None, 0:9]), Gather(own[None, 9:18])
-    g0.near()
-    edges = after(images, own)
-    rows0 = jnp.stack(row_halo(edge_row(edges, 0), edge_row(edges, tile_h - 1)))
     g0.join(rows0)
     g0.far()
     g0.low()
@@ -1572,6 +1549,7 @@
     halo1 = halo(edges1, batch)
     s1 = after(s1, g1.line_high, g1.low_x, g1.low_y)
     wt_mine = lax.all_gather(after(own[18:], s1), ("img", "ha"), axis=0, tiled=False)
+    g1.high(s1)
 
     cot_tasks = after(cot_tasks, z1)
     depth_pick = jnp.arange(TASKS) == 1
@@ -1587,25 +1565,31 @@
     grid = jnp.concatenate([left, grid, right], axis=3)
     go3 = jnp.stack([grid[:, :, :, k : k + half_w] for k in range(3)], axis=1)
     go3 = go3.reshape(TASKS, 3, half_h + 2, q, C)
+    def s1_ha(dep):
+        return halo1
+
     def s1_img(dep):
-        g1.high(dep)
-        return halo1
-
-    s1 = after(sum_all(s1, img=s1_img), g1.high_x, g1.high_y)
-    g1.corner_a(s1)
-    g1.corner_b(s1)
-    u3, hp, hc, hs = mid(idx, s1, gb1, z1, *halo1, down, batch, count_all)
-    hs = after(hs, g1.corner_low, g1.corner_high)
-    w1 = g1.pieces(hs)
+        g1.corner_a(dep, g1.high_x, g1.high_y)
+        g1.corner_b(dep, g1.high_x, g1.high_y)
+        return g1.high_x, g1.high_y
+
+    s1 = sum_all(s1, ha=s1_ha, img=s1_img)
+    w1 = g1.pieces(s1)
+    u3, hp, hc, hs = mid(
+        after(idx, *w1[8:14]), s1, gb1, z1, *halo1, down, batch, count_all
+    )
+    corners = tuple(swap(after(part, hs), "wa", 1) for part in w1[6:8])
+    w1 = w1[:14] + corners
+    hs = after(hs, *corners)
     kept = {}
 
-    def s2_ha1(dep):
+    def s2_img(dep):
         kept["z2"], kept["s2"], kept["edges2"] = conv(
             idx, after(u3, dep), w1, False, F32, "conv_second", batch
         )
         return (kept["s2"],)
 
-    hs = sum_all(hs, ("wa", "img", "ha"), ha=s2_ha1)
+    hs = sum_all(hs, ("wa", "img", "ha"), img=s2_img)
     z2, s2 = kept["z2"], kept["s2"]
     halo2 = halo(kept["edges2"], batch)
     h, hcb, ms = hidden(hs, gbd, hp, hc, up, tall, count_all)
@@ -1618,15 +1602,15 @@
     se, so, pooled = attend(
         idx, s2, gb2, ms, gbu, z2, *halo2, h, hcb, up, batch, count_all
     )
-    halves_t = task_wgrad(idx, se, so, go3)
+    wt_mine = after(wt_mine, s2m)
+    wt = (wt_mine, swap(wt_mine, "wa", 1))
+    halves_t = task_wgrad(after(idx, wt[1]), se, so, go3)
     if lax.axis_size("wa") == 2:
         part_t = lax.psum_scatter(halves_t, "wa", scatter_dimension=0, tiled=True)[0]
     else:
         mine_t = lax.dynamic_index_in_dim(halves_t, wa % 2, keepdims=False)
         other_t = lax.dynamic_index_in_dim(halves_t, 1 - wa % 2, keepdims=False)
         part_t = add_low(mine_t, swap(other_t, "wa", 1))
-    wt_mine = after(wt_mine, s2m)
-    wt = (wt_mine, swap(wt_mine, "wa", 1))
     da = task_back(after(idx, halves_t), go3, wt)
     dym, dy2, gsum, *edges2 = attend_back(
         s2, gb2, ms, gbu, z2, h, up, da, cot, batch, count_all
@@ -1678,46 +1662,49 @@
     y3 = norm_back(
         after(idx, r1.corner), s1, gb1, gs1, dy1, dhalo1, z1, halo1, batch, count_all, "first_norm_back"
     )
-    r1.high_sum(y3)
-    r1.low_sum(y3)
+    r0 = Scatter(*wgrad(idx, x3, y3, "wgrad_first"))
+    state = (conv_left, conv_right, conv_left_root, conv_right_root, conv_weight)
+    r0.wa(r1.to_x, r1.to_y)
+    r1.high_sum(r0.mine)
     r1.high_send()
-    r1.low_send(*r1.high)
-    r0 = Scatter(*wgrad(after(idx, *r1.high, *r1.low), x3, y3, "wgrad_first"))
-    state = (conv_left, conv_right, conv_left_root, conv_right_root, conv_weight)
-    r0.wa(r1.high_x, r1.high_y, r1.low_x, r1.low_y)
-    r0.corner_sum()
-    r0.corner_send()
+    r1.low_sum(*r1.high)
+    r1.low_send()
+    r0.corner_sum(*r1.low)
+    r0.corner_send(r1.high_x, r1.high_y)
     r1.far_sum(r0.corner)
     r1.far_send()
     image_grad = conv(after(idx, r0.corner, r1.far), y3, w0, True, BF, "conv_first_back")
     image_grad = after(image_grad, r0.to_x, r0.to_y, r1.from_far)
-    gradt = after(grad_t[0], image_grad)
+    r1.near_sum(image_grad)
+    r1.near_send()
+    r0.high_sum(r1.near)
+    r0.high_send()
+    r0.low_sum(*r0.high)
+    r0.low_send()
+    r0.far_sum(*r0.low)
+    r0.far_send()
+    grad1, grad1_other = r1.finish(r0.far)
+    gradt = after(grad_t[0], grad1)
     step = 2
     while step < lax.axis_size("wa"):
         gradt = add_low(gradt, swap(gradt, "wa", step))
         step *= 2
     gradt_other = swap(gradt, "wa", 1)
-    r0.high_sum(image_grad)
-    r0.high_send()
-    r0.low_sum(*r0.high)
-    r0.low_send()
-    r1.near_sum(*r0.low)
-    r1.near_send()
-    new = shampoo_conv(after(idx, *r0.low, r1.near), gradt, gradt_other, state, 18, ())
-    r0.far_sum(new[0], r0.low_x, r0.low_y, r1.from_near)
-    r0.far_send()
-    grad1, grad1_other = r1.finish(r0.far)
-    new = shampoo_conv(
-        after(idx, grad1), grad1[: 9 * HB], grad1_other[: 9 * HB], state, 9, new
-    )
+    new = shampoo_conv(after(idx, grad1), gradt, gradt_other, state, 18, (), 0)
     r0.near_sum(new[0])
     r0.near_send()
-    proj = gather_proj_line(after(grad1[9 * HB :], r0.near))
-    grad0, grad0_other = r0.finish(proj)
-    proj_total = gather_proj(after(proj, grad0))
+    proj = ring_gather(gather_proj_core(after(grad1[9 * HB :], r0.near)), "ha")
+    new = shampoo_conv(after(idx, r0.near), gradt, gradt_other, state, 18, new, 9)
+    grad0, grad0_other = r0.finish(new[0])
+    proj_total = ring_gather(after(proj, grad0), "img")
+    new = shampoo_conv(after(idx, grad0, proj), gradt, gradt_other, state, 18, new, 18)
+    new = shampoo_conv(
+        after(idx, new[0]), grad1[: 9 * HB], grad1_other[: 9 * HB], state, 9, new
+    )
     new = shampoo_conv(idx, grad0, grad0_other, state, 0, new)
-    proj_left_new, proj_right_new, proj_weight_new = shampoo_proj(
-        after(proj_total, new[0]), proj_left, proj_right, proj_left_root, proj_right_root, proj_weight
+    proj_total = after(proj_total, new[0]).reshape(TASKS, 2, NB, BLK, BLK)
+    proj_total, proj_left_new, proj_right_new, proj_weight_new = shampoo_proj(
+        proj_total, proj_left, proj_right, proj_left_root, proj_right_root, proj_weight
     )
     conv_total, conv_left_new, conv_right_new, conv_weight_new = new
 

time: 498 us -> 471 us (0.946)
  waiting for transfers between devices: 85.3 us -> 69.2 us
  Pallas kernels: 198 us -> 186 us
  starting transfers between devices: 116 us -> 121 us
    ppermute x6 -> x0, waiting for transfers between devices: 14 us -> none  [ring_gather(): lax.ppermute(value, axis, [(i, (i + step) % count) for i in range(count)])]
    ppermute x103 -> x109, starting transfers between devices: 92.2 us -> 106 us  [swap(): return lax.ppermute(value, axis, pairs(axis, step))]
    ppermute x103 -> x109, waiting for transfers between devices: 71.2 us -> 58.4 us  [swap(): return lax.ppermute(value, axis, pairs(axis, step))]
    ppermute x6 -> x0, starting transfers between devices: 8.49 us -> none  [ring_gather(): lax.ppermute(value, axis, [(i, (i + step) % count) for i in range(count)])]
    ppermute x12, waiting for transfers between devices: 0.03 us -> 8.26 us  [row_halo(): lax.ppermute(send, 'ha', [(i, pairing.get(i, i)) for i in range(count)])]
    pallas_call x4, Pallas kernels: 45.7 us -> 39.3 us  [conv(): pl.pallas_call(functools.partial(conv_kernel, len(pieces), batch, transpo...]
    pallas_call x3 -> x5, Pallas kernels: 15.5 us -> 18.4 us  [shampoo_conv(): pl.pallas_call(functools.partial(shampoo_kernel, len(prev)), grid=(n // e...]
    convert_element_type x14 -> x16, other arithmetic: 17.6 us -> 16.8 us  [add_low(): return total.astype(BF)]
  transfers between devices with their start and end apart: 124 -> 124, of which waited for: 43 -> 44; matrix products, arithmetic and copies ran while one was open for 12% -> 13% of each run, Pallas kernels for 39% -> 37%
where the time goes in v3:
time: 471 us; the launch traced here: 462 us
  Pallas kernels  186 us (39%)
  starting transfers between devices  121 us (26%)
  waiting for transfers between devices  69.2 us (15%)
  other arithmetic  43.8 us (9%)
  local copies, waits for them, and re-layouts  25.2 us (5%)
  between operations  16.5 us (4%)
    ppermute x109, starting transfers between devices, swap(): return lax.ppermute(value, axis, pairs(axis, step))  106 us
    ppermute x109, waiting for transfers between devices, swap(): return lax.ppermute(value, axis, pairs(axis, step))  58.4 us
    pallas_call x4, Pallas kernels, conv(): pl.pallas_call(functools.partial(conv_kernel, len(pieces), batch, transpo...  39.3 us
    pallas_call x2, Pallas kernels, wgrad(): pl.pallas_call(functools.partial(wgrad_kernel, len(extra)), in_specs=[SM,...  18.8 us
    pallas_call x5, Pallas kernels, shampoo_conv(): pl.pallas_call(functools.partial(shampoo_kernel, len(prev)), grid=(n // e...  18.4 us
    convert_element_type x16, other arithmetic, add_low(): return total.astype(BF)  16.8 us
    pallas_call x1, Pallas kernels, task_back(): pl.pallas_call(da_kernel, grid=(TASKS,), in_specs=[SM, pl.BlockSpec((1,)...  15.8 us
    ppermute x12, starting transfers between devices, row_halo(): lax.ppermute(send, 'ha', [(i, pairing.get(i, i)) for i in range(count)])  15.6 us
  transfers between devices with their start and end apart: 124, of which 44 were waited for; matrix products, arithmetic and copies ran while one was open for 13% of the time, Pallas kernels for 37%

profile of v3, /device:TPU:0, one launch (start us, length us, event | category | flops | bytes accessed | tf_op | source)
XLA Modules:
  0.0 461.8 jit_solution(15090172494366969838)
XLA Ops:
  8.3 3.1 collective-permute-start.1
  14.3 3.8 collective-permute-start
  18.9 6.0 %collective-permute-done = bf16[1,9,64,128]{3,2,1,0:T(8,128)(2,1)S(1)} collective-permute-done((bf16[1,9,64,128]{3,2,1,0:T(8,128)(2,1)S(1)}, bf16[1,9,64,128]{3,2,1,0:T(8,128)(2,1)S(1)}, u32[]{:S(2)}, u32[]{:S(2)}) %collective-permute-start) | collective-permute-done | bytes 147488 | tf_op jit(solution)/shard_map/ppermute | solution.py:54
  25.0 1.6 collective-permute-start.5
  35.9 3.4 collective-permute-start.4
  41.0 4.5 shift_copies.1.x_hbm
  46.0 1.6 collective-permute-start.9
  48.1 4.2 collective-permute-done.11.refs_6_
  55.5 1.6 collective-permute-start.22
  58.6 10.2 %conv_first.1 = (f32[16,64,512]{2,1,0:T(8,128)}, f32[2,512]{1,0:T(2,128)}, bf16[2,64,512]{2,1,0:T(8,128)(2,1)}, f32[16,8,512]{2,1,0:T(8,128)}) custom-call(s32[7]{0:T(128)} %stack.133.idx.idx_ref, bf16[3,18,64,512]{3,2,1,0:T(8,128)(2,1)} %shift_copies.1.x_hbm, bf16[2,9,64,128]{3,2,1,0:T(8,128)(2,1)} %copy-done.6, bf16[2,9,64,128]{3,2,1,0:T(8,128)(2,1)} %copy-done.9, ...), custom_call_target="tpu_custom_call" | custom-call | flops 301989888 | bytes 625000 | tf_op jit(solution)/shard_map/conv_first/pallas_call | solution.py:504
  73.6 2.0 collective-permute-start.25
  79.2 3.9 collective-permute-done.27
  85.6 2.8 collective-permute-start.32
  90.1 6.4 %collective-permute-start.59 = (bf16[3,1,4,8,512]{4,3,2,1,0:T(8,128)(2,1)S(1)}, bf16[3,1,4,8,512]{4,3,2,1,0:T(8,128)(2,1)S(1)}, u32[]{:S(2)}, u32[]{:S(2)}) collective-permute-start(bf16[3,1,4,8,512]{4,3,2,1,0:T(8,128)(2,1)S(1)} %get-tuple-element.282), channel_id=1, source_target_pairs={{0,2},{2,0},{4,6},{6,4},{1,3},{3,1},{5,7},{7,5},{8,10},{10,8},{12,... | collective-permute-start | bytes 294920 | tf_op jit(solution)/shard_map/ppermute | solution.py:83
  98.6 4.3 collective-permute-done.59
  109.3 6.9 %mid.1 = (bf16[3,18,64,512]{3,2,1,0:T(8,128)(2,1)}, f32[1152,384]{1,0:T(8,128)}, f32[144,384]{1,0:T(8,128)}, f32[2,384]{1,0:T(2,128)}) custom-call(s32[7]{0:T(128)} %stack.133.idx.idx_ref, f32[2,512]{1,0:T(2,128)} %add_add_fusion.6.st, f32[2,512]{1,0:T(2,128)} %get-tuple-element.357.gb, f32[16,64,512]{2,1,0:T(8,128)} %get-tuple-element.167.z_ref.z, ...), custom_call_target="tpu_custom_call" | custom-call | flops 28311552 | bytes 625000 | tf_op jit(solution)/shard_map/mid/pallas_call | solution.py:578
  121.5 1.5 collective-permute-start.48
  123.5 1.6 collective-permute-start.46
  125.1 10.2 %conv_second.1 = (f32[16,64,512]{2,1,0:T(8,128)}, f32[2,512]{1,0:T(2,128)}, bf16[2,64,512]{2,1,0:T(8,128)(2,1)}, f32[16,8,512]{2,1,0:T(8,128)}) custom-call(s32[7]{0:T(128)} %stack.133.idx.idx_ref, bf16[3,18,64,512]{3,2,1,0:T(8,128)(2,1)} %get-tuple-element.175.x_hbm.u3, bf16[2,9,64,128]{3,2,1,0:T(8,128)(2,1)} %copy-done.7, ...), custom_call_target="tpu_custom_call" | custom-call | flops 301989888 | bytes 625000 | tf_op jit(solution)/shard_map/conv_second/pallas_call | solution.py:504
  135.4 1.9 collective-permute-start.51
  137.3 7.0 %collective-permute-start.50 = (f32[2,384]{1,0:T(2,128)S(1)}, f32[2,384]{1,0:T(2,128)S(1)}, u32[]{:S(2)}, u32[]{:S(2)}) collective-permute-start(f32[2,384]{1,0:T(2,128)S(1)} %add_add_fusion.11), channel_id=1, source_target_pairs={{0,4},{2,6},{4,0},{6,2},{1,5},{3,7},{5,1},{7,3},{8,12},{10,14},{12... | collective-permute-start | bytes 9224 | tf_op jit(solution)/shard_map/ppermute | solution.py:54
  144.2 1.9 pad_maximum_fusion.go
  146.2 1.7 collective-permute-done.49
  148.6 5.9 %hidden.1 = (bf16[1152,384]{1,0:T(8,128)(2,1)}, bf16[144,384]{1,0:T(8,128)(2,1)}, f32[6,512]{1,0:T(8,128)}) custom-call(f32[2,384]{1,0:T(2,128)} %add_add_fusion.10.st.hst, f32[2,384]{1,0:T(2,128)} %slice.567.gb.hgb, f32[1152,384]{1,0:T(8,128)} %get-tuple-element.178.hp, f32[144,384]{1,0:T(8,128)} %get-tuple-element.179.hc, bf16[3,128,512]{2,1,0:T(8,128)(2,1)} %bitcast.308), custom_call_target="tpu_custom_call" | custom-call | flops 28311552 | bytes 312500 | tf_op jit(solution)/shard_map/hidden/pallas_call | solution.py:637
  157.4 1.9 collective-permute-start.55
  166.4 2.1 collective-permute-start.64
  168.4 2.4 collective-permute-start.63
  172.2 3.0 collective-permute-done.63
  175.2 2.4 all-gather.3.cloned.1.call-done
  179.5 8.6 %attend.1 = (bf16[3,3,9,32,512]{4,3,2,1,0:T(8,128)(2,1)}, bf16[3,3,8,32,512]{4,3,2,1,0:T(8,128)(2,1)}, bf16[8,32,512]{2,1,0:T(8,128)(2,1)}) custom-call(s32[7]{0:T(128)} %stack.133.idx.idx_ref, f32[2,512]{1,0:T(2,128)} %slice.698.st, f32[2,512]{1,0:T(2,128)} %get-tuple-element.356.gb, f32[6,512]{1,0:T(8,128)} %slice.699.mst, f32[6,512]{1,0:T(8,128)} %reshape.298.mgb, ...), custom_call_target="tpu_custom_call" | custom-call | flops 28311552 | bytes 937500 | tf_op jit(solution)/shard_map/attend/pallas_call | solution.py:821
  189.2 9.5 %task_wgrad.1 = bf16[2,16,1728,128]{3,2,1,0:T(8,128)(2,1)} custom-call(s32[7]{0:T(128)} %stack.133.idx.idx_ref, bf16[3,3,9,32,512]{4,3,2,1,0:T(8,128)(2,1)} %get-tuple-element.192.se, bf16[3,3,8,32,512]{4,3,2,1,0:T(8,128)(2,1)} %get-tuple-element.193.so, bf16[3,3,10,32,512]{4,3,2,1,0:T(8,128)(2,1)} %pad_maximum_fusion.go), custom_call_target="tpu_custom_call" | custom-call | flops 226492416 | bytes 1500000 | tf_op jit(solution)/shard_map/task_wgrad/pallas_call | solution.py:1278
  200.5 15.8 %task_back.1 = bf16[3,8,2,2,32,512]{5,4,3,2,1,0:T(8,128)(2,1)} custom-call(s32[7]{0:T(128)} %stack.133.idx.idx_ref, bf16[3,3,10,32,512]{4,3,2,1,0:T(8,128)(2,1)} %pad_maximum_fusion.go, bf16[16,27,64,128]{3,2,1,0:T(8,128)(2,1)} %bitcast.305, bf16[16,27,64,128]{3,2,1,0:T(8,128)(2,1)} %collective-permute-done.65.other), custom_call_target="tpu_custom_call" | custom-call | flops 402653184 | bytes 1500000 | tf_op jit(solution)/shard_map/task_back/pallas_call | solution.py:708
  216.3 11.9 %attend_back.1 = (bf16[3,16,64,512]{3,2,1,0:T(8,128)(2,1)}, f32[16,64,512]{2,1,0:T(8,128)}, f32[14,512]{1,0:T(8,128)}, bf16[2,64,512]{2,1,0:T(8,128)(2,1)}, f32[16,8,512]{2,1,0:T(8,128)}) custom-call(f32[2,512]{1,0:T(2,128)} %slice.698.st, f32[2,512]{1,0:T(2,128)} %get-tuple-element.356.gb, f32[6,512]{1,0:T(8,128)} %slice.699.mst, f32[6,512]{1,0:T(8,128)} %reshape.298.mgb, ...), custom_call_target="tpu_custom_call" | custom-call | flops 25165824 | bytes 937500 | tf_op jit(solution)/shard_map/attend_back/pallas_call | solution.py:905
  231.3 3.7 collective-permute-start.68
  235.5 11.1 %task_fwd.1 = bf16[3,8,32,512]{3,2,1,0:T(8,128)(2,1)} custom-call(s32[7]{0:T(128)} %stack.133.idx.idx_ref, bf16[3,3,9,32,512]{4,3,2,1,0:T(8,128)(2,1)} %get-tuple-element.192.se, bf16[3,3,8,32,512]{4,3,2,1,0:T(8,128)(2,1)} %get-tuple-element.193.so, bf16[16,27,64,128]{3,2,1,0:T(8,128)(2,1)} %bitcast.306, bf16[16,27,64,128]{3,2,1,0:T(8,128)(2,1)} %collective-permute-done.65.other), custom_call_target="tpu_custom_call" | custom-call | flops 226492416 | bytes 1250000 | tf_op jit(solution)/shard_map/task_fwd/pallas_call | solution.py:1314
  249.1 1.9 collective-permute-start.75
  252.6 1.8 collective-permute-done.75
  256.4 8.4 %mask_back.1 = (f32[3,128,512]{2,1,0:T(8,128)}, f32[1024,384]{1,0:T(8,128)}, f32[2,384]{1,0:T(2,128)}) custom-call(f32[6,512]{1,0:T(8,128)} %slice.699.mst, f32[6,512]{1,0:T(8,128)} %reshape.298.mgb, f32[6,512]{1,0:T(8,128)} %slice.707.msum, f32[2,384]{1,0:T(2,128)} %add_add_fusion.10.st.hst, f32[2,384]{1,0:T(2,128)} %slice.567.gb.hgb, ...), custom_call_target="tpu_custom_call" | custom-call | flops 75497472 | bytes 500000 | tf_op jit(solution)/shard_map/mask_back/pallas_call | solution.py:984
  267.0 2.8 collective-permute-start.79
  272.0 4.2 second_back.1.x_hbm.g_hbm
  279.8 9.6 %conv_second_back.1.part = f32[16,64,512]{2,1,0:T(8,128)} custom-call(s32[7]{0:T(128)} %stack.133.idx.idx_ref, bf16[3,18,64,512]{3,2,1,0:T(8,128)(2,1)} %second_back.1.x_hbm.g_hbm, bf16[2,9,64,128]{3,2,1,0:T(8,128)(2,1)} %copy-done.7, bf16[2,9,64,128]{3,2,1,0:T(8,128)(2,1)} %collective-permute-done.20.refs_1_, ...), custom_call_target="tpu_custom_call" | custom-call | flops 301989888 | bytes 625000 | tf_op jit(solution)/shard_map/conv_second_back/pallas_call | solution.py:504
  290.0 8.5 %first_back.1 = (f32[512,384]{1,0:T(8,128)}, f32[16,64,512]{2,1,0:T(8,128)}, f32[2,512]{1,0:T(2,128)}, bf16[2,64,512]{2,1,0:T(8,128)(2,1)}, f32[16,8,512]{2,1,0:T(8,128)}) custom-call(f32[2,384]{1,0:T(2,128)} %add_add_fusion.10.st.hst, f32[2,384]{1,0:T(2,128)} %slice.567.gb.hgb, f32[2,384]{1,0:T(2,128)} %add_add_fusion.8.hsum.dhs, ...), custom_call_target="tpu_custom_call" | custom-call | flops 50331648 | bytes 750000 | tf_op jit(solution)/shard_map/first_back/pallas_call | solution.py:1116
  302.9 2.9 collective-permute-start.86
  305.8 3.1 collective-permute-start.85
  308.8 9.8 %wgrad_second.1 = (bf16[4,4,672,128]{3,2,1,0:T(8,128)(2,1)}, bf16[4,4,672,128]{3,2,1,0:T(8,128)(2,1)}) custom-call(s32[7]{0:T(128)} %stack.133.idx.idx_ref, bf16[3,18,64,512]{3,2,1,0:T(8,128)(2,1)} %get-tuple-element.175.x_hbm.u3, bf16[3,18,64,512]{3,2,1,0:T(8,128)(2,1)} %second_back.1.x_hbm.g_hbm, f32[512,384]{1,0:T(8,128)} %get-tuple-element.210.refs_0_, ...), custom_call_target="tpu_custom_call" | custom-call | flops 301989888 | bytes 625000 | tf_op jit(solution)/shard_map/wgrad_second/pallas_call | solution.py:1244
  331.1 5.2 %first_norm_back.1.g_hbm.x_hbm = bf16[3,18,64,512]{3,2,1,0:T(8,128)(2,1)} custom-call(s32[7]{0:T(128)} %stack.133.idx.idx_ref, f32[2,512]{1,0:T(2,128)} %add_add_fusion.6.st, f32[2,512]{1,0:T(2,128)} %get-tuple-element.357.gb, f32[2,512]{1,0:T(2,128)} %add_add_fusion.4.gs.gs1, f32[16,64,512]{2,1,0:T(8,128)} %get-tuple-element.220.dy, ...), custom_call_target="tpu_custom_call" | custom-call | bytes 625000 | tf_op jit(solution)/shard_map/first_norm_back/pallas_call | solution.py:1051
  336.3 9.0 %wgrad_first.1 = (bf16[4,4,576,128]{3,2,1,0:T(8,128)(2,1)}, bf16[4,4,576,128]{3,2,1,0:T(8,128)(2,1)}) custom-call(s32[7]{0:T(128)} %stack.133.idx.idx_ref, bf16[3,18,64,512]{3,2,1,0:T(8,128)(2,1)} %shift_copies.1.x_hbm, bf16[3,18,64,512]{3,2,1,0:T(8,128)(2,1)} %first_norm_back.1.g_hbm.x_hbm), custom_call_target="tpu_custom_call" | custom-call | flops 301989888 | bytes 625000 | tf_op jit(solution)/shard_map/wgrad_first/pallas_call | solution.py:1244
  351.8 1.8 collective-permute-start.102
  353.6 1.6 fusion.9
  355.2 3.9 collective-permute-done.98
  360.7 2.1 collective-permute-start.101
  365.4 9.4 %conv_first_back.1 = bf16[16,64,512]{2,1,0:T(8,128)(2,1)} custom-call(s32[7]{0:T(128)} %stack.133.idx.idx_ref, bf16[3,18,64,512]{3,2,1,0:T(8,128)(2,1)} %first_norm_back.1.g_hbm.x_hbm, bf16[2,9,64,128]{3,2,1,0:T(8,128)(2,1)} %copy-done.6, bf16[2,9,64,128]{3,2,1,0:T(8,128)(2,1)} %copy-done.9, bf16[2,9,64,128]{3,2,1,0:T(8,128)(2,1)} %collective-permute-done.5.refs_2_, ...), custom_call_target="tpu_custom_call" | custom-call | flops 301989888 | bytes 625000 | tf_op jit(solution)/shard_map/conv_first_back/pallas_call | solution.py:504
  384.5 2.0 collective-permute-done.104
  387.6 5.0 %collective-permute-done.106 = bf16[672,128]{1,0:T(8,128)(2,1)S(1)} collective-permute-done((bf16[672,128]{1,0:T(8,128)(2,1)S(1)}, bf16[672,128]{1,0:T(8,128)(2,1)S(1)}, u32[]{:S(2)}, u32[]{:S(2)}) %collective-permute-start.106) | collective-permute-done | bytes 172064 | tf_op jit(solution)/shard_map/ppermute | solution.py:54
  397.1 3.7 shampoo_conv.5
  400.8 2.5 collective-permute-done.109
  407.5 1.8 collective-permute-start.116
  409.4 2.6 collective-permute-start.114
  413.4 3.7 shampoo_conv.6
  417.2 5.5 %collective-permute-done.111 = bf16[576,128]{1,0:T(8,128)(2,1)S(1)} collective-permute-done((bf16[576,128]{1,0:T(8,128)(2,1)S(1)}, bf16[576,128]{1,0:T(8,128)(2,1)S(1)}, u32[]{:S(2)}, u32[]{:S(2)}) %collective-permute-start.111) | collective-permute-done | bytes 147488 | tf_op jit(solution)/shard_map/ppermute | solution.py:54
  434.2 3.7 shampoo_conv.7
  437.9 3.7 shampoo_conv.8
  442.2 3.7 shampoo_conv.9
  447.3 7.4 %shampoo_proj.1 = (f32[3,2,4,128,128]{4,3,2,1,0:T(8,128)}, f32[3,2,4,128,128]{4,3,2,1,0:T(8,128)}, f32[3,2,4,128,128]{4,3,2,1,0:T(8,128)}, f32[3,2,4,128,128]{4,3,2,1,0:T(8,128)}) custom-call(bf16[3,2,4,128,128]{4,3,2,1,0:T(8,128)(2,1)} %bitcast.320, f32[3,2,4,128,128]{4,3,2,1,0:T(8,128)} %left.11, f32[3,2,4,128,128]{4,3,2,1,0:T(8,128)} %right.11, ...), custom_call_target="tpu_custom_call" | custom-call | flops 25165824 | bytes 884736 | tf_op jit(solution)/shard_map/shampoo_proj/pallas_call | solution.py:1404
  (481 shorter events, 144.0 us)
Async XLA Ops:
  7.2 170.4 %all-gather.3.cloned.1.call-start = ((), (), s32[]{:S(2)}) async-start(), calls=%async_computation.4 | async-start | bytes 7520256 | tf_op jit(solution)/shard_map/all_gather | solution.py:1551
  8.3 9.9 %collective-permute-start.1 = (bf16[64,512]{1,0:T(8,128)(2,1)S(1)}, bf16[64,512]{1,0:T(8,128)(2,1)S(1)}, u32[]{:S(2)}, u32[]{:S(2)}) collective-permute-start(bf16[64,512]{1,0:T(8,128)(2,1)S(1)} %bitcast.352), channel_id=1, source_target_pairs={{0,2},{2,0},{4,6},{6,4},{1,3},{3,1},{5,7},{7,5},{8,10},{10,8},{12,... | collective-permute-start | bytes 196616 | tf_op jit(solution)/shard_map/ppermute | solution.py:83
  14.3 10.6 %collective-permute-start = (bf16[1,9,64,128]{3,2,1,0:T(8,128)(2,1)S(1)}, bf16[1,9,64,128]{3,2,1,0:T(8,128)(2,1)S(1)}, u32[]{:S(2)}, u32[]{:S(2)}) collective-permute-start(bf16[1,9,64,128]{3,2,1,0:T(8,128)(2,1)S(1)} %get-tuple-element.286), channel_id=1, source_target_pairs={{0,4},{2,6},{4,0},{6,2},{1,5},{3,7},{5,1},{7,3},{8,12},{10,14},{12... | collective-permute-start | bytes 442376 | tf_op jit(solution)/shard_map/ppermute | solution.py:54
  29.2 10.0 %collective-permute-start.10 = (bf16[18,4,512]{2,1,0:T(4,128)(2,1)S(1)}, bf16[18,4,512]{2,1,0:T(4,128)(2,1)}, u32[]{:S(2)}, u32[]{:S(2)}) collective-permute-start(bf16[18,4,512]{2,1,0:T(4,128)(2,1)S(1)} %maximum_select_fusion), channel_id=1, source_target_pairs={{0,1},{1,0},{2,3},{3,2},{4,5},{5,4},{6,7},{7,6},{8,9},{9,8},{10,11... | collective-permute-start | bytes 221192 | tf_op jit(solution)/shard_map/ppermute | solution.py:54
  30.4 17.6 %collective-permute-start.12 = (bf16[2,9,64,128]{3,2,1,0:T(8,128)(2,1)S(1)}, bf16[2,9,64,128]{3,2,1,0:T(8,128)(2,1)S(1)}, u32[]{:S(2)}, u32[]{:S(2)}) collective-permute-start(bf16[2,9,64,128]{3,2,1,0:T(8,128)(2,1)S(1)} %pad_maximum_fusion.9.refs_0_), channel_id=1, source_target_pairs={{0,1},{1,0},{2,3},{3,2},{4,5},{5,4},{6,7},{7,6},{8,9},{9,8},{10,11... | collective-permute-start | bytes 884744 | tf_op jit(solution)/shard_map/ppermute | solution.py:54
  33.8 12.1 %collective-permute-start.7 = (bf16[2,9,64,128]{3,2,1,0:T(8,128)(2,1)S(1)}, bf16[2,9,64,128]{3,2,1,0:T(8,128)(2,1)S(1)}, u32[]{:S(2)}, u32[]{:S(2)}) collective-permute-start(bf16[2,9,64,128]{3,2,1,0:T(8,128)(2,1)S(1)} %collective-permute-done.3.refs_1_), channel_id=1, source_target_pairs={{0,16},{8,24},{16,0},{24,8},{1,17},{9,25},{17,1},{25,9},{2,18},{10... | collective-permute-start | bytes 884744 | tf_op jit(solution)/shard_map/ppermute | solution.py:54
  35.3 10.6 %collective-permute-start.8 = (bf16[2,9,64,128]{3,2,1,0:T(8,128)(2,1)S(1)}, bf16[2,9,64,128]{3,2,1,0:T(8,128)(2,1)S(1)}, u32[]{:S(2)}, u32[]{:S(2)}) collective-permute-start(bf16[2,9,64,128]{3,2,1,0:T(8,128)(2,1)S(1)} %collective-permute-done.3.refs_1_), channel_id=1, source_target_pairs={{0,8},{8,0},{16,24},{24,16},{1,9},{9,1},{17,25},{25,17},{2,10},{10... | collective-permute-start | bytes 884744 | tf_op jit(solution)/shard_map/ppermute | solution.py:54
  35.9 10.1 %collective-permute-start.4 = (bf16[1,9,64,128]{3,2,1,0:T(8,128)(2,1)}, bf16[1,9,64,128]{3,2,1,0:T(8,128)(2,1)S(1)}, u32[]{:S(2)}, u32[]{:S(2)}) collective-permute-start(bf16[1,9,64,128]{3,2,1,0:T(8,128)(2,1)} %get-tuple-element.146), channel_id=1, source_target_pairs={{0,4},{2,6},{4,0},{6,2},{1,5},{3,7},{5,1},{7,3},{8,12},{10,14},{12... | collective-permute-start | bytes 442376 | tf_op jit(solution)/shard_map/ppermute | solution.py:54
  53.5 15.3 %collective-permute-start.20 = (bf16[2,9,64,128]{3,2,1,0:T(8,128)(2,1)S(1)}, bf16[2,9,64,128]{3,2,1,0:T(8,128)(2,1)}, u32[]{:S(2)}, u32[]{:S(2)}) collective-permute-start(bf16[2,9,64,128]{3,2,1,0:T(8,128)(2,1)S(1)} %pad_maximum_fusion.10.refs_0_), channel_id=1, source_target_pairs={{0,2},{2,0},{4,6},{6,4},{1,3},{3,1},{5,7},{7,5},{8,10},{10,8},{12,... | collective-permute-start | bytes 884744 | tf_op jit(solution)/shard_map/ppermute | solution.py:54
  54.0 14.9 %collective-permute-start.21 = (bf16[2,9,64,128]{3,2,1,0:T(8,128)(2,1)S(1)}, bf16[2,9,64,128]{3,2,1,0:T(8,128)(2,1)}, u32[]{:S(2)}, u32[]{:S(2)}) collective-permute-start(bf16[2,9,64,128]{3,2,1,0:T(8,128)(2,1)S(1)} %pad_maximum_fusion.10.refs_0_), channel_id=1, source_target_pairs={{0,8},{8,0},{16,24},{24,16},{1,9},{9,1},{17,25},{25,17},{2,10},{10... | collective-permute-start | bytes 884744 | tf_op jit(solution)/shard_map/ppermute | solution.py:54
  55.5 13.4 %collective-permute-start.22 = (bf16[2,9,64,128]{3,2,1,0:T(8,128)(2,1)S(1)}, bf16[2,9,64,128]{3,2,1,0:T(8,128)(2,1)}, u32[]{:S(2)}, u32[]{:S(2)}) collective-permute-start(bf16[2,9,64,128]{3,2,1,0:T(8,128)(2,1)S(1)} %pad_maximum_fusion.10.refs_0_), channel_id=1, source_target_pairs={{0,16},{8,24},{16,0},{24,8},{1,17},{9,25},{17,1},{25,9},{2,18},{10... | collective-permute-start | bytes 884744 | tf_op jit(solution)/shard_map/ppermute | solution.py:54
  68.9 159.3 %reduce-scatter.3.cloned.1.call-start = ((), (), s32[]{:S(2)}) async-start(), calls=%async_computation.2 | async-start | bytes 21233664 | tf_op jit(solution)/shard_map/reduce_scatter | solution.py:1609
  69.8 28.1 %collective-permute-start.33 = (bf16[2,9,64,128]{3,2,1,0:T(8,128)(2,1)}, bf16[2,9,64,128]{3,2,1,0:T(8,128)(2,1)S(1)}, u32[]{:S(2)}, u32[]{:S(2)}) collective-permute-start(bf16[2,9,64,128]{3,2,1,0:T(8,128)(2,1)} %collective-permute-done.20.refs_1_), channel_id=1, source_target_pairs={{0,8},{8,0},{16,24},{24,16},{1,9},{9,1},{17,25},{25,17},{2,10},{10... | collective-permute-start | bytes 884744 | tf_op jit(solution)/shard_map/ppermute | solution.py:54
  70.4 27.5 %collective-permute-start.34 = (bf16[2,9,64,128]{3,2,1,0:T(8,128)(2,1)}, bf16[2,9,64,128]{3,2,1,0:T(8,128)(2,1)S(1)}, u32[]{:S(2)}, u32[]{:S(2)}) collective-permute-start(bf16[2,9,64,128]{3,2,1,0:T(8,128)(2,1)} %collective-permute-done.20.refs_1_), channel_id=1, source_target_pairs={{0,16},{8,24},{16,0},{24,8},{1,17},{9,25},{17,1},{25,9},{2,18},{10... | collective-permute-start | bytes 884744 | tf_op jit(solution)/shard_map/ppermute | solution.py:54
  88.4 8.1 %collective-permute-start.31 = (f32[2,512]{1,0:T(2,128)S(1)}, f32[2,512]{1,0:T(2,128)S(1)}, u32[]{:S(2)}, u32[]{:S(2)}) collective-permute-start(f32[2,512]{1,0:T(2,128)S(1)} %add_add_fusion.7), channel_id=1, source_target_pairs={{0,16},{8,24},{16,0},{24,8},{1,17},{9,25},{17,1},{25,9},{2,18},{10... | collective-permute-start | bytes 12296 | tf_op jit(solution)/shard_map/ppermute | solution.py:54
  88.5 8.8 %collective-permute-start.30 = (f32[2,512]{1,0:T(2,128)S(1)}, f32[2,512]{1,0:T(2,128)S(1)}, u32[]{:S(2)}, u32[]{:S(2)}) collective-permute-start(f32[2,512]{1,0:T(2,128)S(1)} %add_add_fusion.7), channel_id=1, source_target_pairs={{0,8},{8,0},{16,24},{24,16},{1,9},{9,1},{17,25},{25,17},{2,10},{10... | collective-permute-start | bytes 12296 | tf_op jit(solution)/shard_map/ppermute | solution.py:54
  90.1 12.9 %collective-permute-start.59 = (bf16[3,1,4,8,512]{4,3,2,1,0:T(8,128)(2,1)S(1)}, bf16[3,1,4,8,512]{4,3,2,1,0:T(8,128)(2,1)S(1)}, u32[]{:S(2)}, u32[]{:S(2)}) collective-permute-start(bf16[3,1,4,8,512]{4,3,2,1,0:T(8,128)(2,1)S(1)} %get-tuple-element.282), channel_id=1, source_target_pairs={{0,2},{2,0},{4,6},{6,4},{1,3},{3,1},{5,7},{7,5},{8,10},{10,8},{12,... | collective-permute-start | bytes 294920 | tf_op jit(solution)/shard_map/ppermute | solution.py:83
  103.8 12.3 %collective-permute-start.41 = (bf16[2,9,64,128]{3,2,1,0:T(8,128)(2,1)}, bf16[2,9,64,128]{3,2,1,0:T(8,128)(2,1)}, u32[]{:S(2)}, u32[]{:S(2)}) collective-permute-start(bf16[2,9,64,128]{3,2,1,0:T(8,128)(2,1)} %collective-permute-done.21.refs_2_), channel_id=1, source_target_pairs={{0,16},{8,24},{16,0},{24,8},{1,17},{9,25},{17,1},{25,9},{2,18},{10... | collective-permute-start | bytes 884744 | tf_op jit(solution)/shard_map/ppermute | solution.py:54
  105.0 11.9 %collective-permute-start.43 = (bf16[2,9,64,128]{3,2,1,0:T(8,128)(2,1)S(1)}, bf16[2,9,64,128]{3,2,1,0:T(8,128)(2,1)}, u32[]{:S(2)}, u32[]{:S(2)}) collective-permute-start(bf16[2,9,64,128]{3,2,1,0:T(8,128)(2,1)S(1)} %collective-permute-done.34.refs_5_), channel_id=1, source_target_pairs={{0,8},{8,0},{16,24},{24,16},{1,9},{9,1},{17,25},{25,17},{2,10},{10... | collective-permute-start | bytes 884744 | tf_op jit(solution)/shard_map/ppermute | solution.py:54
  107.4 11.0 %collective-permute-start.61 = (bf16[3,10,4,1,512]{4,3,2,1,0:T(2,128)(2,1)}, bf16[3,10,4,1,512]{4,3,2,1,0:T(2,128)(2,1)}, u32[]{:S(2)}, u32[]{:S(2)}) collective-permute-start(bf16[3,10,4,1,512]{4,3,2,1,0:T(2,128)(2,1)} %broadcast_select_fusion.2), channel_id=1, source_target_pairs={{0,1},{1,0},{2,3},{3,2},{4,5},{5,4},{6,7},{7,6},{8,9},{9,8},{10,11... | collective-permute-start | bytes 368648 | tf_op jit(solution)/shard_map/ppermute | solution.py:54
  121.5 13.8 %collective-permute-start.48 = (f32[2,384]{1,0:T(2,128)S(1)}, f32[2,384]{1,0:T(2,128)S(1)}, u32[]{:S(2)}, u32[]{:S(2)}) collective-permute-start(f32[2,384]{1,0:T(2,128)S(1)} %add.316), channel_id=1, source_target_pairs={{0,24},{8,16},{16,8},{24,0},{1,25},{9,17},{17,9},{25,1},{2,26},{10... | collective-permute-start | bytes 9224 | tf_op jit(solution)/shard_map/ppermute | solution.py:54
  123.0 12.3 %collective-permute-start.47 = (f32[2,384]{1,0:T(2,128)S(1)}, f32[2,384]{1,0:T(2,128)S(1)}, u32[]{:S(2)}, u32[]{:S(2)}) collective-permute-start(f32[2,384]{1,0:T(2,128)S(1)} %add.316), channel_id=1, source_target_pairs={{0,16},{8,24},{16,0},{24,8},{1,17},{9,25},{17,1},{25,9},{2,18},{10... | collective-permute-start | bytes 9224 | tf_op jit(solution)/shard_map/ppermute | solution.py:54
  123.5 11.9 %collective-permute-start.46 = (f32[2,384]{1,0:T(2,128)S(1)}, f32[2,384]{1,0:T(2,128)S(1)}, u32[]{:S(2)}, u32[]{:S(2)}) collective-permute-start(f32[2,384]{1,0:T(2,128)S(1)} %add.316), channel_id=1, source_target_pairs={{0,8},{8,0},{16,24},{24,16},{1,9},{9,1},{17,25},{25,17},{2,10},{10... | collective-permute-start | bytes 9224 | tf_op jit(solution)/shard_map/ppermute | solution.py:54
  135.4 10.8 %collective-permute-start.51 = (f32[2,384]{1,0:T(2,128)S(1)}, f32[2,384]{1,0:T(2,128)S(1)}, u32[]{:S(2)}, u32[]{:S(2)}) collective-permute-start(f32[2,384]{1,0:T(2,128)S(1)} %add_add_fusion.11), channel_id=1, source_target_pairs={{0,6},{2,4},{4,2},{6,0},{1,7},{3,5},{5,3},{7,1},{8,14},{10,12},{12... | collective-permute-start | bytes 9224 | tf_op jit(solution)/shard_map/ppermute | solution.py:54
  137.3 9.0 %collective-permute-start.50 = (f32[2,384]{1,0:T(2,128)S(1)}, f32[2,384]{1,0:T(2,128)S(1)}, u32[]{:S(2)}, u32[]{:S(2)}) collective-permute-start(f32[2,384]{1,0:T(2,128)S(1)} %add_add_fusion.11), channel_id=1, source_target_pairs={{0,4},{2,6},{4,0},{6,2},{1,5},{3,7},{5,1},{7,3},{8,12},{10,14},{12... | collective-permute-start | bytes 9224 | tf_op jit(solution)/shard_map/ppermute | solution.py:54
  155.3 8.7 %collective-permute-start.56 = (bf16[64,512]{1,0:T(8,128)(2,1)S(1)}, bf16[64,512]{1,0:T(8,128)(2,1)S(1)}, u32[]{:S(2)}, u32[]{:S(2)}) collective-permute-start(bf16[64,512]{1,0:T(8,128)(2,1)S(1)} %get-tuple-element.312), channel_id=1, source_target_pairs={{0,2},{2,0},{4,6},{6,4},{1,3},{3,1},{5,7},{7,5},{8,10},{10,8},{12,... | collective-permute-start | bytes 196616 | tf_op jit(solution)/shard_map/ppermute | solution.py:83
  155.6 8.4 %collective-permute-start.57 = (bf16[64,512]{1,0:T(8,128)(2,1)S(1)}, bf16[64,512]{1,0:T(8,128)(2,1)S(1)}, u32[]{:S(2)}, u32[]{:S(2)}) collective-permute-start(bf16[64,512]{1,0:T(8,128)(2,1)S(1)} %get-tuple-element.313), channel_id=1, source_target_pairs={{0,0},{2,4},{4,2},{6,6},{1,1},{3,5},{5,3},{7,7},{8,8},{10,12},{12,... | collective-permute-start | bytes 196616 | tf_op jit(solution)/shard_map/ppermute | solution.py:83
  177.6 11.6 %collective-permute-start.65 = (bf16[16,27,64,128]{3,2,1,0:T(8,128)(2,1)}, bf16[16,27,64,128]{3,2,1,0:T(8,128)(2,1)}, u32[]{:S(2)}, u32[]{:S(2)}) collective-permute-start(bf16[16,27,64,128]{3,2,1,0:T(8,128)(2,1)} %bitcast.304), channel_id=1, source_target_pairs={{0,1},{1,0},{2,3},{3,2},{4,5},{5,4},{6,7},{7,6},{8,9},{9,8},{10,11... | collective-permute-start | bytes 21233672 | tf_op jit(solution)/shard_map/ppermute | solution.py:54
  198.7 195.1 %reduce-scatter.5.cloned.1.call-start = ((), (), s32[]{:S(2)}) async-start(), calls=%async_computation.3 | async-start | bytes 7520256 | tf_op jit(solution)/shard_map/reduce_scatter | solution.py:1619
  229.1 17.5 %collective-permute-start.70 = (bf16[64,512]{1,0:T(8,128)(2,1)S(1)}, bf16[64,512]{1,0:T(8,128)(2,1)S(1)}, u32[]{:S(2)}, u32[]{:S(2)}) collective-permute-start(bf16[64,512]{1,0:T(8,128)(2,1)S(1)} %get-tuple-element.306), channel_id=1, source_target_pairs={{0,2},{2,0},{4,6},{6,4},{1,3},{3,1},{5,7},{7,5},{8,10},{10,8},{12,... | collective-permute-start | bytes 196616 | tf_op jit(solution)/shard_map/ppermute | solution.py:83
  229.2 17.4 %collective-permute-start.71 = (bf16[64,512]{1,0:T(8,128)(2,1)S(1)}, bf16[64,512]{1,0:T(8,128)(2,1)S(1)}, u32[]{:S(2)}, u32[]{:S(2)}) collective-permute-start(bf16[64,512]{1,0:T(8,128)(2,1)S(1)} %get-tuple-element.307), channel_id=1, source_target_pairs={{0,0},{2,4},{4,2},{6,6},{1,1},{3,5},{5,3},{7,7},{8,8},{10,12},{12,... | collective-permute-start | bytes 196616 | tf_op jit(solution)/shard_map/ppermute | solution.py:83
  230.2 16.4 %collective-permute-start.69 = (f32[14,512]{1,0:T(8,128)S(1)}, f32[14,512]{1,0:T(8,128)S(1)}, u32[]{:S(2)}, u32[]{:S(2)}) collective-permute-start(f32[14,512]{1,0:T(8,128)S(1)} %add.330), channel_id=1, source_target_pairs={{0,6},{2,4},{4,2},{6,0},{1,7},{3,5},{5,3},{7,1},{8,14},{10,12},{12... | collective-permute-start | bytes 86024 | tf_op jit(solution)/shard_map/ppermute | solution.py:54
  231.3 15.3 %collective-permute-start.68 = (f32[14,512]{1,0:T(8,128)S(1)}, f32[14,512]{1,0:T(8,128)S(1)}, u32[]{:S(2)}, u32[]{:S(2)}) collective-permute-start(f32[14,512]{1,0:T(8,128)S(1)} %add.330), channel_id=1, source_target_pairs={{0,4},{2,6},{4,0},{6,2},{1,5},{3,7},{5,1},{7,3},{8,12},{10,14},{12... | collective-permute-start | bytes 86024 | tf_op jit(solution)/shard_map/ppermute | solution.py:54
  235.0 11.6 %collective-permute-start.67 = (f32[14,512]{1,0:T(8,128)S(1)}, f32[14,512]{1,0:T(8,128)S(1)}, u32[]{:S(2)}, u32[]{:S(2)}) collective-permute-start(f32[14,512]{1,0:T(8,128)S(1)} %add.330), channel_id=1, source_target_pairs={{0,2},{2,0},{4,6},{6,4},{1,3},{3,1},{5,7},{7,5},{8,10},{10,8},{12,... | collective-permute-start | bytes 86024 | tf_op jit(solution)/shard_map/ppermute | solution.py:54
  267.0 9.2 %collective-permute-start.79 = (f32[2,384]{1,0:T(2,128)S(1)}, f32[2,384]{1,0:T(2,128)S(1)}, u32[]{:S(2)}, u32[]{:S(2)}) collective-permute-start(f32[2,384]{1,0:T(2,128)S(1)} %add.337), channel_id=1, source_target_pairs={{0,6},{2,4},{4,2},{6,0},{1,7},{3,5},{5,3},{7,1},{8,14},{10,12},{12... | collective-permute-start | bytes 9224 | tf_op jit(solution)/shard_map/ppermute | solution.py:54
  276.2 13.1 %collective-permute-start.82 = (f32[2,384]{1,0:T(2,128)S(1)}, f32[2,384]{1,0:T(2,128)S(1)}, u32[]{:S(2)}, u32[]{:S(2)}) collective-permute-start(f32[2,384]{1,0:T(2,128)S(1)} %add_add_fusion.9), channel_id=1, source_target_pairs={{0,24},{8,16},{16,8},{24,0},{1,25},{9,17},{17,9},{25,1},{2,26},{10... | collective-permute-start | bytes 9224 | tf_op jit(solution)/shard_map/ppermute | solution.py:54
  277.7 11.7 %collective-permute-start.81 = (f32[2,384]{1,0:T(2,128)S(1)}, f32[2,384]{1,0:T(2,128)S(1)}, u32[]{:S(2)}, u32[]{:S(2)}) collective-permute-start(f32[2,384]{1,0:T(2,128)S(1)} %add_add_fusion.9), channel_id=1, source_target_pairs={{0,16},{8,24},{16,0},{24,8},{1,17},{9,25},{17,1},{25,9},{2,18},{10... | collective-permute-start | bytes 9224 | tf_op jit(solution)/shard_map/ppermute | solution.py:54
  278.4 11.0 %collective-permute-start.80 = (f32[2,384]{1,0:T(2,128)S(1)}, f32[2,384]{1,0:T(2,128)S(1)}, u32[]{:S(2)}, u32[]{:S(2)}) collective-permute-start(f32[2,384]{1,0:T(2,128)S(1)} %add_add_fusion.9), channel_id=1, source_target_pairs={{0,8},{8,0},{16,24},{24,16},{1,9},{9,1},{17,25},{25,17},{2,10},{10... | collective-permute-start | bytes 9224 | tf_op jit(solution)/shard_map/ppermute | solution.py:54
  299.5 19.2 %collective-permute-start.87 = (bf16[64,512]{1,0:T(8,128)(2,1)S(1)}, bf16[64,512]{1,0:T(8,128)(2,1)S(1)}, u32[]{:S(2)}, u32[]{:S(2)}) collective-permute-start(bf16[64,512]{1,0:T(8,128)(2,1)S(1)} %get-tuple-element.300), channel_id=1, source_target_pairs={{0,2},{2,0},{4,6},{6,4},{1,3},{3,1},{5,7},{7,5},{8,10},{10,8},{12,... | collective-permute-start | bytes 196616 | tf_op jit(solution)/shard_map/ppermute | solution.py:83
  300.3 18.4 %collective-permute-start.88 = (bf16[64,512]{1,0:T(8,128)(2,1)S(1)}, bf16[64,512]{1,0:T(8,128)(2,1)S(1)}, u32[]{:S(2)}, u32[]{:S(2)}) collective-permute-start(bf16[64,512]{1,0:T(8,128)(2,1)S(1)} %get-tuple-element.301), channel_id=1, source_target_pairs={{0,0},{2,4},{4,2},{6,6},{1,1},{3,5},{5,3},{7,7},{8,8},{10,12},{12,... | collective-permute-start | bytes 196616 | tf_op jit(solution)/shard_map/ppermute | solution.py:83
  302.9 15.8 %collective-permute-start.86 = (f32[2,512]{1,0:T(2,128)S(1)}, f32[2,512]{1,0:T(2,128)S(1)}, u32[]{:S(2)}, u32[]{:S(2)}) collective-permute-start(f32[2,512]{1,0:T(2,128)S(1)} %add.344), channel_id=1, source_target_pairs={{0,6},{2,4},{4,2},{6,0},{1,7},{3,5},{5,3},{7,1},{8,14},{10,12},{12... | collective-permute-start | bytes 12296 | tf_op jit(solution)/shard_map/ppermute | solution.py:54
  305.8 12.9 %collective-permute-start.85 = (f32[2,512]{1,0:T(2,128)S(1)}, f32[2,512]{1,0:T(2,128)S(1)}, u32[]{:S(2)}, u32[]{:S(2)}) collective-permute-start(f32[2,512]{1,0:T(2,128)S(1)} %add.344), channel_id=1, source_target_pairs={{0,4},{2,6},{4,0},{6,2},{1,5},{3,7},{5,1},{7,3},{8,12},{10,14},{12... | collective-permute-start | bytes 12296 | tf_op jit(solution)/shard_map/ppermute | solution.py:54
  308.8 9.8 %collective-permute-start.84 = (f32[2,512]{1,0:T(2,128)S(1)}, f32[2,512]{1,0:T(2,128)S(1)}, u32[]{:S(2)}, u32[]{:S(2)}) collective-permute-start(f32[2,512]{1,0:T(2,128)S(1)} %add.344), channel_id=1, source_target_pairs={{0,2},{2,0},{4,6},{6,4},{1,3},{3,1},{5,7},{7,5},{8,10},{10,8},{12,... | collective-permute-start | bytes 12296 | tf_op jit(solution)/shard_map/ppermute | solution.py:54
  328.9 16.4 %collective-permute-start.94 = (bf16[2,672,128]{2,1,0:T(8,128)(2,1)S(1)}, bf16[2,672,128]{2,1,0:T(8,128)(2,1)S(1)}, u32[]{:S(2)}, u32[]{:S(2)}) collective-permute-start(bf16[2,672,128]{2,1,0:T(8,128)(2,1)S(1)} %get-tuple-element.289), channel_id=1, source_target_pairs={{0,8},{8,0},{16,24},{24,16},{1,9},{9,1},{17,25},{25,17},{2,10},{10... | collective-permute-start | bytes 1032200 | tf_op jit(solution)/shard_map/ppermute | solution.py:54
  330.4 15.3 %collective-permute-start.95 = (bf16[2,672,128]{2,1,0:T(8,128)(2,1)S(1)}, bf16[2,672,128]{2,1,0:T(8,128)(2,1)S(1)}, u32[]{:S(2)}, u32[]{:S(2)}) collective-permute-start(bf16[2,672,128]{2,1,0:T(8,128)(2,1)S(1)} %get-tuple-element.288), channel_id=1, source_target_pairs={{0,16},{8,24},{16,0},{24,8},{1,17},{9,25},{17,1},{25,9},{2,18},{10... | collective-permute-start | bytes 1032200 | tf_op jit(solution)/shard_map/ppermute | solution.py:54
  346.6 12.5 %collective-permute-start.98 = (bf16[2,672,128]{2,1,0:T(8,128)(2,1)S(1)}, bf16[2,672,128]{2,1,0:T(8,128)(2,1)S(1)}, u32[]{:S(2)}, u32[]{:S(2)}) collective-permute-start(bf16[2,672,128]{2,1,0:T(8,128)(2,1)S(1)} %fusion.14), channel_id=1, source_target_pairs={{0,16},{8,24},{16,0},{24,8},{1,17},{9,25},{17,1},{25,9},{2,18},{10... | collective-permute-start | bytes 1032200 | tf_op jit(solution)/shard_map/ppermute | solution.py:54
  348.8 11.0 %collective-permute-start.97 = (bf16[2,672,128]{2,1,0:T(8,128)(2,1)S(1)}, bf16[2,672,128]{2,1,0:T(8,128)(2,1)S(1)}, u32[]{:S(2)}, u32[]{:S(2)}) collective-permute-start(bf16[2,672,128]{2,1,0:T(8,128)(2,1)S(1)} %fusion.8), channel_id=1, source_target_pairs={{0,8},{8,0},{16,24},{24,16},{1,9},{9,1},{17,25},{25,17},{2,10},{10... | collective-permute-start | bytes 1032200 | tf_op jit(solution)/shard_map/ppermute | solution.py:54
  351.2 23.6 %collective-permute-start.103 = (bf16[2,672,128]{2,1,0:T(8,128)(2,1)}, bf16[2,672,128]{2,1,0:T(8,128)(2,1)}, u32[]{:S(2)}, u32[]{:S(2)}) collective-permute-start(bf16[2,672,128]{2,1,0:T(8,128)(2,1)} %fusion.7), channel_id=1, source_target_pairs={{0,16},{8,24},{16,0},{24,8},{1,17},{9,25},{17,1},{25,9},{2,18},{10... | collective-permute-start | bytes 1032200 | tf_op jit(solution)/shard_map/ppermute | solution.py:54
  351.8 23.1 %collective-permute-start.102 = (bf16[2,672,128]{2,1,0:T(8,128)(2,1)}, bf16[2,672,128]{2,1,0:T(8,128)(2,1)}, u32[]{:S(2)}, u32[]{:S(2)}) collective-permute-start(bf16[2,672,128]{2,1,0:T(8,128)(2,1)} %fusion.15), channel_id=1, source_target_pairs={{0,8},{8,0},{16,24},{24,16},{1,9},{9,1},{17,25},{25,17},{2,10},{10... | collective-permute-start | bytes 1032200 | tf_op jit(solution)/shard_map/ppermute | solution.py:54
  360.7 14.1 %collective-permute-start.101 = (bf16[2,672,128]{2,1,0:T(8,128)(2,1)}, bf16[2,672,128]{2,1,0:T(8,128)(2,1)}, u32[]{:S(2)}, u32[]{:S(2)}) collective-permute-start(bf16[2,672,128]{2,1,0:T(8,128)(2,1)} %fusion.6), channel_id=1, source_target_pairs={{0,2},{2,0},{4,6},{6,4},{1,3},{3,1},{5,7},{7,5},{8,10},{10,8},{12,... | collective-permute-start | bytes 1032200 | tf_op jit(solution)/shard_map/ppermute | solution.py:54
  363.7 11.1 %collective-permute-start.99 = (bf16[2,576,128]{2,1,0:T(8,128)(2,1)}, bf16[2,576,128]{2,1,0:T(8,128)(2,1)}, u32[]{:S(2)}, u32[]{:S(2)}) collective-permute-start(bf16[2,576,128]{2,1,0:T(8,128)(2,1)} %get-tuple-element.291), channel_id=1, source_target_pairs={{0,8},{8,0},{16,24},{24,16},{1,9},{9,1},{17,25},{25,17},{2,10},{10... | collective-permute-start | bytes 884744 | tf_op jit(solution)/shard_map/ppermute | solution.py:54
  364.7 10.1 %collective-permute-start.100 = (bf16[2,576,128]{2,1,0:T(8,128)(2,1)}, bf16[2,576,128]{2,1,0:T(8,128)(2,1)}, u32[]{:S(2)}, u32[]{:S(2)}) collective-permute-start(bf16[2,576,128]{2,1,0:T(8,128)(2,1)} %get-tuple-element.290), channel_id=1, source_target_pairs={{0,16},{8,24},{16,0},{24,8},{1,17},{9,25},{17,1},{25,9},{2,18},{10... | collective-permute-start | bytes 884744 | tf_op jit(solution)/shard_map/ppermute | solution.py:54
  382.9 9.6 %collective-permute-start.106 = (bf16[672,128]{1,0:T(8,128)(2,1)S(1)}, bf16[672,128]{1,0:T(8,128)(2,1)S(1)}, u32[]{:S(2)}, u32[]{:S(2)}) collective-permute-start(bf16[672,128]{1,0:T(8,128)(2,1)S(1)} %fusion.18), channel_id=1, source_target_pairs={{0,4},{2,6},{4,0},{6,2},{1,5},{3,7},{5,1},{7,3},{8,12},{10,14},{12... | collective-permute-start | bytes 516104 | tf_op jit(solution)/shard_map/ppermute | solution.py:54
  393.9 9.4 %collective-permute-start.109 = (bf16[2,576,128]{2,1,0:T(8,128)(2,1)S(1)}, bf16[2,576,128]{2,1,0:T(8,128)(2,1)S(1)}, u32[]{:S(2)}, u32[]{:S(2)}) collective-permute-start(bf16[2,576,128]{2,1,0:T(8,128)(2,1)S(1)} %fusion.12), channel_id=1, source_target_pairs={{0,16},{8,24},{16,0},{24,8},{1,17},{9,25},{17,1},{25,9},{2,18},{10... | collective-permute-start | bytes 884744 | tf_op jit(solution)/shard_map/ppermute | solution.py:54
  395.3 9.1 %collective-permute-start.108 = (bf16[2,576,128]{2,1,0:T(8,128)(2,1)S(1)}, bf16[2,576,128]{2,1,0:T(8,128)(2,1)S(1)}, u32[]{:S(2)}, u32[]{:S(2)}) collective-permute-start(bf16[2,576,128]{2,1,0:T(8,128)(2,1)S(1)} %fusion.20), channel_id=1, source_target_pairs={{0,8},{8,0},{16,24},{24,16},{1,9},{9,1},{17,25},{25,17},{2,10},{10... | collective-permute-start | bytes 884744 | tf_op jit(solution)/shard_map/ppermute | solution.py:54
  396.4 8.8 %collective-permute-start.110 = (bf16[2,576,128]{2,1,0:T(8,128)(2,1)S(1)}, bf16[2,576,128]{2,1,0:T(8,128)(2,1)S(1)}, u32[]{:S(2)}, u32[]{:S(2)}) collective-permute-start(bf16[2,576,128]{2,1,0:T(8,128)(2,1)S(1)} %fusion.11), channel_id=1, source_target_pairs={{0,2},{2,0},{4,6},{6,4},{1,3},{3,1},{5,7},{7,5},{8,10},{10,8},{12,... | collective-permute-start | bytes 884744 | tf_op jit(solution)/shard_map/ppermute | solution.py:54
  407.5 9.5 %collective-permute-start.116 = (bf16[1,2,96,128]{3,2,1,0:T(8,128)(2,1)S(1)}, bf16[1,2,96,128]{3,2,1,0:T(8,128)(2,1)S(1)}, u32[]{:S(2)}, u32[]{:S(2)}) collective-permute-start(bf16[1,2,96,128]{3,2,1,0:T(8,128)(2,1)S(1)} %maximum_bitcast_fusion.1), channel_id=1, source_target_pairs={{0,6},{2,4},{4,2},{6,0},{1,7},{3,5},{5,3},{7,1},{8,14},{10,12},{12... | collective-permute-start | bytes 147464 | tf_op jit(solution)/shard_map/ppermute | solution.py:54
  409.4 7.7 %collective-permute-start.114 = (bf16[1,2,96,128]{3,2,1,0:T(8,128)(2,1)S(1)}, bf16[1,2,96,128]{3,2,1,0:T(8,128)(2,1)S(1)}, u32[]{:S(2)}, u32[]{:S(2)}) collective-permute-start(bf16[1,2,96,128]{3,2,1,0:T(8,128)(2,1)S(1)} %maximum_bitcast_fusion.1), channel_id=1, source_target_pairs={{0,2},{2,0},{4,6},{6,4},{1,3},{3,1},{5,7},{7,5},{8,10},{10,8},{12,... | collective-permute-start | bytes 147464 | tf_op jit(solution)/shard_map/ppermute | solution.py:54
  412.9 20.6 %collective-permute-start.117 = (bf16[672,128]{1,0:T(8,128)(2,1)S(1)}, bf16[672,128]{1,0:T(8,128)(2,1)S(1)}, u32[]{:S(2)}, u32[]{:S(2)}) collective-permute-start(bf16[672,128]{1,0:T(8,128)(2,1)S(1)} %fusion.17), channel_id=1, source_target_pairs={{0,1},{1,0},{2,3},{3,2},{4,5},{5,4},{6,7},{7,6},{8,9},{9,8},{10,11... | collective-permute-start | bytes 516104 | tf_op jit(solution)/shard_map/ppermute | solution.py:54
  413.0 9.8 %collective-permute-start.111 = (bf16[576,128]{1,0:T(8,128)(2,1)S(1)}, bf16[576,128]{1,0:T(8,128)(2,1)S(1)}, u32[]{:S(2)}, u32[]{:S(2)}) collective-permute-start(bf16[576,128]{1,0:T(8,128)(2,1)S(1)} %fusion.23), channel_id=1, source_target_pairs={{0,4},{2,6},{4,0},{6,2},{1,5},{3,7},{5,1},{7,3},{8,12},{10,14},{12... | collective-permute-start | bytes 442376 | tf_op jit(solution)/shard_map/ppermute | solution.py:54
  423.8 17.8 %collective-permute-start.112 = (bf16[576,128]{1,0:T(8,128)(2,1)S(1)}, bf16[576,128]{1,0:T(8,128)(2,1)S(1)}, u32[]{:S(2)}, u32[]{:S(2)}) collective-permute-start(bf16[576,128]{1,0:T(8,128)(2,1)S(1)} %fusion.22.mine), channel_id=1, source_target_pairs={{0,1},{1,0},{2,3},{3,2},{4,5},{5,4},{6,7},{7,6},{8,9},{9,8},{10,11... | collective-permute-start | bytes 442376 | tf_op jit(solution)/shard_map/ppermute | solution.py:54
  423.9 22.0 %collective-permute-start.120 = (bf16[1,4,2,96,128]{4,3,2,1,0:T(8,128)(2,1)S(1)}, bf16[1,4,2,96,128]{4,3,2,1,0:T(8,128)(2,1)S(1)}, u32[]{:S(2)}, u32[]{:S(2)}) collective-permute-start(bf16[1,4,2,96,128]{4,3,2,1,0:T(8,128)(2,1)S(1)} %bitcast.324), channel_id=1, source_target_pairs={{0,24},{8,16},{16,8},{24,0},{1,25},{9,17},{17,9},{25,1},{2,26},{10... | collective-permute-start | bytes 589832 | tf_op jit(solution)/shard_map/ppermute | solution.py:54
  425.0 20.9 %collective-permute-start.119 = (bf16[1,4,2,96,128]{4,3,2,1,0:T(8,128)(2,1)S(1)}, bf16[1,4,2,96,128]{4,3,2,1,0:T(8,128)(2,1)S(1)}, u32[]{:S(2)}, u32[]{:S(2)}) collective-permute-start(bf16[1,4,2,96,128]{4,3,2,1,0:T(8,128)(2,1)S(1)} %bitcast.325), channel_id=1, source_target_pairs={{0,16},{8,24},{16,0},{24,8},{1,17},{9,25},{17,1},{25,9},{2,18},{10... | collective-permute-start | bytes 589832 | tf_op jit(solution)/shard_map/ppermute | solution.py:54
  426.4 19.5 %collective-permute-start.118 = (bf16[1,4,2,96,128]{4,3,2,1,0:T(8,128)(2,1)S(1)}, bf16[1,4,2,96,128]{4,3,2,1,0:T(8,128)(2,1)S(1)}, u32[]{:S(2)}, u32[]{:S(2)}) collective-permute-start(bf16[1,4,2,96,128]{4,3,2,1,0:T(8,128)(2,1)S(1)} %bitcast.326), channel_id=1, source_target_pairs={{0,8},{8,0},{16,24},{24,16},{1,9},{9,1},{17,25},{25,17},{2,10},{10... | collective-permute-start | bytes 589832 | tf_op jit(solution)/shard_map/ppermute | solution.py:54
  (113 other events, 755.3 us)
Sparse Core Ops, SparseCore 0:
  69.0 108.5 all-gather.2
  198.8 21.6 reduce-scatter.2
  228.4 162.0 reduce-scatter.4

commit v4 on v3

--- a/solution.py
+++ b/solution.py
@@ -668,7 +668,7 @@
     return slot
 
 
-def da_kernel(idx, go, mine, other, da, wv, ws, sems):
+def task_kernel(idx, go, se, so, mine, other, da, out, wv, ws, sems):
     q = go.shape[3]
     half_h = go.shape[2] - 2
     slot = task_weights(idx, (mine, other), wv, sems)
@@ -702,25 +702,43 @@
                     acc = piece if acc is None else acc + piece
             da[0, :, a, bb] = acc.reshape(half_h, q, C).astype(BF)
 
-
-def task_back(idx, go, pieces):
+    acc = None
+    for dy in range(3):
+        for dx in range(3):
+            if dy == 1:
+                view = so[0, dx]
+            else:
+                view = se[0, dx, dy // 2 : dy // 2 + half_h]
+            piece = jnp.dot(
+                view.reshape(half_h * q, C), tap(wv.at[slot], 3 * dy + dx), preferred_element_type=F32
+            )
+            acc = piece if acc is None else acc + piece
+    out[0] = (acc * 0.25).reshape(half_h, q, C).astype(BF)
+
+
+def task_convs(idx, go, se, so, pieces):
     half_h, q = go.shape[2] - 2, go.shape[3]
-    out = pl.pallas_call(
-        da_kernel,
+    back, out = pl.pallas_call(
+        task_kernel,
         grid=(TASKS,),
-        in_specs=[SM, pl.BlockSpec((1,) + go.shape[1:], lambda t: (t, 0, 0, 0, 0)), ANY, ANY],
-        out_specs=pl.BlockSpec((1, half_h, 2, 2, q, C), lambda t: (t, 0, 0, 0, 0, 0)),
-        out_shape=sds((TASKS, half_h, 2, 2, q, C), BF),
+        in_specs=[SM]
+        + [pl.BlockSpec((1,) + a.shape[1:], lambda t: (t, 0, 0, 0, 0)) for a in (go, se, so)]
+        + [ANY, ANY],
+        out_specs=[
+            pl.BlockSpec((1, half_h, 2, 2, q, C), lambda t: (t, 0, 0, 0, 0, 0)),
+            pl.BlockSpec((1, half_h, q, C), lambda t: (t, 0, 0, 0)),
+        ],
+        out_shape=[sds((TASKS, half_h, 2, 2, q, C), BF), sds((TASKS, half_h, q, C), BF)],
         scratch_shapes=[
             pltpu.VMEM((2,) + WEIGHTS, BF),
             pltpu.VMEM((2, 2, 2, 2, C, C), BF),
             pltpu.SemaphoreType.DMA((2, 2)),
         ],
         compiler_params=params(),
-        cost_estimate=cost(TASKS * 2 * 16 * C * C * half_h * q, 24e6),
-        name="task_back",
-    )(idx, go, *pieces)
-    return out.reshape(TASKS, 2 * half_h, 2 * q, C)
+        cost_estimate=cost(TASKS * 2 * 25 * C * C * half_h * q, 30e6),
+        name="task_convs",
+    )(idx, go, se, so, *pieces)
+    return back.reshape(TASKS, 2 * half_h, 2 * q, C), out
 
 
 def attend_kernel(
@@ -1290,44 +1308,6 @@
         cost_estimate=cost(TASKS * 2 * 9 * C * C * half * q, 24e6),
         name="task_wgrad",
     )(idx, se, so, go)
-
-
-def task_fwd_kernel(idx, se, so, mine, other, out, wv, sems):
-    half, q = so.shape[2], so.shape[3]
-    slot = task_weights(idx, (mine, other), wv, sems)
-    acc = None
-    for dy in range(3):
-        for dx in range(3):
-            if dy == 1:
-                view = so[0, dx]
-            else:
-                view = se[0, dx, dy // 2 : dy // 2 + half]
-            piece = jnp.dot(
-                view.reshape(half * q, C), tap(wv.at[slot], 3 * dy + dx), preferred_element_type=F32
-            )
-            acc = piece if acc is None else acc + piece
-    out[0] = (acc * 0.25).reshape(half, q, C).astype(BF)
-
-
-def task_fwd(idx, se, so, pieces):
-    half, q = so.shape[2], so.shape[3]
-    return pl.pallas_call(
-        task_fwd_kernel,
-        grid=(TASKS,),
-        in_specs=[
-            SM,
-            pl.BlockSpec((1,) + se.shape[1:], lambda t: (t, 0, 0, 0, 0)),
-            pl.BlockSpec((1,) + so.shape[1:], lambda t: (t, 0, 0, 0, 0)),
-            ANY,
-            ANY,
-        ],
-        out_specs=pl.BlockSpec((1, half, q, C), lambda t: (t, 0, 0, 0)),
-        out_shape=sds((TASKS, half, q, C), BF),
-        scratch_shapes=[pltpu.VMEM((2,) + WEIGHTS, BF), pltpu.SemaphoreType.DMA((2, 2))],
-        compiler_params=params(),
-        cost_estimate=cost(TASKS * 2 * 9 * C * C * half * q, 20e6),
-        name="task_fwd",
-    )(idx, se, so, *pieces)
 
 
 def shampoo_steps(grads, left, right, lroot, rroot, weight, rate):
@@ -1602,16 +1582,16 @@
     se, so, pooled = attend(
         idx, s2, gb2, ms, gbu, z2, *halo2, h, hcb, up, batch, count_all
     )
-    wt_mine = after(wt_mine, s2m)
+    wt_mine = after(wt_mine, pooled)
     wt = (wt_mine, swap(wt_mine, "wa", 1))
-    halves_t = task_wgrad(after(idx, wt[1]), se, so, go3)
+    halves_t = after(task_wgrad(after(idx, wt_mine), se, so, go3), wt[1])
     if lax.axis_size("wa") == 2:
         part_t = lax.psum_scatter(halves_t, "wa", scatter_dimension=0, tiled=True)[0]
     else:
         mine_t = lax.dynamic_index_in_dim(halves_t, wa % 2, keepdims=False)
         other_t = lax.dynamic_index_in_dim(halves_t, 1 - wa % 2, keepdims=False)
         part_t = add_low(mine_t, swap(other_t, "wa", 1))
-    da = task_back(after(idx, halves_t), go3, wt)
+    da, task_out = task_convs(after(idx, halves_t), go3, se, so, wt)
     dym, dy2, gsum, *edges2 = attend_back(
         s2, gb2, ms, gbu, z2, h, up, da, cot, batch, count_all
     )
@@ -1622,11 +1602,10 @@
 
     dhalo2 = halo(edges2, batch)
 
-    def run_task_fwd(dep):
-        kept["task_out"] = task_fwd(after(idx, dep), se, so, wt)
-        return (kept["task_out"],) + tuple(dhalo2)
-
-    gsum = sum_all(gsum, ha=run_task_fwd)
+    def with_halo(dep):
+        return dhalo2
+
+    gsum = sum_all(gsum, ha=with_halo)
     dup, dh, dhs = mask_back(ms, gbu, gsum[0:6], hs, gbd, dym, h, hp, up, tall, count_all)
 
     def run_second_back(dep):
@@ -1693,15 +1672,15 @@
     new = shampoo_conv(after(idx, grad1), gradt, gradt_other, state, 18, (), 0)
     r0.near_sum(new[0])
     r0.near_send()
-    proj = ring_gather(gather_proj_core(after(grad1[9 * HB :], r0.near)), "ha")
     new = shampoo_conv(after(idx, r0.near), gradt, gradt_other, state, 18, new, 9)
+    new = shampoo_conv(after(idx, new[0]), gradt, gradt_other, state, 18, new, 18)
     grad0, grad0_other = r0.finish(new[0])
-    proj_total = ring_gather(after(proj, grad0), "img")
-    new = shampoo_conv(after(idx, grad0, proj), gradt, gradt_other, state, 18, new, 18)
+    proj = ring_gather(gather_proj_core(after(grad1[9 * HB :], grad0)), "ha")
     new = shampoo_conv(
-        after(idx, new[0]), grad1[: 9 * HB], grad1_other[: 9 * HB], state, 9, new
+        after(idx, grad0), grad1[: 9 * HB], grad1_other[: 9 * HB], state, 9, new
     )
-    new = shampoo_conv(idx, grad0, grad0_other, state, 0, new)
+    proj_total = ring_gather(after(proj, new[0]), "img")
+    new = shampoo_conv(after(idx, proj), grad0, grad0_other, state, 0, new)
     proj_total = after(proj_total, new[0]).reshape(TASKS, 2, NB, BLK, BLK)
     proj_total, proj_left_new, proj_right_new, proj_weight_new = shampoo_proj(
         proj_total, proj_left, proj_right, proj_left_root, proj_right_root, proj_weight
@@ -1710,7 +1689,7 @@
 
     image_grad = from_rows(image_grad, batch)
     task_out = jnp.transpose(
-        kept["task_out"].reshape(TASKS, half_h, batch, half_w, C), (2, 1, 3, 0, 4)
+        task_out.reshape(TASKS, half_h, batch, half_w, C), (2, 1, 3, 0, 4)
     ).reshape(batch, half_h, half_w, TASKS * C)
     shared_out = jnp.transpose(
         pooled.reshape(half_h, batch, half_w, C), (1, 0, 2, 3)

time: 471 us -> 461 us (0.979)
  Pallas kernels: 186 us -> 178 us
    pallas_call x2 -> x1, Pallas kernels: 26.8 us -> 19.6 us  [task_convs(): pl.pallas_call(task_kernel, grid=(TASKS,), in_specs=[SM] + [pl.BlockSpec(...]
    ppermute x109, waiting for transfers between devices: 58.4 us -> 63.3 us  [swap(): return lax.ppermute(value, axis, pairs(axis, step))]
  transfers between devices with their start and end apart: 124 -> 124, of which waited for: 44 -> 42; matrix products, arithmetic and copies ran while one was open for 13% -> 13% of each run, Pallas kernels for 37% -> 38%
where the time goes in v4:
time: 461 us; the launch traced here: 452 us
  Pallas kernels  178 us (39%)
  starting transfers between devices  122 us (26%)
  waiting for transfers between devices  67.4 us (15%)
  other arithmetic  43.5 us (9%)
  local copies, waits for them, and re-layouts  25.3 us (5%)
  between operations  15.8 us (3%)
    ppermute x109, starting transfers between devices, swap(): return lax.ppermute(value, axis, pairs(axis, step))  106 us
    ppermute x109, waiting for transfers between devices, swap(): return lax.ppermute(value, axis, pairs(axis, step))  63.3 us
    pallas_call x4, Pallas kernels, conv(): pl.pallas_call(functools.partial(conv_kernel, len(pieces), batch, transpo...  39.3 us
    pallas_call x1, Pallas kernels, task_convs(): pl.pallas_call(task_kernel, grid=(TASKS,), in_specs=[SM] + [pl.BlockSpec(...  19.6 us
    pallas_call x2, Pallas kernels, wgrad(): pl.pallas_call(functools.partial(wgrad_kernel, len(extra)), in_specs=[SM,...  18.8 us
    pallas_call x5, Pallas kernels, shampoo_conv(): pl.pallas_call(functools.partial(shampoo_kernel, len(prev)), grid=(n // e...  18.7 us
    convert_element_type x16, other arithmetic, add_low(): return total.astype(BF)  17.6 us
    ppermute x12, starting transfers between devices, row_halo(): lax.ppermute(send, 'ha', [(i, pairing.get(i, i)) for i in range(count)])  16.4 us
  transfers between devices with their start and end apart: 124, of which 42 were waited for; matrix products, arithmetic and copies ran while one was open for 13% of the time, Pallas kernels for 38%

profile of v4, /device:TPU:0, one launch (start us, length us, event | category | flops | bytes accessed | tf_op | source)
XLA Modules:
  0.0 452.2 jit_solution(9771354406955093498)
XLA Ops:
  8.3 3.1 collective-permute-start.1
  14.3 3.8 collective-permute-start
  18.9 6.0 %collective-permute-done = bf16[1,9,64,128]{3,2,1,0:T(8,128)(2,1)S(1)} collective-permute-done((bf16[1,9,64,128]{3,2,1,0:T(8,128)(2,1)S(1)}, bf16[1,9,64,128]{3,2,1,0:T(8,128)(2,1)S(1)}, u32[]{:S(2)}, u32[]{:S(2)}) %collective-permute-start) | collective-permute-done | bytes 147488 | tf_op jit(solution)/shard_map/ppermute | solution.py:54
  24.9 1.6 collective-permute-start.5
  35.9 3.4 collective-permute-start.4
  41.0 4.4 shift_copies.1.x_hbm
  48.0 4.1 collective-permute-done.11.refs_6_
  58.5 10.2 %conv_first.1 = (f32[16,64,512]{2,1,0:T(8,128)}, f32[2,512]{1,0:T(2,128)}, bf16[2,64,512]{2,1,0:T(8,128)(2,1)}, f32[16,8,512]{2,1,0:T(8,128)}) custom-call(s32[7]{0:T(128)} %stack.133.idx.idx_ref, bf16[3,18,64,512]{3,2,1,0:T(8,128)(2,1)} %shift_copies.1.x_hbm, bf16[2,9,64,128]{3,2,1,0:T(8,128)(2,1)} %copy-done.5, ...), custom_call_target="tpu_custom_call" | custom-call | flops 301989888 | bytes 625000 | tf_op jit(solution)/shard_map/conv_first/pallas_call | solution.py:504
  72.7 1.8 collective-permute-start.24
  74.4 2.7 collective-permute-start.26
  80.0 3.5 collective-permute-done.27
  89.5 4.6 %collective-permute-start.59 = (bf16[3,1,4,8,512]{4,3,2,1,0:T(8,128)(2,1)S(1)}, bf16[3,1,4,8,512]{4,3,2,1,0:T(8,128)(2,1)S(1)}, u32[]{:S(2)}, u32[]{:S(2)}) collective-permute-start(bf16[3,1,4,8,512]{4,3,2,1,0:T(8,128)(2,1)S(1)} %get-tuple-element.288), channel_id=1, source_target_pairs={{0,2},{2,0},{4,6},{6,4},{1,3},{3,1},{5,7},{7,5},{8,10},{10,8},{12,... | collective-permute-start | bytes 294920 | tf_op jit(solution)/shard_map/ppermute | solution.py:83
  103.7 6.8 %mid.1 = (bf16[3,18,64,512]{3,2,1,0:T(8,128)(2,1)}, f32[1152,384]{1,0:T(8,128)}, f32[144,384]{1,0:T(8,128)}, f32[2,384]{1,0:T(2,128)}) custom-call(s32[7]{0:T(128)} %stack.133.idx.idx_ref, f32[2,512]{1,0:T(2,128)} %add_add_fusion.6.st, f32[2,512]{1,0:T(2,128)} %get-tuple-element.363.gb, f32[16,64,512]{2,1,0:T(8,128)} %get-tuple-element.170.z_ref.z, ...), custom_call_target="tpu_custom_call" | custom-call | flops 28311552 | bytes 625000 | tf_op jit(solution)/shard_map/mid/pallas_call | solution.py:578
  110.5 2.8 collective-permute-done.43.refs_7_
  120.6 10.2 %conv_second.1 = (f32[16,64,512]{2,1,0:T(8,128)}, f32[2,512]{1,0:T(2,128)}, bf16[2,64,512]{2,1,0:T(8,128)(2,1)}, f32[16,8,512]{2,1,0:T(8,128)}) custom-call(s32[7]{0:T(128)} %stack.133.idx.idx_ref, bf16[3,18,64,512]{3,2,1,0:T(8,128)(2,1)} %get-tuple-element.178.x_hbm.u3, bf16[2,9,64,128]{3,2,1,0:T(8,128)(2,1)} %copy-done.6, ...), custom_call_target="tpu_custom_call" | custom-call | flops 301989888 | bytes 625000 | tf_op jit(solution)/shard_map/conv_second/pallas_call | solution.py:504
  130.9 6.2 %collective-permute-start.49 = (f32[2,384]{1,0:T(2,128)S(1)}, f32[2,384]{1,0:T(2,128)S(1)}, u32[]{:S(2)}, u32[]{:S(2)}) collective-permute-start(f32[2,384]{1,0:T(2,128)S(1)} %add_add_fusion.11), channel_id=1, source_target_pairs={{0,2},{2,0},{4,6},{6,4},{1,3},{3,1},{5,7},{7,5},{8,10},{10,8},{12,... | collective-permute-start | bytes 9224 | tf_op jit(solution)/shard_map/ppermute | solution.py:54
  137.8 1.8 collective-permute-start.51
  139.5 1.9 pad_maximum_fusion.go
  143.9 5.9 %hidden.1 = (bf16[1152,384]{1,0:T(8,128)(2,1)}, bf16[144,384]{1,0:T(8,128)(2,1)}, f32[6,512]{1,0:T(8,128)}) custom-call(f32[2,384]{1,0:T(2,128)} %add_add_fusion.10.st.hst, f32[2,384]{1,0:T(2,128)} %slice.567.gb.hgb, f32[1152,384]{1,0:T(8,128)} %get-tuple-element.181.hp, f32[144,384]{1,0:T(8,128)} %get-tuple-element.182.hc, bf16[3,128,512]{2,1,0:T(8,128)(2,1)} %bitcast.304), custom_call_target="tpu_custom_call" | custom-call | flops 28311552 | bytes 312500 | tf_op jit(solution)/shard_map/hidden/pallas_call | solution.py:637
  157.9 2.0 collective-permute-done.55
  162.3 4.7 %collective-permute-start.62 = (f32[8,512]{1,0:T(8,128)S(1)}, f32[8,512]{1,0:T(8,128)S(1)}, u32[]{:S(2)}, u32[]{:S(2)}) collective-permute-start(f32[8,512]{1,0:T(8,128)S(1)} %add_add_fusion.3), channel_id=1, source_target_pairs={{0,2},{2,0},{4,6},{6,4},{1,3},{3,1},{5,7},{7,5},{8,10},{10,8},{12,... | collective-permute-start | bytes 49160 | tf_op jit(solution)/shard_map/ppermute | solution.py:54
  167.0 2.4 collective-permute-start.64
  170.3 2.6 collective-permute-done.63
  174.1 8.6 %attend.1 = (bf16[3,3,9,32,512]{4,3,2,1,0:T(8,128)(2,1)}, bf16[3,3,8,32,512]{4,3,2,1,0:T(8,128)(2,1)}, bf16[8,32,512]{2,1,0:T(8,128)(2,1)}) custom-call(s32[7]{0:T(128)} %stack.133.idx.idx_ref, f32[2,512]{1,0:T(2,128)} %slice.698.st, f32[2,512]{1,0:T(2,128)} %get-tuple-element.362.gb, f32[6,512]{1,0:T(8,128)} %slice.699.mst, f32[6,512]{1,0:T(8,128)} %reshape.298.mgb, ...), custom_call_target="tpu_custom_call" | custom-call | flops 28311552 | bytes 937500 | tf_op jit(solution)/shard_map/attend/pallas_call | solution.py:839
  182.9 9.5 %task_wgrad.1 = bf16[2,16,1728,128]{3,2,1,0:T(8,128)(2,1)} custom-call(s32[7]{0:T(128)} %stack.133.idx.idx_ref, bf16[3,3,9,32,512]{4,3,2,1,0:T(8,128)(2,1)} %get-tuple-element.195.se, bf16[3,3,8,32,512]{4,3,2,1,0:T(8,128)(2,1)} %get-tuple-element.196.so, bf16[3,3,10,32,512]{4,3,2,1,0:T(8,128)(2,1)} %pad_maximum_fusion.go), custom_call_target="tpu_custom_call" | custom-call | flops 226492416 | bytes 1500000 | tf_op jit(solution)/shard_map/task_wgrad/pallas_call | solution.py:1296
  192.4 2.1 collective-permute-done.65.other
  195.4 19.6 %task_convs.1 = (bf16[3,8,2,2,32,512]{5,4,3,2,1,0:T(8,128)(2,1)}, bf16[3,8,32,512]{3,2,1,0:T(8,128)(2,1)}) custom-call(s32[7]{0:T(128)} %stack.133.idx.idx_ref, bf16[3,3,10,32,512]{4,3,2,1,0:T(8,128)(2,1)} %pad_maximum_fusion.go, bf16[3,3,9,32,512]{4,3,2,1,0:T(8,128)(2,1)} %get-tuple-element.195.se, bf16[3,3,8,32,512]{4,3,2,1,0:T(8,128)(2,1)} %get-tuple-element.196.so, ...), custom_call_target="tpu_custom_call" | custom-call | flops 629145600 | bytes 1875000 | tf_op jit(solution)/shard_map/task_convs/pallas_call | solution.py:721
  215.0 11.7 %attend_back.1 = (bf16[3,16,64,512]{3,2,1,0:T(8,128)(2,1)}, f32[16,64,512]{2,1,0:T(8,128)}, f32[14,512]{1,0:T(8,128)}, bf16[2,64,512]{2,1,0:T(8,128)(2,1)}, f32[16,8,512]{2,1,0:T(8,128)}) custom-call(f32[2,512]{1,0:T(2,128)} %slice.698.st, f32[2,512]{1,0:T(2,128)} %get-tuple-element.362.gb, f32[6,512]{1,0:T(8,128)} %slice.699.mst, f32[6,512]{1,0:T(8,128)} %reshape.298.mgb, ...), custom_call_target="tpu_custom_call" | custom-call | flops 25165824 | bytes 937500 | tf_op jit(solution)/shard_map/attend_back/pallas_call | solution.py:923
  230.2 2.6 collective-permute-start.67
  233.6 1.6 collective-permute-start.69
  235.2 6.0 %collective-permute-done.68 = f32[14,512]{1,0:T(8,128)S(1)} collective-permute-done((f32[14,512]{1,0:T(8,128)S(1)}, f32[14,512]{1,0:T(8,128)S(1)}, u32[]{:S(2)}, u32[]{:S(2)}) %collective-permute-start.68) | collective-permute-done | bytes 28704 | tf_op jit(solution)/shard_map/ppermute | solution.py:54
  243.7 3.5 collective-permute-start.75
  247.6 2.1 collective-permute-done.75
  250.3 8.4 %mask_back.1 = (f32[3,128,512]{2,1,0:T(8,128)}, f32[1024,384]{1,0:T(8,128)}, f32[2,384]{1,0:T(2,128)}) custom-call(f32[6,512]{1,0:T(8,128)} %slice.699.mst, f32[6,512]{1,0:T(8,128)} %reshape.298.mgb, f32[6,512]{1,0:T(8,128)} %slice.707.msum, f32[2,384]{1,0:T(2,128)} %add_add_fusion.10.st.hst, f32[2,384]{1,0:T(2,128)} %slice.567.gb.hgb, ...), custom_call_target="tpu_custom_call" | custom-call | flops 75497472 | bytes 500000 | tf_op jit(solution)/shard_map/mask_back/pallas_call | solution.py:1002
  260.9 1.7 collective-permute-start.77
  263.5 1.8 collective-permute-start.79
  265.9 4.2 second_back.1.x_hbm.g_hbm
  271.3 2.1 collective-permute-start.81
  273.6 9.6 %conv_second_back.1.part = f32[16,64,512]{2,1,0:T(8,128)} custom-call(s32[7]{0:T(128)} %stack.133.idx.idx_ref, bf16[3,18,64,512]{3,2,1,0:T(8,128)(2,1)} %second_back.1.x_hbm.g_hbm, bf16[2,9,64,128]{3,2,1,0:T(8,128)(2,1)} %copy-done.6, bf16[2,9,64,128]{3,2,1,0:T(8,128)(2,1)} %collective-permute-done.20.refs_1_, ...), custom_call_target="tpu_custom_call" | custom-call | flops 301989888 | bytes 625000 | tf_op jit(solution)/shard_map/conv_second_back/pallas_call | solution.py:504
  283.9 8.6 %first_back.1 = (f32[512,384]{1,0:T(8,128)}, f32[16,64,512]{2,1,0:T(8,128)}, f32[2,512]{1,0:T(2,128)}, bf16[2,64,512]{2,1,0:T(8,128)(2,1)}, f32[16,8,512]{2,1,0:T(8,128)}) custom-call(f32[2,384]{1,0:T(2,128)} %add_add_fusion.10.st.hst, f32[2,384]{1,0:T(2,128)} %slice.567.gb.hgb, f32[2,384]{1,0:T(2,128)} %add_add_fusion.8.hsum.dhs, ...), custom_call_target="tpu_custom_call" | custom-call | flops 50331648 | bytes 750000 | tf_op jit(solution)/shard_map/first_back/pallas_call | solution.py:1134
  298.7 3.4 collective-permute-start.84
  302.5 2.0 collective-permute-start.86
  304.5 9.8 %wgrad_second.1 = (bf16[4,4,672,128]{3,2,1,0:T(8,128)(2,1)}, bf16[4,4,672,128]{3,2,1,0:T(8,128)(2,1)}) custom-call(s32[7]{0:T(128)} %stack.133.idx.idx_ref, bf16[3,18,64,512]{3,2,1,0:T(8,128)(2,1)} %get-tuple-element.178.x_hbm.u3, bf16[3,18,64,512]{3,2,1,0:T(8,128)(2,1)} %second_back.1.x_hbm.g_hbm, f32[512,384]{1,0:T(8,128)} %get-tuple-element.215.refs_0_, ...), custom_call_target="tpu_custom_call" | custom-call | flops 301989888 | bytes 625000 | tf_op jit(solution)/shard_map/wgrad_second/pallas_call | solution.py:1262
  318.3 1.9 collective-permute-start.92
  322.0 2.8 collective-permute-done.93
  327.5 4.3 first_norm_back.1.g_hbm.x_hbm
  331.8 9.0 %wgrad_first.1 = (bf16[4,4,576,128]{3,2,1,0:T(8,128)(2,1)}, bf16[4,4,576,128]{3,2,1,0:T(8,128)(2,1)}) custom-call(s32[7]{0:T(128)} %stack.133.idx.idx_ref, bf16[3,18,64,512]{3,2,1,0:T(8,128)(2,1)} %shift_copies.1.x_hbm, bf16[3,18,64,512]{3,2,1,0:T(8,128)(2,1)} %first_norm_back.1.g_hbm.x_hbm), custom_call_target="tpu_custom_call" | custom-call | flops 301989888 | bytes 625000 | tf_op jit(solution)/shard_map/wgrad_first/pallas_call | solution.py:1262
  344.3 1.9 collective-permute-start.97
  349.9 5.7 %collective-permute-done.98 = bf16[2,672,128]{2,1,0:T(8,128)(2,1)S(1)} collective-permute-done((bf16[2,672,128]{2,1,0:T(8,128)(2,1)S(1)}, bf16[2,672,128]{2,1,0:T(8,128)(2,1)S(1)}, u32[]{:S(2)}, u32[]{:S(2)}) %collective-permute-start.98) | collective-permute-done | bytes 344096 | tf_op jit(solution)/shard_map/ppermute | solution.py:54
  360.1 9.4 %conv_first_back.1 = bf16[16,64,512]{2,1,0:T(8,128)(2,1)} custom-call(s32[7]{0:T(128)} %stack.133.idx.idx_ref, bf16[3,18,64,512]{3,2,1,0:T(8,128)(2,1)} %first_norm_back.1.g_hbm.x_hbm, bf16[2,9,64,128]{3,2,1,0:T(8,128)(2,1)} %copy-done.5, bf16[2,9,64,128]{3,2,1,0:T(8,128)(2,1)} %collective-permute-done.3.refs_1_, bf16[2,9,64,128]{3,2,1,0:T(8,128)(2,1)} %copy-done.7, ...), custom_call_target="tpu_custom_call" | custom-call | flops 301989888 | bytes 625000 | tf_op jit(solution)/shard_map/conv_first_back/pallas_call | solution.py:504
  375.4 1.8 fusion.20
  377.2 1.9 fusion.12
  381.8 1.8 fusion.11
  383.6 5.5 %collective-permute-done.106 = bf16[672,128]{1,0:T(8,128)(2,1)S(1)} collective-permute-done((bf16[672,128]{1,0:T(8,128)(2,1)S(1)}, bf16[672,128]{1,0:T(8,128)(2,1)S(1)}, u32[]{:S(2)}, u32[]{:S(2)}) %collective-permute-start.106) | collective-permute-done | bytes 172064 | tf_op jit(solution)/shard_map/ppermute | solution.py:54
  393.6 3.7 shampoo_conv.5
  397.3 2.7 collective-permute-done.109
  404.6 3.9 shampoo_conv.6
  408.5 3.7 shampoo_conv.7
  413.6 1.8 collective-permute-start.113
  416.2 1.9 collective-permute-start.115
  419.4 3.8 shampoo_conv.8
  425.0 1.9 collective-permute-start.120
  433.0 3.7 shampoo_conv.9
  438.1 7.4 %shampoo_proj.1 = (f32[3,2,4,128,128]{4,3,2,1,0:T(8,128)}, f32[3,2,4,128,128]{4,3,2,1,0:T(8,128)}, f32[3,2,4,128,128]{4,3,2,1,0:T(8,128)}, f32[3,2,4,128,128]{4,3,2,1,0:T(8,128)}) custom-call(bf16[3,2,4,128,128]{4,3,2,1,0:T(8,128)(2,1)} %bitcast.317, f32[3,2,4,128,128]{4,3,2,1,0:T(8,128)} %left.11, f32[3,2,4,128,128]{4,3,2,1,0:T(8,128)} %right.11, ...), custom_call_target="tpu_custom_call" | custom-call | flops 25165824 | bytes 884736 | tf_op jit(solution)/shard_map/shampoo_proj/pallas_call | solution.py:1384
  (468 shorter events, 140.8 us)
Async XLA Ops:
  7.2 175.6 %all-gather.3.cloned.1.call-start = ((), (), s32[]{:S(2)}) async-start(), calls=%async_computation.4 | async-start | bytes 7520256 | tf_op jit(solution)/shard_map/all_gather | solution.py:1531
  8.3 9.9 %collective-permute-start.1 = (bf16[64,512]{1,0:T(8,128)(2,1)S(1)}, bf16[64,512]{1,0:T(8,128)(2,1)S(1)}, u32[]{:S(2)}, u32[]{:S(2)}) collective-permute-start(bf16[64,512]{1,0:T(8,128)(2,1)S(1)} %bitcast.351), channel_id=1, source_target_pairs={{0,2},{2,0},{4,6},{6,4},{1,3},{3,1},{5,7},{7,5},{8,10},{10,8},{12,... | collective-permute-start | bytes 196616 | tf_op jit(solution)/shard_map/ppermute | solution.py:83
  14.3 10.6 %collective-permute-start = (bf16[1,9,64,128]{3,2,1,0:T(8,128)(2,1)S(1)}, bf16[1,9,64,128]{3,2,1,0:T(8,128)(2,1)S(1)}, u32[]{:S(2)}, u32[]{:S(2)}) collective-permute-start(bf16[1,9,64,128]{3,2,1,0:T(8,128)(2,1)S(1)} %get-tuple-element.292), channel_id=1, source_target_pairs={{0,4},{2,6},{4,0},{6,2},{1,5},{3,7},{5,1},{7,3},{8,12},{10,14},{12... | collective-permute-start | bytes 442376 | tf_op jit(solution)/shard_map/ppermute | solution.py:54
  26.5 7.3 %collective-permute-start.6 = (bf16[2,9,64,128]{3,2,1,0:T(8,128)(2,1)S(1)}, bf16[2,9,64,128]{3,2,1,0:T(8,128)(2,1)}, u32[]{:S(2)}, u32[]{:S(2)}) collective-permute-start(bf16[2,9,64,128]{3,2,1,0:T(8,128)(2,1)S(1)} %pad_maximum_fusion.9.refs_0_), channel_id=1, source_target_pairs={{0,16},{8,24},{16,0},{24,8},{1,17},{9,25},{17,1},{25,9},{2,18},{10... | collective-permute-start | bytes 884744 | tf_op jit(solution)/shard_map/ppermute | solution.py:54
  29.1 10.1 %collective-permute-start.10 = (bf16[18,4,512]{2,1,0:T(4,128)(2,1)S(1)}, bf16[18,4,512]{2,1,0:T(4,128)(2,1)}, u32[]{:S(2)}, u32[]{:S(2)}) collective-permute-start(bf16[18,4,512]{2,1,0:T(4,128)(2,1)S(1)} %maximum_select_fusion), channel_id=1, source_target_pairs={{0,1},{1,0},{2,3},{3,2},{4,5},{5,4},{6,7},{7,6},{8,9},{9,8},{10,11... | collective-permute-start | bytes 221192 | tf_op jit(solution)/shard_map/ppermute | solution.py:54
  30.3 21.8 %collective-permute-start.12 = (bf16[2,9,64,128]{3,2,1,0:T(8,128)(2,1)S(1)}, bf16[2,9,64,128]{3,2,1,0:T(8,128)(2,1)S(1)}, u32[]{:S(2)}, u32[]{:S(2)}) collective-permute-start(bf16[2,9,64,128]{3,2,1,0:T(8,128)(2,1)S(1)} %pad_maximum_fusion.9.refs_0_), channel_id=1, source_target_pairs={{0,1},{1,0},{2,3},{3,2},{4,5},{5,4},{6,7},{7,6},{8,9},{9,8},{10,11... | collective-permute-start | bytes 884744 | tf_op jit(solution)/shard_map/ppermute | solution.py:54
  33.8 12.1 %collective-permute-start.7 = (bf16[2,9,64,128]{3,2,1,0:T(8,128)(2,1)}, bf16[2,9,64,128]{3,2,1,0:T(8,128)(2,1)S(1)}, u32[]{:S(2)}, u32[]{:S(2)}) collective-permute-start(bf16[2,9,64,128]{3,2,1,0:T(8,128)(2,1)} %collective-permute-done.3.refs_1_), channel_id=1, source_target_pairs={{0,16},{8,24},{16,0},{24,8},{1,17},{9,25},{17,1},{25,9},{2,18},{10... | collective-permute-start | bytes 884744 | tf_op jit(solution)/shard_map/ppermute | solution.py:54
  35.3 10.6 %collective-permute-start.8 = (bf16[2,9,64,128]{3,2,1,0:T(8,128)(2,1)}, bf16[2,9,64,128]{3,2,1,0:T(8,128)(2,1)S(1)}, u32[]{:S(2)}, u32[]{:S(2)}) collective-permute-start(bf16[2,9,64,128]{3,2,1,0:T(8,128)(2,1)} %collective-permute-done.3.refs_1_), channel_id=1, source_target_pairs={{0,8},{8,0},{16,24},{24,16},{1,9},{9,1},{17,25},{25,17},{2,10},{10... | collective-permute-start | bytes 884744 | tf_op jit(solution)/shard_map/ppermute | solution.py:54
  35.9 10.1 %collective-permute-start.4 = (bf16[1,9,64,128]{3,2,1,0:T(8,128)(2,1)}, bf16[1,9,64,128]{3,2,1,0:T(8,128)(2,1)S(1)}, u32[]{:S(2)}, u32[]{:S(2)}) collective-permute-start(bf16[1,9,64,128]{3,2,1,0:T(8,128)(2,1)} %get-tuple-element.149), channel_id=1, source_target_pairs={{0,4},{2,6},{4,0},{6,2},{1,5},{3,7},{5,1},{7,3},{8,12},{10,14},{12... | collective-permute-start | bytes 442376 | tf_op jit(solution)/shard_map/ppermute | solution.py:54
  53.9 14.8 %collective-permute-start.20 = (bf16[2,9,64,128]{3,2,1,0:T(8,128)(2,1)S(1)}, bf16[2,9,64,128]{3,2,1,0:T(8,128)(2,1)}, u32[]{:S(2)}, u32[]{:S(2)}) collective-permute-start(bf16[2,9,64,128]{3,2,1,0:T(8,128)(2,1)S(1)} %pad_maximum_fusion.10.refs_0_), channel_id=1, source_target_pairs={{0,2},{2,0},{4,6},{6,4},{1,3},{3,1},{5,7},{7,5},{8,10},{10,8},{12,... | collective-permute-start | bytes 884744 | tf_op jit(solution)/shard_map/ppermute | solution.py:54
  54.2 14.6 %collective-permute-start.21 = (bf16[2,9,64,128]{3,2,1,0:T(8,128)(2,1)S(1)}, bf16[2,9,64,128]{3,2,1,0:T(8,128)(2,1)}, u32[]{:S(2)}, u32[]{:S(2)}) collective-permute-start(bf16[2,9,64,128]{3,2,1,0:T(8,128)(2,1)S(1)} %pad_maximum_fusion.10.refs_0_), channel_id=1, source_target_pairs={{0,8},{8,0},{16,24},{24,16},{1,9},{9,1},{17,25},{25,17},{2,10},{10... | collective-permute-start | bytes 884744 | tf_op jit(solution)/shard_map/ppermute | solution.py:54
  55.7 13.1 %collective-permute-start.22 = (bf16[2,9,64,128]{3,2,1,0:T(8,128)(2,1)S(1)}, bf16[2,9,64,128]{3,2,1,0:T(8,128)(2,1)}, u32[]{:S(2)}, u32[]{:S(2)}) collective-permute-start(bf16[2,9,64,128]{3,2,1,0:T(8,128)(2,1)S(1)} %pad_maximum_fusion.10.refs_0_), channel_id=1, source_target_pairs={{0,16},{8,24},{16,0},{24,8},{1,17},{9,25},{17,1},{25,9},{2,18},{10... | collective-permute-start | bytes 884744 | tf_op jit(solution)/shard_map/ppermute | solution.py:54
  68.8 157.9 %reduce-scatter.3.cloned.1.call-start = ((), (), s32[]{:S(2)}) async-start(), calls=%async_computation.2 | async-start | bytes 21233664 | tf_op jit(solution)/shard_map/reduce_scatter | solution.py:1589
  69.6 26.0 %collective-permute-start.33 = (bf16[2,9,64,128]{3,2,1,0:T(8,128)(2,1)}, bf16[2,9,64,128]{3,2,1,0:T(8,128)(2,1)S(1)}, u32[]{:S(2)}, u32[]{:S(2)}) collective-permute-start(bf16[2,9,64,128]{3,2,1,0:T(8,128)(2,1)} %collective-permute-done.20.refs_1_), channel_id=1, source_target_pairs={{0,8},{8,0},{16,24},{24,16},{1,9},{9,1},{17,25},{25,17},{2,10},{10... | collective-permute-start | bytes 884744 | tf_op jit(solution)/shard_map/ppermute | solution.py:54
  70.3 25.3 %collective-permute-start.34 = (bf16[2,9,64,128]{3,2,1,0:T(8,128)(2,1)}, bf16[2,9,64,128]{3,2,1,0:T(8,128)(2,1)}, u32[]{:S(2)}, u32[]{:S(2)}) collective-permute-start(bf16[2,9,64,128]{3,2,1,0:T(8,128)(2,1)} %collective-permute-done.20.refs_1_), channel_id=1, source_target_pairs={{0,16},{8,24},{16,0},{24,8},{1,17},{9,25},{17,1},{25,9},{2,18},{10... | collective-permute-start | bytes 884744 | tf_op jit(solution)/shard_map/ppermute | solution.py:54
  96.9 16.4 %collective-permute-start.43 = (bf16[2,9,64,128]{3,2,1,0:T(8,128)(2,1)}, bf16[2,9,64,128]{3,2,1,0:T(8,128)(2,1)}, u32[]{:S(2)}, u32[]{:S(2)}) collective-permute-start(bf16[2,9,64,128]{3,2,1,0:T(8,128)(2,1)} %collective-permute-done.34.refs_5_), channel_id=1, source_target_pairs={{0,8},{8,0},{16,24},{24,16},{1,9},{9,1},{17,25},{25,17},{2,10},{10... | collective-permute-start | bytes 884744 | tf_op jit(solution)/shard_map/ppermute | solution.py:54
  100.0 13.3 %collective-permute-start.41 = (bf16[2,9,64,128]{3,2,1,0:T(8,128)(2,1)}, bf16[2,9,64,128]{3,2,1,0:T(8,128)(2,1)}, u32[]{:S(2)}, u32[]{:S(2)}) collective-permute-start(bf16[2,9,64,128]{3,2,1,0:T(8,128)(2,1)} %collective-permute-done.21.refs_2_), channel_id=1, source_target_pairs={{0,16},{8,24},{16,0},{24,8},{1,17},{9,25},{17,1},{25,9},{2,18},{10... | collective-permute-start | bytes 884744 | tf_op jit(solution)/shard_map/ppermute | solution.py:54
  101.9 13.4 %collective-permute-start.61 = (bf16[3,10,4,1,512]{4,3,2,1,0:T(2,128)(2,1)}, bf16[3,10,4,1,512]{4,3,2,1,0:T(2,128)(2,1)S(1)}, u32[]{:S(2)}, u32[]{:S(2)}) collective-permute-start(bf16[3,10,4,1,512]{4,3,2,1,0:T(2,128)(2,1)} %broadcast_select_fusion.2), channel_id=1, source_target_pairs={{0,1},{1,0},{2,3},{3,2},{4,5},{5,4},{6,7},{7,6},{8,9},{9,8},{10,11... | collective-permute-start | bytes 368648 | tf_op jit(solution)/shard_map/ppermute | solution.py:54
  117.1 13.7 %collective-permute-start.46 = (f32[2,384]{1,0:T(2,128)S(1)}, f32[2,384]{1,0:T(2,128)S(1)}, u32[]{:S(2)}, u32[]{:S(2)}) collective-permute-start(f32[2,384]{1,0:T(2,128)S(1)} %add.316), channel_id=1, source_target_pairs={{0,8},{8,0},{16,24},{24,16},{1,9},{9,1},{17,25},{25,17},{2,10},{10... | collective-permute-start | bytes 9224 | tf_op jit(solution)/shard_map/ppermute | solution.py:54
  118.5 12.3 %collective-permute-start.47 = (f32[2,384]{1,0:T(2,128)S(1)}, f32[2,384]{1,0:T(2,128)S(1)}, u32[]{:S(2)}, u32[]{:S(2)}) collective-permute-start(f32[2,384]{1,0:T(2,128)S(1)} %add.316), channel_id=1, source_target_pairs={{0,16},{8,24},{16,0},{24,8},{1,17},{9,25},{17,1},{25,9},{2,18},{10... | collective-permute-start | bytes 9224 | tf_op jit(solution)/shard_map/ppermute | solution.py:54
  119.2 11.6 %collective-permute-start.48 = (f32[2,384]{1,0:T(2,128)S(1)}, f32[2,384]{1,0:T(2,128)S(1)}, u32[]{:S(2)}, u32[]{:S(2)}) collective-permute-start(f32[2,384]{1,0:T(2,128)S(1)} %add.316), channel_id=1, source_target_pairs={{0,24},{8,16},{16,8},{24,0},{1,25},{9,17},{17,9},{25,1},{2,26},{10... | collective-permute-start | bytes 9224 | tf_op jit(solution)/shard_map/ppermute | solution.py:54
  130.9 10.6 %collective-permute-start.49 = (f32[2,384]{1,0:T(2,128)S(1)}, f32[2,384]{1,0:T(2,128)S(1)}, u32[]{:S(2)}, u32[]{:S(2)}) collective-permute-start(f32[2,384]{1,0:T(2,128)S(1)} %add_add_fusion.11), channel_id=1, source_target_pairs={{0,2},{2,0},{4,6},{6,4},{1,3},{3,1},{5,7},{7,5},{8,10},{10,8},{12,... | collective-permute-start | bytes 9224 | tf_op jit(solution)/shard_map/ppermute | solution.py:54
  150.6 9.3 %collective-permute-start.56 = (bf16[64,512]{1,0:T(8,128)(2,1)S(1)}, bf16[64,512]{1,0:T(8,128)(2,1)S(1)}, u32[]{:S(2)}, u32[]{:S(2)}) collective-permute-start(bf16[64,512]{1,0:T(8,128)(2,1)S(1)} %get-tuple-element.318), channel_id=1, source_target_pairs={{0,2},{2,0},{4,6},{6,4},{1,3},{3,1},{5,7},{7,5},{8,10},{10,8},{12,... | collective-permute-start | bytes 196616 | tf_op jit(solution)/shard_map/ppermute | solution.py:83
  150.8 9.1 %collective-permute-start.57 = (bf16[64,512]{1,0:T(8,128)(2,1)S(1)}, bf16[64,512]{1,0:T(8,128)(2,1)S(1)}, u32[]{:S(2)}, u32[]{:S(2)}) collective-permute-start(bf16[64,512]{1,0:T(8,128)(2,1)S(1)} %get-tuple-element.319), channel_id=1, source_target_pairs={{0,0},{2,4},{4,2},{6,6},{1,1},{3,5},{5,3},{7,7},{8,8},{10,12},{12,... | collective-permute-start | bytes 196616 | tf_op jit(solution)/shard_map/ppermute | solution.py:83
  162.3 8.0 %collective-permute-start.62 = (f32[8,512]{1,0:T(8,128)S(1)}, f32[8,512]{1,0:T(8,128)S(1)}, u32[]{:S(2)}, u32[]{:S(2)}) collective-permute-start(f32[8,512]{1,0:T(8,128)S(1)} %add_add_fusion.3), channel_id=1, source_target_pairs={{0,2},{2,0},{4,6},{6,4},{1,3},{3,1},{5,7},{7,5},{8,10},{10,8},{12,... | collective-permute-start | bytes 49160 | tf_op jit(solution)/shard_map/ppermute | solution.py:54
  182.8 11.7 %collective-permute-start.65 = (bf16[16,27,64,128]{3,2,1,0:T(8,128)(2,1)}, bf16[16,27,64,128]{3,2,1,0:T(8,128)(2,1)}, u32[]{:S(2)}, u32[]{:S(2)}) collective-permute-start(bf16[16,27,64,128]{3,2,1,0:T(8,128)(2,1)} %bitcast.309), channel_id=1, source_target_pairs={{0,1},{1,0},{2,3},{3,2},{4,5},{5,4},{6,7},{7,6},{8,9},{9,8},{10,11... | collective-permute-start | bytes 21233672 | tf_op jit(solution)/shard_map/ppermute | solution.py:54
  194.5 195.8 %reduce-scatter.5.cloned.1.call-start = ((), (), s32[]{:S(2)}) async-start(), calls=%async_computation.3 | async-start | bytes 7520256 | tf_op jit(solution)/shard_map/reduce_scatter | solution.py:1599
  227.7 13.6 %collective-permute-start.70 = (bf16[64,512]{1,0:T(8,128)(2,1)S(1)}, bf16[64,512]{1,0:T(8,128)(2,1)S(1)}, u32[]{:S(2)}, u32[]{:S(2)}) collective-permute-start(bf16[64,512]{1,0:T(8,128)(2,1)S(1)} %get-tuple-element.312), channel_id=1, source_target_pairs={{0,2},{2,0},{4,6},{6,4},{1,3},{3,1},{5,7},{7,5},{8,10},{10,8},{12,... | collective-permute-start | bytes 196616 | tf_op jit(solution)/shard_map/ppermute | solution.py:83
  229.2 12.1 %collective-permute-start.71 = (bf16[64,512]{1,0:T(8,128)(2,1)S(1)}, bf16[64,512]{1,0:T(8,128)(2,1)S(1)}, u32[]{:S(2)}, u32[]{:S(2)}) collective-permute-start(bf16[64,512]{1,0:T(8,128)(2,1)S(1)} %get-tuple-element.313), channel_id=1, source_target_pairs={{0,0},{2,4},{4,2},{6,6},{1,1},{3,5},{5,3},{7,7},{8,8},{10,12},{12,... | collective-permute-start | bytes 196616 | tf_op jit(solution)/shard_map/ppermute | solution.py:83
  232.7 8.5 %collective-permute-start.68 = (f32[14,512]{1,0:T(8,128)S(1)}, f32[14,512]{1,0:T(8,128)S(1)}, u32[]{:S(2)}, u32[]{:S(2)}) collective-permute-start(f32[14,512]{1,0:T(8,128)S(1)} %add.330), channel_id=1, source_target_pairs={{0,4},{2,6},{4,0},{6,2},{1,5},{3,7},{5,1},{7,3},{8,12},{10,14},{12... | collective-permute-start | bytes 86024 | tf_op jit(solution)/shard_map/ppermute | solution.py:54
  233.6 7.6 %collective-permute-start.69 = (f32[14,512]{1,0:T(8,128)S(1)}, f32[14,512]{1,0:T(8,128)S(1)}, u32[]{:S(2)}, u32[]{:S(2)}) collective-permute-start(f32[14,512]{1,0:T(8,128)S(1)} %add.330), channel_id=1, source_target_pairs={{0,6},{2,4},{4,2},{6,0},{1,7},{3,5},{5,3},{7,1},{8,14},{10,12},{12... | collective-permute-start | bytes 86024 | tf_op jit(solution)/shard_map/ppermute | solution.py:54
  260.9 9.2 %collective-permute-start.77 = (f32[2,384]{1,0:T(2,128)S(1)}, f32[2,384]{1,0:T(2,128)S(1)}, u32[]{:S(2)}, u32[]{:S(2)}) collective-permute-start(f32[2,384]{1,0:T(2,128)S(1)} %add.337), channel_id=1, source_target_pairs={{0,2},{2,0},{4,6},{6,4},{1,3},{3,1},{5,7},{7,5},{8,10},{10,8},{12,... | collective-permute-start | bytes 9224 | tf_op jit(solution)/shard_map/ppermute | solution.py:54
  262.6 7.5 %collective-permute-start.78 = (f32[2,384]{1,0:T(2,128)S(1)}, f32[2,384]{1,0:T(2,128)S(1)}, u32[]{:S(2)}, u32[]{:S(2)}) collective-permute-start(f32[2,384]{1,0:T(2,128)S(1)} %add.337), channel_id=1, source_target_pairs={{0,4},{2,6},{4,0},{6,2},{1,5},{3,7},{5,1},{7,3},{8,12},{10,14},{12... | collective-permute-start | bytes 9224 | tf_op jit(solution)/shard_map/ppermute | solution.py:54
  270.1 13.2 %collective-permute-start.80 = (f32[2,384]{1,0:T(2,128)S(1)}, f32[2,384]{1,0:T(2,128)S(1)}, u32[]{:S(2)}, u32[]{:S(2)}) collective-permute-start(f32[2,384]{1,0:T(2,128)S(1)} %add_add_fusion.9), channel_id=1, source_target_pairs={{0,8},{8,0},{16,24},{24,16},{1,9},{9,1},{17,25},{25,17},{2,10},{10... | collective-permute-start | bytes 9224 | tf_op jit(solution)/shard_map/ppermute | solution.py:54
  271.3 12.0 %collective-permute-start.81 = (f32[2,384]{1,0:T(2,128)S(1)}, f32[2,384]{1,0:T(2,128)S(1)}, u32[]{:S(2)}, u32[]{:S(2)}) collective-permute-start(f32[2,384]{1,0:T(2,128)S(1)} %add_add_fusion.9), channel_id=1, source_target_pairs={{0,16},{8,24},{16,0},{24,8},{1,17},{9,25},{17,1},{25,9},{2,18},{10... | collective-permute-start | bytes 9224 | tf_op jit(solution)/shard_map/ppermute | solution.py:54
  273.5 9.8 %collective-permute-start.82 = (f32[2,384]{1,0:T(2,128)S(1)}, f32[2,384]{1,0:T(2,128)S(1)}, u32[]{:S(2)}, u32[]{:S(2)}) collective-permute-start(f32[2,384]{1,0:T(2,128)S(1)} %add_add_fusion.9), channel_id=1, source_target_pairs={{0,24},{8,16},{16,8},{24,0},{1,25},{9,17},{17,9},{25,1},{2,26},{10... | collective-permute-start | bytes 9224 | tf_op jit(solution)/shard_map/ppermute | solution.py:54
  293.4 20.9 %collective-permute-start.87 = (bf16[64,512]{1,0:T(8,128)(2,1)S(1)}, bf16[64,512]{1,0:T(8,128)(2,1)S(1)}, u32[]{:S(2)}, u32[]{:S(2)}) collective-permute-start(bf16[64,512]{1,0:T(8,128)(2,1)S(1)} %get-tuple-element.306), channel_id=1, source_target_pairs={{0,2},{2,0},{4,6},{6,4},{1,3},{3,1},{5,7},{7,5},{8,10},{10,8},{12,... | collective-permute-start | bytes 196616 | tf_op jit(solution)/shard_map/ppermute | solution.py:83
  294.5 19.9 %collective-permute-start.88 = (bf16[64,512]{1,0:T(8,128)(2,1)S(1)}, bf16[64,512]{1,0:T(8,128)(2,1)S(1)}, u32[]{:S(2)}, u32[]{:S(2)}) collective-permute-start(bf16[64,512]{1,0:T(8,128)(2,1)S(1)} %get-tuple-element.307), channel_id=1, source_target_pairs={{0,0},{2,4},{4,2},{6,6},{1,1},{3,5},{5,3},{7,7},{8,8},{10,12},{12,... | collective-permute-start | bytes 196616 | tf_op jit(solution)/shard_map/ppermute | solution.py:83
  298.7 15.6 %collective-permute-start.84 = (f32[2,512]{1,0:T(2,128)S(1)}, f32[2,512]{1,0:T(2,128)S(1)}, u32[]{:S(2)}, u32[]{:S(2)}) collective-permute-start(f32[2,512]{1,0:T(2,128)S(1)} %add.344), channel_id=1, source_target_pairs={{0,2},{2,0},{4,6},{6,4},{1,3},{3,1},{5,7},{7,5},{8,10},{10,8},{12,... | collective-permute-start | bytes 12296 | tf_op jit(solution)/shard_map/ppermute | solution.py:54
  302.1 12.2 %collective-permute-start.85 = (f32[2,512]{1,0:T(2,128)S(1)}, f32[2,512]{1,0:T(2,128)S(1)}, u32[]{:S(2)}, u32[]{:S(2)}) collective-permute-start(f32[2,512]{1,0:T(2,128)S(1)} %add.344), channel_id=1, source_target_pairs={{0,4},{2,6},{4,0},{6,2},{1,5},{3,7},{5,1},{7,3},{8,12},{10,14},{12... | collective-permute-start | bytes 12296 | tf_op jit(solution)/shard_map/ppermute | solution.py:54
  302.5 11.9 %collective-permute-start.86 = (f32[2,512]{1,0:T(2,128)S(1)}, f32[2,512]{1,0:T(2,128)S(1)}, u32[]{:S(2)}, u32[]{:S(2)}) collective-permute-start(f32[2,512]{1,0:T(2,128)S(1)} %add.344), channel_id=1, source_target_pairs={{0,6},{2,4},{4,2},{6,0},{1,7},{3,5},{5,3},{7,1},{8,14},{10,12},{12... | collective-permute-start | bytes 12296 | tf_op jit(solution)/shard_map/ppermute | solution.py:54
  316.8 8.6 %collective-permute-start.90 = (bf16[4,4,672,128]{3,2,1,0:T(8,128)(2,1)}, bf16[4,4,672,128]{3,2,1,0:T(8,128)(2,1)S(1)}, u32[]{:S(2)}, u32[]{:S(2)}) collective-permute-start(bf16[4,4,672,128]{3,2,1,0:T(8,128)(2,1)} %get-tuple-element.222), channel_id=1, source_target_pairs={{0,1},{1,0},{2,3},{3,2},{4,5},{5,4},{6,7},{7,6},{8,9},{9,8},{10,11... | collective-permute-start | bytes 8257544 | tf_op jit(solution)/shard_map/ppermute | solution.py:54
  326.7 14.1 %collective-permute-start.95 = (bf16[2,672,128]{2,1,0:T(8,128)(2,1)S(1)}, bf16[2,672,128]{2,1,0:T(8,128)(2,1)S(1)}, u32[]{:S(2)}, u32[]{:S(2)}) collective-permute-start(bf16[2,672,128]{2,1,0:T(8,128)(2,1)S(1)} %get-tuple-element.294), channel_id=1, source_target_pairs={{0,16},{8,24},{16,0},{24,8},{1,17},{9,25},{17,1},{25,9},{2,18},{10... | collective-permute-start | bytes 1032200 | tf_op jit(solution)/shard_map/ppermute | solution.py:54
  326.9 14.0 %collective-permute-start.94 = (bf16[2,672,128]{2,1,0:T(8,128)(2,1)S(1)}, bf16[2,672,128]{2,1,0:T(8,128)(2,1)S(1)}, u32[]{:S(2)}, u32[]{:S(2)}) collective-permute-start(bf16[2,672,128]{2,1,0:T(8,128)(2,1)S(1)} %get-tuple-element.295), channel_id=1, source_target_pairs={{0,8},{8,0},{16,24},{24,16},{1,9},{9,1},{17,25},{25,17},{2,10},{10... | collective-permute-start | bytes 1032200 | tf_op jit(solution)/shard_map/ppermute | solution.py:54
  341.7 13.9 %collective-permute-start.98 = (bf16[2,672,128]{2,1,0:T(8,128)(2,1)S(1)}, bf16[2,672,128]{2,1,0:T(8,128)(2,1)S(1)}, u32[]{:S(2)}, u32[]{:S(2)}) collective-permute-start(bf16[2,672,128]{2,1,0:T(8,128)(2,1)S(1)} %fusion.14), channel_id=1, source_target_pairs={{0,16},{8,24},{16,0},{24,8},{1,17},{9,25},{17,1},{25,9},{2,18},{10... | collective-permute-start | bytes 1032200 | tf_op jit(solution)/shard_map/ppermute | solution.py:54
  344.3 11.3 %collective-permute-start.97 = (bf16[2,672,128]{2,1,0:T(8,128)(2,1)S(1)}, bf16[2,672,128]{2,1,0:T(8,128)(2,1)S(1)}, u32[]{:S(2)}, u32[]{:S(2)}) collective-permute-start(bf16[2,672,128]{2,1,0:T(8,128)(2,1)S(1)} %fusion.8), channel_id=1, source_target_pairs={{0,8},{8,0},{16,24},{24,16},{1,9},{9,1},{17,25},{25,17},{2,10},{10... | collective-permute-start | bytes 1032200 | tf_op jit(solution)/shard_map/ppermute | solution.py:54
  347.9 21.6 %collective-permute-start.103 = (bf16[2,672,128]{2,1,0:T(8,128)(2,1)}, bf16[2,672,128]{2,1,0:T(8,128)(2,1)}, u32[]{:S(2)}, u32[]{:S(2)}) collective-permute-start(bf16[2,672,128]{2,1,0:T(8,128)(2,1)} %fusion.7), channel_id=1, source_target_pairs={{0,16},{8,24},{16,0},{24,8},{1,17},{9,25},{17,1},{25,9},{2,18},{10... | collective-permute-start | bytes 1032200 | tf_op jit(solution)/shard_map/ppermute | solution.py:54
  348.0 21.5 %collective-permute-start.102 = (bf16[2,672,128]{2,1,0:T(8,128)(2,1)}, bf16[2,672,128]{2,1,0:T(8,128)(2,1)}, u32[]{:S(2)}, u32[]{:S(2)}) collective-permute-start(bf16[2,672,128]{2,1,0:T(8,128)(2,1)} %fusion.15), channel_id=1, source_target_pairs={{0,8},{8,0},{16,24},{24,16},{1,9},{9,1},{17,25},{25,17},{2,10},{10... | collective-permute-start | bytes 1032200 | tf_op jit(solution)/shard_map/ppermute | solution.py:54
  356.5 13.0 %collective-permute-start.101 = (bf16[2,672,128]{2,1,0:T(8,128)(2,1)}, bf16[2,672,128]{2,1,0:T(8,128)(2,1)}, u32[]{:S(2)}, u32[]{:S(2)}) collective-permute-start(bf16[2,672,128]{2,1,0:T(8,128)(2,1)} %fusion.6), channel_id=1, source_target_pairs={{0,2},{2,0},{4,6},{6,4},{1,3},{3,1},{5,7},{7,5},{8,10},{10,8},{12,... | collective-permute-start | bytes 1032200 | tf_op jit(solution)/shard_map/ppermute | solution.py:54
  358.5 11.0 %collective-permute-start.100 = (bf16[2,576,128]{2,1,0:T(8,128)(2,1)}, bf16[2,576,128]{2,1,0:T(8,128)(2,1)}, u32[]{:S(2)}, u32[]{:S(2)}) collective-permute-start(bf16[2,576,128]{2,1,0:T(8,128)(2,1)} %get-tuple-element.296), channel_id=1, source_target_pairs={{0,16},{8,24},{16,0},{24,8},{1,17},{9,25},{17,1},{25,9},{2,18},{10... | collective-permute-start | bytes 884744 | tf_op jit(solution)/shard_map/ppermute | solution.py:54
  358.8 10.7 %collective-permute-start.99 = (bf16[2,576,128]{2,1,0:T(8,128)(2,1)}, bf16[2,576,128]{2,1,0:T(8,128)(2,1)}, u32[]{:S(2)}, u32[]{:S(2)}) collective-permute-start(bf16[2,576,128]{2,1,0:T(8,128)(2,1)} %get-tuple-element.297), channel_id=1, source_target_pairs={{0,8},{8,0},{16,24},{24,16},{1,9},{9,1},{17,25},{25,17},{2,10},{10... | collective-permute-start | bytes 884744 | tf_op jit(solution)/shard_map/ppermute | solution.py:54
  372.9 8.7 %collective-permute-start.104 = (bf16[2,576,128]{2,1,0:T(8,128)(2,1)S(1)}, bf16[2,576,128]{2,1,0:T(8,128)(2,1)S(1)}, u32[]{:S(2)}, u32[]{:S(2)}) collective-permute-start(bf16[2,576,128]{2,1,0:T(8,128)(2,1)S(1)} %fusion.13), channel_id=1, source_target_pairs={{0,8},{8,0},{16,24},{24,16},{1,9},{9,1},{17,25},{25,17},{2,10},{10... | collective-permute-start | bytes 884744 | tf_op jit(solution)/shard_map/ppermute | solution.py:54
  373.9 7.8 %collective-permute-start.105 = (bf16[2,576,128]{2,1,0:T(8,128)(2,1)S(1)}, bf16[2,576,128]{2,1,0:T(8,128)(2,1)S(1)}, u32[]{:S(2)}, u32[]{:S(2)}) collective-permute-start(bf16[2,576,128]{2,1,0:T(8,128)(2,1)S(1)} %fusion.19), channel_id=1, source_target_pairs={{0,16},{8,24},{16,0},{24,8},{1,17},{9,25},{17,1},{25,9},{2,18},{10... | collective-permute-start | bytes 884744 | tf_op jit(solution)/shard_map/ppermute | solution.py:54
  379.1 10.0 %collective-permute-start.106 = (bf16[672,128]{1,0:T(8,128)(2,1)S(1)}, bf16[672,128]{1,0:T(8,128)(2,1)S(1)}, u32[]{:S(2)}, u32[]{:S(2)}) collective-permute-start(bf16[672,128]{1,0:T(8,128)(2,1)S(1)} %fusion.18), channel_id=1, source_target_pairs={{0,4},{2,6},{4,0},{6,2},{1,5},{3,7},{5,1},{7,3},{8,12},{10,14},{12... | collective-permute-start | bytes 516104 | tf_op jit(solution)/shard_map/ppermute | solution.py:54
  390.4 9.6 %collective-permute-start.109 = (bf16[2,576,128]{2,1,0:T(8,128)(2,1)}, bf16[2,576,128]{2,1,0:T(8,128)(2,1)S(1)}, u32[]{:S(2)}, u32[]{:S(2)}) collective-permute-start(bf16[2,576,128]{2,1,0:T(8,128)(2,1)} %fusion.12), channel_id=1, source_target_pairs={{0,16},{8,24},{16,0},{24,8},{1,17},{9,25},{17,1},{25,9},{2,18},{10... | collective-permute-start | bytes 884744 | tf_op jit(solution)/shard_map/ppermute | solution.py:54
  391.6 9.3 %collective-permute-start.108 = (bf16[2,576,128]{2,1,0:T(8,128)(2,1)}, bf16[2,576,128]{2,1,0:T(8,128)(2,1)S(1)}, u32[]{:S(2)}, u32[]{:S(2)}) collective-permute-start(bf16[2,576,128]{2,1,0:T(8,128)(2,1)} %fusion.20), channel_id=1, source_target_pairs={{0,8},{8,0},{16,24},{24,16},{1,9},{9,1},{17,25},{25,17},{2,10},{10... | collective-permute-start | bytes 884744 | tf_op jit(solution)/shard_map/ppermute | solution.py:54
  392.9 9.0 %collective-permute-start.110 = (bf16[2,576,128]{2,1,0:T(8,128)(2,1)}, bf16[2,576,128]{2,1,0:T(8,128)(2,1)S(1)}, u32[]{:S(2)}, u32[]{:S(2)}) collective-permute-start(bf16[2,576,128]{2,1,0:T(8,128)(2,1)} %fusion.11), channel_id=1, source_target_pairs={{0,2},{2,0},{4,6},{6,4},{1,3},{3,1},{5,7},{7,5},{8,10},{10,8},{12,... | collective-permute-start | bytes 884744 | tf_op jit(solution)/shard_map/ppermute | solution.py:54
  402.9 9.3 %collective-permute-start.111 = (bf16[576,128]{1,0:T(8,128)(2,1)S(1)}, bf16[576,128]{1,0:T(8,128)(2,1)S(1)}, u32[]{:S(2)}, u32[]{:S(2)}) collective-permute-start(bf16[576,128]{1,0:T(8,128)(2,1)S(1)} %fusion.23), channel_id=1, source_target_pairs={{0,4},{2,6},{4,0},{6,2},{1,5},{3,7},{5,1},{7,3},{8,12},{10,14},{12... | collective-permute-start | bytes 442376 | tf_op jit(solution)/shard_map/ppermute | solution.py:54
  413.6 9.6 %collective-permute-start.113 = (bf16[1,2,96,128]{3,2,1,0:T(8,128)(2,1)S(1)}, bf16[1,2,96,128]{3,2,1,0:T(8,128)(2,1)S(1)}, u32[]{:S(2)}, u32[]{:S(2)}) collective-permute-start(bf16[1,2,96,128]{3,2,1,0:T(8,128)(2,1)S(1)} %maximum_bitcast_fusion.1), channel_id=1, source_target_pairs={{0,2},{2,0},{4,6},{6,4},{1,3},{3,1},{5,7},{7,5},{8,10},{10,8},{12,... | collective-permute-start | bytes 147464 | tf_op jit(solution)/shard_map/ppermute | solution.py:54
  415.4 7.8 %collective-permute-start.114 = (bf16[1,2,96,128]{3,2,1,0:T(8,128)(2,1)S(1)}, bf16[1,2,96,128]{3,2,1,0:T(8,128)(2,1)S(1)}, u32[]{:S(2)}, u32[]{:S(2)}) collective-permute-start(bf16[1,2,96,128]{3,2,1,0:T(8,128)(2,1)S(1)} %maximum_bitcast_fusion.1), channel_id=1, source_target_pairs={{0,4},{2,6},{4,0},{6,2},{1,5},{3,7},{5,1},{7,3},{8,12},{10,14},{12... | collective-permute-start | bytes 147464 | tf_op jit(solution)/shard_map/ppermute | solution.py:54
  419.4 12.9 %collective-permute-start.116 = (bf16[576,128]{1,0:T(8,128)(2,1)S(1)}, bf16[576,128]{1,0:T(8,128)(2,1)S(1)}, u32[]{:S(2)}, u32[]{:S(2)}) collective-permute-start(bf16[576,128]{1,0:T(8,128)(2,1)S(1)} %fusion.22.mine), channel_id=1, source_target_pairs={{0,1},{1,0},{2,3},{3,2},{4,5},{5,4},{6,7},{7,6},{8,9},{9,8},{10,11... | collective-permute-start | bytes 442376 | tf_op jit(solution)/shard_map/ppermute | solution.py:54
  423.3 13.3 %collective-permute-start.118 = (bf16[1,4,2,96,128]{4,3,2,1,0:T(8,128)(2,1)S(1)}, bf16[1,4,2,96,128]{4,3,2,1,0:T(8,128)(2,1)S(1)}, u32[]{:S(2)}, u32[]{:S(2)}) collective-permute-start(bf16[1,4,2,96,128]{4,3,2,1,0:T(8,128)(2,1)S(1)} %bitcast.322), channel_id=1, source_target_pairs={{0,8},{8,0},{16,24},{24,16},{1,9},{9,1},{17,25},{25,17},{2,10},{10... | collective-permute-start | bytes 589832 | tf_op jit(solution)/shard_map/ppermute | solution.py:54
  424.2 12.5 %collective-permute-start.119 = (bf16[1,4,2,96,128]{4,3,2,1,0:T(8,128)(2,1)S(1)}, bf16[1,4,2,96,128]{4,3,2,1,0:T(8,128)(2,1)S(1)}, u32[]{:S(2)}, u32[]{:S(2)}) collective-permute-start(bf16[1,4,2,96,128]{4,3,2,1,0:T(8,128)(2,1)S(1)} %bitcast.323), channel_id=1, source_target_pairs={{0,16},{8,24},{16,0},{24,8},{1,17},{9,25},{17,1},{25,9},{2,18},{10... | collective-permute-start | bytes 589832 | tf_op jit(solution)/shard_map/ppermute | solution.py:54
  425.0 11.7 %collective-permute-start.120 = (bf16[1,4,2,96,128]{4,3,2,1,0:T(8,128)(2,1)S(1)}, bf16[1,4,2,96,128]{4,3,2,1,0:T(8,128)(2,1)S(1)}, u32[]{:S(2)}, u32[]{:S(2)}) collective-permute-start(bf16[1,4,2,96,128]{4,3,2,1,0:T(8,128)(2,1)S(1)} %bitcast.324), channel_id=1, source_target_pairs={{0,24},{8,16},{16,8},{24,0},{1,25},{9,17},{17,9},{25,1},{2,26},{10... | collective-permute-start | bytes 589832 | tf_op jit(solution)/shard_map/ppermute | solution.py:54
  (107 other events, 609.8 us)
Sparse Core Ops, SparseCore 0:
  68.9 107.3 all-gather.2
  194.7 21.3 reduce-scatter.2
  226.9 160.0 reduce-scatter.4
